TPU v7x, 32 devices: a whole 2x2x4 slice. The times are simulated.
32 devices in a mesh: grp: 2 (over x), seq: 16 (over z, y, core).
Axes of the slice: x: 2, y: 2, z: 4, core: 2. Of those that a mesh axis runs over, the one named last changes fastest.
Arguments:
- signal: bfloat16 [32768, 768], P(('grp', 'seq')), parts along dimension 0, may hold values from -6 to 6
- dilated_tap_weight: bfloat16 [4, 3, 768, 384], replicated, may hold values from -0.125 to 0.125
- point_weight: bfloat16 [4, 384, 768], replicated, may hold values from -0.3125 to 0.3125
Outputs:
- activations: bfloat16 [4, 32768, 768], P(None, ('grp', 'seq')), parts along dimension 1
There are 2 independent parts, one for each index of `grp`. A program takes and returns all parts, laid end to end along the dimension named above; an argument that names none is the same for every part. Nothing has to cross between parts.
All inputs are finite; a program needn't handle non-finite values.
Results may differ from a plain program's by a relative error of at most 0.0075.
Values may be sent and summed in bfloat16 or wider, within the bound.
No kernel may reach another device: no remote copies, remote signals or barrier semaphores. Data moves between devices by JAX's collectives and lax.ppermute only.
A program may use at most 64 MiB of HBM per device.

v0:
```python
import jax
import jax.numpy as jnp
from jax import lax
from jax.sharding import PartitionSpec as P

FIRST_DILATION = 256


def passed_along(value, axis, by):
    size = lax.axis_size(axis)
    pairs = [(i, i + by) for i in range(size) if 0 <= i + by < size]
    return lax.ppermute(value, axis, pairs)


def move_sides(lower_tap_source, high_source, dilation_step):
    length = lower_tap_source.shape[0]
    if dilation_step < length:
        lower = passed_along(lower_tap_source[length - dilation_step :], "seq", 1)
        upper = passed_along(high_source[:dilation_step], "seq", -1)
        lower_neighbour_rows = jnp.concatenate(
            [lower, lower_tap_source[: length - dilation_step]], axis=0
        )
        above_side = jnp.concatenate([high_source[dilation_step:], upper], axis=0)
        return (lower_neighbour_rows, above_side)
    distance = dilation_step // length
    lower_neighbour_rows = passed_along(lower_tap_source, "seq", distance)
    above_side = passed_along(high_source, "seq", -distance)
    return (lower_neighbour_rows, above_side)


def shards(signal, dilated_tap_weight, point_weight):
    current = signal
    outputs = []
    for block_layer_index in range(dilated_tap_weight.shape[0]):
        dilation_step = FIRST_DILATION * 2**block_layer_index
        low_terms = jnp.dot(
            current, dilated_tap_weight[block_layer_index, 0], preferred_element_type=jnp.float32
        ).astype(jnp.bfloat16)
        upper_tap_terms = jnp.dot(
            current, dilated_tap_weight[block_layer_index, 2], preferred_element_type=jnp.float32
        ).astype(jnp.bfloat16)
        below_terms, above_terms = move_sides(low_terms, upper_tap_terms, dilation_step)
        convolved = jnp.dot(
            current, dilated_tap_weight[block_layer_index, 1], preferred_element_type=jnp.float32
        )
        convolved = convolved + below_terms.astype(jnp.float32)
        convolved = convolved + above_terms.astype(jnp.float32)
        hidden = jax.nn.gelu(convolved, approximate=True).astype(jnp.bfloat16)
        residual_branch = jnp.dot(
            hidden, point_weight[block_layer_index], preferred_element_type=jnp.float32
        )
        current = (current.astype(jnp.float32) + residual_branch).astype(jnp.bfloat16)
        outputs.append(current)
    return jnp.stack(outputs)


def solution(mesh):
    in_specs = (P(("grp", "seq"), None), P(), P())
    out_specs = P(None, ("grp", "seq"), None)
    return jax.shard_map(shards, mesh=mesh, in_specs=in_specs, out_specs=out_specs, check_vma=False)
```

profile of v0, /device:TPU:1, one launch (start us, length us, event | category | flops | bytes accessed | tf_op | source)
XLA Modules:
  0.0 127.2 jit_solution(15200863757853966297)
XLA Ops:
  0.0 2.6 %convolution_convert_fusion.6 = bf16[1024,384]{1,0:T(8,128)(2,1)S(1)} fusion(bf16[1024,768]{1,0:T(8,128)(2,1)} %param.3, bf16[4,3,768,384]{3,2,1,0:T(8,128)(2,1)} %param.4), kind=kOutput, calls=%fused_computation.48 | convolution fusion | flops 604372992 | bytes 2949120 | tf_op jit(solution)/shard_map/dot_general | solution.py:39
  2.7 2.0 %collective-permute-start.1 = (bf16[256,384]{1,0:T(8,128)(2,1)S(1)}, bf16[256,384]{1,0:T(8,128)(2,1)S(1)}, u32[]{:S(2)}, u32[]{:S(2)}) collective-permute-start(bf16[256,384]{1,0:T(8,128)(2,1)S(1)} %slice.99), channel_id=1, source_target_pairs={{1,0},{2,1},{3,2},{4,3},{5,4},{6,5},{7,6},{8,7},{9,8},{10,9},{11,1... | collective-permute-start | bytes 589832 | tf_op jit(solution)/shard_map/ppermute | solution.py:12
  4.6 2.0 %convolution_convert_fusion.7 = bf16[1024,384]{1,0:T(8,128)(2,1)S(1)} fusion(bf16[1024,768]{1,0:T(8,128)(2,1)S(1)} %copy-done.1, bf16[4,3,768,384]{3,2,1,0:T(8,128)(2,1)} %param.4), kind=kOutput, calls=%fused_computation.49 | convolution fusion | flops 604372992 | bytes 2949120 | tf_op jit(solution)/shard_map/dot_general | solution.py:36
  6.7 4.5 %collective-permute-start = (bf16[256,384]{1,0:T(8,128)(2,1)S(1)}, bf16[256,384]{1,0:T(8,128)(2,1)S(1)}, u32[]{:S(2)}, u32[]{:S(2)}) collective-permute-start(bf16[256,384]{1,0:T(8,128)(2,1)S(1)} %slice.96), channel_id=1, source_target_pairs={{0,1},{1,2},{2,3},{3,4},{4,5},{5,6},{6,7},{7,8},{8,9},{9,10},{10,1... | collective-permute-start | bytes 589832 | tf_op jit(solution)/shard_map/ppermute | solution.py:12
  11.2 0.1 slice.98
  11.4 2.4 %collective-permute-done = bf16[256,384]{1,0:T(8,128)(2,1)S(1)} collective-permute-done((bf16[256,384]{1,0:T(8,128)(2,1)S(1)}, bf16[256,384]{1,0:T(8,128)(2,1)S(1)}, u32[]{:S(2)}, u32[]{:S(2)}) %collective-permute-start) | collective-permute-done | bytes 196640 | tf_op jit(solution)/shard_map/ppermute | solution.py:12
  13.8 4.3 %add_convert_fusion.3 = bf16[1024,768]{1,0:T(8,128)(2,1)S(1)} fusion(bf16[1024,768]{1,0:T(8,128)(2,1)} %param.3, bf16[768,384]{1,0:T(8,128)(2,1)S(1)} %slice.97, bf16[256,384]{1,0:T(8,128)(2,1)S(1)} %collective-permute-done, bf16[256,384]{1,0:T(8,128)(2,1)S(1)} %collective-permute-done.1, bf16[768,384]{1,0:T(8,128)(2,1)S(1)} %slice.98, ...), kind=kOutput, calls=%fused_computation.4 | convolution fusion | flops 1217789952 | bytes 7471104 | tf_op jit(solution)/shard_map/dot_general | solution.py:49
  18.1 2.0 %convolution_convert_fusion.5 = bf16[1024,384]{1,0:T(8,128)(2,1)S(1)} fusion(bf16[1024,768]{1,0:T(8,128)(2,1)S(1)} %add_convert_fusion.3, bf16[4,3,768,384]{3,2,1,0:T(8,128)(2,1)} %param.4), kind=kOutput, calls=%fused_computation.47 | convolution fusion | flops 604372992 | bytes 2949120 | tf_op jit(solution)/shard_map/dot_general | solution.py:36
  20.1 2.0 %convolution_convert_fusion.4 = bf16[1024,384]{1,0:T(8,128)(2,1)S(1)} fusion(bf16[1024,768]{1,0:T(8,128)(2,1)S(1)} %add_convert_fusion.3, bf16[4,3,768,384]{3,2,1,0:T(8,128)(2,1)} %param.4), kind=kOutput, calls=%fused_computation.46 | convolution fusion | flops 604372992 | bytes 2949120 | tf_op jit(solution)/shard_map/dot_general | solution.py:39
  22.2 0.1 fusion.140
  22.3 4.4 %collective-permute-start.2 = (bf16[512,384]{1,0:T(8,128)(2,1)S(1)}, bf16[512,384]{1,0:T(8,128)(2,1)S(1)}, u32[]{:S(2)}, u32[]{:S(2)}) collective-permute-start(bf16[512,384]{1,0:T(8,128)(2,1)S(1)} %get-tuple-element.7), channel_id=1, source_target_pairs={{0,1},{1,2},{2,3},{3,4},{4,5},{5,6},{6,7},{7,8},{8,9},{9,10},{10,1... | collective-permute-start | bytes 1179656 | tf_op jit(solution)/shard_map/ppermute | solution.py:12
  26.7 0.8 fusion.139
  27.5 1.9 %collective-permute-start.3 = (bf16[512,384]{1,0:T(8,128)(2,1)S(1)}, bf16[512,384]{1,0:T(8,128)(2,1)S(1)}, u32[]{:S(2)}, u32[]{:S(2)}) collective-permute-start(bf16[512,384]{1,0:T(8,128)(2,1)S(1)} %get-tuple-element.6), channel_id=1, source_target_pairs={{1,0},{2,1},{3,2},{4,3},{5,4},{6,5},{7,6},{8,7},{9,8},{10,9},{11,1... | collective-permute-start | bytes 1179656 | tf_op jit(solution)/shard_map/ppermute | solution.py:12
  29.4 2.0 %collective-permute-done.2 = bf16[512,384]{1,0:T(8,128)(2,1)S(1)} collective-permute-done((bf16[512,384]{1,0:T(8,128)(2,1)S(1)}, bf16[512,384]{1,0:T(8,128)(2,1)S(1)}, u32[]{:S(2)}, u32[]{:S(2)}) %collective-permute-start.2) | collective-permute-done | bytes 393248 | tf_op jit(solution)/shard_map/ppermute | solution.py:12
  31.4 5.2 %collective-permute-done.3 = bf16[512,384]{1,0:T(8,128)(2,1)S(1)} collective-permute-done((bf16[512,384]{1,0:T(8,128)(2,1)S(1)}, bf16[512,384]{1,0:T(8,128)(2,1)S(1)}, u32[]{:S(2)}, u32[]{:S(2)}) %collective-permute-start.3) | collective-permute-done | bytes 393248 | tf_op jit(solution)/shard_map/ppermute | solution.py:12
  36.6 0.7 copy-done.3
  37.3 3.6 %add_convert_fusion.2 = bf16[1024,768]{1,0:T(8,128)(2,1)S(1)} fusion(bf16[1024,768]{1,0:T(8,128)(2,1)S(1)} %add_convert_fusion.3, bf16[512,384]{1,0:T(8,128)(2,1)S(1)} %get-tuple-element.8, bf16[512,384]{1,0:T(8,128)(2,1)} %copy-done.2, bf16[512,384]{1,0:T(8,128)(2,1)} %copy-done.3, bf16[512,384]{1,0:T(8,128)(2,1)} %get-tuple-element.5, ...), kind=kOutput, calls=%fused_computation.3 | convolution fusion | flops 1217789952 | bytes 7471104 | tf_op jit(solution)/shard_map/dot_general | solution.py:49
  40.9 2.0 %convolution_convert_fusion.3 = bf16[1024,384]{1,0:T(8,128)(2,1)S(1)} fusion(bf16[1024,768]{1,0:T(8,128)(2,1)S(1)} %add_convert_fusion.2, bf16[4,3,768,384]{3,2,1,0:T(8,128)(2,1)} %param.4), kind=kOutput, calls=%fused_computation.45 | convolution fusion | flops 604372992 | bytes 2949120 | tf_op jit(solution)/shard_map/dot_general | solution.py:36
  43.0 2.0 %convolution_convert_fusion.2 = bf16[1024,384]{1,0:T(8,128)(2,1)S(1)} fusion(bf16[1024,768]{1,0:T(8,128)(2,1)S(1)} %add_convert_fusion.2, bf16[4,3,768,384]{3,2,1,0:T(8,128)(2,1)} %param.4), kind=kOutput, calls=%fused_computation.44 | convolution fusion | flops 604372992 | bytes 2949120 | tf_op jit(solution)/shard_map/dot_general | solution.py:39
  45.0 1.9 %collective-permute-start.5 = (bf16[1024,384]{1,0:T(8,128)(2,1)S(1)}, bf16[1024,384]{1,0:T(8,128)(2,1)}, u32[]{:S(2)}, u32[]{:S(2)}) collective-permute-start(bf16[1024,384]{1,0:T(8,128)(2,1)S(1)} %convolution_convert_fusion.2), channel_id=1, source_target_pairs={{1,0},{2,1},{3,2},{4,3},{5,4},{6,5},{7,6},{8,7},{9,8},{10,9},{11,1... | collective-permute-start | bytes 2359304 | tf_op jit(solution)/shard_map/ppermute | solution.py:12
  47.0 3.6 %collective-permute-start.4 = (bf16[1024,384]{1,0:T(8,128)(2,1)S(1)}, bf16[1024,384]{1,0:T(8,128)(2,1)}, u32[]{:S(2)}, u32[]{:S(2)}) collective-permute-start(bf16[1024,384]{1,0:T(8,128)(2,1)S(1)} %convolution_convert_fusion.3), channel_id=1, source_target_pairs={{0,1},{1,2},{2,3},{3,4},{4,5},{5,6},{6,7},{7,8},{8,9},{9,10},{10,1... | collective-permute-start | bytes 2359304 | tf_op jit(solution)/shard_map/ppermute | solution.py:12
  50.6 7.8 %collective-permute-done.5 = bf16[1024,384]{1,0:T(8,128)(2,1)} collective-permute-done((bf16[1024,384]{1,0:T(8,128)(2,1)S(1)}, bf16[1024,384]{1,0:T(8,128)(2,1)}, u32[]{:S(2)}, u32[]{:S(2)}) %collective-permute-start.5) | collective-permute-done | bytes 786464 | tf_op jit(solution)/shard_map/ppermute | solution.py:12
  58.5 9.5 %collective-permute-done.4 = bf16[1024,384]{1,0:T(8,128)(2,1)} collective-permute-done((bf16[1024,384]{1,0:T(8,128)(2,1)S(1)}, bf16[1024,384]{1,0:T(8,128)(2,1)}, u32[]{:S(2)}, u32[]{:S(2)}) %collective-permute-start.4) | collective-permute-done | bytes 786464 | tf_op jit(solution)/shard_map/ppermute | solution.py:12
  68.0 4.9 %add_convert_fusion.1 = bf16[1024,768]{1,0:T(8,128)(2,1)} fusion(bf16[1024,768]{1,0:T(8,128)(2,1)S(1)} %add_convert_fusion.2, bf16[1024,384]{1,0:T(8,128)(2,1)} %collective-permute-done.5, bf16[1024,384]{1,0:T(8,128)(2,1)} %collective-permute-done.4, bf16[4,384,768]{2,1,0:T(8,128)(2,1)} %param.5, bf16[4,3,768,384]{3,2,1,0:T(8,128)(2,1)} %param.4), kind=kOutput, calls=%fused_computation.2 | convolution fusion | flops 1215430656 | bytes 7471104 | tf_op jit(solution)/shard_map/dot_general | solution.py:49
  72.9 2.6 %convolution_convert_fusion.1 = bf16[1024,384]{1,0:T(8,128)(2,1)S(1)} fusion(bf16[1024,768]{1,0:T(8,128)(2,1)} %add_convert_fusion.1, bf16[4,3,768,384]{3,2,1,0:T(8,128)(2,1)} %param.4), kind=kOutput, calls=%fused_computation.43 | convolution fusion | flops 604372992 | bytes 2949120 | tf_op jit(solution)/shard_map/dot_general | solution.py:36
  75.5 2.0 %convolution_convert_fusion = bf16[1024,384]{1,0:T(8,128)(2,1)S(1)} fusion(bf16[1024,768]{1,0:T(8,128)(2,1)S(1)} %copy-done, bf16[4,3,768,384]{3,2,1,0:T(8,128)(2,1)} %param.4), kind=kOutput, calls=%fused_computation.42 | convolution fusion | flops 604372992 | bytes 2949120 | tf_op jit(solution)/shard_map/dot_general | solution.py:39
  77.6 1.3 %collective-permute-start.7 = (bf16[1024,384]{1,0:T(8,128)(2,1)S(1)}, bf16[1024,384]{1,0:T(8,128)(2,1)}, u32[]{:S(2)}, u32[]{:S(2)}) collective-permute-start(bf16[1024,384]{1,0:T(8,128)(2,1)S(1)} %convolution_convert_fusion), channel_id=1, source_target_pairs={{2,0},{3,1},{4,2},{5,3},{6,4},{7,5},{8,6},{9,7},{10,8},{11,9},{12,... | collective-permute-start | bytes 2359304 | tf_op jit(solution)/shard_map/ppermute | solution.py:12
  78.9 4.9 %collective-permute-start.6 = (bf16[1024,384]{1,0:T(8,128)(2,1)S(1)}, bf16[1024,384]{1,0:T(8,128)(2,1)}, u32[]{:S(2)}, u32[]{:S(2)}) collective-permute-start(bf16[1024,384]{1,0:T(8,128)(2,1)S(1)} %convolution_convert_fusion.1), channel_id=1, source_target_pairs={{0,2},{1,3},{2,4},{3,5},{4,6},{5,7},{6,8},{7,9},{8,10},{9,11},{10,... | collective-permute-start | bytes 2359304 | tf_op jit(solution)/shard_map/ppermute | solution.py:12
  83.7 13.9 %collective-permute-done.7 = bf16[1024,384]{1,0:T(8,128)(2,1)} collective-permute-done((bf16[1024,384]{1,0:T(8,128)(2,1)S(1)}, bf16[1024,384]{1,0:T(8,128)(2,1)}, u32[]{:S(2)}, u32[]{:S(2)}) %collective-permute-start.7) | collective-permute-done | bytes 786464 | tf_op jit(solution)/shard_map/ppermute | solution.py:12
  97.6 18.6 %collective-permute-done.6 = bf16[1024,384]{1,0:T(8,128)(2,1)} collective-permute-done((bf16[1024,384]{1,0:T(8,128)(2,1)S(1)}, bf16[1024,384]{1,0:T(8,128)(2,1)}, u32[]{:S(2)}, u32[]{:S(2)}) %collective-permute-start.6) | collective-permute-done | bytes 786464 | tf_op jit(solution)/shard_map/ppermute | solution.py:12
  116.3 5.9 %fusion.32 = bf16[1,1024,768]{2,1,0:T(8,128)(2,1)} fusion(bf16[1024,768]{1,0:T(8,128)(2,1)} %add_convert_fusion.1, bf16[1024,384]{1,0:T(8,128)(2,1)} %collective-permute-done.7, bf16[1024,384]{1,0:T(8,128)(2,1)} %collective-permute-done.6, bf16[4,384,768]{2,1,0:T(8,128)(2,1)} %param.5, bf16[4,3,768,384]{3,2,1,0:T(8,128)(2,1)} %param.4), kind=kOutput, calls=%fused_computation.41 | convolution fusion | flops 1215430656 | bytes 7471104 | tf_op jit(solution)/shard_map/dot_general | solution.py:49
  122.2 5.1 %pad_maximum_fusion = bf16[4,1024,768]{2,1,0:T(8,128)(2,1)} fusion(bf16[1,1024,768]{2,1,0:T(8,128)(2,1)} %fusion.32, bf16[1,1024,768]{2,1,0:T(8,128)(2,1)} %bitcast.83, bf16[1,1024,768]{2,1,0:T(8,128)(2,1)S(1)} %bitcast.82, bf16[1,1024,768]{2,1,0:T(8,128)(2,1)S(1)} %bitcast.81), kind=kLoop, calls=%fused_computation | loop fusion | flops 9437184 | bytes 12582912 | tf_op jit(solution)/shard_map/stack | solution.py:54
  (11 shorter events, 0.1 us)
Async XLA Ops:
  0.0 4.6 %copy-start.1 = (bf16[1024,768]{1,0:T(8,128)(2,1)S(1)}, bf16[1024,768]{1,0:T(8,128)(2,1)}, u32[]{:S(2)}) copy-start(bf16[1024,768]{1,0:T(8,128)(2,1)} %param.3) | copy-start | bytes 4718596
  2.7 8.7 %collective-permute-start.1 = (bf16[256,384]{1,0:T(8,128)(2,1)S(1)}, bf16[256,384]{1,0:T(8,128)(2,1)S(1)}, u32[]{:S(2)}, u32[]{:S(2)}) collective-permute-start(bf16[256,384]{1,0:T(8,128)(2,1)S(1)} %slice.99), channel_id=1, source_target_pairs={{1,0},{2,1},{3,2},{4,3},{5,4},{6,5},{7,6},{8,7},{9,8},{10,9},{11,1... | collective-permute-start | bytes 589832 | tf_op jit(solution)/shard_map/ppermute | solution.py:12
  6.7 7.1 %collective-permute-start = (bf16[256,384]{1,0:T(8,128)(2,1)S(1)}, bf16[256,384]{1,0:T(8,128)(2,1)S(1)}, u32[]{:S(2)}, u32[]{:S(2)}) collective-permute-start(bf16[256,384]{1,0:T(8,128)(2,1)S(1)} %slice.96), channel_id=1, source_target_pairs={{0,1},{1,2},{2,3},{3,4},{4,5},{5,6},{6,7},{7,8},{8,9},{9,10},{10,1... | collective-permute-start | bytes 589832 | tf_op jit(solution)/shard_map/ppermute | solution.py:12
  22.3 9.1 %collective-permute-start.2 = (bf16[512,384]{1,0:T(8,128)(2,1)S(1)}, bf16[512,384]{1,0:T(8,128)(2,1)S(1)}, u32[]{:S(2)}, u32[]{:S(2)}) collective-permute-start(bf16[512,384]{1,0:T(8,128)(2,1)S(1)} %get-tuple-element.7), channel_id=1, source_target_pairs={{0,1},{1,2},{2,3},{3,4},{4,5},{5,6},{6,7},{7,8},{8,9},{9,10},{10,1... | collective-permute-start | bytes 1179656 | tf_op jit(solution)/shard_map/ppermute | solution.py:12
  27.5 9.1 %collective-permute-start.3 = (bf16[512,384]{1,0:T(8,128)(2,1)S(1)}, bf16[512,384]{1,0:T(8,128)(2,1)S(1)}, u32[]{:S(2)}, u32[]{:S(2)}) collective-permute-start(bf16[512,384]{1,0:T(8,128)(2,1)S(1)} %get-tuple-element.6), channel_id=1, source_target_pairs={{1,0},{2,1},{3,2},{4,3},{5,4},{6,5},{7,6},{8,7},{9,8},{10,9},{11,1... | collective-permute-start | bytes 1179656 | tf_op jit(solution)/shard_map/ppermute | solution.py:12
  31.4 5.2 %copy-start.2 = (bf16[512,384]{1,0:T(8,128)(2,1)}, bf16[512,384]{1,0:T(8,128)(2,1)S(1)}, u32[]{:S(2)}) copy-start(bf16[512,384]{1,0:T(8,128)(2,1)S(1)} %collective-permute-done.2) | copy-start | bytes 1179652
  36.6 0.7 copy-start.3
  45.0 13.4 %collective-permute-start.5 = (bf16[1024,384]{1,0:T(8,128)(2,1)S(1)}, bf16[1024,384]{1,0:T(8,128)(2,1)}, u32[]{:S(2)}, u32[]{:S(2)}) collective-permute-start(bf16[1024,384]{1,0:T(8,128)(2,1)S(1)} %convolution_convert_fusion.2), channel_id=1, source_target_pairs={{1,0},{2,1},{3,2},{4,3},{5,4},{6,5},{7,6},{8,7},{9,8},{10,9},{11,1... | collective-permute-start | bytes 2359304 | tf_op jit(solution)/shard_map/ppermute | solution.py:12
  47.0 21.0 %collective-permute-start.4 = (bf16[1024,384]{1,0:T(8,128)(2,1)S(1)}, bf16[1024,384]{1,0:T(8,128)(2,1)}, u32[]{:S(2)}, u32[]{:S(2)}) collective-permute-start(bf16[1024,384]{1,0:T(8,128)(2,1)S(1)} %convolution_convert_fusion.3), channel_id=1, source_target_pairs={{0,1},{1,2},{2,3},{3,4},{4,5},{5,6},{6,7},{7,8},{8,9},{9,10},{10,1... | collective-permute-start | bytes 2359304 | tf_op jit(solution)/shard_map/ppermute | solution.py:12
  72.9 2.6 %copy-start = (bf16[1024,768]{1,0:T(8,128)(2,1)S(1)}, bf16[1024,768]{1,0:T(8,128)(2,1)}, u32[]{:S(2)}) copy-start(bf16[1024,768]{1,0:T(8,128)(2,1)} %add_convert_fusion.1) | copy-start | bytes 4718596
  77.6 20.1 %collective-permute-start.7 = (bf16[1024,384]{1,0:T(8,128)(2,1)S(1)}, bf16[1024,384]{1,0:T(8,128)(2,1)}, u32[]{:S(2)}, u32[]{:S(2)}) collective-permute-start(bf16[1024,384]{1,0:T(8,128)(2,1)S(1)} %convolution_convert_fusion), channel_id=1, source_target_pairs={{2,0},{3,1},{4,2},{5,3},{6,4},{7,5},{8,6},{9,7},{10,8},{11,9},{12,... | collective-permute-start | bytes 2359304 | tf_op jit(solution)/shard_map/ppermute | solution.py:12
  78.9 37.4 %collective-permute-start.6 = (bf16[1024,384]{1,0:T(8,128)(2,1)S(1)}, bf16[1024,384]{1,0:T(8,128)(2,1)}, u32[]{:S(2)}, u32[]{:S(2)}) collective-permute-start(bf16[1024,384]{1,0:T(8,128)(2,1)S(1)} %convolution_convert_fusion.1), channel_id=1, source_target_pairs={{0,2},{1,3},{2,4},{3,5},{4,6},{5,7},{6,8},{7,9},{8,10},{9,11},{10,... | collective-permute-start | bytes 2359304 | tf_op jit(solution)/shard_map/ppermute | solution.py:12
where the time goes:
time: 128 us; the launch traced here: 127 us
  waiting for transfers between devices  59.5 us (46%)
  matrix products  36.2 us (28%)
  starting transfers between devices  24.5 us (19%)
  other arithmetic  5.08 us (4%)
  local copies, waits for them, and re-layouts  1.82 us (1%)
    ppermute x8, waiting for transfers between devices, passed_along(): return lax.ppermute(value, axis, pairs)  59.5 us
    ppermute x8, starting transfers between devices, passed_along(): return lax.ppermute(value, axis, pairs)  24.5 us
    dot_general x4, matrix products, shards(): jnp.dot(hidden, point_weight[block_layer_index], preferred_element_type=j...  18.7 us
    dot_general x4, matrix products, shards(): jnp.dot(current, dilated_tap_weight[block_layer_index, 2], preferred_elem...  8.74 us
    dot_general x4, matrix products, shards(): jnp.dot(current, dilated_tap_weight[block_layer_index, 0], preferred_elem...  8.73 us
    another operation x1, other arithmetic, shards(): return jnp.stack(outputs)  5.08 us
  transfers between devices with their start and end apart: 8, of which 7 were waited for; matrix products, arithmetic and copies ran while one was open for 2% of the time, Pallas kernels for 0%

commit v1 on v0

v1 whole, which is shorter than its diff:
```python
import functools

import jax
import jax.numpy as jnp
from jax import lax
from jax.experimental import pallas as pl
from jax.experimental.pallas import tpu as pltpu
from jax.sharding import PartitionSpec as P

FIRST_DILATION = 256
GROUP = 4
CHUNKS = 1
ROWS = 256
VMEM_LIMIT = 40 * 2**20

F32, BF16 = jnp.float32, jnp.bfloat16
ANY = pl.BlockSpec(memory_space=pl.ANY)
VMEM = pl.BlockSpec(memory_space=pltpu.VMEM)
SMEM = pl.BlockSpec(memory_space=pltpu.SMEM)


def dot(a, b):
    return jnp.dot(a, b, preferred_element_type=F32)


def gelu(v):
    return 0.5 * v * (1.0 + jnp.tanh(0.7978845608028654 * (v + 0.044715 * (v * v * v))))


def over_rows(rows, body):
    whole = rows // ROWS

    def step(i, _):
        body(pl.multiple_of(i * ROWS, ROWS), ROWS)
        return 0

    if whole:
        lax.fori_loop(0, whole, step, 0)
    if rows % ROWS:
        body(whole * ROWS, rows % ROWS)


def start_all(copies):
    for copy in copies:
        copy.start()
    return copies


def wait_all(copies):
    for copy in copies:
        copy.wait()


def params():
    return pltpu.CompilerParams(vmem_limit_bytes=VMEM_LIMIT)


def cost(flops, bytes_accessed):
    return pl.CostEstimate(flops=int(flops), bytes_accessed=int(bytes_accessed), transcendentals=0)


def tap_copies(taps_hbm, block, taps, w_ref, sems, first):
    width = taps_hbm.shape[3]
    return [
        pltpu.make_async_copy(
            taps_hbm.at[block, tap], w_ref.at[:, pl.ds(i * width, width)], sems.at[first + i]
        )
        for i, tap in enumerate(taps)
    ]


def all_taps(x_ref, w_ref, low_ref, mid_ref, high_ref, rows, low_at=0):
    width = mid_ref.shape[1]

    def body(start, size):
        terms = dot(x_ref[pl.ds(start, size)], w_ref[...])
        low_ref[pl.ds(start + low_at, size)] = terms[:, :width].astype(BF16)
        mid_ref[pl.ds(start, size)] = terms[:, width : 2 * width]
        high_ref[pl.ds(start, size)] = terms[:, 2 * width :].astype(BF16)

    over_rows(rows, body)


def edges_kernel(halo, s_ref, own, r1, r2, r3, even_ref, odd_ref, sem):
    q, parity = s_ref[0], s_ref[1]
    rows = own.shape[0]

    def move(source, target):
        copy = pltpu.make_async_copy(source, target, sem)
        copy.start()
        copy.wait()

    for k, piece in enumerate((own, r1, r2, r3)):
        j = q ^ k
        top = piece.at[pl.ds(rows - halo, halo)]
        bottom = piece.at[pl.ds(0, halo)]
        for at, going_up, going_down in ((0, even_ref, odd_ref), (1, odd_ref, even_ref)):
            pl.when((j == GROUP - 1) & (parity == at))(functools.partial(move, top, going_up))
            pl.when((j == 0) & (parity == at))(functools.partial(move, bottom, going_down))


def edges(scalars, pieces, halo):
    shape = jax.ShapeDtypeStruct((halo, pieces[0].shape[1]), BF16)
    return pl.pallas_call(
        functools.partial(edges_kernel, halo),
        out_shape=(shape, shape),
        in_specs=[SMEM] + [ANY] * GROUP,
        out_specs=(ANY, ANY),
        scratch_shapes=[pltpu.SemaphoreType.DMA],
        compiler_params=params(),
        cost_estimate=cost(0, 4 * shape.size * 2),
    )(scalars, *pieces)


def first_kernel(
    r, s_ref, own, r1, r2, r3, from_even, from_odd, taps_hbm, point_hbm,
    x2_ref, even_ref, odd_ref, g0, g1, g2, g3,
    x0, x1, w0, w1, w2, p0, p1, low, mid, high, h0, h1, sems, wsems,
):
    q, parity, has_lower, has_upper = (s_ref[i] for i in range(4))
    rows = own.shape[0]
    halo = from_even.shape[0]
    length = GROUP * rows
    copies = []
    for k, piece in enumerate((own, r1, r2, r3)):
        at = pl.multiple_of(halo + (q ^ k) * rows, r)
        copies.append(pltpu.make_async_copy(piece, x0.at[pl.ds(at, rows)], sems.at[k]))
    even_at = pl.multiple_of(jnp.where(parity == 0, halo + length, 0), r)
    odd_at = pl.multiple_of(jnp.where(parity == 0, 0, halo + length), r)
    copies.append(pltpu.make_async_copy(from_even, x0.at[pl.ds(even_at, halo)], sems.at[4]))
    copies.append(pltpu.make_async_copy(from_odd, x0.at[pl.ds(odd_at, halo)], sems.at[5]))
    start_all(copies)
    c0 = start_all(tap_copies(taps_hbm, 0, (0, 1, 2), w0, wsems, 0))
    cp0 = pltpu.make_async_copy(point_hbm.at[0], p0, wsems.at[3])
    cp0.start()
    c1 = start_all(tap_copies(taps_hbm, 1, (0, 1, 2), w1, wsems, 4))
    cp1 = pltpu.make_async_copy(point_hbm.at[1], p1, wsems.at[7])
    cp1.start()
    c2 = start_all(tap_copies(taps_hbm, 2, (0, 2), w2, wsems, 8))
    wait_all(copies)

    @pl.when(has_lower == 0)
    def _():
        x0[pl.ds(0, halo)] = jnp.zeros((halo, x0.shape[1]), BF16)

    @pl.when(has_upper == 0)
    def _():
        x0[pl.ds(halo + length, halo)] = jnp.zeros((halo, x0.shape[1]), BF16)

    wait_all(c0)
    all_taps(x0, w0, low, mid, high, length + 2 * halo)
    cp0.wait()
    reach = halo - r

    def block0(start, size):
        v = mid[pl.ds(start + r, size)] + low[pl.ds(start, size)].astype(F32)
        v = v + high[pl.ds(start + 2 * r, size)].astype(F32)
        hidden = gelu(v).astype(BF16)
        h0[pl.ds(start, size)] = hidden
        x1[pl.ds(start, size)] = (
            x0[pl.ds(start + r, size)].astype(F32) + dot(hidden, p0[...])
        ).astype(BF16)

    over_rows(length + 2 * reach, block0)

    @pl.when(has_lower == 0)
    def _():
        x1[pl.ds(0, reach)] = jnp.zeros((reach, x1.shape[1]), BF16)

    @pl.when(has_upper == 0)
    def _():
        x1[pl.ds(reach + length, reach)] = jnp.zeros((reach, x1.shape[1]), BF16)

    wait_all(c1)
    all_taps(x1, w1, low, mid, high, length + 2 * reach)
    cp1.wait()

    def block1(start, size):
        v = mid[pl.ds(start + reach, size)] + low[pl.ds(start, size)].astype(F32)
        v = v + high[pl.ds(start + 2 * reach, size)].astype(F32)
        hidden = gelu(v).astype(BF16)
        h1[pl.ds(start, size)] = hidden
        x2_ref[pl.ds(start, size)] = (
            x1[pl.ds(start + reach, size)].astype(F32) + dot(hidden, p1[...])
        ).astype(BF16)

    over_rows(length, block1)

    wait_all(c2)
    width = even_ref.shape[1]
    send = even_ref.shape[0]
    up = dot(x2_ref[pl.ds(length - send, send)], w2[:, :width])
    down = dot(x2_ref[pl.ds(0, send)], w2[:, width:])
    even_ref[...] = jnp.where(parity == 0, up, down).astype(BF16)
    odd_ref[...] = jnp.where(parity == 0, down, up).astype(BF16)
    for k, piece in enumerate((g0, g1, g2, g3)):
        at = pl.multiple_of((q ^ k) * rows, r)
        piece[0] = h0[pl.ds(reach + at, rows)]
        piece[1] = h1[pl.ds(at, rows)]


def first_blocks(scalars, pieces, from_even, from_odd, taps, point, r):
    rows, c = pieces[0].shape
    h = taps.shape[3]
    halo = from_even.shape[0]
    length = GROUP * rows
    wide = length + 2 * halo
    terms = jax.ShapeDtypeStruct((4 * r, h), BF16)
    piece = jax.ShapeDtypeStruct((2, rows, h), BF16)
    return pl.pallas_call(
        functools.partial(first_kernel, r),
        out_shape=(jax.ShapeDtypeStruct((length, c), BF16), terms, terms) + (piece,) * GROUP,
        in_specs=[SMEM] + [ANY] * (GROUP + 4),
        out_specs=(VMEM,) * (3 + GROUP),
        scratch_shapes=[
            pltpu.VMEM((wide, c), BF16),
            pltpu.VMEM((wide - 2 * r, c), BF16),
            pltpu.VMEM((c, 3 * h), BF16),
            pltpu.VMEM((c, 3 * h), BF16),
            pltpu.VMEM((c, 2 * h), BF16),
            pltpu.VMEM((h, c), BF16),
            pltpu.VMEM((h, c), BF16),
            pltpu.VMEM((wide, h), BF16),
            pltpu.VMEM((wide, h), F32),
            pltpu.VMEM((wide, h), BF16),
            pltpu.VMEM((wide - 2 * r, h), BF16),
            pltpu.VMEM((length, h), BF16),
            pltpu.SemaphoreType.DMA((6,)),
            pltpu.SemaphoreType.DMA((10,)),
        ],
        compiler_params=params(),
        cost_estimate=cost(2 * c * h * (3 * wide + 4 * wide + 2 * length), 10 * 2**20),
    )(scalars, *pieces, from_even, from_odd, taps, point)


def third_kernel(
    r, s_ref, x2, from_even, from_odd, taps_hbm, point_hbm,
    x3_ref, even_ref, odd_ref, g0, g1, g2, g3,
    w2, w3, p2, low, mid, high, h2, wsems,
):
    q, parity, has_lower, has_upper = (s_ref[i] for i in range(4))
    length, rows = x2.shape[0], x2.shape[0] // GROUP
    d = from_even.shape[0]
    width = from_even.shape[1]
    c2 = start_all(tap_copies(taps_hbm, 2, (0, 1, 2), w2, wsems, 0))
    cp2 = pltpu.make_async_copy(point_hbm.at[2], p2, wsems.at[3])
    cp2.start()
    c3 = start_all(tap_copies(taps_hbm, 3, (0, 2), w3, wsems, 4))
    even = from_even[...].astype(F32)
    odd = from_odd[...].astype(F32)
    below = jnp.where(parity == 0, odd, even)
    above = jnp.where(parity == 0, even, odd)
    low[pl.ds(0, d)] = jnp.where(has_lower == 0, 0.0, below).astype(BF16)
    high[pl.ds(length, d)] = jnp.where(has_upper == 0, 0.0, above).astype(BF16)
    wait_all(c2)
    all_taps(x2, w2, low, mid, high, length, low_at=d)
    cp2.wait()

    def block2(start, size):
        v = mid[pl.ds(start, size)] + low[pl.ds(start, size)].astype(F32)
        v = v + high[pl.ds(start + d, size)].astype(F32)
        hidden = gelu(v).astype(BF16)
        h2[pl.ds(start, size)] = hidden
        x3_ref[pl.ds(start, size)] = (
            x2[pl.ds(start, size)].astype(F32) + dot(hidden, p2[...])
        ).astype(BF16)

    over_rows(length, block2)
    wait_all(c3)
    send = even_ref.shape[0]

    def terms(start, size):
        up = dot(x3_ref[pl.ds(length - send + start, size)], w3[:, :width])
        down = dot(x3_ref[pl.ds(start, size)], w3[:, width:])
        even_ref[pl.ds(start, size)] = jnp.where(parity == 0, up, down).astype(BF16)
        odd_ref[pl.ds(start, size)] = jnp.where(parity == 0, down, up).astype(BF16)

    over_rows(send, terms)
    for k, piece in enumerate((g0, g1, g2, g3)):
        piece[...] = h2[pl.ds(pl.multiple_of((q ^ k) * rows, r), rows)]


def third_block(scalars, x2, from_even, from_odd, taps, point, r):
    length, c = x2.shape
    rows = length // GROUP
    h = taps.shape[3]
    d = from_even.shape[0]
    terms = jax.ShapeDtypeStruct((2 * d, h), BF16)
    piece = jax.ShapeDtypeStruct((rows, h), BF16)
    return pl.pallas_call(
        functools.partial(third_kernel, r),
        out_shape=(jax.ShapeDtypeStruct((length, c), BF16), terms, terms) + (piece,) * GROUP,
        in_specs=[SMEM] + [VMEM] * 3 + [ANY] * 2,
        out_specs=(VMEM,) * (3 + GROUP),
        scratch_shapes=[
            pltpu.VMEM((c, 3 * h), BF16),
            pltpu.VMEM((c, 2 * h), BF16),
            pltpu.VMEM((h, c), BF16),
            pltpu.VMEM((length + d, h), BF16),
            pltpu.VMEM((length, h), F32),
            pltpu.VMEM((length + d, h), BF16),
            pltpu.VMEM((length, h), BF16),
            pltpu.SemaphoreType.DMA((6,)),
        ],
        compiler_params=params(),
        cost_estimate=cost(2 * c * h * 5 * length, 8 * 2**20),
    )(scalars, x2, from_even, from_odd, taps, point)


def near_kernel(x3, taps_hbm, near_ref, w, other, wsems):
    length = x3.shape[0]
    half = length // 2
    width = near_ref.shape[1]
    copies = start_all(tap_copies(taps_hbm, 3, (0, 1, 2), w, wsems, 0))
    wait_all(copies)

    def lower_half(start, size):
        terms = dot(x3[pl.ds(start, size)], w[:, : 2 * width])
        other[pl.ds(start, size)] = terms[:, :width].astype(BF16)
        near_ref[pl.ds(start, size)] = terms[:, width:]

    def upper_half(start, size):
        terms = dot(x3[pl.ds(half + start, size)], w[:, width:])
        near_ref[pl.ds(half + start, size)] = (
            terms[:, :width] + other[pl.ds(start, size)].astype(F32)
        )
        near_ref[pl.ds(start, size)] = near_ref[pl.ds(start, size)] + terms[:, width:].astype(
            BF16
        ).astype(F32)

    over_rows(half, lower_half)
    over_rows(half, upper_half)


def near_terms(x3, taps):
    length, c = x3.shape
    h = taps.shape[3]
    return pl.pallas_call(
        near_kernel,
        out_shape=jax.ShapeDtypeStruct((length, h), F32),
        in_specs=[VMEM, ANY],
        out_specs=VMEM,
        scratch_shapes=[
            pltpu.VMEM((c, 3 * h), BF16),
            pltpu.VMEM((length // 2, h), BF16),
            pltpu.SemaphoreType.DMA((3,)),
        ],
        compiler_params=params(),
        cost_estimate=cost(2 * c * h * 2 * length, 5 * 2**20),
    )(x3, taps)


def last_kernel(r, s_ref, near, from_even, from_odd, g0, g1, g2, g3, h3):
    q, parity, has_lower, has_upper = (s_ref[i] for i in range(4))
    length, rows = near.shape[0], near.shape[0] // GROUP
    half = length // 2

    def body(start, size):
        even = from_even[pl.ds(start, size)].astype(F32)
        odd = from_odd[pl.ds(start, size)].astype(F32)
        below = jnp.where(has_lower == 0, 0.0, jnp.where(parity == 0, odd, even))
        above = jnp.where(has_upper == 0, 0.0, jnp.where(parity == 0, even, odd))
        h3[pl.ds(start, size)] = gelu(near[pl.ds(start, size)] + below).astype(BF16)
        h3[pl.ds(half + start, size)] = gelu(near[pl.ds(half + start, size)] + above).astype(BF16)

    over_rows(half, body)
    for k, piece in enumerate((g0, g1, g2, g3)):
        piece[...] = h3[pl.ds(pl.multiple_of((q ^ k) * rows, r), rows)]


def last_hidden(scalars, near, from_even, from_odd, r):
    length, h = near.shape
    piece = jax.ShapeDtypeStruct((length // GROUP, h), BF16)
    return pl.pallas_call(
        functools.partial(last_kernel, r),
        out_shape=(piece,) * GROUP,
        in_specs=[SMEM] + [VMEM] * 3,
        out_specs=(VMEM,) * GROUP,
        scratch_shapes=[pltpu.VMEM((length, h), BF16)],
        compiler_params=params(),
        cost_estimate=cost(20 * length * h, 5 * 2**20),
    )(scalars, near, from_even, from_odd)


def early_out_kernel(ch, s_ref, x_hbm, a0, a1, a2, a3, b0, b1, b2, b3, point, out, xs, ys, sems, osems):
    q = s_ref[0]
    places, r, c = xs.shape[1], xs.shape[2], xs.shape[3]
    reads = start_all(
        [
            pltpu.make_async_copy(x_hbm.at[:, q ^ k, ch], xs.at[k], sems.at[k])
            for k in range(GROUP)
        ]
    )
    writes = []
    for k, (first, second) in enumerate(((a0, b0), (a1, b1), (a2, b2), (a3, b3))):
        reads[k].wait()
        x = xs[k].reshape(places * r, c)
        for b, hidden in enumerate((first[0], first[1], second[...])):
            x = (x.astype(F32) + dot(hidden, point[b])).astype(BF16)
            ys[b, k] = x.reshape(places, r, c)
            writes.append(
                pltpu.make_async_copy(ys.at[b, k], out.at[b, :, q ^ k, ch], osems.at[b, k])
            )
            writes[-1].start()
    wait_all(writes)


def late_out_kernel(ch, s_ref, a0, a1, a2, a3, point, before, out, xs, ys, sems, osems):
    q = s_ref[0]
    places, r, c = xs.shape[1], xs.shape[2], xs.shape[3]
    last = out.shape[0] - 1
    reads = start_all(
        [
            pltpu.make_async_copy(out.at[last - 1, :, q ^ k, ch], xs.at[k], sems.at[k])
            for k in range(GROUP)
        ]
    )
    writes = []
    for k, hidden in enumerate((a0, a1, a2, a3)):
        reads[k].wait()
        x = xs[k].reshape(places * r, c)
        x = (x.astype(F32) + dot(hidden[...], point[0])).astype(BF16)
        ys[k] = x.reshape(places, r, c)
        writes.append(pltpu.make_async_copy(ys.at[k], out.at[last, :, q ^ k, ch], osems.at[k]))
        writes[-1].start()
    wait_all(writes)


def early_outputs(ch, scalars, x, firsts, thirds, point, before):
    places, group, chunks, r, c = x.shape
    blocks = point.shape[0]
    shape = jax.ShapeDtypeStruct((blocks, places, group, chunks, r, c), BF16)
    operands = [scalars, x, *firsts, *thirds, point[: blocks - 1]]
    specs = [SMEM, ANY] + [VMEM] * (2 * GROUP + 1)
    kernel = functools.partial(early_out_kernel, ch)
    aliases = {}
    if before is not None:
        aliases = {len(operands): 0}
        operands.append(before)
        specs.append(ANY)
        kernel = lambda *refs: early_out_kernel(ch, *refs[: len(operands) - 1], *refs[len(operands) :])
    return pl.pallas_call(
        kernel,
        out_shape=shape,
        in_specs=specs,
        out_specs=ANY,
        scratch_shapes=[
            pltpu.VMEM((GROUP, places, r, c), BF16),
            pltpu.VMEM((blocks - 1, GROUP, places, r, c), BF16),
            pltpu.SemaphoreType.DMA((GROUP,)),
            pltpu.SemaphoreType.DMA((blocks - 1, GROUP)),
        ],
        input_output_aliases=aliases,
        compiler_params=params(),
        cost_estimate=cost(2 * 3 * GROUP * places * r * c * point.shape[1], 10 * 2**20),
    )(*operands)


def late_outputs(ch, scalars, hiddens, point, before):
    blocks, places, group, chunks, r, c = before.shape
    operands = [scalars, *hiddens, point[blocks - 1 :], before]
    return pl.pallas_call(
        functools.partial(late_out_kernel, ch),
        out_shape=jax.ShapeDtypeStruct(before.shape, BF16),
        in_specs=[SMEM] + [VMEM] * (GROUP + 1) + [ANY],
        out_specs=ANY,
        scratch_shapes=[
            pltpu.VMEM((GROUP, places, r, c), BF16),
            pltpu.VMEM((GROUP, places, r, c), BF16),
            pltpu.SemaphoreType.DMA((GROUP,)),
            pltpu.SemaphoreType.DMA((GROUP,)),
        ],
        input_output_aliases={len(operands) - 1: 0},
        compiler_params=params(),
        cost_estimate=cost(2 * GROUP * places * r * c * point.shape[1], 4 * 2**20),
    )(*operands)


def neighbour_pairs(size, parity):
    groups = size // GROUP
    pairs = []
    for i in range(size):
        group = i // GROUP
        other = group + 1 if group % 2 == parity else group - 1
        pairs.append((i, i + (other - group) * GROUP if 0 <= other < groups else i ^ 1))
    return pairs


def by_residue(signal, taps, point):
    size = lax.axis_size("seq")
    me = lax.axis_index("seq")
    length, c = signal.shape
    places = length // FIRST_DILATION
    r = FIRST_DILATION // GROUP // CHUNKS
    q, group = me % GROUP, me // GROUP
    scalars = jnp.stack(
        [q, group % 2, (group > 0).astype(jnp.int32), (group < size // GROUP - 1).astype(jnp.int32)]
    ).astype(jnp.int32)
    even_pairs, odd_pairs = neighbour_pairs(size, 0), neighbour_pairs(size, 1)
    x = signal.reshape(places, GROUP, CHUNKS, r, c)

    def swap(value, k):
        return lax.ppermute(value, "seq", [(i, i ^ k) for i in range(size)])

    def back(pieces):
        return [pieces[0]] + [swap(pieces[k], k) for k in range(1, GROUP)]

    def across(even, odd):
        return lax.ppermute(even, "seq", even_pairs), lax.ppermute(odd, "seq", odd_pairs)

    out = None
    firsts, thirds, lasts = [], [], []
    for ch in range(CHUNKS):
        pieces = [
            lax.dynamic_index_in_dim(x[:, :, ch], q ^ k, 1, keepdims=False).reshape(places * r, c)
            for k in range(GROUP)
        ]
        pieces = back(pieces)
        halos = across(*edges(scalars, pieces, 3 * r))
        x2, even, odd, *hidden = first_blocks(scalars, pieces, *halos, taps, point, r)
        terms = across(even, odd)
        firsts.append(back(hidden))
        x3, even, odd, *hidden = third_block(scalars, x2, *terms, taps, point, r)
        terms = across(even, odd)
        near = near_terms(x3, taps)
        thirds.append(back(hidden))
        hidden = last_hidden(scalars, near, *terms, r)
        lasts.append(back(hidden))
    for ch in range(CHUNKS):
        out = early_outputs(ch, scalars, x, firsts[ch], thirds[ch], point, out)
    for ch in range(CHUNKS):
        out = late_outputs(ch, scalars, lasts[ch], point, out)
    return out.reshape(point.shape[0], length, c)


def passed_along(value, by):
    size = lax.axis_size("seq")
    pairs = [(i, i + by) for i in range(size) if 0 <= i + by < size]
    return lax.ppermute(value, "seq", pairs)


def by_neighbours(signal, taps, point):
    length = signal.shape[0]
    current = signal
    outputs = []
    for block in range(taps.shape[0]):
        step = FIRST_DILATION * 2**block
        low = dot(current, taps[block, 0]).astype(BF16)
        high = dot(current, taps[block, 2]).astype(BF16)
        if step < length:
            below = jnp.concatenate([passed_along(low[length - step :], 1), low[: length - step]])
            above = jnp.concatenate([high[step:], passed_along(high[:step], -1)])
        else:
            below = passed_along(low, step // length)
            above = passed_along(high, -(step // length))
        v = dot(current, taps[block, 1]) + below.astype(F32) + above.astype(F32)
        hidden = jax.nn.gelu(v, approximate=True).astype(BF16)
        current = (current.astype(F32) + dot(hidden, point[block])).astype(BF16)
        outputs.append(current)
    return jnp.stack(outputs)


def shards(signal, taps, point):
    fits = (
        taps.shape[0] == 4
        and signal.shape[0] == GROUP * FIRST_DILATION
        and lax.axis_size("seq") % GROUP == 0
    )
    return (by_residue if fits else by_neighbours)(signal, taps, point)


def solution(mesh):
    in_specs = (P(("grp", "seq"), None), P(), P())
    out_specs = P(None, ("grp", "seq"), None)
    return jax.shard_map(shards, mesh=mesh, in_specs=in_specs, out_specs=out_specs, check_vma=False)
```

time: 128 us -> 106 us (0.83)
  Pallas kernels: 0 us -> 36.5 us
  matrix products: 36.2 us -> 0 us
  waiting for transfers between devices: 59.5 us -> 49.1 us
  starting transfers between devices: 24.5 us -> 17.1 us
  other arithmetic: 5.08 us -> 0.08 us
    pallas_call x0 -> x7, Pallas kernels: none -> 36.5 us  [the longest x1 15.2 us: first_blocks(): pl.pallas_call(functools.partial(first_kernel, r), out_shape=(jax.ShapeDt...]
    dot_general x12 -> x0, matrix products: 36.2 us -> none  [the longest x4 18.7 us: shards(): jnp.dot(hidden, point_weight[block_layer_index], preferred_element_type=j...]
    ppermute x8 -> x18, waiting for transfers between devices: 59.5 us -> 49.1 us  [the longest x12 32.1 us: swap(): return lax.ppermute(value, 'seq', [(i, i ^ k) for i in range(size)])]
    ppermute x8 -> x18, starting transfers between devices: 24.5 us -> 17.1 us  [the longest x12 9.68 us: swap(): return lax.ppermute(value, 'seq', [(i, i ^ k) for i in range(size)])]
    another operation x1, other arithmetic: 5.08 us -> 0.08 us  [by_residue(): jnp.stack([q, group % 2, (group > 0).astype(jnp.int32), (group < size //...]
    dynamic_slice x0 -> x1, local copies, waits for them, and re-layouts: none -> 2.55 us  [by_residue(): lax.dynamic_index_in_dim(x[:, :, ch], q ^ k, 1, keepdims=False)]
  transfers between devices with their start and end apart: 8 -> 18, of which waited for: 7 -> 9; matrix products, arithmetic and copies ran while one was open for 2% -> 0% of each run, Pallas kernels for 0% -> 15%
where the time goes in v1:
time: 106 us
  waiting for transfers between devices  49.1 us (46%)
  Pallas kernels  36.5 us (34%)
  starting transfers between devices  17.1 us (16%)
  local copies, waits for them, and re-layouts  2.72 us (3%)
    ppermute x12, waiting for transfers between devices, swap(): return lax.ppermute(value, 'seq', [(i, i ^ k) for i in range(size)])  32.1 us
    ppermute x3, waiting for transfers between devices, across(): lax.ppermute(even, 'seq', even_pairs)  17 us
    pallas_call x1, Pallas kernels, first_blocks(): pl.pallas_call(functools.partial(first_kernel, r), out_shape=(jax.ShapeDt...  15.2 us
    ppermute x12, starting transfers between devices, swap(): return lax.ppermute(value, 'seq', [(i, i ^ k) for i in range(size)])  9.68 us
    pallas_call x1, Pallas kernels, third_block(): pl.pallas_call(functools.partial(third_kernel, r), out_shape=(jax.ShapeDt...  6.96 us
    ppermute x3, starting transfers between devices, across(): lax.ppermute(even, 'seq', even_pairs)  5.78 us
    pallas_call x1, Pallas kernels, early_outputs(): pl.pallas_call(kernel, out_shape=shape, in_specs=specs, out_specs=ANY, sc...  5.1 us
    pallas_call x1, Pallas kernels, late_outputs(): pl.pallas_call(functools.partial(late_out_kernel, ch), out_shape=jax.Shap...  4.12 us
  transfers between devices with their start and end apart: 18, of which 9 were waited for; matrix products, arithmetic and copies ran while one was open for 0% of the time, Pallas kernels for 15%

profile of v1, /device:TPU:1, one launch (start us, length us, event | category | flops | bytes accessed | tf_op | source)
XLA Modules:
  0.0 105.8 jit_solution(17662408714479063083)
XLA Ops:
  0.0 2.5 %constant_dynamic-slice_fusion = (bf16[4,1,64,768]{3,2,1,0:T(8,128)(2,1)}, bf16[4,1,64,768]{3,2,1,0:T(8,128)(2,1)}, bf16[4,1,64,768]{3,2,1,0:T(8,128)(2,1)}, bf16[4,1,64,768]{3,2,1,0:T(8,128)(2,1)S(1)}) fusion(bf16[4,4,64,768]{3,2,1,0:T(8,128)(2,1)} %bitcast.21, s32[]{:T(128)S(6)} %select_n.34, s32[]{:T(128)S(6)} %select_n.33, s32[]{:T(128)S(6)} %select_n.32, ...), kind=kLoop, calls=%fused_computation | loop fusion | bytes 3145744 | tf_op jit(solution)/shard_map/jit(dynamic_index_in_dim)/dynamic_slice | solution.py:515
  2.5 2.1 %collective-permute-start.1 = (bf16[256,768]{1,0:T(8,128)(2,1)}, bf16[256,768]{1,0:T(8,128)(2,1)S(1)}, u32[]{:S(2)}, u32[]{:S(2)}) collective-permute-start(bf16[256,768]{1,0:T(8,128)(2,1)} %bitcast.7), channel_id=1, source_target_pairs={{0,2},{1,3},{2,0},{3,1},{4,6},{5,7},{6,4},{7,5},{8,10},{9,11},{10,... | collective-permute-start | bytes 1179656 | tf_op jit(solution)/shard_map/ppermute | solution.py:503
  4.6 0.6 collective-permute-start.2
  5.2 0.4 collective-permute-start
  5.7 8.0 %collective-permute-done.1.r2 = bf16[256,768]{1,0:T(8,128)(2,1)S(1)} collective-permute-done((bf16[256,768]{1,0:T(8,128)(2,1)}, bf16[256,768]{1,0:T(8,128)(2,1)S(1)}, u32[]{:S(2)}, u32[]{:S(2)}) %collective-permute-start.1) | collective-permute-done | bytes 393248 | tf_op jit(solution)/shard_map/ppermute | solution.py:503
  13.7 9.0 %collective-permute-done.2.r3 = bf16[256,768]{1,0:T(8,128)(2,1)S(1)} collective-permute-done((bf16[256,768]{1,0:T(8,128)(2,1)}, bf16[256,768]{1,0:T(8,128)(2,1)S(1)}, u32[]{:S(2)}, u32[]{:S(2)}) %collective-permute-start.2) | collective-permute-done | bytes 393248 | tf_op jit(solution)/shard_map/ppermute | solution.py:503
  22.6 1.6 %shard_map.37 = (bf16[192,768]{1,0:T(8,128)(2,1)S(1)}, bf16[192,768]{1,0:T(8,128)(2,1)S(1)}) custom-call(s32[4]{0:T(128)S(1)} %pad_add_fusion.s_ref, bf16[256,768]{1,0:T(8,128)(2,1)S(1)} %bitcast.23, bf16[256,768]{1,0:T(8,128)(2,1)} %collective-permute-done.r1, bf16[256,768]{1,0:T(8,128)(2,1)S(1)} %collective-permute-done.1.r2, ...), custom_call_target="tpu_custom_call" | custom-call | bytes 1179648 | tf_op jit(solution)/shard_map/pallas_call | solution.py:104
  24.3 1.6 %collective-permute-start.3 = (bf16[192,768]{1,0:T(8,128)(2,1)S(1)}, bf16[192,768]{1,0:T(8,128)(2,1)S(1)}, u32[]{:S(2)}, u32[]{:S(2)}) collective-permute-start(bf16[192,768]{1,0:T(8,128)(2,1)S(1)} %get-tuple-element.25), channel_id=1, source_target_pairs={{0,4},{1,5},{2,6},{3,7},{4,0},{5,1},{6,2},{7,3},{8,12},{9,13},{10,... | collective-permute-start | bytes 884744 | tf_op jit(solution)/shard_map/ppermute | solution.py:509
  25.9 6.8 %collective-permute-done.3.from_even = bf16[192,768]{1,0:T(8,128)(2,1)S(1)} collective-permute-done((bf16[192,768]{1,0:T(8,128)(2,1)S(1)}, bf16[192,768]{1,0:T(8,128)(2,1)S(1)}, u32[]{:S(2)}, u32[]{:S(2)}) %collective-permute-start.3) | collective-permute-done | bytes 294944 | tf_op jit(solution)/shard_map/ppermute | solution.py:509
  32.7 15.2 %shard_map.38 = (bf16[1024,768]{1,0:T(8,128)(2,1)S(1)}, bf16[256,384]{1,0:T(8,128)(2,1)S(1)}, bf16[256,384]{1,0:T(8,128)(2,1)S(1)}, bf16[2,256,384]{2,1,0:T(8,12...) custom-call(s32[4]{0:T(128)S(1)} %pad_add_fusion.s_ref, ...), custom_call_target="tpu_custom_call" | custom-call | flops 7021264896 | bytes 10485760 | tf_op jit(solution)/shard_map/pallas_call | solution.py:210
  47.9 2.5 %collective-permute-start.5 = (bf16[256,384]{1,0:T(8,128)(2,1)S(1)}, bf16[256,384]{1,0:T(8,128)(2,1)S(1)}, u32[]{:S(2)}, u32[]{:S(2)}) collective-permute-start(bf16[256,384]{1,0:T(8,128)(2,1)S(1)} %get-tuple-element.28), channel_id=1, source_target_pairs={{0,4},{1,5},{2,6},{3,7},{4,0},{5,1},{6,2},{7,3},{8,12},{9,13},{10,... | collective-permute-start | bytes 589832 | tf_op jit(solution)/shard_map/ppermute | solution.py:509
  50.4 0.4 collective-permute-start.6
  50.9 4.6 %collective-permute-done.5.from_even = bf16[256,384]{1,0:T(8,128)(2,1)S(1)} collective-permute-done((bf16[256,384]{1,0:T(8,128)(2,1)S(1)}, bf16[256,384]{1,0:T(8,128)(2,1)S(1)}, u32[]{:S(2)}, u32[]{:S(2)}) %collective-permute-start.5) | collective-permute-done | bytes 196640 | tf_op jit(solution)/shard_map/ppermute | solution.py:509
  55.5 7.0 %shard_map.39 = (bf16[1024,768]{1,0:T(8,128)(2,1)S(1)}, bf16[512,384]{1,0:T(8,128)(2,1)S(1)}, bf16[512,384]{1,0:T(8,128)(2,1)S(1)}, bf16[256,384]{1,0:T(8,128)(2...) custom-call(s32[4]{0:T(128)S(1)} %pad_add_fusion.s_ref, ...), custom_call_target="tpu_custom_call" | custom-call | flops 3019898880 | bytes 8388608 | tf_op jit(solution)/shard_map/pallas_call | solution.py:290
  62.5 1.7 %collective-permute-start.7 = (bf16[512,384]{1,0:T(8,128)(2,1)S(1)}, bf16[512,384]{1,0:T(8,128)(2,1)S(1)}, u32[]{:S(2)}, u32[]{:S(2)}) collective-permute-start(bf16[512,384]{1,0:T(8,128)(2,1)S(1)} %get-tuple-element.31), channel_id=1, source_target_pairs={{0,4},{1,5},{2,6},{3,7},{4,0},{5,1},{6,2},{7,3},{8,12},{9,13},{10,... | collective-permute-start | bytes 1179656 | tf_op jit(solution)/shard_map/ppermute | solution.py:509
  64.2 1.2 %collective-permute-start.8 = (bf16[512,384]{1,0:T(8,128)(2,1)S(1)}, bf16[512,384]{1,0:T(8,128)(2,1)S(1)}, u32[]{:S(2)}, u32[]{:S(2)}) collective-permute-start(bf16[512,384]{1,0:T(8,128)(2,1)S(1)} %get-tuple-element.32), channel_id=1, source_target_pairs={{0,1},{1,0},{2,3},{3,2},{4,8},{5,9},{6,10},{7,11},{8,4},{9,5},{10,... | collective-permute-start | bytes 1179656 | tf_op jit(solution)/shard_map/ppermute | solution.py:509
  65.4 0.1 collective-permute-start.13
  65.5 1.5 %collective-permute-start.14 = (bf16[2,256,384]{2,1,0:T(8,128)(2,1)S(1)}, bf16[2,256,384]{2,1,0:T(8,128)(2,1)S(1)}, u32[]{:S(2)}, u32[]{:S(2)}) collective-permute-start(bf16[2,256,384]{2,1,0:T(8,128)(2,1)S(1)} %get-tuple-element.40), channel_id=1, source_target_pairs={{0,3},{1,2},{2,1},{3,0},{4,7},{5,6},{6,5},{7,4},{8,11},{9,10},{10,... | collective-permute-start | bytes 1179656 | tf_op jit(solution)/shard_map/ppermute | solution.py:503
  67.0 0.2 collective-permute-start.15
  67.2 5.6 %collective-permute-done.7.from_even = bf16[512,384]{1,0:T(8,128)(2,1)S(1)} collective-permute-done((bf16[512,384]{1,0:T(8,128)(2,1)S(1)}, bf16[512,384]{1,0:T(8,128)(2,1)S(1)}, u32[]{:S(2)}, u32[]{:S(2)}) %collective-permute-start.7) | collective-permute-done | bytes 393248 | tf_op jit(solution)/shard_map/ppermute | solution.py:509
  72.8 3.1 %collective-permute-start.17 = (bf16[256,384]{1,0:T(8,128)(2,1)S(1)}, bf16[256,384]{1,0:T(8,128)(2,1)S(1)}, u32[]{:S(2)}, u32[]{:S(2)}) collective-permute-start(bf16[256,384]{1,0:T(8,128)(2,1)S(1)} %get-tuple-element.44), channel_id=1, source_target_pairs={{0,3},{1,2},{2,1},{3,0},{4,7},{5,6},{6,5},{7,4},{8,11},{9,10},{10,... | collective-permute-start | bytes 589832 | tf_op jit(solution)/shard_map/ppermute | solution.py:503
  75.9 2.2 %shard_map.40.near = f32[1024,384]{1,0:T(8,128)S(1)} custom-call(bf16[1024,768]{1,0:T(8,128)(2,1)S(1)} %get-tuple-element.30.x3, bf16[4,3,768,384]{3,2,1,0:T(8,128)(2,1)S(1)} %bitcast.20), custom_call_target="tpu_custom_call" | custom-call | flops 1207959552 | bytes 5242880 | tf_op jit(solution)/shard_map/pallas_call | solution.py:338
  78.1 1.3 %shard_map.41 = (bf16[256,384]{1,0:T(8,128)(2,1)S(1)}, bf16[256,384]{1,0:T(8,128)(2,1)S(1)}, bf16[256,384]{1,0:T(8,128)(2,1)S(1)}, bf16[256,384]{1,0:T(8,128)(2,1)S(1)}) custom-call(s32[4]{0:T(128)S(1)} %pad_add_fusion.s_ref, f32[1024,384]{1,0:T(8,128)S(1)} %shard_map.40.near, bf16[512,384]{1,0:T(8,128)(2,1)S(1)} %collective-permute-done.7.from_even, ...), custom_call_target="tpu_custom_call" | custom-call | flops 7864320 | bytes 5242880 | tf_op jit(solution)/shard_map/pallas_call | solution.py:374
  79.6 5.5 %collective-permute-done.14.a3 = bf16[2,256,384]{2,1,0:T(8,128)(2,1)S(1)} collective-permute-done((bf16[2,256,384]{2,1,0:T(8,128)(2,1)S(1)}, bf16[2,256,384]{2,1,0:T(8,128)(2,1)S(1)}, u32[]{:S(2)}, u32[]{:S(2)}) %collective-permute-start.14) | collective-permute-done | bytes 393248 | tf_op jit(solution)/shard_map/ppermute | solution.py:503
  85.0 0.1 collective-permute-start.10
  85.1 1.4 %collective-permute-start.11 = (bf16[256,384]{1,0:T(8,128)(2,1)S(1)}, bf16[256,384]{1,0:T(8,128)(2,1)S(1)}, u32[]{:S(2)}, u32[]{:S(2)}) collective-permute-start(bf16[256,384]{1,0:T(8,128)(2,1)S(1)} %get-tuple-element.36), channel_id=1, source_target_pairs={{0,3},{1,2},{2,1},{3,0},{4,7},{5,6},{6,5},{7,4},{8,11},{9,10},{10,... | collective-permute-start | bytes 589832 | tf_op jit(solution)/shard_map/ppermute | solution.py:503
  86.6 0.1 slice.7.point
  86.7 2.0 %collective-permute-done.16.b2 = bf16[256,384]{1,0:T(8,128)(2,1)S(1)} collective-permute-done((bf16[256,384]{1,0:T(8,128)(2,1)S(1)}, bf16[256,384]{1,0:T(8,128)(2,1)S(1)}, u32[]{:S(2)}, u32[]{:S(2)}) %collective-permute-start.16) | collective-permute-done | bytes 196640 | tf_op jit(solution)/shard_map/ppermute | solution.py:503
  88.7 4.7 %collective-permute-done.17.b3 = bf16[256,384]{1,0:T(8,128)(2,1)S(1)} collective-permute-done((bf16[256,384]{1,0:T(8,128)(2,1)S(1)}, bf16[256,384]{1,0:T(8,128)(2,1)S(1)}, u32[]{:S(2)}, u32[]{:S(2)}) %collective-permute-start.17) | collective-permute-done | bytes 196640 | tf_op jit(solution)/shard_map/ppermute | solution.py:503
  93.4 5.1 %shard_map.42.before = bf16[4,4,4,1,64,768]{5,4,3,2,1,0:T(8,128)(2,1)} custom-call(s32[4]{0:T(128)S(1)} %pad_add_fusion.s_ref, bf16[4,4,1,64,768]{4,3,2,1,0:T(8,128)(2,1)S(1)} %bitcast.22, bf16[2,256,384]{2,1,0:T(8,128)(2,1)S(1)} %get-tuple-element.37.a0, bf16[2,256,384]{2,1,0:T(8,128)(2,1)S(1)} %collective-permute-done.12.a1, ...), custom_call_target="tpu_custom_call" | custom-call | flops 1811939328 | bytes 10485760 | tf_op jit(solution)/shard_map/pallas_call | solution.py:442
  98.6 2.9 %collective-permute-done.11.a3 = bf16[256,384]{1,0:T(8,128)(2,1)S(1)} collective-permute-done((bf16[256,384]{1,0:T(8,128)(2,1)S(1)}, bf16[256,384]{1,0:T(8,128)(2,1)S(1)}, u32[]{:S(2)}, u32[]{:S(2)}) %collective-permute-start.11) | collective-permute-done | bytes 196640 | tf_op jit(solution)/shard_map/ppermute | solution.py:503
  101.5 4.1 %shard_map.43 = bf16[4,4,4,1,64,768]{5,4,3,2,1,0:T(8,128)(2,1)} custom-call(s32[4]{0:T(128)S(1)} %pad_add_fusion.s_ref, bf16[256,384]{1,0:T(8,128)(2,1)S(1)} %get-tuple-element.33.a0, bf16[256,384]{1,0:T(8,128)(2,1)S(1)} %collective-permute-done.9.a1, bf16[256,384]{1,0:T(8,128)(2,1)S(1)} %collective-permute-done.10.a2, ...), custom_call_target="tpu_custom_call", output_to_operand_aliasing={{}: (6, {})} | custom-call | flops 603979776 | bytes 4194304 | tf_op jit(solution)/shard_map/pallas_call | solution.py:462
  (24 shorter events, 0.3 us)
Async XLA Ops:
  0.0 32.7 %copy-start = (bf16[4,384,768]{2,1,0:T(8,128)(2,1)S(1)}, bf16[4,384,768]{2,1,0:T(8,128)(2,1)}, u32[]{:S(2)}) copy-start(bf16[4,384,768]{2,1,0:T(8,128)(2,1)} %point_hbm.3) | copy-start | bytes 7077892
  2.5 11.1 %collective-permute-start.1 = (bf16[256,768]{1,0:T(8,128)(2,1)}, bf16[256,768]{1,0:T(8,128)(2,1)S(1)}, u32[]{:S(2)}, u32[]{:S(2)}) collective-permute-start(bf16[256,768]{1,0:T(8,128)(2,1)} %bitcast.7), channel_id=1, source_target_pairs={{0,2},{1,3},{2,0},{3,1},{4,6},{5,7},{6,4},{7,5},{8,10},{9,11},{10,... | collective-permute-start | bytes 1179656 | tf_op jit(solution)/shard_map/ppermute | solution.py:503
  4.6 18.0 %collective-permute-start.2 = (bf16[256,768]{1,0:T(8,128)(2,1)}, bf16[256,768]{1,0:T(8,128)(2,1)S(1)}, u32[]{:S(2)}, u32[]{:S(2)}) collective-permute-start(bf16[256,768]{1,0:T(8,128)(2,1)} %bitcast.8), channel_id=1, source_target_pairs={{0,3},{1,2},{2,1},{3,0},{4,7},{5,6},{6,5},{7,4},{8,11},{9,10},{10,... | collective-permute-start | bytes 1179656 | tf_op jit(solution)/shard_map/ppermute | solution.py:503
  5.2 17.4 %collective-permute-start = (bf16[256,768]{1,0:T(8,128)(2,1)}, bf16[256,768]{1,0:T(8,128)(2,1)}, u32[]{:S(2)}, u32[]{:S(2)}) collective-permute-start(bf16[256,768]{1,0:T(8,128)(2,1)} %bitcast.6), channel_id=1, source_target_pairs={{0,1},{1,0},{2,3},{3,2},{4,5},{5,4},{6,7},{7,6},{8,9},{9,8},{10,11... | collective-permute-start | bytes 1179656 | tf_op jit(solution)/shard_map/ppermute | solution.py:503
  24.3 8.4 %collective-permute-start.3 = (bf16[192,768]{1,0:T(8,128)(2,1)S(1)}, bf16[192,768]{1,0:T(8,128)(2,1)S(1)}, u32[]{:S(2)}, u32[]{:S(2)}) collective-permute-start(bf16[192,768]{1,0:T(8,128)(2,1)S(1)} %get-tuple-element.25), channel_id=1, source_target_pairs={{0,4},{1,5},{2,6},{3,7},{4,0},{5,1},{6,2},{7,3},{8,12},{9,13},{10,... | collective-permute-start | bytes 884744 | tf_op jit(solution)/shard_map/ppermute | solution.py:509
  25.9 29.6 %slice-start = ((s8[7077888]{0:T(1024)(128)(4,1)}), s8[4194304]{0:T(1024)(128)(4,1)S(1)}, s32[]{:S(2)}) async-start(s8[7077888]{0:T(1024)(128)(4,1)} %bitcast.19), calls=%async_computation | async-start | bytes 8388608
  25.9 29.6 %slice-start.1 = ((s8[7077888]{0:T(1024)(128)(4,1)}), s8[2883584]{0:T(1024)(128)(4,1)S(1)}, s32[]{:S(2)}) async-start(s8[7077888]{0:T(1024)(128)(4,1)} %bitcast.19), calls=%async_computation.1 | async-start | bytes 5767168
  25.9 6.8 %collective-permute-start.4 = (bf16[192,768]{1,0:T(8,128)(2,1)S(1)}, bf16[192,768]{1,0:T(8,128)(2,1)S(1)}, u32[]{:S(2)}, u32[]{:S(2)}) collective-permute-start(bf16[192,768]{1,0:T(8,128)(2,1)S(1)} %get-tuple-element.26), channel_id=1, source_target_pairs={{0,1},{1,0},{2,3},{3,2},{4,8},{5,9},{6,10},{7,11},{8,4},{9,5},{10,... | collective-permute-start | bytes 884744 | tf_op jit(solution)/shard_map/ppermute | solution.py:509
  47.9 7.6 %collective-permute-start.5 = (bf16[256,384]{1,0:T(8,128)(2,1)S(1)}, bf16[256,384]{1,0:T(8,128)(2,1)S(1)}, u32[]{:S(2)}, u32[]{:S(2)}) collective-permute-start(bf16[256,384]{1,0:T(8,128)(2,1)S(1)} %get-tuple-element.28), channel_id=1, source_target_pairs={{0,4},{1,5},{2,6},{3,7},{4,0},{5,1},{6,2},{7,3},{8,12},{9,13},{10,... | collective-permute-start | bytes 589832 | tf_op jit(solution)/shard_map/ppermute | solution.py:509
  50.4 5.1 %collective-permute-start.6 = (bf16[256,384]{1,0:T(8,128)(2,1)S(1)}, bf16[256,384]{1,0:T(8,128)(2,1)S(1)}, u32[]{:S(2)}, u32[]{:S(2)}) collective-permute-start(bf16[256,384]{1,0:T(8,128)(2,1)S(1)} %get-tuple-element.29), channel_id=1, source_target_pairs={{0,1},{1,0},{2,3},{3,2},{4,8},{5,9},{6,10},{7,11},{8,4},{9,5},{10,... | collective-permute-start | bytes 589832 | tf_op jit(solution)/shard_map/ppermute | solution.py:509
  50.8 16.2 %collective-permute-start.12 = (bf16[2,256,384]{2,1,0:T(8,128)(2,1)S(1)}, bf16[2,256,384]{2,1,0:T(8,128)(2,1)S(1)}, u32[]{:S(2)}, u32[]{:S(2)}) collective-permute-start(bf16[2,256,384]{2,1,0:T(8,128)(2,1)S(1)} %get-tuple-element.38), channel_id=1, source_target_pairs={{0,1},{1,0},{2,3},{3,2},{4,5},{5,4},{6,7},{7,6},{8,9},{9,8},{10,11... | collective-permute-start | bytes 1179656 | tf_op jit(solution)/shard_map/ppermute | solution.py:503
  62.5 10.3 %collective-permute-start.7 = (bf16[512,384]{1,0:T(8,128)(2,1)S(1)}, bf16[512,384]{1,0:T(8,128)(2,1)S(1)}, u32[]{:S(2)}, u32[]{:S(2)}) collective-permute-start(bf16[512,384]{1,0:T(8,128)(2,1)S(1)} %get-tuple-element.31), channel_id=1, source_target_pairs={{0,4},{1,5},{2,6},{3,7},{4,0},{5,1},{6,2},{7,3},{8,12},{9,13},{10,... | collective-permute-start | bytes 1179656 | tf_op jit(solution)/shard_map/ppermute | solution.py:509
  64.2 8.6 %collective-permute-start.8 = (bf16[512,384]{1,0:T(8,128)(2,1)S(1)}, bf16[512,384]{1,0:T(8,128)(2,1)S(1)}, u32[]{:S(2)}, u32[]{:S(2)}) collective-permute-start(bf16[512,384]{1,0:T(8,128)(2,1)S(1)} %get-tuple-element.32), channel_id=1, source_target_pairs={{0,1},{1,0},{2,3},{3,2},{4,8},{5,9},{6,10},{7,11},{8,4},{9,5},{10,... | collective-permute-start | bytes 1179656 | tf_op jit(solution)/shard_map/ppermute | solution.py:509
  65.4 14.1 %collective-permute-start.13 = (bf16[2,256,384]{2,1,0:T(8,128)(2,1)S(1)}, bf16[2,256,384]{2,1,0:T(8,128)(2,1)S(1)}, u32[]{:S(2)}, u32[]{:S(2)}) collective-permute-start(bf16[2,256,384]{2,1,0:T(8,128)(2,1)S(1)} %get-tuple-element.39), channel_id=1, source_target_pairs={{0,2},{1,3},{2,0},{3,1},{4,6},{5,7},{6,4},{7,5},{8,10},{9,11},{10,... | collective-permute-start | bytes 1179656 | tf_op jit(solution)/shard_map/ppermute | solution.py:503
  65.5 19.5 %collective-permute-start.14 = (bf16[2,256,384]{2,1,0:T(8,128)(2,1)S(1)}, bf16[2,256,384]{2,1,0:T(8,128)(2,1)S(1)}, u32[]{:S(2)}, u32[]{:S(2)}) collective-permute-start(bf16[2,256,384]{2,1,0:T(8,128)(2,1)S(1)} %get-tuple-element.40), channel_id=1, source_target_pairs={{0,3},{1,2},{2,1},{3,0},{4,7},{5,6},{6,5},{7,4},{8,11},{9,10},{10,... | collective-permute-start | bytes 1179656 | tf_op jit(solution)/shard_map/ppermute | solution.py:503
  67.0 18.1 %collective-permute-start.15 = (bf16[256,384]{1,0:T(8,128)(2,1)S(1)}, bf16[256,384]{1,0:T(8,128)(2,1)S(1)}, u32[]{:S(2)}, u32[]{:S(2)}) collective-permute-start(bf16[256,384]{1,0:T(8,128)(2,1)S(1)} %get-tuple-element.42), channel_id=1, source_target_pairs={{0,1},{1,0},{2,3},{3,2},{4,5},{5,4},{6,7},{7,6},{8,9},{9,8},{10,11... | collective-permute-start | bytes 589832 | tf_op jit(solution)/shard_map/ppermute | solution.py:503
  72.8 16.0 %collective-permute-start.16 = (bf16[256,384]{1,0:T(8,128)(2,1)S(1)}, bf16[256,384]{1,0:T(8,128)(2,1)S(1)}, u32[]{:S(2)}, u32[]{:S(2)}) collective-permute-start(bf16[256,384]{1,0:T(8,128)(2,1)S(1)} %get-tuple-element.43), channel_id=1, source_target_pairs={{0,2},{1,3},{2,0},{3,1},{4,6},{5,7},{6,4},{7,5},{8,10},{9,11},{10,... | collective-permute-start | bytes 589832 | tf_op jit(solution)/shard_map/ppermute | solution.py:503
  72.8 20.6 %collective-permute-start.17 = (bf16[256,384]{1,0:T(8,128)(2,1)S(1)}, bf16[256,384]{1,0:T(8,128)(2,1)S(1)}, u32[]{:S(2)}, u32[]{:S(2)}) collective-permute-start(bf16[256,384]{1,0:T(8,128)(2,1)S(1)} %get-tuple-element.44), channel_id=1, source_target_pairs={{0,3},{1,2},{2,1},{3,0},{4,7},{5,6},{6,5},{7,4},{8,11},{9,10},{10,... | collective-permute-start | bytes 589832 | tf_op jit(solution)/shard_map/ppermute | solution.py:503
  79.5 19.1 %collective-permute-start.9 = (bf16[256,384]{1,0:T(8,128)(2,1)S(1)}, bf16[256,384]{1,0:T(8,128)(2,1)S(1)}, u32[]{:S(2)}, u32[]{:S(2)}) collective-permute-start(bf16[256,384]{1,0:T(8,128)(2,1)S(1)} %get-tuple-element.34), channel_id=1, source_target_pairs={{0,1},{1,0},{2,3},{3,2},{4,5},{5,4},{6,7},{7,6},{8,9},{9,8},{10,11... | collective-permute-start | bytes 589832 | tf_op jit(solution)/shard_map/ppermute | solution.py:503
  85.0 13.5 %collective-permute-start.10 = (bf16[256,384]{1,0:T(8,128)(2,1)S(1)}, bf16[256,384]{1,0:T(8,128)(2,1)S(1)}, u32[]{:S(2)}, u32[]{:S(2)}) collective-permute-start(bf16[256,384]{1,0:T(8,128)(2,1)S(1)} %get-tuple-element.35), channel_id=1, source_target_pairs={{0,2},{1,3},{2,0},{3,1},{4,6},{5,7},{6,4},{7,5},{8,10},{9,11},{10,... | collective-permute-start | bytes 589832 | tf_op jit(solution)/shard_map/ppermute | solution.py:503
  85.1 16.4 %collective-permute-start.11 = (bf16[256,384]{1,0:T(8,128)(2,1)S(1)}, bf16[256,384]{1,0:T(8,128)(2,1)S(1)}, u32[]{:S(2)}, u32[]{:S(2)}) collective-permute-start(bf16[256,384]{1,0:T(8,128)(2,1)S(1)} %get-tuple-element.36), channel_id=1, source_target_pairs={{0,3},{1,2},{2,1},{3,0},{4,7},{5,6},{6,5},{7,4},{8,11},{9,10},{10,... | collective-permute-start | bytes 589832 | tf_op jit(solution)/shard_map/ppermute | solution.py:503
  86.6 6.8 %copy-start.1 = (bf16[1024,768]{1,0:T(8,128)(2,1)S(1)}, bf16[1024,768]{1,0:T(8,128)(2,1)}, u32[]{:S(2)}) copy-start(bf16[1024,768]{1,0:T(8,128)(2,1)} %param.3) | copy-start | bytes 4718596

commit v2 on v0

v2 whole, which is shorter than its diff:
```python
import functools

import jax
import jax.numpy as jnp
from jax import lax
from jax.experimental import pallas as pl
from jax.experimental.pallas import tpu as pltpu
from jax.sharding import PartitionSpec as P

FIRST_DILATION = 256
GROUP = 4
CHUNKS = 2
ROWS = 512
VMEM_LIMIT = 24 * 2**20

F32, BF16 = jnp.float32, jnp.bfloat16
ANY = pl.BlockSpec(memory_space=pl.ANY)
VMEM = pl.BlockSpec(memory_space=pltpu.VMEM)
SMEM = pl.BlockSpec(memory_space=pltpu.SMEM)
HBM = pl.BlockSpec(memory_space=pltpu.HBM)


def dot(a, b):
    return jnp.dot(a, b, preferred_element_type=F32)


def gelu(v):
    half = 0.5 * v
    inner = v * (0.7978845608028654 + 0.035677408136300125 * (v * v))
    return half + half * jnp.tanh(inner)


def over_rows(rows, body):
    for start in range(0, rows, ROWS):
        body(start, min(ROWS, rows - start))


def start_all(copies):
    for copy in copies:
        copy.start()
    return copies


def wait_all(copies):
    for copy in copies:
        copy.wait()


def call(kernel, outs, operands, specs, out_specs, scratch, flops, moved, aliases=None, after=()):
    count = len(operands)
    operands, specs = [*operands, *after], [*specs, *[ANY] * len(after)]
    body = kernel
    if after:
        kernel = lambda *refs: body(*refs[:count], *refs[count + len(after) :])
    return pl.pallas_call(
        kernel,
        out_shape=outs,
        in_specs=specs,
        out_specs=out_specs,
        scratch_shapes=scratch,
        input_output_aliases=aliases or {},
        compiler_params=pltpu.CompilerParams(vmem_limit_bytes=VMEM_LIMIT),
        cost_estimate=pl.CostEstimate(
            flops=int(flops), bytes_accessed=int(moved), transcendentals=0
        ),
    )(*operands)


def array(*shape, dtype=BF16):
    return jax.ShapeDtypeStruct(shape, dtype)


def split_kernel(s_ref, x, g0, g1, g2, g3, sems):
    q = s_ref[0]
    copies = [
        pltpu.make_async_copy(x.at[:, q ^ k, ch], piece.at[ch], sems.at[k, ch])
        for k, piece in enumerate((g0, g1, g2, g3))
        for ch in range(x.shape[2])
    ]
    wait_all(start_all(copies))


def split(scalars, x):
    places, group, chunks, r, c = x.shape
    pieces = (array(chunks, places, r, c),) * group
    sems = [pltpu.SemaphoreType.DMA((group, chunks))]
    pieces = call(split_kernel, pieces, (scalars, x), [SMEM, HBM], (VMEM,) * group, sems, 0, 4 * x.size)
    return [piece.reshape(chunks * places * r, c) for piece in pieces]


def side_by_side_kernel(taps, w, sems):
    h = taps.shape[3]
    wait_all(
        start_all(
            [
                pltpu.make_async_copy(
                    taps.at[b, t], w.at[b, :, pl.ds(t * h, h)], sems.at[b, t]
                )
                for b in range(taps.shape[0])
                for t in range(3)
            ]
        )
    )


def side_by_side(taps):
    blocks, count, c, h = taps.shape
    sems = [pltpu.SemaphoreType.DMA((blocks, count))]
    return call(side_by_side_kernel, array(blocks, c, count * h), (taps,), [HBM], VMEM, sems, 0, 4 * taps.size)


def place_terms(parity, up, down, even_ref, odd_ref, start, size):
    even_ref[pl.ds(start, size)] = jnp.where(parity == 0, up, down).astype(BF16)
    odd_ref[pl.ds(start, size)] = jnp.where(parity == 0, down, up).astype(BF16)


def arrived(s_ref, from_even, from_odd, start, size):
    even = from_even[pl.ds(start, size)].astype(F32)
    odd = from_odd[pl.ds(start, size)].astype(F32)
    parity, has_lower, has_upper = s_ref[1], s_ref[2], s_ref[3]
    below = jnp.where(has_lower == 0, 0.0, jnp.where(parity == 0, odd, even))
    above = jnp.where(has_upper == 0, 0.0, jnp.where(parity == 0, even, odd))
    return below, above


def open_kernel(r, s_ref, own, r1, r2, r3, w, even_ref, odd_ref, ends):
    q, parity = s_ref[0], s_ref[1]
    part = own.shape[0] // CHUNKS
    h = even_ref.shape[1]

    def fetch(piece, at, to):
        for ch in range(CHUNKS):
            ends[pl.ds(to + ch * r, r)] = piece[pl.ds(ch * part + at, r)]

    for k, piece in enumerate((own, r1, r2, r3)):
        pl.when(q ^ k == GROUP - 1)(functools.partial(fetch, piece, part - r, 0))
        pl.when(q ^ k == 0)(functools.partial(fetch, piece, 0, CHUNKS * r))
    size = CHUNKS * r
    up = dot(ends[pl.ds(0, size)], w[0, :, :h])
    down = dot(ends[pl.ds(size, size)], w[0, :, 2 * h :])
    place_terms(parity, up, down, even_ref, odd_ref, 0, size)


def open_terms(scalars, pieces, w, r):
    c, h = w.shape[1], w.shape[2] // 3
    terms = array(CHUNKS * r, h)
    return call(
        functools.partial(open_kernel, r), (terms, terms), (scalars, *pieces, w),
        [SMEM] + [VMEM] * (GROUP + 1), (VMEM, VMEM), [pltpu.VMEM((2 * CHUNKS * r, c), BF16)],
        4 * CHUNKS * r * c * h, 2**20,
    )


def all_taps(x, w, low, mid, high):
    h = mid.shape[1]

    def body(start, size):
        terms = dot(x[pl.ds(start, size)], w)
        low[pl.ds(start, size)] = terms[:, :h].astype(BF16)
        mid[pl.ds(start, size)] = terms[:, h : 2 * h]
        high[pl.ds(start, size)] = terms[:, 2 * h :].astype(BF16)

    over_rows(x.shape[0], body)


def block_body(reach, x, point, x_ref, h_ref, part_ref, low, mid, high):
    length = x.shape[0] // CHUNKS
    for ch in range(CHUNKS):
        base = ch * length
        edge = 2 * ch * reach
        top = base + length - reach

        def body(start, size, base=base + reach):
            at = base + start
            v = mid[pl.ds(at, size)] + low[pl.ds(at - reach, size)].astype(F32)
            hidden = gelu(v + high[pl.ds(at + reach, size)].astype(F32)).astype(BF16)
            h_ref[pl.ds(at, size)] = hidden
            x_ref[pl.ds(at, size)] = (x[pl.ds(at, size)].astype(F32) + dot(hidden, point)).astype(BF16)

        over_rows(length - 2 * reach, body)
        part_ref[pl.ds(edge, reach)] = mid[pl.ds(base, reach)] + high[
            pl.ds(base + reach, reach)
        ].astype(F32)
        part_ref[pl.ds(edge + reach, reach)] = mid[pl.ds(top, reach)] + low[
            pl.ds(top - reach, reach)
        ].astype(F32)
        for at in (base, top):
            x_ref[pl.ds(at, reach)] = x[pl.ds(at, reach)]
            h_ref[pl.ds(at, reach)] = jnp.zeros((reach, h_ref.shape[1]), BF16)


def first_kernel(reach, s_ref, own, r1, r2, r3, w, point, x_ref, h_ref, part_ref, x, low, mid, high):
    q = s_ref[0]
    part = own.shape[0] // CHUNKS
    h = mid.shape[1]
    for k, piece in enumerate((own, r1, r2, r3)):
        terms = dot(piece[...], w[0])
        for ch in range(CHUNKS):
            here = slice(ch * part, (ch + 1) * part)
            there = pl.ds(pl.multiple_of((ch * GROUP + (q ^ k)) * part, part), part)
            x[there] = piece[here]
            low[there] = terms[here, :h].astype(BF16)
            mid[there] = terms[here, h : 2 * h]
            high[there] = terms[here, 2 * h :].astype(BF16)
    block_body(reach, x, point[0], x_ref, h_ref, part_ref, low, mid, high)


def middle_kernel(block, reach, x, w, point, x_ref, h_ref, part_ref, low, mid, high):
    all_taps(x, w[block], low, mid, high)
    block_body(reach, x, point[block], x_ref, h_ref, part_ref, low, mid, high)


def local_block(block, scalars, x, w, point, reach):
    c, h = w.shape[1], w.shape[2] // 3
    length = GROUP * x[0].shape[0] if block == 0 else x.shape[0]
    outs = (array(length, c), array(length, h), array(2 * CHUNKS * reach, h, dtype=F32))
    scratch = [
        pltpu.VMEM((length, h), BF16),
        pltpu.VMEM((length, h), F32),
        pltpu.VMEM((length, h), BF16),
    ]
    if block == 0:
        kernel = functools.partial(first_kernel, reach)
        operands, specs = (scalars, *x, w, point), [SMEM] + [VMEM] * (GROUP + 2)
        scratch = [pltpu.VMEM((length, c), BF16)] + scratch
    else:
        kernel = functools.partial(middle_kernel, block, reach)
        operands, specs = (x, w, point), [VMEM] * 3
    return call(kernel, outs, operands, specs, (VMEM,) * 3, scratch, 8 * length * c * h, 4 * 2**20)


def give_back(q, reach, hidden, edges, near_refs, far_ref):
    length = hidden.shape[0] // CHUNKS
    rows = length // GROUP
    size = CHUNKS * rows
    for k in range(GROUP):
        ref, to = (near_refs[k], 0) if k < 2 else (far_ref, (k - 2) * size)
        j = q ^ k
        for ch in range(CHUNKS):
            at = pl.multiple_of(ch * length + j * rows, rows)
            ref[pl.ds(to + ch * rows, rows)] = hidden[pl.ds(at, rows)]

        @pl.when(j == 0)
        def _(ref=ref, to=to):
            for ch in range(CHUNKS):
                ref[pl.ds(to + ch * rows, reach)] = edges[2 * ch]

        @pl.when(j == GROUP - 1)
        def _(ref=ref, to=to):
            for ch in range(CHUNKS):
                ref[pl.ds(to + (ch + 1) * rows - reach, reach)] = edges[2 * ch + 1]


def edge_kernel(
    block, reach, ahead, s_ref, x, hidden, part, from_even, from_odd, w, point, x_ref, *refs
):
    q, parity = s_ref[0], s_ref[1]
    length = x.shape[0] // CHUNKS
    h = hidden.shape[1]
    edges = []
    for ch in range(CHUNKS):
        below, above = arrived(s_ref, from_even, from_odd, ch * reach, reach)
        edge = 2 * ch * reach
        edges.append(gelu(part[pl.ds(edge, reach)] + below).astype(BF16))
        edges.append(gelu(part[pl.ds(edge + reach, reach)] + above).astype(BF16))
    more = dot(jnp.concatenate(edges), point[block])
    for i in range(2 * CHUNKS):
        at = (i // 2) * length + (i % 2) * (length - reach)
        new = x[pl.ds(at, reach)].astype(F32) + more[i * reach : (i + 1) * reach]
        x_ref[pl.ds(at, reach)] = new.astype(BF16)
    last = block + 2 == w.shape[0]
    for ch in range(CHUNKS):
        even_ref, odd_ref = refs[2 * ch : 2 * ch + 2] if last else refs[:2]
        up = dot(x_ref[pl.ds((ch + 1) * length - ahead, ahead)], w[block + 1, :, :h])
        down = dot(x_ref[pl.ds(ch * length, ahead)], w[block + 1, :, 2 * h :])
        place_terms(parity, up, down, even_ref, odd_ref, 0 if last else ch * ahead, ahead)
    if last:
        for i in range(2 * CHUNKS):
            refs[-1][pl.ds(i * reach, reach)] = edges[i]
    else:
        give_back(q, reach, hidden, edges, refs[2:4], refs[4])


def finish_edges(block, scalars, x, hidden, part, terms, w, point, reach, ahead):
    c, h = w.shape[1], w.shape[2] // 3
    rows = x.shape[0] // GROUP
    outs = (array(*x.shape),)
    if block + 2 == w.shape[0]:
        outs += (array(ahead, h),) * (2 * CHUNKS) + (array(2 * CHUNKS * reach, h),)
    else:
        outs += (array(CHUNKS * ahead, h),) * 2
        outs += (array(rows, h), array(rows, h), array(2 * rows, h))
    return call(
        functools.partial(edge_kernel, block, reach, ahead), outs,
        (scalars, x, hidden, part, *terms, w, point),
        [SMEM] + [VMEM] * 7, (VMEM,) * len(outs), [],
        2 * c * h * CHUNKS * (2 * reach + 2 * ahead), 4 * 2**20, {1: 0},
    )


def near_kernel(reach, s_ref, x, hidden, ends, w, near_ref, own_ref, core_ref, far_ref, other):
    length = x.shape[0] // CHUNKS
    half = length // 2
    h = near_ref.shape[1]
    block = w.shape[0] - 1
    for ch in range(CHUNKS):
        lower, upper = pl.ds(ch * length, half), pl.ds(ch * length + half, half)
        terms = dot(x[lower], w[block, :, : 2 * h])
        near_ref[lower] = terms[:, h:]
        other[...] = terms[:, :h].astype(BF16)
        terms = dot(x[upper], w[block, :, h:])
        near_ref[upper] = terms[:, :h] + other[...].astype(F32)
        near_ref[lower] = near_ref[lower] + terms[:, h:].astype(BF16).astype(F32)
    edges = [ends[pl.ds(i * reach, reach)] for i in range(2 * CHUNKS)]
    give_back(s_ref[0], reach, hidden, edges, (own_ref, core_ref), far_ref)


def near_terms(scalars, x, hidden, ends, w, reach):
    c, h = w.shape[1], w.shape[2] // 3
    rows = x.shape[0] // GROUP
    scratch = [pltpu.VMEM((x.shape[0] // CHUNKS // 2, h), BF16)]
    outs = (array(x.shape[0], h, dtype=F32), array(rows, h), array(rows, h), array(2 * rows, h))
    return call(
        functools.partial(near_kernel, reach), outs, (scalars, x, hidden, ends, w),
        [SMEM] + [VMEM] * 4, (VMEM,) * 4, scratch, 4 * x.shape[0] * c * h, 4 * 2**20,
    )


def forward_kernel(*refs):
    count = (len(refs) - 1) // 2
    out = refs[-1]
    for i in range(count):
        own, arrived_ref = refs[2 * i : 2 * i + 2]
        rows = own.shape[0]
        out[2 * i] = own[...]
        out[2 * i + 1] = arrived_ref[pl.ds(rows, rows)]


def forward(own, passing, after):
    operands = [v for pair in zip(own, passing) for v in pair]
    out = array(len(operands), *own[0].shape)
    return call(forward_kernel, out, operands, [VMEM] * len(operands), VMEM, [], 0, 4 * out.size, after=after)


def last_kernel(ch, s_ref, near, from_even, from_odd, g0, g1, g2, g3, hidden):
    q = s_ref[0]
    length = near.shape[0] // CHUNKS
    half, rows = length // 2, length // GROUP
    below, above = arrived(s_ref, from_even, from_odd, 0, half)
    base = ch * length
    hidden[pl.ds(0, half)] = gelu(near[pl.ds(base, half)] + below).astype(BF16)
    hidden[pl.ds(half, half)] = gelu(near[pl.ds(base + half, half)] + above).astype(BF16)
    for k, piece in enumerate((g0, g1, g2, g3)):
        piece[...] = hidden[pl.ds(pl.multiple_of((q ^ k) * rows, rows), rows)]


def last_hidden(ch, scalars, near, terms, after):
    length, h = near.shape[0] // CHUNKS, near.shape[1]
    return call(
        functools.partial(last_kernel, ch), (array(length // GROUP, h),) * GROUP,
        (scalars, near, *terms), [SMEM] + [VMEM] * 3, (VMEM,) * GROUP,
        [pltpu.VMEM((length, h), BF16)], 20 * length * h, 2 * 2**20, after=after,
    )


def early_out_kernel(first, count, s_ref, x, *refs):
    own, far = refs[:count], refs[count : 2 * count]
    core, point = refs[2 * count : 2 * count + 2]
    out, last, xs, ys, sems, osems = refs[-6:]
    q = s_ref[0]
    places, r, c = xs.shape[2:]
    rows = CHUNKS * places * r
    if first == 0:
        reads = start_all(
            [
                pltpu.make_async_copy(x.at[:, q ^ k, ch], xs.at[k, ch], sems.at[k, ch])
                for k in range(GROUP)
                for ch in range(CHUNKS)
            ]
        )
    writes = []
    for k in range(GROUP):
        if first == 0:
            wait_all(reads[k * CHUNKS : (k + 1) * CHUNKS])
        now = (xs if first == 0 else x)[k].reshape(rows, c)
        for b in range(count):
            hidden = (own[b][...], core[2 * b], far[b][pl.ds(0, rows)], core[2 * b + 1])[k]
            now = (now.astype(F32) + dot(hidden, point[first + b])).astype(BF16)
            target = last if b + 1 == count else ys.at[b]
            target[k] = now.reshape(CHUNKS, places, r, c)
            for ch in range(CHUNKS):
                writes.append(
                    pltpu.make_async_copy(
                        target.at[k, ch], out.at[first + b, :, q ^ k, ch], osems.at[b, k, ch]
                    )
                )
                writes[-1].start()
    wait_all(writes)


def early_outputs(first, scalars, x, own, far, core, point, after, before=None):
    blocks, h = point.shape[:2]
    count = len(own)
    if first == 0:
        places, group, chunks, r, c = x.shape
    else:
        group, chunks, places, r, c = x.shape
    operands = [scalars, x, *own, *far, core, point]
    specs = [SMEM, HBM if first == 0 else VMEM] + [VMEM] * (2 * count + 2)
    aliases = {}
    if before is not None:
        aliases = {len(operands): 0}
        operands.append(before)
        specs.append(HBM)
    scratch = [
        pltpu.VMEM((group, chunks, places, r, c), BF16),
        pltpu.VMEM((count, group, chunks, places, r, c), BF16),
        pltpu.SemaphoreType.DMA((group, chunks)),
        pltpu.SemaphoreType.DMA((count, group, chunks)),
    ]
    return call(
        functools.partial(early_out_kernel, first, count),
        (array(blocks, places, group, chunks, r, c), array(group, chunks, places, r, c)),
        operands, specs, (HBM, VMEM), scratch, 2 * count * x.size * h, 2 * count * 2**20, aliases, after,
    )


def late_out_kernel(ch, s_ref, a0, a1, a2, a3, point, xs, before, out, ys, osems):
    q = s_ref[0]
    places, r, c = xs.shape[2:]
    last = out.shape[0] - 1
    writes = []
    for k, hidden in enumerate((a0, a1, a2, a3)):
        x = xs[k, ch].reshape(places * r, c).astype(F32) + dot(hidden[...], point[last])
        ys[k] = x.astype(BF16).reshape(places, r, c)
        writes.append(pltpu.make_async_copy(ys.at[k], out.at[last, :, q ^ k, ch], osems.at[k]))
        writes[-1].start()
    wait_all(writes)


def late_outputs(ch, scalars, hiddens, point, xs, before):
    blocks, places, group, chunks, r, c = before.shape
    operands = (scalars, *hiddens, point, xs, before)
    scratch = [pltpu.VMEM((group, places, r, c), BF16), pltpu.SemaphoreType.DMA((group,))]
    return call(
        functools.partial(late_out_kernel, ch), array(*before.shape), operands,
        [SMEM] + [VMEM] * (GROUP + 2) + [HBM], HBM, scratch,
        2 * group * places * r * c * point.shape[1], 2 * 2**20, {len(operands) - 1: 0},
    )


def neighbour_pairs(size, parity):
    groups = size // GROUP
    pairs = []
    for i in range(size):
        group = i // GROUP
        other = group + 1 if group % 2 == parity else group - 1
        pairs.append((i, i + (other - group) * GROUP if 0 <= other < groups else i ^ 1))
    return pairs


def by_residue(signal, taps, point):
    size = lax.axis_size("seq")
    me = lax.axis_index("seq")
    length, c = signal.shape
    places = length // FIRST_DILATION
    r = FIRST_DILATION // GROUP // CHUNKS
    q, group = me % GROUP, me // GROUP
    scalars = jnp.stack(
        [q, group % 2, (group > 0).astype(jnp.int32), (group < size // GROUP - 1).astype(jnp.int32)]
    ).astype(jnp.int32)
    even_pairs, odd_pairs = neighbour_pairs(size, 0), neighbour_pairs(size, 1)
    x = signal.reshape(places, GROUP, CHUNKS, r, c)

    def swap(value, k):
        return lax.ppermute(value, "seq", [(i, i ^ k) for i in range(size)])

    def back(pieces):
        return [pieces[0]] + [swap(pieces[k], k) for k in range(1, GROUP)]

    def across(even, odd):
        return lax.ppermute(even, "seq", even_pairs), lax.ppermute(odd, "seq", odd_pairs)

    pieces = back(split(scalars, x))
    w = side_by_side(taps)
    terms = across(*open_terms(scalars, pieces, w, r))
    current = pieces
    own, core, far = [], [], []
    for block in range(2):
        reach = r * 2**block
        current, hidden, part = local_block(block, scalars, current, w, point, reach)
        current, even, odd, mine, beside, over = finish_edges(
            block, scalars, current, hidden, part, terms, w, point, reach, 2 * reach
        )
        terms = across(even, odd)
        own.append(mine)
        core.append(beside)
        far.append(swap(over, 2))
    reach = 4 * r
    current, hidden, part = local_block(2, scalars, current, w, point, reach)
    current, *sent, ends = finish_edges(
        2, scalars, current, hidden, part, terms, w, point, reach, 2 * reach
    )
    terms = [across(*sent[2 * ch : 2 * ch + 2]) for ch in range(CHUNKS)]
    near, mine, beside, over = near_terms(scalars, current, hidden, ends, w, reach)
    own.append(mine)
    core.append(beside)
    far.append(swap(over, 2))
    lasts, after = [], ()
    for ch in range(CHUNKS):
        hidden = last_hidden(ch, scalars, near, terms[ch], after)
        lasts.append(back(hidden))
        after = hidden[:1]
        if ch == 0:
            early = swap(forward(core[:2], far[:2], after), 1)
    late = swap(forward(core[2:], far[2:], after), 1)
    out, xs = early_outputs(0, scalars, x, own[:2], far[:2], early, point, after)
    out, xs = early_outputs(2, scalars, xs, own[2:], far[2:], late, point, (), out)
    for ch in range(CHUNKS):
        out = late_outputs(ch, scalars, lasts[ch], point, xs, out)
    return out.reshape(point.shape[0], length, c)


def passed_along(value, by):
    size = lax.axis_size("seq")
    pairs = [(i, i + by) for i in range(size) if 0 <= i + by < size]
    return lax.ppermute(value, "seq", pairs)


def by_neighbours(signal, taps, point):
    length = signal.shape[0]
    current = signal
    outputs = []
    for block in range(taps.shape[0]):
        step = FIRST_DILATION * 2**block
        low = dot(current, taps[block, 0]).astype(BF16)
        high = dot(current, taps[block, 2]).astype(BF16)
        if step < length:
            below = jnp.concatenate([passed_along(low[length - step :], 1), low[: length - step]])
            above = jnp.concatenate([high[step:], passed_along(high[:step], -1)])
        else:
            below = passed_along(low, step // length)
            above = passed_along(high, -(step // length))
        v = dot(current, taps[block, 1]) + below.astype(F32) + above.astype(F32)
        hidden = jax.nn.gelu(v, approximate=True).astype(BF16)
        current = (current.astype(F32) + dot(hidden, point[block])).astype(BF16)
        outputs.append(current)
    return jnp.stack(outputs)


def shards(signal, taps, point):
    fits = (
        taps.shape[0] == 4
        and signal.shape[0] == GROUP * FIRST_DILATION
        and lax.axis_size("seq") % GROUP == 0
    )
    return (by_residue if fits else by_neighbours)(signal, taps, point)


def solution(mesh):
    in_specs = (P(("grp", "seq"), None), P(), P())
    out_specs = P(None, ("grp", "seq"), None)
    return jax.shard_map(shards, mesh=mesh, in_specs=in_specs, out_specs=out_specs, check_vma=False)
```

time: 128 us -> 81.7 us (0.64)
  waiting for transfers between devices: 59.5 us -> 20.4 us
  matrix products: 36.2 us -> 0 us
  Pallas kernels: 0 us -> 32.8 us
  other arithmetic: 5.08 us -> 0.08 us
  local copies, waits for them, and re-layouts: 1.82 us -> 4.42 us
    ppermute x8 -> x24, waiting for transfers between devices: 59.5 us -> 20.4 us  [the longest x14 13.9 us: swap(): return lax.ppermute(value, 'seq', [(i, i ^ k) for i in range(size)])]
    dot_general x12 -> x0, matrix products: 36.2 us -> none  [the longest x4 18.7 us: shards(): jnp.dot(hidden, point_weight[block_layer_index], preferred_element_type=j...]
    pallas_call x0 -> x18, Pallas kernels: none -> 32.8 us  [call(): pl.pallas_call(kernel, out_shape=outs, in_specs=specs, out_specs=out_spec...]
    another operation x1, other arithmetic: 5.08 us -> 0.08 us  [by_residue(): jnp.stack([q, group % 2, (group > 0).astype(jnp.int32), (group < size //...]
    unnamed x8, local copies, waits for them, and re-layouts: 0.76 us -> 4.42 us
    ppermute x8 -> x24, starting transfers between devices: 24.5 us -> 23.4 us  [the longest x14 12.4 us: swap(): return lax.ppermute(value, 'seq', [(i, i ^ k) for i in range(size)])]
  transfers between devices with their start and end apart: 8 -> 24, of which waited for: 7 -> 5; matrix products, arithmetic and copies ran while one was open for 2% -> 0% of each run, Pallas kernels for 0% -> 34%
where the time goes in v2:
time: 81.7 us; the launch traced here: 81.5 us
  Pallas kernels  32.8 us (40%)
  starting transfers between devices  23.4 us (29%)
  waiting for transfers between devices  20.4 us (25%)
  local copies, waits for them, and re-layouts  4.42 us (5%)
    pallas_call x18, Pallas kernels, call(): pl.pallas_call(kernel, out_shape=outs, in_specs=specs, out_specs=out_spec...  32.8 us
    ppermute x14, waiting for transfers between devices, swap(): return lax.ppermute(value, 'seq', [(i, i ^ k) for i in range(size)])  13.9 us
    ppermute x14, starting transfers between devices, swap(): return lax.ppermute(value, 'seq', [(i, i ^ k) for i in range(size)])  12.4 us
    ppermute x5, waiting for transfers between devices, across(): lax.ppermute(even, 'seq', even_pairs)  6.5 us
    ppermute x5, starting transfers between devices, across(): lax.ppermute(even, 'seq', even_pairs)  6.46 us
    ppermute x5, starting transfers between devices, across(): lax.ppermute(odd, 'seq', odd_pairs)  4.59 us
    unnamed x8, local copies, waits for them, and re-layouts  4.42 us
  transfers between devices with their start and end apart: 24, of which 5 were waited for; matrix products, arithmetic and copies ran while one was open for 0% of the time, Pallas kernels for 34%

profile of v2, /device:TPU:1, one launch (start us, length us, event | category | flops | bytes accessed | tf_op | source)
XLA Modules:
  0.0 81.5 jit_solution(11302573711079181411)
XLA Ops:
  0.1 1.4 %copy-done.2 = bf16[1024,768]{1,0:T(8,128)(2,1)S(1)} copy-done((bf16[1024,768]{1,0:T(8,128)(2,1)S(1)}, bf16[1024,768]{1,0:T(8,128)(2,1)}, u32[]{:S(2)}) %copy-start.2) | copy-done | bytes 1572888
  1.5 1.1 %shard_map.37 = (bf16[2,4,32,768]{3,2,1,0:T(8,128)(2,1)S(1)}, bf16[2,4,32,768]{3,2,1,0:T(8,128)(2,1)S(1)}, bf16[2,4,32,768]{3,2,1,0:T(8,128)(2,1)S(1)}, bf16[2,4,32,768]{3,2,1,0:T(8,128)(2,1)S(1)}) custom-call(s32[4]{0:T(128)S(1)} %pad_add_fusion.s_ref.refs_0_, bf16[4,4,2,32,768]{4,3,2,1,0:T(8,128)(2,1)S(1)} %bitcast.10), custom_call_target="tpu_custom_call" | custom-call | bytes 3145728 | tf_op jit(solution)/shard_map/pallas_call | solution.py:55
  2.8 2.7 %collective-permute-start.1 = (bf16[256,768]{1,0:T(8,128)(2,1)S(1)}, bf16[256,768]{1,0:T(8,128)(2,1)S(1)}, u32[]{:S(2)}, u32[]{:S(2)}) collective-permute-start(bf16[256,768]{1,0:T(8,128)(2,1)S(1)} %bitcast.15), channel_id=1, source_target_pairs={{0,2},{1,3},{2,0},{3,1},{4,6},{5,7},{6,4},{7,5},{8,10},{9,11},{10,... | collective-permute-start | bytes 1179656 | tf_op jit(solution)/shard_map/ppermute | solution.py:476
  5.5 3.0 %copy-done.1 = bf16[4,3,768,384]{3,2,1,0:T(8,128)(2,1)S(1)} copy-done((bf16[4,3,768,384]{3,2,1,0:T(8,128)(2,1)S(1)}, bf16[4,3,768,384]{3,2,1,0:T(8,128)(2,1)}, u32[]{:S(2)}) %copy-start.1) | copy-done | bytes 7077912
  9.4 5.5 %collective-permute-done.1.r2 = bf16[256,768]{1,0:T(8,128)(2,1)S(1)} collective-permute-done((bf16[256,768]{1,0:T(8,128)(2,1)S(1)}, bf16[256,768]{1,0:T(8,128)(2,1)S(1)}, u32[]{:S(2)}, u32[]{:S(2)}) %collective-permute-start.1) | collective-permute-done | bytes 393248 | tf_op jit(solution)/shard_map/ppermute | solution.py:476
  14.8 8.4 %collective-permute-done.2.r3 = bf16[256,768]{1,0:T(8,128)(2,1)S(1)} collective-permute-done((bf16[256,768]{1,0:T(8,128)(2,1)S(1)}, bf16[256,768]{1,0:T(8,128)(2,1)S(1)}, u32[]{:S(2)}, u32[]{:S(2)}) %collective-permute-start.2) | collective-permute-done | bytes 393248 | tf_op jit(solution)/shard_map/ppermute | solution.py:476
  24.2 1.6 %collective-permute-start.3 = (bf16[64,384]{1,0:T(8,128)(2,1)S(1)}, bf16[64,384]{1,0:T(8,128)(2,1)S(1)}, u32[]{:S(2)}, u32[]{:S(2)}) collective-permute-start(bf16[64,384]{1,0:T(8,128)(2,1)S(1)} %get-tuple-element.61), channel_id=1, source_target_pairs={{0,4},{1,5},{2,6},{3,7},{4,0},{5,1},{6,2},{7,3},{8,12},{9,13},{10,... | collective-permute-start | bytes 147464 | tf_op jit(solution)/shard_map/ppermute | solution.py:482
  26.3 4.0 %shard_map.39 = (bf16[1024,768]{1,0:T(8,128)(2,1)S(1)}, bf16[1024,384]{1,0:T(8,128)(2,1)S(1)}, f32[128,384]{1,0:T(8,128)S(1)}) custom-call(s32[4]{0:T(128)S(1)} %pad_add_fusion.s_ref.refs_0_, bf16[256,768]{1,0:T(8,128)(2,1)S(1)} %bitcast.13, bf16[256,768]{1,0:T(8,128)(2,1)S(1)} %collective-permute-done.r1, bf16[256,768]{1,0:T(8,128)(2,1)S(1)} %collective-permute-done.1.r2, ...), custom_call_target="tpu_custom_call" | custom-call | flops 2415919104 | bytes 4194304 | tf_op jit(solution)/shard_map/pallas_call | solution.py:55
  30.3 1.3 %shard_map.41 = (bf16[1024,768]{1,0:T(8,128)(2,1)S(1)}, bf16[128,384]{1,0:T(8,128)(2,1)S(1)}, bf16[128,384]{1,0:T(8,128)(2,1)S(1)}, bf16[256,384]{1,0:T(8,128)(2...) custom-call(s32[4]{0:T(128)S(1)} %pad_add_fusion.s_ref.refs_0_, ...), custom_call_target="tpu_custom_call", output_to_operand_aliasing={{0}: (1, {})} | custom-call | flops 226492416 | bytes 4194304 | tf_op jit(solution)/shard_map/pallas_call | solution.py:55
  31.6 2.1 %collective-permute-start.5 = (bf16[128,384]{1,0:T(8,128)(2,1)S(1)}, bf16[128,384]{1,0:T(8,128)(2,1)S(1)}, u32[]{:S(2)}, u32[]{:S(2)}) collective-permute-start(bf16[128,384]{1,0:T(8,128)(2,1)S(1)} %get-tuple-element.67), channel_id=1, source_target_pairs={{0,4},{1,5},{2,6},{3,7},{4,0},{5,1},{6,2},{7,3},{8,12},{9,13},{10,... | collective-permute-start | bytes 294920 | tf_op jit(solution)/shard_map/ppermute | solution.py:482
  33.7 1.1 %collective-permute-start.6 = (bf16[128,384]{1,0:T(8,128)(2,1)S(1)}, bf16[128,384]{1,0:T(8,128)(2,1)S(1)}, u32[]{:S(2)}, u32[]{:S(2)}) collective-permute-start(bf16[128,384]{1,0:T(8,128)(2,1)S(1)} %get-tuple-element.68), channel_id=1, source_target_pairs={{0,1},{1,0},{2,3},{3,2},{4,8},{5,9},{6,10},{7,11},{8,4},{9,5},{10,... | collective-permute-start | bytes 294920 | tf_op jit(solution)/shard_map/ppermute | solution.py:482
  34.8 1.2 %collective-permute-start.16 = (bf16[512,384]{1,0:T(8,128)(2,1)S(1)}, bf16[512,384]{1,0:T(8,128)(2,1)S(1)}, u32[]{:S(2)}, u32[]{:S(2)}) collective-permute-start(bf16[512,384]{1,0:T(8,128)(2,1)S(1)} %get-tuple-element.89), channel_id=1, source_target_pairs={{0,2},{1,3},{2,0},{3,1},{4,6},{5,7},{6,4},{7,5},{8,10},{9,11},{10,... | collective-permute-start | bytes 1179656 | tf_op jit(solution)/shard_map/ppermute | solution.py:476
  36.1 3.0 %shard_map.42 = (bf16[1024,768]{1,0:T(8,128)(2,1)S(1)}, bf16[1024,384]{1,0:T(8,128)(2,1)S(1)}, f32[256,384]{1,0:T(8,128)S(1)}) custom-call(bf16[1024,768]{1,0:T(8,128)(2,1)S(1)} %get-tuple-element.63.x, bf16[4,768,1152]{2,1,0:T(8,128)(2,1)S(1)} %shard_map.38.w, bf16[4,384,768]{2,1,0:T(8,128)(2,1)S(1)} %copy-done), custom_call_target="tpu_custom_call" | custom-call | flops 2415919104 | bytes 4194304 | tf_op jit(solution)/shard_map/pallas_call | solution.py:55
  39.1 1.8 %shard_map.43 = (bf16[1024,768]{1,0:T(8,128)(2,1)S(1)}, bf16[256,384]{1,0:T(8,128)(2,1)S(1)}, bf16[256,384]{1,0:T(8,128)(2,1)S(1)}, bf16[256,384]{1,0:T(8,128)(2...) custom-call(s32[4]{0:T(128)S(1)} %pad_add_fusion.s_ref.refs_0_, ...), custom_call_target="tpu_custom_call", output_to_operand_aliasing={{0}: (1, {})} | custom-call | flops 452984832 | bytes 4194304 | tf_op jit(solution)/shard_map/pallas_call | solution.py:55
  40.9 1.0 %collective-permute-start.8 = (bf16[256,384]{1,0:T(8,128)(2,1)S(1)}, bf16[256,384]{1,0:T(8,128)(2,1)S(1)}, u32[]{:S(2)}, u32[]{:S(2)}) collective-permute-start(bf16[256,384]{1,0:T(8,128)(2,1)S(1)} %get-tuple-element.74), channel_id=1, source_target_pairs={{0,1},{1,0},{2,3},{3,2},{4,8},{5,9},{6,10},{7,11},{8,4},{9,5},{10,... | collective-permute-start | bytes 589832 | tf_op jit(solution)/shard_map/ppermute | solution.py:482
  42.6 2.8 %shard_map.44 = (bf16[1024,768]{1,0:T(8,128)(2,1)S(1)}, bf16[1024,384]{1,0:T(8,128)(2,1)S(1)}, f32[512,384]{1,0:T(8,128)S(1)}) custom-call(bf16[1024,768]{1,0:T(8,128)(2,1)S(1)} %get-tuple-element.69.x, bf16[4,768,1152]{2,1,0:T(8,128)(2,1)S(1)} %shard_map.38.w, bf16[4,384,768]{2,1,0:T(8,128)(2,1)S(1)} %copy-done), custom_call_target="tpu_custom_call" | custom-call | flops 2415919104 | bytes 4194304 | tf_op jit(solution)/shard_map/pallas_call | solution.py:55
  45.4 1.7 %collective-permute-done.7.from_even = bf16[256,384]{1,0:T(8,128)(2,1)S(1)} collective-permute-done((bf16[256,384]{1,0:T(8,128)(2,1)S(1)}, bf16[256,384]{1,0:T(8,128)(2,1)S(1)}, u32[]{:S(2)}, u32[]{:S(2)}) %collective-permute-start.7) | collective-permute-done | bytes 196640 | tf_op jit(solution)/shard_map/ppermute | solution.py:482
  47.2 2.2 %shard_map.45 = (bf16[1024,768]{1,0:T(8,128)(2,1)S(1)}, bf16[256,384]{1,0:T(8,128)(2,1)S(1)}, bf16[256,384]{1,0:T(8,128)(2,1)S(1)}, bf16[256,384]{1,0:T(8,128)(2...) custom-call(s32[4]{0:T(128)S(1)} %pad_add_fusion.s_ref.refs_0_, ...), custom_call_target="tpu_custom_call", output_to_operand_aliasing={{0}: (1, {})} | custom-call | flops 905969664 | bytes 4194304 | tf_op jit(solution)/shard_map/pallas_call | solution.py:55
  49.4 1.2 %collective-permute-start.11 = (bf16[256,384]{1,0:T(8,128)(2,1)S(1)}, bf16[256,384]{1,0:T(8,128)(2,1)S(1)}, u32[]{:S(2)}, u32[]{:S(2)}) collective-permute-start(bf16[256,384]{1,0:T(8,128)(2,1)S(1)} %get-tuple-element.80), channel_id=1, source_target_pairs={{0,4},{1,5},{2,6},{3,7},{4,0},{5,1},{6,2},{7,3},{8,12},{9,13},{10,... | collective-permute-start | bytes 589832 | tf_op jit(solution)/shard_map/ppermute | solution.py:482
  50.6 1.7 %collective-permute-start.12 = (bf16[256,384]{1,0:T(8,128)(2,1)S(1)}, bf16[256,384]{1,0:T(8,128)(2,1)S(1)}, u32[]{:S(2)}, u32[]{:S(2)}) collective-permute-start(bf16[256,384]{1,0:T(8,128)(2,1)S(1)} %get-tuple-element.81), channel_id=1, source_target_pairs={{0,1},{1,0},{2,3},{3,2},{4,8},{5,9},{6,10},{7,11},{8,4},{9,5},{10,... | collective-permute-start | bytes 589832 | tf_op jit(solution)/shard_map/ppermute | solution.py:482
  52.3 2.1 %shard_map.46 = (f32[1024,384]{1,0:T(8,128)S(1)}, bf16[256,384]{1,0:T(8,128)(2,1)S(1)}, bf16[256,384]{1,0:T(8,128)(2,1)S(1)}, bf16[512,384]{1,0:T(8,128)(2,1)S(1)}) custom-call(s32[4]{0:T(128)S(1)} %pad_add_fusion.s_ref.refs_0_, bf16[1024,768]{1,0:T(8,128)(2,1)S(1)} %get-tuple-element.75.x, bf16[1024,384]{1,0:T(8,128)(2,1)S(1)} %get-tuple-element.71.hidden, ...), custom_call_target="tpu_custom_call" | custom-call | flops 1207959552 | bytes 4194304 | tf_op jit(solution)/shard_map/pallas_call | solution.py:55
  54.8 1.1 %shard_map.47 = (bf16[128,384]{1,0:T(8,128)(2,1)S(1)}, bf16[128,384]{1,0:T(8,128)(2,1)S(1)}, bf16[128,384]{1,0:T(8,128)(2,1)S(1)}, bf16[128,384]{1,0:T(8,128)(2,1)S(1)}) custom-call(s32[4]{0:T(128)S(1)} %pad_add_fusion.s_ref.refs_0_, f32[1024,384]{1,0:T(8,128)S(1)} %get-tuple-element.77.near.refs_1_, bf16[256,384]{1,0:T(8,128)(2,1)S(1)} %collective-permute-done.11.from_even, ...), custom_call_target="tpu_custom_call" | custom-call | flops 3932160 | bytes 2097152 | tf_op jit(solution)/shard_map/pallas_call | solution.py:55
  55.9 2.1 %collective-permute-start.18 = (bf16[4,256,384]{2,1,0:T(8,128)(2,1)S(1)}, bf16[4,256,384]{2,1,0:T(8,128)(2,1)S(1)}, u32[]{:S(2)}, u32[]{:S(2)}) collective-permute-start(bf16[4,256,384]{2,1,0:T(8,128)(2,1)S(1)} %shard_map.49), channel_id=1, source_target_pairs={{0,1},{1,0},{2,3},{3,2},{4,5},{5,4},{6,7},{7,6},{8,9},{9,8},{10,11... | collective-permute-start | bytes 2359304 | tf_op jit(solution)/shard_map/ppermute | solution.py:476
  58.0 1.5 %collective-permute-start.9 = (bf16[256,384]{1,0:T(8,128)(2,1)S(1)}, bf16[256,384]{1,0:T(8,128)(2,1)S(1)}, u32[]{:S(2)}, u32[]{:S(2)}) collective-permute-start(bf16[256,384]{1,0:T(8,128)(2,1)S(1)} %get-tuple-element.78), channel_id=1, source_target_pairs={{0,4},{1,5},{2,6},{3,7},{4,0},{5,1},{6,2},{7,3},{8,12},{9,13},{10,... | collective-permute-start | bytes 589832 | tf_op jit(solution)/shard_map/ppermute | solution.py:482
  59.8 4.7 %collective-permute-done.9.refs_2_ = bf16[256,384]{1,0:T(8,128)(2,1)S(1)} collective-permute-done((bf16[256,384]{1,0:T(8,128)(2,1)S(1)}, bf16[256,384]{1,0:T(8,128)(2,1)S(1)}, u32[]{:S(2)}, u32[]{:S(2)}) %collective-permute-start.9) | collective-permute-done | bytes 196640 | tf_op jit(solution)/shard_map/ppermute | solution.py:482
  64.5 1.1 %shard_map.48 = (bf16[128,384]{1,0:T(8,128)(2,1)S(1)}, bf16[128,384]{1,0:T(8,128)(2,1)S(1)}, bf16[128,384]{1,0:T(8,128)(2,1)S(1)}, bf16[128,384]{1,0:T(8,128)(2,1)S(1)}) custom-call(s32[4]{0:T(128)S(1)} %pad_add_fusion.s_ref.refs_0_, f32[1024,384]{1,0:T(8,128)S(1)} %get-tuple-element.77.near.refs_1_, bf16[256,384]{1,0:T(8,128)(2,1)S(1)} %collective-permute-done.9.refs_2_, ...), custom_call_target="tpu_custom_call" | custom-call | flops 3932160 | bytes 2097152 | tf_op jit(solution)/shard_map/pallas_call | solution.py:55
  66.8 1.9 %collective-permute-start.23 = (bf16[128,384]{1,0:T(8,128)(2,1)S(1)}, bf16[128,384]{1,0:T(8,128)(2,1)S(1)}, u32[]{:S(2)}, u32[]{:S(2)}) collective-permute-start(bf16[128,384]{1,0:T(8,128)(2,1)S(1)} %get-tuple-element.101), channel_id=1, source_target_pairs={{0,3},{1,2},{2,1},{3,0},{4,7},{5,6},{6,5},{7,4},{8,11},{9,10},{10,... | collective-permute-start | bytes 294920 | tf_op jit(solution)/shard_map/ppermute | solution.py:476
  69.0 1.9 %collective-permute-start.15 = (bf16[128,384]{1,0:T(8,128)(2,1)S(1)}, bf16[128,384]{1,0:T(8,128)(2,1)S(1)}, u32[]{:S(2)}, u32[]{:S(2)}) collective-permute-start(bf16[128,384]{1,0:T(8,128)(2,1)S(1)} %get-tuple-element.86), channel_id=1, source_target_pairs={{0,3},{1,2},{2,1},{3,0},{4,7},{5,6},{6,5},{7,4},{8,11},{9,10},{10,... | collective-permute-start | bytes 294920 | tf_op jit(solution)/shard_map/ppermute | solution.py:476
  70.9 4.3 %shard_map.50 = (bf16[4,4,4,2,32,768]{5,4,3,2,1,0:T(8,128)(2,1)}, bf16[4,2,4,32,768]{4,3,2,1,0:T(8,128)(2,1)S(1)}) custom-call(s32[4]{0:T(128)S(1)} %pad_add_fusion.s_ref.refs_0_, bf16[4,4,2,32,768]{4,3,2,1,0:T(8,128)(2,1)S(1)} %bitcast.11, bf16[256,384]{1,0:T(8,128)(2,1)S(1)} %get-tuple-element.87.refs_2_, bf16[256,384]{1,0:T(8,128)(2,1)S(1)} %get-tuple-element.88.refs_3_, ...), custom_call_target="tpu_custom_call" | custom-call | flops 1207959552 | bytes 4194304 | tf_op jit(solution)/shard_map/pallas_call | solution.py:55
  75.2 2.4 %shard_map.52 = (bf16[4,4,4,2,32,768]{5,4,3,2,1,0:T(8,128)(2,1)}, bf16[4,2,4,32,768]{4,3,2,1,0:T(8,128)(2,1)S(1)}) custom-call(s32[4]{0:T(128)S(1)} %pad_add_fusion.s_ref.refs_0_, bf16[4,2,4,32,768]{4,3,2,1,0:T(8,128)(2,1)S(1)} %get-tuple-element.93.x, bf16[256,384]{1,0:T(8,128)(2,1)S(1)} %get-tuple-element.94.refs_0_, ...), custom_call_target="tpu_custom_call", output_to_operand_aliasing={{0}: (6, {})} | custom-call | flops 603979776 | bytes 2097152 | tf_op jit(solution)/shard_map/pallas_call | solution.py:55
  77.7 1.8 %shard_map.53.before = bf16[4,4,4,2,32,768]{5,4,3,2,1,0:T(8,128)(2,1)} custom-call(s32[4]{0:T(128)S(1)} %pad_add_fusion.s_ref.refs_0_, bf16[128,384]{1,0:T(8,128)(2,1)S(1)} %get-tuple-element.82.refs_4_.a0, bf16[128,384]{1,0:T(8,128)(2,1)S(1)} %collective-permute-done.21.a1, ...), custom_call_target="tpu_custom_call", output_to_operand_aliasing={{}: (7, {})} | custom-call | flops 301989888 | bytes 2097152 | tf_op jit(solution)/shard_map/pallas_call | solution.py:55
  79.5 1.8 %shard_map.54 = bf16[4,4,4,2,32,768]{5,4,3,2,1,0:T(8,128)(2,1)} custom-call(s32[4]{0:T(128)S(1)} %pad_add_fusion.s_ref.refs_0_, bf16[128,384]{1,0:T(8,128)(2,1)S(1)} %get-tuple-element.83.refs_8_.refs_2_.a0, bf16[128,384]{1,0:T(8,128)(2,1)S(1)} %collective-permute-done.13.a1, ...), custom_call_target="tpu_custom_call", output_to_operand_aliasing={{}: (7, {})} | custom-call | flops 301989888 | bytes 2097152 | tf_op jit(solution)/shard_map/pallas_call | solution.py:55
  (43 shorter events, 5.6 us)
Async XLA Ops:
  0.1 1.4 %copy-start.2 = (bf16[1024,768]{1,0:T(8,128)(2,1)S(1)}, bf16[1024,768]{1,0:T(8,128)(2,1)}, u32[]{:S(2)}) copy-start(bf16[1024,768]{1,0:T(8,128)(2,1)} %param.3) | copy-start | bytes 4718596
  2.6 6.7 %collective-permute-start = (bf16[256,768]{1,0:T(8,128)(2,1)S(1)}, bf16[256,768]{1,0:T(8,128)(2,1)S(1)}, u32[]{:S(2)}, u32[]{:S(2)}) collective-permute-start(bf16[256,768]{1,0:T(8,128)(2,1)S(1)} %bitcast.16), channel_id=1, source_target_pairs={{0,1},{1,0},{2,3},{3,2},{4,5},{5,4},{6,7},{7,6},{8,9},{9,8},{10,11... | collective-permute-start | bytes 1179656 | tf_op jit(solution)/shard_map/ppermute | solution.py:476
  2.8 12.1 %collective-permute-start.1 = (bf16[256,768]{1,0:T(8,128)(2,1)S(1)}, bf16[256,768]{1,0:T(8,128)(2,1)S(1)}, u32[]{:S(2)}, u32[]{:S(2)}) collective-permute-start(bf16[256,768]{1,0:T(8,128)(2,1)S(1)} %bitcast.15), channel_id=1, source_target_pairs={{0,2},{1,3},{2,0},{3,1},{4,6},{5,7},{6,4},{7,5},{8,10},{9,11},{10,... | collective-permute-start | bytes 1179656 | tf_op jit(solution)/shard_map/ppermute | solution.py:476
  5.5 17.8 %collective-permute-start.2 = (bf16[256,768]{1,0:T(8,128)(2,1)S(1)}, bf16[256,768]{1,0:T(8,128)(2,1)S(1)}, u32[]{:S(2)}, u32[]{:S(2)}) collective-permute-start(bf16[256,768]{1,0:T(8,128)(2,1)S(1)} %bitcast.14), channel_id=1, source_target_pairs={{0,3},{1,2},{2,1},{3,0},{4,7},{5,6},{6,5},{7,4},{8,11},{9,10},{10,... | collective-permute-start | bytes 1179656 | tf_op jit(solution)/shard_map/ppermute | solution.py:476
  5.5 3.0 %copy-start.1 = (bf16[4,3,768,384]{3,2,1,0:T(8,128)(2,1)S(1)}, bf16[4,3,768,384]{3,2,1,0:T(8,128)(2,1)}, u32[]{:S(2)}) copy-start(bf16[4,3,768,384]{3,2,1,0:T(8,128)(2,1)} %taps.1) | copy-start | bytes 21233668
  23.3 3.0 %copy-start = (bf16[4,384,768]{2,1,0:T(8,128)(2,1)S(1)}, bf16[4,384,768]{2,1,0:T(8,128)(2,1)}, u32[]{:S(2)}) copy-start(bf16[4,384,768]{2,1,0:T(8,128)(2,1)} %point.15) | copy-start | bytes 7077892
  24.2 6.1 %collective-permute-start.3 = (bf16[64,384]{1,0:T(8,128)(2,1)S(1)}, bf16[64,384]{1,0:T(8,128)(2,1)S(1)}, u32[]{:S(2)}, u32[]{:S(2)}) collective-permute-start(bf16[64,384]{1,0:T(8,128)(2,1)S(1)} %get-tuple-element.61), channel_id=1, source_target_pairs={{0,4},{1,5},{2,6},{3,7},{4,0},{5,1},{6,2},{7,3},{8,12},{9,13},{10,... | collective-permute-start | bytes 147464 | tf_op jit(solution)/shard_map/ppermute | solution.py:482
  25.7 4.5 %collective-permute-start.4 = (bf16[64,384]{1,0:T(8,128)(2,1)S(1)}, bf16[64,384]{1,0:T(8,128)(2,1)S(1)}, u32[]{:S(2)}, u32[]{:S(2)}) collective-permute-start(bf16[64,384]{1,0:T(8,128)(2,1)S(1)} %get-tuple-element.62), channel_id=1, source_target_pairs={{0,1},{1,0},{2,3},{3,2},{4,8},{5,9},{6,10},{7,11},{8,4},{9,5},{10,... | collective-permute-start | bytes 147464 | tf_op jit(solution)/shard_map/ppermute | solution.py:482
  31.6 7.5 %collective-permute-start.5 = (bf16[128,384]{1,0:T(8,128)(2,1)S(1)}, bf16[128,384]{1,0:T(8,128)(2,1)S(1)}, u32[]{:S(2)}, u32[]{:S(2)}) collective-permute-start(bf16[128,384]{1,0:T(8,128)(2,1)S(1)} %get-tuple-element.67), channel_id=1, source_target_pairs={{0,4},{1,5},{2,6},{3,7},{4,0},{5,1},{6,2},{7,3},{8,12},{9,13},{10,... | collective-permute-start | bytes 294920 | tf_op jit(solution)/shard_map/ppermute | solution.py:482
  33.7 5.3 %collective-permute-start.6 = (bf16[128,384]{1,0:T(8,128)(2,1)S(1)}, bf16[128,384]{1,0:T(8,128)(2,1)S(1)}, u32[]{:S(2)}, u32[]{:S(2)}) collective-permute-start(bf16[128,384]{1,0:T(8,128)(2,1)S(1)} %get-tuple-element.68), channel_id=1, source_target_pairs={{0,1},{1,0},{2,3},{3,2},{4,8},{5,9},{6,10},{7,11},{8,4},{9,5},{10,... | collective-permute-start | bytes 294920 | tf_op jit(solution)/shard_map/ppermute | solution.py:482
  34.8 21.0 %collective-permute-start.16 = (bf16[512,384]{1,0:T(8,128)(2,1)S(1)}, bf16[512,384]{1,0:T(8,128)(2,1)S(1)}, u32[]{:S(2)}, u32[]{:S(2)}) collective-permute-start(bf16[512,384]{1,0:T(8,128)(2,1)S(1)} %get-tuple-element.89), channel_id=1, source_target_pairs={{0,2},{1,3},{2,0},{3,1},{4,6},{5,7},{6,4},{7,5},{8,10},{9,11},{10,... | collective-permute-start | bytes 1179656 | tf_op jit(solution)/shard_map/ppermute | solution.py:476
  40.9 6.3 %collective-permute-start.7 = (bf16[256,384]{1,0:T(8,128)(2,1)S(1)}, bf16[256,384]{1,0:T(8,128)(2,1)S(1)}, u32[]{:S(2)}, u32[]{:S(2)}) collective-permute-start(bf16[256,384]{1,0:T(8,128)(2,1)S(1)} %get-tuple-element.73), channel_id=1, source_target_pairs={{0,4},{1,5},{2,6},{3,7},{4,0},{5,1},{6,2},{7,3},{8,12},{9,13},{10,... | collective-permute-start | bytes 589832 | tf_op jit(solution)/shard_map/ppermute | solution.py:482
  40.9 6.2 %collective-permute-start.8 = (bf16[256,384]{1,0:T(8,128)(2,1)S(1)}, bf16[256,384]{1,0:T(8,128)(2,1)S(1)}, u32[]{:S(2)}, u32[]{:S(2)}) collective-permute-start(bf16[256,384]{1,0:T(8,128)(2,1)S(1)} %get-tuple-element.74), channel_id=1, source_target_pairs={{0,1},{1,0},{2,3},{3,2},{4,8},{5,9},{6,10},{7,11},{8,4},{9,5},{10,... | collective-permute-start | bytes 589832 | tf_op jit(solution)/shard_map/ppermute | solution.py:482
  41.9 14.0 %collective-permute-start.17 = (bf16[512,384]{1,0:T(8,128)(2,1)S(1)}, bf16[512,384]{1,0:T(8,128)(2,1)S(1)}, u32[]{:S(2)}, u32[]{:S(2)}) collective-permute-start(bf16[512,384]{1,0:T(8,128)(2,1)S(1)} %get-tuple-element.90), channel_id=1, source_target_pairs={{0,2},{1,3},{2,0},{3,1},{4,6},{5,7},{6,4},{7,5},{8,10},{9,11},{10,... | collective-permute-start | bytes 1179656 | tf_op jit(solution)/shard_map/ppermute | solution.py:476
  49.4 5.4 %collective-permute-start.11 = (bf16[256,384]{1,0:T(8,128)(2,1)S(1)}, bf16[256,384]{1,0:T(8,128)(2,1)S(1)}, u32[]{:S(2)}, u32[]{:S(2)}) collective-permute-start(bf16[256,384]{1,0:T(8,128)(2,1)S(1)} %get-tuple-element.80), channel_id=1, source_target_pairs={{0,4},{1,5},{2,6},{3,7},{4,0},{5,1},{6,2},{7,3},{8,12},{9,13},{10,... | collective-permute-start | bytes 589832 | tf_op jit(solution)/shard_map/ppermute | solution.py:482
  50.6 4.2 %collective-permute-start.12 = (bf16[256,384]{1,0:T(8,128)(2,1)S(1)}, bf16[256,384]{1,0:T(8,128)(2,1)S(1)}, u32[]{:S(2)}, u32[]{:S(2)}) collective-permute-start(bf16[256,384]{1,0:T(8,128)(2,1)S(1)} %get-tuple-element.81), channel_id=1, source_target_pairs={{0,1},{1,0},{2,3},{3,2},{4,8},{5,9},{6,10},{7,11},{8,4},{9,5},{10,... | collective-permute-start | bytes 589832 | tf_op jit(solution)/shard_map/ppermute | solution.py:482
  54.4 11.2 %collective-permute-start.19 = (bf16[512,384]{1,0:T(8,128)(2,1)S(1)}, bf16[512,384]{1,0:T(8,128)(2,1)S(1)}, u32[]{:S(2)}, u32[]{:S(2)}) collective-permute-start(bf16[512,384]{1,0:T(8,128)(2,1)S(1)} %get-tuple-element.95), channel_id=1, source_target_pairs={{0,2},{1,3},{2,0},{3,1},{4,6},{5,7},{6,4},{7,5},{8,10},{9,11},{10,... | collective-permute-start | bytes 1179656 | tf_op jit(solution)/shard_map/ppermute | solution.py:476
  55.9 13.0 %collective-permute-start.18 = (bf16[4,256,384]{2,1,0:T(8,128)(2,1)S(1)}, bf16[4,256,384]{2,1,0:T(8,128)(2,1)S(1)}, u32[]{:S(2)}, u32[]{:S(2)}) collective-permute-start(bf16[4,256,384]{2,1,0:T(8,128)(2,1)S(1)} %shard_map.49), channel_id=1, source_target_pairs={{0,1},{1,0},{2,3},{3,2},{4,5},{5,4},{6,7},{7,6},{8,9},{9,8},{10,11... | collective-permute-start | bytes 2359304 | tf_op jit(solution)/shard_map/ppermute | solution.py:476
  58.0 6.5 %collective-permute-start.9 = (bf16[256,384]{1,0:T(8,128)(2,1)S(1)}, bf16[256,384]{1,0:T(8,128)(2,1)S(1)}, u32[]{:S(2)}, u32[]{:S(2)}) collective-permute-start(bf16[256,384]{1,0:T(8,128)(2,1)S(1)} %get-tuple-element.78), channel_id=1, source_target_pairs={{0,4},{1,5},{2,6},{3,7},{4,0},{5,1},{6,2},{7,3},{8,12},{9,13},{10,... | collective-permute-start | bytes 589832 | tf_op jit(solution)/shard_map/ppermute | solution.py:482
  59.5 11.4 %copy-start.3 = (bf16[1024,768]{1,0:T(8,128)(2,1)S(1)}, bf16[1024,768]{1,0:T(8,128)(2,1)}, u32[]{:S(2)}) copy-start(bf16[1024,768]{1,0:T(8,128)(2,1)} %param.3) | copy-start | bytes 4718596
  59.5 5.0 %collective-permute-start.10 = (bf16[256,384]{1,0:T(8,128)(2,1)S(1)}, bf16[256,384]{1,0:T(8,128)(2,1)S(1)}, u32[]{:S(2)}, u32[]{:S(2)}) collective-permute-start(bf16[256,384]{1,0:T(8,128)(2,1)S(1)} %get-tuple-element.79), channel_id=1, source_target_pairs={{0,1},{1,0},{2,3},{3,2},{4,8},{5,9},{6,10},{7,11},{8,4},{9,5},{10,... | collective-permute-start | bytes 589832 | tf_op jit(solution)/shard_map/ppermute | solution.py:482
  65.6 3.1 %collective-permute-start.20 = (bf16[2,256,384]{2,1,0:T(8,128)(2,1)S(1)}, bf16[2,256,384]{2,1,0:T(8,128)(2,1)S(1)}, u32[]{:S(2)}, u32[]{:S(2)}) collective-permute-start(bf16[2,256,384]{2,1,0:T(8,128)(2,1)S(1)} %shard_map.51), channel_id=1, source_target_pairs={{0,1},{1,0},{2,3},{3,2},{4,5},{5,4},{6,7},{7,6},{8,9},{9,8},{10,11... | collective-permute-start | bytes 1179656 | tf_op jit(solution)/shard_map/ppermute | solution.py:476
  66.6 2.1 %collective-permute-start.21 = (bf16[128,384]{1,0:T(8,128)(2,1)S(1)}, bf16[128,384]{1,0:T(8,128)(2,1)S(1)}, u32[]{:S(2)}, u32[]{:S(2)}) collective-permute-start(bf16[128,384]{1,0:T(8,128)(2,1)S(1)} %get-tuple-element.99), channel_id=1, source_target_pairs={{0,1},{1,0},{2,3},{3,2},{4,5},{5,4},{6,7},{7,6},{8,9},{9,8},{10,11... | collective-permute-start | bytes 294920 | tf_op jit(solution)/shard_map/ppermute | solution.py:476
  66.6 11.0 %collective-permute-start.22 = (bf16[128,384]{1,0:T(8,128)(2,1)S(1)}, bf16[128,384]{1,0:T(8,128)(2,1)S(1)}, u32[]{:S(2)}, u32[]{:S(2)}) collective-permute-start(bf16[128,384]{1,0:T(8,128)(2,1)S(1)} %get-tuple-element.100), channel_id=1, source_target_pairs={{0,2},{1,3},{2,0},{3,1},{4,6},{5,7},{6,4},{7,5},{8,10},{9,11},{10,... | collective-permute-start | bytes 294920 | tf_op jit(solution)/shard_map/ppermute | solution.py:476
  66.8 10.8 %collective-permute-start.23 = (bf16[128,384]{1,0:T(8,128)(2,1)S(1)}, bf16[128,384]{1,0:T(8,128)(2,1)S(1)}, u32[]{:S(2)}, u32[]{:S(2)}) collective-permute-start(bf16[128,384]{1,0:T(8,128)(2,1)S(1)} %get-tuple-element.101), channel_id=1, source_target_pairs={{0,3},{1,2},{2,1},{3,0},{4,7},{5,6},{6,5},{7,4},{8,11},{9,10},{10,... | collective-permute-start | bytes 294920 | tf_op jit(solution)/shard_map/ppermute | solution.py:476
  68.7 10.8 %collective-permute-start.13 = (bf16[128,384]{1,0:T(8,128)(2,1)S(1)}, bf16[128,384]{1,0:T(8,128)(2,1)S(1)}, u32[]{:S(2)}, u32[]{:S(2)}) collective-permute-start(bf16[128,384]{1,0:T(8,128)(2,1)S(1)} %get-tuple-element.84), channel_id=1, source_target_pairs={{0,1},{1,0},{2,3},{3,2},{4,5},{5,4},{6,7},{7,6},{8,9},{9,8},{10,11... | collective-permute-start | bytes 294920 | tf_op jit(solution)/shard_map/ppermute | solution.py:476
  68.7 10.8 %collective-permute-start.14 = (bf16[128,384]{1,0:T(8,128)(2,1)S(1)}, bf16[128,384]{1,0:T(8,128)(2,1)S(1)}, u32[]{:S(2)}, u32[]{:S(2)}) collective-permute-start(bf16[128,384]{1,0:T(8,128)(2,1)S(1)} %get-tuple-element.85), channel_id=1, source_target_pairs={{0,2},{1,3},{2,0},{3,1},{4,6},{5,7},{6,4},{7,5},{8,10},{9,11},{10,... | collective-permute-start | bytes 294920 | tf_op jit(solution)/shard_map/ppermute | solution.py:476
  69.0 10.5 %collective-permute-start.15 = (bf16[128,384]{1,0:T(8,128)(2,1)S(1)}, bf16[128,384]{1,0:T(8,128)(2,1)S(1)}, u32[]{:S(2)}, u32[]{:S(2)}) collective-permute-start(bf16[128,384]{1,0:T(8,128)(2,1)S(1)} %get-tuple-element.86), channel_id=1, source_target_pairs={{0,3},{1,2},{2,1},{3,0},{4,7},{5,6},{6,5},{7,4},{8,11},{9,10},{10,... | collective-permute-start | bytes 294920 | tf_op jit(solution)/shard_map/ppermute | solution.py:476

commit v3 on v2

v3 whole, which is shorter than its diff:
```python
import functools

import jax
import jax.numpy as jnp
from jax import lax
from jax.experimental import pallas as pl
from jax.experimental.pallas import tpu as pltpu
from jax.sharding import PartitionSpec as P

FIRST_DILATION = 256
GROUP = 4
ROWS = 512
VMEM_LIMIT = 24 * 2**20

F32, BF16 = jnp.float32, jnp.bfloat16
ANY = pl.BlockSpec(memory_space=pl.ANY)
VMEM = pl.BlockSpec(memory_space=pltpu.VMEM)
SMEM = pl.BlockSpec(memory_space=pltpu.SMEM)
HBM = pl.BlockSpec(memory_space=pltpu.HBM)


def dot(a, b):
    return jnp.dot(a, b, preferred_element_type=F32)


def gelu(v):
    half = 0.5 * v
    inner = v * (0.7978845608028654 + 0.035677408136300125 * (v * v))
    return half + half * jnp.tanh(inner)


def over_rows(rows, body):
    for start in range(0, rows, ROWS):
        body(start, min(ROWS, rows - start))


def start_all(copies):
    for copy in copies:
        copy.start()
    return copies


def wait_all(copies):
    for copy in copies:
        copy.wait()


def call(kernel, outs, operands, specs, out_specs, scratch, flops, moved, aliases=None, after=()):
    count = len(operands)
    operands, specs = [*operands, *after], [*specs, *[ANY] * len(after)]
    body = kernel
    if after:
        kernel = lambda *refs: body(*refs[:count], *refs[count + len(after) :])
    return pl.pallas_call(
        kernel,
        out_shape=outs,
        in_specs=specs,
        out_specs=out_specs,
        scratch_shapes=scratch,
        input_output_aliases=aliases or {},
        compiler_params=pltpu.CompilerParams(vmem_limit_bytes=VMEM_LIMIT),
        cost_estimate=pl.CostEstimate(
            flops=int(flops), bytes_accessed=int(moved), transcendentals=0
        ),
    )(*operands)


def array(*shape, dtype=BF16):
    return jax.ShapeDtypeStruct(shape, dtype)


def split_kernel(s_ref, x, g0, g1, g2, g3, sems):
    q = s_ref[0]
    copies = [
        pltpu.make_async_copy(x.at[:, q ^ k], piece, sems.at[k])
        for k, piece in enumerate((g0, g1, g2, g3))
    ]
    wait_all(start_all(copies))


def split(scalars, x):
    places, group, r, c = x.shape
    pieces = (array(places, r, c),) * group
    sems = [pltpu.SemaphoreType.DMA((group,))]
    pieces = call(split_kernel, pieces, (scalars, x), [SMEM, HBM], (VMEM,) * group, sems, 0, 4 * x.size)
    return [piece.reshape(places * r, c) for piece in pieces]


def side_by_side_kernel(taps, w, sems):
    h = taps.shape[3]
    wait_all(
        start_all(
            [
                pltpu.make_async_copy(
                    taps.at[b, t], w.at[b, :, pl.ds(t * h, h)], sems.at[b, t]
                )
                for b in range(taps.shape[0])
                for t in range(3)
            ]
        )
    )


def side_by_side(taps):
    blocks, count, c, h = taps.shape
    sems = [pltpu.SemaphoreType.DMA((blocks, count))]
    return call(side_by_side_kernel, array(blocks, c, count * h), (taps,), [HBM], VMEM, sems, 0, 4 * taps.size)


def place_terms(parity, up, down, even_ref, odd_ref, start, size):
    even_ref[pl.ds(start, size)] = jnp.where(parity == 0, up, down).astype(BF16)
    odd_ref[pl.ds(start, size)] = jnp.where(parity == 0, down, up).astype(BF16)


def arrived(s_ref, from_even, from_odd, start, size):
    even = from_even[pl.ds(start, size)].astype(F32)
    odd = from_odd[pl.ds(start, size)].astype(F32)
    parity, has_lower, has_upper = s_ref[1], s_ref[2], s_ref[3]
    below = jnp.where(has_lower == 0, 0.0, jnp.where(parity == 0, odd, even))
    above = jnp.where(has_upper == 0, 0.0, jnp.where(parity == 0, even, odd))
    return below, above


def open_kernel(r, s_ref, own, r1, r2, r3, w, even_ref, odd_ref, ends):
    q, parity = s_ref[0], s_ref[1]
    rows = own.shape[0]
    h = even_ref.shape[1]

    def fetch(piece, at, to):
        ends[pl.ds(to, r)] = piece[pl.ds(at, r)]

    for k, piece in enumerate((own, r1, r2, r3)):
        pl.when(q ^ k == GROUP - 1)(functools.partial(fetch, piece, rows - r, 0))
        pl.when(q ^ k == 0)(functools.partial(fetch, piece, 0, r))
    up = dot(ends[pl.ds(0, r)], w[0, :, :h])
    down = dot(ends[pl.ds(r, r)], w[0, :, 2 * h :])
    place_terms(parity, up, down, even_ref, odd_ref, 0, r)


def open_terms(scalars, pieces, w, r, after):
    c, h = w.shape[1], w.shape[2] // 3
    terms = array(r, h)
    return call(
        functools.partial(open_kernel, r), (terms, terms), (scalars, *pieces, w),
        [SMEM] + [VMEM] * (GROUP + 1), (VMEM, VMEM), [pltpu.VMEM((2 * r, c), BF16)],
        4 * r * c * h, 2**20, after=after,
    )


def keep_terms(at, terms, low, mid, high):
    h = mid.shape[1]
    low[at] = terms[:, :h].astype(BF16)
    mid[at] = terms[:, h : 2 * h]
    high[at] = terms[:, 2 * h :].astype(BF16)


def piece_taps(q, first, pieces, w, x, low, mid, high):
    for i, piece in enumerate(pieces):
        rows = piece.shape[0]
        at = pl.ds(pl.multiple_of((q ^ (first + i)) * rows, rows), rows)
        x[at] = piece[...]
        keep_terms(at, dot(piece[...], w[0]), low, mid, high)


def block_body(reach, x, point, x_ref, h_ref, part_ref, low, mid, high):
    length = x.shape[0]
    top = length - reach

    def body(start, size):
        at = reach + start
        v = mid[pl.ds(at, size)] + low[pl.ds(start, size)].astype(F32)
        hidden = gelu(v + high[pl.ds(at + reach, size)].astype(F32)).astype(BF16)
        h_ref[pl.ds(at, size)] = hidden
        x_ref[pl.ds(at, size)] = (x[pl.ds(at, size)].astype(F32) + dot(hidden, point)).astype(BF16)

    over_rows(length - 2 * reach, body)
    part_ref[pl.ds(0, reach)] = mid[pl.ds(0, reach)] + high[pl.ds(reach, reach)].astype(F32)
    part_ref[pl.ds(reach, reach)] = mid[pl.ds(top, reach)] + low[pl.ds(top - reach, reach)].astype(F32)
    for at in (0, top):
        x_ref[pl.ds(at, reach)] = x[pl.ds(at, reach)]
        h_ref[pl.ds(at, reach)] = jnp.zeros((reach, h_ref.shape[1]), BF16)


def early_taps_kernel(s_ref, own, r1, w, x, low, mid, high):
    piece_taps(s_ref[0], 0, (own, r1), w, x, low, mid, high)


def early_taps(scalars, pieces, w):
    c, h = w.shape[1], w.shape[2] // 3
    rows = pieces[0].shape[0]
    length = GROUP * rows
    outs = (array(length, c), array(length, h), array(length, h, dtype=F32), array(length, h))
    return call(
        early_taps_kernel, outs, (scalars, *pieces, w), [SMEM] + [VMEM] * 3, (VMEM,) * 4, [],
        12 * rows * c * h, 2**20,
    )


def first_kernel(reach, s_ref, r2, r3, x, low, mid, high, w, point, *refs):
    piece_taps(s_ref[0], 2, (r2, r3), w, x, low, mid, high)
    block_body(reach, x, point[0], *refs[:3], low, mid, high)


def first_block(scalars, early, pieces, w, point, reach):
    c, h = w.shape[1], w.shape[2] // 3
    length = early[0].shape[0]
    outs = (array(length, c), array(length, h), array(2 * reach, h, dtype=F32))
    outs += tuple(array(*e.shape, dtype=e.dtype) for e in early)
    results = call(
        functools.partial(first_kernel, reach), outs, (scalars, *pieces, *early, w, point),
        [SMEM] + [VMEM] * 8, (VMEM,) * 7, [], 8 * length * c * h, 4 * 2**20,
        {3: 3, 4: 4, 5: 5, 6: 6},
    )
    return results[:3]


def middle_kernel(block, reach, parity_ref, x, w, point, x_ref, h_ref, part_ref, *refs):
    sent, (low, mid, high) = refs[:-3], refs[-3:]
    h = mid.shape[1]

    def body(start, size):
        at = pl.ds(start, size)
        keep_terms(at, dot(x[at], w[block]), low, mid, high)

    over_rows(x.shape[0], body)
    block_body(reach, x, point[block], x_ref, h_ref, part_ref, low, mid, high)
    if sent:
        middle = x.shape[0] // 2
        up = dot(x_ref[pl.ds(middle, reach)], w[block + 1, :, :h])
        down = dot(x_ref[pl.ds(middle - reach, reach)], w[block + 1, :, 2 * h :])
        place_terms(parity_ref[1], up, down, *sent, 0, reach)


def middle_block(block, scalars, x, w, point, reach):
    c, h = w.shape[1], w.shape[2] // 3
    length = x.shape[0]
    outs = (array(length, c), array(length, h), array(2 * reach, h, dtype=F32))
    if block + 2 == w.shape[0]:
        outs += (array(reach, h),) * 2
    scratch = [
        pltpu.VMEM((length, h), BF16),
        pltpu.VMEM((length, h), F32),
        pltpu.VMEM((length, h), BF16),
    ]
    return call(
        functools.partial(middle_kernel, block, reach), outs, (scalars, x, w, point),
        [SMEM] + [VMEM] * 3, (VMEM,) * len(outs), scratch, 8 * length * c * h, 4 * 2**20,
    )


def give_back(q, hidden, reach, edges, refs, first):
    rows = hidden.shape[0] // GROUP
    for i, ref in enumerate(refs):
        j = q ^ (first + i)
        ref[...] = hidden[pl.ds(pl.multiple_of(j * rows, rows), rows)]

        @pl.when(j == 0)
        def _(ref=ref):
            ref[pl.ds(0, reach)] = edges[0]

        @pl.when(j == GROUP - 1)
        def _(ref=ref):
            ref[pl.ds(rows - reach, reach)] = edges[1]


def edge_kernel(
    block, reach, ahead, s_ref, x, hidden, part, from_even, from_odd, w, point,
    x_ref, even_ref, odd_ref, far_ref, *refs
):
    q, parity = s_ref[0], s_ref[1]
    length = x.shape[0]
    h = hidden.shape[1]
    rows = length // GROUP
    below, above = arrived(s_ref, from_even, from_odd, 0, reach)
    edges = (
        gelu(part[pl.ds(0, reach)] + below).astype(BF16),
        gelu(part[pl.ds(reach, reach)] + above).astype(BF16),
    )
    more = dot(jnp.concatenate(edges), point[block])
    for i, at in enumerate((0, length - reach)):
        new = x[pl.ds(at, reach)].astype(F32) + more[i * reach : (i + 1) * reach]
        x_ref[pl.ds(at, reach)] = new.astype(BF16)
    up = dot(x_ref[pl.ds(length - ahead, ahead)], w[block + 1, :, :h])
    down = dot(x_ref[pl.ds(0, ahead)], w[block + 1, :, 2 * h :])
    place_terms(parity, up, down, even_ref, odd_ref, 0, ahead)
    give_back(q, hidden, reach, edges, (far_ref.at[0], far_ref.at[1]), 2)
    if block + 2 < w.shape[0]:
        give_back(q, hidden, reach, edges, refs, 1)
    else:
        refs[0][0] = edges[0]
        refs[0][1] = edges[1]


def finish_edges(block, scalars, x, hidden, part, terms, w, point, reach, ahead, after=()):
    c, h = w.shape[1], w.shape[2] // 3
    rows = x.shape[0] // GROUP
    outs = (array(*x.shape),) + (array(ahead, h),) * 2 + (array(2, rows, h),)
    outs += (array(2, reach, h),) if block + 2 == w.shape[0] else (array(rows, h),)
    return call(
        functools.partial(edge_kernel, block, reach, ahead), outs,
        (scalars, x, hidden, part, *terms, w, point),
        [SMEM] + [VMEM] * 7, (VMEM,) * len(outs), [],
        2 * c * h * (2 * reach + 2 * ahead), 4 * 2**20, {1: 0}, after,
    )


def near_kernel(reach, s_ref, x, hidden, ends, from_even, from_odd, w, h_ref, near_ref, core_ref, other):
    length = x.shape[0]
    half = length // 2
    h = near_ref.shape[1]
    block = w.shape[0] - 1
    terms = dot(x[pl.ds(0, half)], w[block, :, : 2 * h])
    other[...] = terms[:, :h].astype(BF16)
    near_ref[...] = terms[:, h:]
    terms = dot(x[pl.ds(half, half)], w[block, :, h:])
    high = terms[:, h:].astype(BF16).astype(F32)
    lower = near_ref[...] + high
    upper = terms[:, :h] + other[...].astype(F32)
    below, above = arrived(s_ref, from_even, from_odd, 0, reach)
    h_ref[0] = gelu(lower[:reach] + below).astype(BF16)
    h_ref[1] = gelu(upper[reach:] + above).astype(BF16)
    near_ref[pl.ds(0, reach)] = lower[reach:]
    near_ref[pl.ds(reach, reach)] = upper[:reach]
    give_back(s_ref[0], hidden, reach, (ends[0], ends[1]), (core_ref,), 1)


def near_terms(scalars, x, hidden, ends, terms, w, reach):
    c, h = w.shape[1], w.shape[2] // 3
    rows = x.shape[0] // GROUP
    half = x.shape[0] // 2
    scratch = [pltpu.VMEM((half, h), BF16)]
    outs = (array(2, reach, h), array(half, h, dtype=F32), array(rows, h))
    return call(
        functools.partial(near_kernel, reach), outs, (scalars, x, hidden, ends, *terms, w),
        [SMEM] + [VMEM] * 6, (VMEM,) * 3, scratch, 4 * x.shape[0] * c * h, 4 * 2**20,
    )


def forward_kernel(*refs):
    out = refs[-1]
    for i in range((len(refs) - 1) // 2):
        out[2 * i] = refs[2 * i][...]
        out[2 * i + 1] = refs[2 * i + 1][1]


def forward(own, passing, after):
    operands = [v for pair in zip(own, passing) for v in pair]
    out = array(len(operands), *own[0].shape)
    return call(forward_kernel, out, operands, [VMEM] * len(operands), VMEM, [], 0, 4 * out.size, after=after)


def last_kernel(s_ref, outer, near, from_even, from_odd, g0, g1, g2, g3, hidden):
    q = s_ref[0]
    reach, h = outer.shape[1:]
    below, above = arrived(s_ref, from_even, from_odd, 0, reach)
    hidden[0] = outer[0]
    hidden[1] = gelu(near[pl.ds(0, reach)] + below).astype(BF16)
    hidden[2] = gelu(near[pl.ds(reach, reach)] + above).astype(BF16)
    hidden[3] = outer[1]
    for k, piece in enumerate((g0, g1, g2, g3)):
        piece[...] = hidden[q ^ k]


def last_hidden(scalars, outer, near, terms, after):
    half, h = near.shape
    return call(
        last_kernel, (array(half // 2, h),) * GROUP, (scalars, outer, near, *terms),
        [SMEM] + [VMEM] * 4, (VMEM,) * GROUP, [pltpu.VMEM((GROUP, half // 2, h), BF16)],
        20 * half * h, 2 * 2**20, after=after,
    )


def early_out_kernel(count, s_ref, x, *refs):
    own, far = refs[:count], refs[count : 2 * count]
    core, lasts, point = refs[2 * count], refs[2 * count + 1 : 2 * count + 3], refs[2 * count + 3]
    out, last, xs, ys, sems, osems = refs[-6:]
    q = s_ref[0]
    places, r, c = xs.shape[1:]
    rows = places * r
    here = pl.ds(pl.multiple_of(q * places, places), places)
    writes = []
    for b in range(count):
        writes.append(pltpu.make_async_copy(own[b].at[here], out.at[b, :, q], osems.at[b, 0]))
    start_all(writes)
    reads = start_all(
        [pltpu.make_async_copy(x.at[:, q ^ k], xs.at[k], sems.at[k]) for k in range(1, GROUP)]
    )

    def write(b, k, now):
        target = last if b + 1 == count else ys.at[min(b, count - 1)]
        target[k] = now.reshape(places, r, c)
        writes.append(pltpu.make_async_copy(target.at[k], out.at[b, :, q ^ k], osems.at[b, k]))
        writes[-1].start()

    for k in range(GROUP):
        if k == 0:
            now = own[count - 1][here].reshape(rows, c)
        else:
            reads[k - 1].wait()
            now = xs[k].reshape(rows, c)
            for b in range(count):
                hidden = (core[2 * b], far[b][0], core[2 * b + 1])[k - 1]
                now = (now.astype(F32) + dot(hidden, point[b])).astype(BF16)
                write(b, k, now)
        if k < 2:
            write(count, k, (now.astype(F32) + dot(lasts[k][...], point[count])).astype(BF16))
    wait_all(writes)


def early_outputs(scalars, x, own, far, core, lasts, point):
    blocks, h = point.shape[:2]
    places, group, r, c = x.shape
    count = blocks - 1
    own = [v.reshape(group * places, r, c) for v in own]
    operands = [scalars, x, *own, *far, core, *lasts, point]
    scratch = [
        pltpu.VMEM((group, places, r, c), BF16),
        pltpu.VMEM((count, group, places, r, c), BF16),
        pltpu.SemaphoreType.DMA((group,)),
        pltpu.SemaphoreType.DMA((blocks, group)),
    ]
    return call(
        functools.partial(early_out_kernel, count),
        (array(blocks, places, group, r, c), array(group, places, r, c)),
        operands, [SMEM, HBM] + [VMEM] * (len(operands) - 2), (HBM, VMEM), scratch,
        2 * blocks * x.size * h, 8 * 2**20,
    )


def late_out_kernel(s_ref, a2, a3, xs, point, _, out, ys, osems):
    q = s_ref[0]
    places, r, c = xs.shape[1:]
    last = out.shape[0] - 1
    writes = []
    for i, hidden in enumerate((a2, a3)):
        x = xs[2 + i].reshape(places * r, c).astype(F32) + dot(hidden[...], point[last])
        ys[i] = x.astype(BF16).reshape(places, r, c)
        writes.append(pltpu.make_async_copy(ys.at[i], out.at[last, :, q ^ (2 + i)], osems.at[i]))
        writes[-1].start()
    wait_all(writes)


def late_outputs(scalars, hiddens, xs, point, before):
    blocks, places, group, r, c = before.shape
    operands = (scalars, *hiddens, xs, point, before)
    scratch = [pltpu.VMEM((2, places, r, c), BF16), pltpu.SemaphoreType.DMA((2,))]
    return call(
        late_out_kernel, array(*before.shape), operands,
        [SMEM] + [VMEM] * 4 + [HBM], HBM, scratch,
        4 * places * r * c * point.shape[1], 2 * 2**20, {len(operands) - 1: 0},
    )


def neighbour_pairs(size, parity):
    groups = size // GROUP
    pairs = []
    for i in range(size):
        group = i // GROUP
        other = group + 1 if group % 2 == parity else group - 1
        pairs.append((i, i + (other - group) * GROUP if 0 <= other < groups else i ^ 1))
    return pairs


def by_residue(signal, taps, point):
    size = lax.axis_size("seq")
    me = lax.axis_index("seq")
    length, c = signal.shape
    places = length // FIRST_DILATION
    r = FIRST_DILATION // GROUP
    q, group = me % GROUP, me // GROUP
    scalars = jnp.stack(
        [q, group % 2, (group > 0).astype(jnp.int32), (group < size // GROUP - 1).astype(jnp.int32)]
    ).astype(jnp.int32)
    even_pairs, odd_pairs = neighbour_pairs(size, 0), neighbour_pairs(size, 1)
    x = signal.reshape(places, GROUP, r, c)

    def swap(value, k):
        return lax.ppermute(value, "seq", [(i, i ^ k) for i in range(size)])

    def back(pieces):
        return [pieces[0]] + [swap(pieces[k], k) for k in range(1, GROUP)]

    def across(even, odd):
        return lax.ppermute(even, "seq", even_pairs), lax.ppermute(odd, "seq", odd_pairs)

    pieces = back(split(scalars, x))
    w = side_by_side(taps)
    early = early_taps(scalars, pieces[:2], w)
    terms = across(*open_terms(scalars, pieces, w, r, early[:1]))
    own, core, far = [], [], []
    for block in range(2):
        reach = r * 2**block
        if block == 0:
            current, hidden, part = first_block(scalars, early, pieces[2:], w, point, reach)
        else:
            current, hidden, part = middle_block(block, scalars, current, w, point, reach)
        current, even, odd, over, beside = finish_edges(
            block, scalars, current, hidden, part, terms, w, point, reach, 2 * reach
        )
        terms = across(even, odd)
        own.append(current)
        core.append(beside)
        far.append(swap(over, 2))
    reach = 4 * r
    current, hidden, part, *inner = middle_block(2, scalars, current, w, point, reach)
    inner = across(*inner)
    current, even, odd, over, ends = finish_edges(
        2, scalars, current, hidden, part, terms, w, point, reach, reach, far[:1]
    )
    terms = across(even, odd)
    own.append(current)
    far.append(swap(over, 2))
    outer, near, beside = near_terms(scalars, current, hidden, ends, inner, w, reach)
    core.append(beside)
    hidden = last_hidden(scalars, outer, near, terms, far[1:2])
    after = (hidden[0],)
    lasts = back(hidden)
    beside = swap(forward(core, far, after), 1)
    out, xs = early_outputs(scalars, x, own, far, beside, lasts[:2], point)
    out = late_outputs(scalars, lasts[2:], xs, point, out)
    return out.reshape(point.shape[0], length, c)


def passed_along(value, by):
    size = lax.axis_size("seq")
    pairs = [(i, i + by) for i in range(size) if 0 <= i + by < size]
    return lax.ppermute(value, "seq", pairs)


def by_neighbours(signal, taps, point):
    length = signal.shape[0]
    current = signal
    outputs = []
    for block in range(taps.shape[0]):
        step = FIRST_DILATION * 2**block
        low = dot(current, taps[block, 0]).astype(BF16)
        high = dot(current, taps[block, 2]).astype(BF16)
        if step < length:
            below = jnp.concatenate([passed_along(low[length - step :], 1), low[: length - step]])
            above = jnp.concatenate([high[step:], passed_along(high[:step], -1)])
        else:
            below = passed_along(low, step // length)
            above = passed_along(high, -(step // length))
        v = dot(current, taps[block, 1]) + below.astype(F32) + above.astype(F32)
        hidden = jax.nn.gelu(v, approximate=True).astype(BF16)
        current = (current.astype(F32) + dot(hidden, point[block])).astype(BF16)
        outputs.append(current)
    return jnp.stack(outputs)


def shards(signal, taps, point):
    fits = (
        taps.shape[0] == 4
        and signal.shape[0] == GROUP * FIRST_DILATION
        and lax.axis_size("seq") % GROUP == 0
    )
    return (by_residue if fits else by_neighbours)(signal, taps, point)


def solution(mesh):
    in_specs = (P(("grp", "seq"), None), P(), P())
    out_specs = P(None, ("grp", "seq"), None)
    return jax.shard_map(shards, mesh=mesh, in_specs=in_specs, out_specs=out_specs, check_vma=False)
```

time: 81.7 us -> 75.5 us (0.924)
  starting transfers between devices: 23.4 us -> 19.4 us
  Pallas kernels: 32.8 us -> 29.8 us
    ppermute x14 -> x10, waiting for transfers between devices: 13.9 us -> 18.1 us  [swap(): return lax.ppermute(value, 'seq', [(i, i ^ k) for i in range(size)])]
    ppermute x14 -> x10, starting transfers between devices: 12.4 us -> 8.53 us  [swap(): return lax.ppermute(value, 'seq', [(i, i ^ k) for i in range(size)])]
    ppermute x5, waiting for transfers between devices: 6.5 us -> 3.18 us  [across(): lax.ppermute(even, 'seq', even_pairs)]
    pallas_call x18 -> x15, Pallas kernels: 32.8 us -> 29.8 us  [call(): pl.pallas_call(kernel, out_shape=outs, in_specs=specs, out_specs=out_spec...]
    ppermute x5, starting transfers between devices: 6.46 us -> 3.62 us  [across(): lax.ppermute(even, 'seq', even_pairs)]
    ppermute x5, starting transfers between devices: 4.59 us -> 7.26 us  [across(): lax.ppermute(odd, 'seq', odd_pairs)]
  transfers between devices with their start and end apart: 24 -> 20, of which waited for: 5 -> 7; matrix products, arithmetic and copies ran while one was open for 0% -> 0% of each run, Pallas kernels for 34% -> 33%
where the time goes in v3:
time: 75.5 us; the launch traced here: 75.3 us
  Pallas kernels  29.8 us (39%)
  waiting for transfers between devices  21.2 us (28%)
  starting transfers between devices  19.4 us (26%)
  local copies, waits for them, and re-layouts  4.42 us (6%)
    pallas_call x15, Pallas kernels, call(): pl.pallas_call(kernel, out_shape=outs, in_specs=specs, out_specs=out_spec...  29.8 us
    ppermute x10, waiting for transfers between devices, swap(): return lax.ppermute(value, 'seq', [(i, i ^ k) for i in range(size)])  18.1 us
    ppermute x10, starting transfers between devices, swap(): return lax.ppermute(value, 'seq', [(i, i ^ k) for i in range(size)])  8.53 us
    ppermute x5, starting transfers between devices, across(): lax.ppermute(odd, 'seq', odd_pairs)  7.26 us
    unnamed x8, local copies, waits for them, and re-layouts  4.42 us
    ppermute x5, starting transfers between devices, across(): lax.ppermute(even, 'seq', even_pairs)  3.62 us
    ppermute x5, waiting for transfers between devices, across(): lax.ppermute(even, 'seq', even_pairs)  3.18 us
  transfers between devices with their start and end apart: 20, of which 7 were waited for; matrix products, arithmetic and copies ran while one was open for 0% of the time, Pallas kernels for 33%

profile of v3, /device:TPU:1, one launch (start us, length us, event | category | flops | bytes accessed | tf_op | source)
XLA Modules:
  0.0 75.3 jit_solution(2111871241005741364)
XLA Ops:
  0.1 1.4 %copy-done.2 = bf16[1024,768]{1,0:T(8,128)(2,1)S(1)} copy-done((bf16[1024,768]{1,0:T(8,128)(2,1)S(1)}, bf16[1024,768]{1,0:T(8,128)(2,1)}, u32[]{:S(2)}) %copy-start.2) | copy-done | bytes 1572888
  2.4 2.7 %collective-permute-start.1 = (bf16[256,768]{1,0:T(8,128)(2,1)S(1)}, bf16[256,768]{1,0:T(8,128)(2,1)S(1)}, u32[]{:S(2)}, u32[]{:S(2)}) collective-permute-start(bf16[256,768]{1,0:T(8,128)(2,1)S(1)} %bitcast.21), channel_id=1, source_target_pairs={{0,3},{1,2},{2,1},{3,0},{4,7},{5,6},{6,5},{7,4},{8,11},{9,10},{10,... | collective-permute-start | bytes 1179656 | tf_op jit(solution)/shard_map/ppermute | solution.py:478
  5.2 3.0 %copy-done.1 = bf16[4,3,768,384]{3,2,1,0:T(8,128)(2,1)S(1)} copy-done((bf16[4,3,768,384]{3,2,1,0:T(8,128)(2,1)S(1)}, bf16[4,3,768,384]{3,2,1,0:T(8,128)(2,1)}, u32[]{:S(2)}) %copy-start.1) | copy-done | bytes 7077912
  8.2 0.8 %shard_map.38.w.refs_5_.refs_6_ = bf16[4,768,1152]{2,1,0:T(8,128)(2,1)S(1)} custom-call(bf16[4,3,768,384]{3,2,1,0:T(8,128)(2,1)S(1)} %copy-done.1), custom_call_target="tpu_custom_call" | custom-call | bytes 14155776 | tf_op jit(solution)/shard_map/pallas_call | solution.py:54
  9.0 1.7 %shard_map.39 = (bf16[1024,768]{1,0:T(8,128)(2,1)S(1)}, bf16[1024,384]{1,0:T(8,128)(2,1)S(1)}, f32[1024,384]{1,0:T(8,128)S(1)}, bf16[1024,384]{1,0:T(8,128)(2,1)S(1)}) custom-call(s32[4]{0:T(128)S(1)} %pad_add_fusion.s_ref.refs_0_.parity_ref, bf16[256,768]{1,0:T(8,128)(2,1)S(1)} %bitcast.18, bf16[256,768]{1,0:T(8,128)(2,1)S(1)} %collective-permute-done.2.r1.refs_2_, ...), custom_call_target="tpu_custom_call" | custom-call | flops 905969664 | bytes 1048576 | tf_op jit(solution)/shard_map/pallas_call | solution.py:54
  10.8 4.0 %collective-permute-done.1.r3.refs_4_ = bf16[256,768]{1,0:T(8,128)(2,1)S(1)} collective-permute-done((bf16[256,768]{1,0:T(8,128)(2,1)S(1)}, bf16[256,768]{1,0:T(8,128)(2,1)S(1)}, u32[]{:S(2)}, u32[]{:S(2)}) %collective-permute-start.1) | collective-permute-done | bytes 393248 | tf_op jit(solution)/shard_map/ppermute | solution.py:478
  14.8 8.2 %collective-permute-done.r2.refs_3_ = bf16[256,768]{1,0:T(8,128)(2,1)S(1)} collective-permute-done((bf16[256,768]{1,0:T(8,128)(2,1)S(1)}, bf16[256,768]{1,0:T(8,128)(2,1)S(1)}, u32[]{:S(2)}, u32[]{:S(2)}) %collective-permute-start) | collective-permute-done | bytes 393248 | tf_op jit(solution)/shard_map/ppermute | solution.py:478
  23.0 0.9 %shard_map.41 = (bf16[64,384]{1,0:T(8,128)(2,1)S(1)}, bf16[64,384]{1,0:T(8,128)(2,1)S(1)}) custom-call(s32[4]{0:T(128)S(1)} %pad_add_fusion.s_ref.refs_0_.parity_ref, bf16[256,768]{1,0:T(8,128)(2,1)S(1)} %bitcast.19, bf16[256,768]{1,0:T(8,128)(2,1)S(1)} %collective-permute-done.2.r1.refs_2_, bf16[256,768]{1,0:T(8,128)(2,1)S(1)} %collective-permute-done.r2.refs_3_, ...), custom_call_target="tpu_custom_call" | custom-call | flops 75497472 | bytes 1048576 | tf_op jit(solution)/shard_map/pallas_call | solution.py:54
  23.9 1.2 %collective-permute-start.3 = (bf16[64,384]{1,0:T(8,128)(2,1)S(1)}, bf16[64,384]{1,0:T(8,128)(2,1)S(1)}, u32[]{:S(2)}, u32[]{:S(2)}) collective-permute-start(bf16[64,384]{1,0:T(8,128)(2,1)S(1)} %get-tuple-element.61), channel_id=1, source_target_pairs={{0,4},{1,5},{2,6},{3,7},{4,0},{5,1},{6,2},{7,3},{8,12},{9,13},{10,... | collective-permute-start | bytes 147464 | tf_op jit(solution)/shard_map/ppermute | solution.py:484
  25.1 1.2 %collective-permute-start.4 = (bf16[64,384]{1,0:T(8,128)(2,1)S(1)}, bf16[64,384]{1,0:T(8,128)(2,1)S(1)}, u32[]{:S(2)}, u32[]{:S(2)}) collective-permute-start(bf16[64,384]{1,0:T(8,128)(2,1)S(1)} %get-tuple-element.62), channel_id=1, source_target_pairs={{0,1},{1,0},{2,3},{3,2},{4,8},{5,9},{6,10},{7,11},{8,4},{9,5},{10,... | collective-permute-start | bytes 147464 | tf_op jit(solution)/shard_map/ppermute | solution.py:484
  26.4 3.0 %shard_map.40 = (bf16[1024,768]{1,0:T(8,128)(2,1)S(1)}, bf16[1024,384]{1,0:T(8,128)(2,1)S(1)}, f32[128,384]{1,0:T(8,128)S(1)}, bf16[1024,768]{1,0:T(8,128)(2,1)S...) custom-call(s32[4]{0:T(128)S(1)} %pad_add_fusion.s_ref.refs_0_.parit, ...), custom_call_target="tpu_custom_call", output_to_operand_aliasing={{3}: (3, {}), {4}: (4, {}), {5}: (5, {}), {6}: (6, {})} | custom-call | flops 2415919104 | bytes 4194304 | tf_op jit(solution)/shard_map/pallas_call | solution.py:54
  29.3 1.2 %shard_map.42 = (bf16[1024,768]{1,0:T(8,128)(2,1)S(1)}, bf16[128,384]{1,0:T(8,128)(2,1)S(1)}, bf16[128,384]{1,0:T(8,128)(2,1)S(1)}, bf16[2,256,384]{2,1,0:T(8,128)(2,1)S(1)}, bf16[256,384]{1,0:T(8,128)(2,1)S(1)}) custom-call(s32[4]{0:T(128)S(1)} %pad_add_fusion.s_ref.refs_0_.parity_ref, ...), custom_call_target="tpu_custom_call", output_to_operand_aliasing={{0}: (1, {})} | custom-call | flops 226492416 | bytes 4194304 | tf_op jit(solution)/shard_map/pallas_call | solution.py:54
  30.6 1.4 %collective-permute-start.5 = (bf16[128,384]{1,0:T(8,128)(2,1)S(1)}, bf16[128,384]{1,0:T(8,128)(2,1)S(1)}, u32[]{:S(2)}, u32[]{:S(2)}) collective-permute-start(bf16[128,384]{1,0:T(8,128)(2,1)S(1)} %get-tuple-element.67), channel_id=1, source_target_pairs={{0,4},{1,5},{2,6},{3,7},{4,0},{5,1},{6,2},{7,3},{8,12},{9,13},{10,... | collective-permute-start | bytes 294920 | tf_op jit(solution)/shard_map/ppermute | solution.py:484
  32.0 1.8 %collective-permute-start.6 = (bf16[128,384]{1,0:T(8,128)(2,1)S(1)}, bf16[128,384]{1,0:T(8,128)(2,1)S(1)}, u32[]{:S(2)}, u32[]{:S(2)}) collective-permute-start(bf16[128,384]{1,0:T(8,128)(2,1)S(1)} %get-tuple-element.68), channel_id=1, source_target_pairs={{0,1},{1,0},{2,3},{3,2},{4,8},{5,9},{6,10},{7,11},{8,4},{9,5},{10,... | collective-permute-start | bytes 294920 | tf_op jit(solution)/shard_map/ppermute | solution.py:484
  33.8 1.2 %collective-permute-start.9 = (bf16[2,256,384]{2,1,0:T(8,128)(2,1)S(1)}, bf16[2,256,384]{2,1,0:T(8,128)(2,1)S(1)}, u32[]{:S(2)}, u32[]{:S(2)}) collective-permute-start(bf16[2,256,384]{2,1,0:T(8,128)(2,1)S(1)} %get-tuple-element.75), channel_id=1, source_target_pairs={{0,2},{1,3},{2,0},{3,1},{4,6},{5,7},{6,4},{7,5},{8,10},{9,11},{10,... | collective-permute-start | bytes 1179656 | tf_op jit(solution)/shard_map/ppermute | solution.py:478
  35.0 3.6 %shard_map.43 = (bf16[1024,768]{1,0:T(8,128)(2,1)S(1)}, bf16[1024,384]{1,0:T(8,128)(2,1)S(1)}, f32[256,384]{1,0:T(8,128)S(1)}) custom-call(s32[4]{0:T(128)S(1)} %pad_add_fusion.s_ref.refs_0_.parity_ref, bf16[1024,768]{1,0:T(8,128)(2,1)S(1)} %get-tuple-element.63.x, bf16[4,768,1152]{2,1,0:T(8,128)(2,1)S(1)} %shard_map.38.w.refs_5_.refs_6_, ...), custom_call_target="tpu_custom_call" | custom-call | flops 2415919104 | bytes 4194304 | tf_op jit(solution)/shard_map/pallas_call | solution.py:54
  38.6 1.7 %shard_map.44 = (bf16[1024,768]{1,0:T(8,128)(2,1)S(1)}, bf16[256,384]{1,0:T(8,128)(2,1)S(1)}, bf16[256,384]{1,0:T(8,128)(2,1)S(1)}, bf16[2,256,384]{2,1,0:T(8,128)(2,1)S(1)}, bf16[256,384]{1,0:T(8,128)(2,1)S(1)}) custom-call(s32[4]{0:T(128)S(1)} %pad_add_fusion.s_ref.refs_0_.parity_ref, ...), custom_call_target="tpu_custom_call", output_to_operand_aliasing={{0}: (1, {})} | custom-call | flops 452984832 | bytes 4194304 | tf_op jit(solution)/shard_map/pallas_call | solution.py:54
  40.4 1.4 %collective-permute-start.8 = (bf16[256,384]{1,0:T(8,128)(2,1)S(1)}, bf16[256,384]{1,0:T(8,128)(2,1)S(1)}, u32[]{:S(2)}, u32[]{:S(2)}) collective-permute-start(bf16[256,384]{1,0:T(8,128)(2,1)S(1)} %get-tuple-element.74), channel_id=1, source_target_pairs={{0,1},{1,0},{2,3},{3,2},{4,8},{5,9},{6,10},{7,11},{8,4},{9,5},{10,... | collective-permute-start | bytes 589832 | tf_op jit(solution)/shard_map/ppermute | solution.py:484
  42.1 3.9 %shard_map.45 = (bf16[1024,768]{1,0:T(8,128)(2,1)S(1)}, bf16[1024,384]{1,0:T(8,128)(2,1)S(1)}, f32[512,384]{1,0:T(8,128)S(1)}, bf16[256,384]{1,0:T(8,128)(2,1)S(1)}, bf16[256,384]{1,0:T(8,128)(2,1)S(1)}) custom-call(s32[4]{0:T(128)S(1)} %pad_add_fusion.s_ref.refs_0_.parity_ref, bf16[1024,768]{1,0:T(8,128)(2,1)S(1)} %get-tuple-element.69.x, ...), custom_call_target="tpu_custom_call" | custom-call | flops 2415919104 | bytes 4194304 | tf_op jit(solution)/shard_map/pallas_call | solution.py:54
  46.0 0.9 %collective-permute-start.10 = (bf16[256,384]{1,0:T(8,128)(2,1)S(1)}, bf16[256,384]{1,0:T(8,128)(2,1)S(1)}, u32[]{:S(2)}, u32[]{:S(2)}) collective-permute-start(bf16[256,384]{1,0:T(8,128)(2,1)S(1)} %get-tuple-element.78), channel_id=1, source_target_pairs={{0,4},{1,5},{2,6},{3,7},{4,0},{5,1},{6,2},{7,3},{8,12},{9,13},{10,... | collective-permute-start | bytes 589832 | tf_op jit(solution)/shard_map/ppermute | solution.py:484
  46.9 2.0 %shard_map.46 = (bf16[1024,768]{1,0:T(8,128)(2,1)S(1)}, bf16[256,384]{1,0:T(8,128)(2,1)S(1)}, bf16[256,384]{1,0:T(8,128)(2,1)S(1)}, bf16[2,256,384]{2,1,0:T(8,128)(2,1)S(1)}, bf16[2,256,384]{2,1,0:T(8,128)(2,1)S(1)}) custom-call(s32[4]{0:T(128)S(1)} %pad_add_fusion.s_ref.refs_0_.parity_ref, ...), custom_call_target="tpu_custom_call", output_to_operand_aliasing={{0}: (1, {})} | custom-call | flops 603979776 | bytes 4194304 | tf_op jit(solution)/shard_map/pallas_call | solution.py:54
  48.9 1.3 %collective-permute-start.17 = (bf16[2,256,384]{2,1,0:T(8,128)(2,1)S(1)}, bf16[2,256,384]{2,1,0:T(8,128)(2,1)S(1)}, u32[]{:S(2)}, u32[]{:S(2)}) collective-permute-start(bf16[2,256,384]{2,1,0:T(8,128)(2,1)S(1)} %get-tuple-element.87), channel_id=1, source_target_pairs={{0,2},{1,3},{2,0},{3,1},{4,6},{5,7},{6,4},{7,5},{8,10},{9,11},{10,... | collective-permute-start | bytes 1179656 | tf_op jit(solution)/shard_map/ppermute | solution.py:478
  50.2 1.7 %collective-permute-start.11 = (bf16[256,384]{1,0:T(8,128)(2,1)S(1)}, bf16[256,384]{1,0:T(8,128)(2,1)S(1)}, u32[]{:S(2)}, u32[]{:S(2)}) collective-permute-start(bf16[256,384]{1,0:T(8,128)(2,1)S(1)} %get-tuple-element.79), channel_id=1, source_target_pairs={{0,1},{1,0},{2,3},{3,2},{4,8},{5,9},{6,10},{7,11},{8,4},{9,5},{10,... | collective-permute-start | bytes 589832 | tf_op jit(solution)/shard_map/ppermute | solution.py:484
  52.3 1.1 %collective-permute-start.13 = (bf16[256,384]{1,0:T(8,128)(2,1)S(1)}, bf16[256,384]{1,0:T(8,128)(2,1)S(1)}, u32[]{:S(2)}, u32[]{:S(2)}) collective-permute-start(bf16[256,384]{1,0:T(8,128)(2,1)S(1)} %get-tuple-element.83), channel_id=1, source_target_pairs={{0,1},{1,0},{2,3},{3,2},{4,8},{5,9},{6,10},{7,11},{8,4},{9,5},{10,... | collective-permute-start | bytes 589832 | tf_op jit(solution)/shard_map/ppermute | solution.py:484
  53.4 2.2 %shard_map.47 = (bf16[2,256,384]{2,1,0:T(8,128)(2,1)S(1)}, f32[512,384]{1,0:T(8,128)S(1)}, bf16[256,384]{1,0:T(8,128)(2,1)S(1)}) custom-call(s32[4]{0:T(128)S(1)} %pad_add_fusion.s_ref.refs_0_.parity_ref, bf16[1024,768]{1,0:T(8,128)(2,1)S(1)} %get-tuple-element.76.x, bf16[1024,384]{1,0:T(8,128)(2,1)S(1)} %get-tuple-element.71.refs_2_.hidden, ...), custom_call_target="tpu_custom_call" | custom-call | flops 1207959552 | bytes 4194304 | tf_op jit(solution)/shard_map/pallas_call | solution.py:54
  55.6 2.8 %collective-permute-done.12.refs_3_ = bf16[256,384]{1,0:T(8,128)(2,1)S(1)} collective-permute-done((bf16[256,384]{1,0:T(8,128)(2,1)S(1)}, bf16[256,384]{1,0:T(8,128)(2,1)S(1)}, u32[]{:S(2)}, u32[]{:S(2)}) %collective-permute-start.12) | collective-permute-done | bytes 196640 | tf_op jit(solution)/shard_map/ppermute | solution.py:484
  58.4 1.2 %shard_map.48 = (bf16[256,384]{1,0:T(8,128)(2,1)S(1)}, bf16[256,384]{1,0:T(8,128)(2,1)S(1)}, bf16[256,384]{1,0:T(8,128)(2,1)S(1)}, bf16[256,384]{1,0:T(8,128)(2,1)S(1)}) custom-call(s32[4]{0:T(128)S(1)} %pad_add_fusion.s_ref.refs_0_.parity_ref, bf16[2,256,384]{2,1,0:T(8,128)(2,1)S(1)} %get-tuple-element.80.refs_1_, ...), custom_call_target="tpu_custom_call" | custom-call | flops 3932160 | bytes 2097152 | tf_op jit(solution)/shard_map/pallas_call | solution.py:54
  59.6 1.9 %collective-permute-done.17.refs_5_ = bf16[2,256,384]{2,1,0:T(8,128)(2,1)S(1)} collective-permute-done((bf16[2,256,384]{2,1,0:T(8,128)(2,1)S(1)}, bf16[2,256,384]{2,1,0:T(8,128)(2,1)S(1)}, u32[]{:S(2)}, u32[]{:S(2)}) %collective-permute-start.17) | collective-permute-done | bytes 393248 | tf_op jit(solution)/shard_map/ppermute | solution.py:478
  62.4 1.2 %collective-permute-start.15 = (bf16[256,384]{1,0:T(8,128)(2,1)S(1)}, bf16[256,384]{1,0:T(8,128)(2,1)S(1)}, u32[]{:S(2)}, u32[]{:S(2)}) collective-permute-start(bf16[256,384]{1,0:T(8,128)(2,1)S(1)} %get-tuple-element.85), channel_id=1, source_target_pairs={{0,2},{1,3},{2,0},{3,1},{4,6},{5,7},{6,4},{7,5},{8,10},{9,11},{10,... | collective-permute-start | bytes 589832 | tf_op jit(solution)/shard_map/ppermute | solution.py:478
  65.1 4.7 %shard_map.50 = (bf16[4,4,4,64,768]{4,3,2,1,0:T(8,128)(2,1)}, bf16[4,4,64,768]{3,2,1,0:T(8,128)(2,1)S(1)}) custom-call(s32[4]{0:T(128)S(1)} %pad_add_fusion.s_ref.refs_0_.parity_ref, bf16[4,4,64,768]{3,2,1,0:T(8,128)(2,1)S(1)} %bitcast.17, bf16[16,64,768]{2,1,0:T(8,128)(2,1)S(1)} %bitcast.13, bf16[16,64,768]{2,1,0:T(8,128)(2,1)S(1)} %bitcast.15, ...), custom_call_target="tpu_custom_call" | custom-call | flops 2415919104 | bytes 8388608 | tf_op jit(solution)/shard_map/pallas_call | solution.py:54
  69.9 3.4 %collective-permute-done.16.a3 = bf16[256,384]{1,0:T(8,128)(2,1)S(1)} collective-permute-done((bf16[256,384]{1,0:T(8,128)(2,1)S(1)}, bf16[256,384]{1,0:T(8,128)(2,1)S(1)}, u32[]{:S(2)}, u32[]{:S(2)}) %collective-permute-start.16) | collective-permute-done | bytes 196640 | tf_op jit(solution)/shard_map/ppermute | solution.py:478
  73.3 1.9 %shard_map.51 = bf16[4,4,4,64,768]{4,3,2,1,0:T(8,128)(2,1)} custom-call(s32[4]{0:T(128)S(1)} %pad_add_fusion.s_ref.refs_0_.parity_ref, bf16[256,384]{1,0:T(8,128)(2,1)S(1)} %collective-permute-done.15.a2, bf16[256,384]{1,0:T(8,128)(2,1)S(1)} %collective-permute-done.16.a3, ...), custom_call_target="tpu_custom_call", output_to_operand_aliasing={{}: (5, {})} | custom-call | flops 301989888 | bytes 2097152 | tf_op jit(solution)/shard_map/pallas_call | solution.py:54
  (32 shorter events, 4.2 us)
Async XLA Ops:
  0.1 1.4 %copy-start.2 = (bf16[1024,768]{1,0:T(8,128)(2,1)S(1)}, bf16[1024,768]{1,0:T(8,128)(2,1)}, u32[]{:S(2)}) copy-start(bf16[1024,768]{1,0:T(8,128)(2,1)} %param.3) | copy-start | bytes 4718596
  2.3 6.7 %collective-permute-start.2 = (bf16[256,768]{1,0:T(8,128)(2,1)S(1)}, bf16[256,768]{1,0:T(8,128)(2,1)S(1)}, u32[]{:S(2)}, u32[]{:S(2)}) collective-permute-start(bf16[256,768]{1,0:T(8,128)(2,1)S(1)} %bitcast.22), channel_id=1, source_target_pairs={{0,1},{1,0},{2,3},{3,2},{4,5},{5,4},{6,7},{7,6},{8,9},{9,8},{10,11... | collective-permute-start | bytes 1179656 | tf_op jit(solution)/shard_map/ppermute | solution.py:478
  2.4 12.3 %collective-permute-start.1 = (bf16[256,768]{1,0:T(8,128)(2,1)S(1)}, bf16[256,768]{1,0:T(8,128)(2,1)S(1)}, u32[]{:S(2)}, u32[]{:S(2)}) collective-permute-start(bf16[256,768]{1,0:T(8,128)(2,1)S(1)} %bitcast.21), channel_id=1, source_target_pairs={{0,3},{1,2},{2,1},{3,0},{4,7},{5,6},{6,5},{7,4},{8,11},{9,10},{10,... | collective-permute-start | bytes 1179656 | tf_op jit(solution)/shard_map/ppermute | solution.py:478
  5.1 17.9 %collective-permute-start = (bf16[256,768]{1,0:T(8,128)(2,1)S(1)}, bf16[256,768]{1,0:T(8,128)(2,1)S(1)}, u32[]{:S(2)}, u32[]{:S(2)}) collective-permute-start(bf16[256,768]{1,0:T(8,128)(2,1)S(1)} %bitcast.20), channel_id=1, source_target_pairs={{0,2},{1,3},{2,0},{3,1},{4,6},{5,7},{6,4},{7,5},{8,10},{9,11},{10,... | collective-permute-start | bytes 1179656 | tf_op jit(solution)/shard_map/ppermute | solution.py:478
  5.2 3.0 %copy-start.1 = (bf16[4,3,768,384]{3,2,1,0:T(8,128)(2,1)S(1)}, bf16[4,3,768,384]{3,2,1,0:T(8,128)(2,1)}, u32[]{:S(2)}) copy-start(bf16[4,3,768,384]{3,2,1,0:T(8,128)(2,1)} %taps.1) | copy-start | bytes 21233668
  23.0 3.4 %copy-start = (bf16[4,384,768]{2,1,0:T(8,128)(2,1)S(1)}, bf16[4,384,768]{2,1,0:T(8,128)(2,1)}, u32[]{:S(2)}) copy-start(bf16[4,384,768]{2,1,0:T(8,128)(2,1)} %point.11) | copy-start | bytes 7077892
  23.9 5.4 %collective-permute-start.3 = (bf16[64,384]{1,0:T(8,128)(2,1)S(1)}, bf16[64,384]{1,0:T(8,128)(2,1)S(1)}, u32[]{:S(2)}, u32[]{:S(2)}) collective-permute-start(bf16[64,384]{1,0:T(8,128)(2,1)S(1)} %get-tuple-element.61), channel_id=1, source_target_pairs={{0,4},{1,5},{2,6},{3,7},{4,0},{5,1},{6,2},{7,3},{8,12},{9,13},{10,... | collective-permute-start | bytes 147464 | tf_op jit(solution)/shard_map/ppermute | solution.py:484
  25.1 4.2 %collective-permute-start.4 = (bf16[64,384]{1,0:T(8,128)(2,1)S(1)}, bf16[64,384]{1,0:T(8,128)(2,1)S(1)}, u32[]{:S(2)}, u32[]{:S(2)}) collective-permute-start(bf16[64,384]{1,0:T(8,128)(2,1)S(1)} %get-tuple-element.62), channel_id=1, source_target_pairs={{0,1},{1,0},{2,3},{3,2},{4,8},{5,9},{6,10},{7,11},{8,4},{9,5},{10,... | collective-permute-start | bytes 147464 | tf_op jit(solution)/shard_map/ppermute | solution.py:484
  30.6 8.0 %collective-permute-start.5 = (bf16[128,384]{1,0:T(8,128)(2,1)S(1)}, bf16[128,384]{1,0:T(8,128)(2,1)S(1)}, u32[]{:S(2)}, u32[]{:S(2)}) collective-permute-start(bf16[128,384]{1,0:T(8,128)(2,1)S(1)} %get-tuple-element.67), channel_id=1, source_target_pairs={{0,4},{1,5},{2,6},{3,7},{4,0},{5,1},{6,2},{7,3},{8,12},{9,13},{10,... | collective-permute-start | bytes 294920 | tf_op jit(solution)/shard_map/ppermute | solution.py:484
  32.0 6.6 %collective-permute-start.6 = (bf16[128,384]{1,0:T(8,128)(2,1)S(1)}, bf16[128,384]{1,0:T(8,128)(2,1)S(1)}, u32[]{:S(2)}, u32[]{:S(2)}) collective-permute-start(bf16[128,384]{1,0:T(8,128)(2,1)S(1)} %get-tuple-element.68), channel_id=1, source_target_pairs={{0,1},{1,0},{2,3},{3,2},{4,8},{5,9},{6,10},{7,11},{8,4},{9,5},{10,... | collective-permute-start | bytes 294920 | tf_op jit(solution)/shard_map/ppermute | solution.py:484
  33.8 13.1 %collective-permute-start.9 = (bf16[2,256,384]{2,1,0:T(8,128)(2,1)S(1)}, bf16[2,256,384]{2,1,0:T(8,128)(2,1)S(1)}, u32[]{:S(2)}, u32[]{:S(2)}) collective-permute-start(bf16[2,256,384]{2,1,0:T(8,128)(2,1)S(1)} %get-tuple-element.75), channel_id=1, source_target_pairs={{0,2},{1,3},{2,0},{3,1},{4,6},{5,7},{6,4},{7,5},{8,10},{9,11},{10,... | collective-permute-start | bytes 1179656 | tf_op jit(solution)/shard_map/ppermute | solution.py:478
  40.3 6.6 %collective-permute-start.7 = (bf16[256,384]{1,0:T(8,128)(2,1)S(1)}, bf16[256,384]{1,0:T(8,128)(2,1)S(1)}, u32[]{:S(2)}, u32[]{:S(2)}) collective-permute-start(bf16[256,384]{1,0:T(8,128)(2,1)S(1)} %get-tuple-element.73), channel_id=1, source_target_pairs={{0,4},{1,5},{2,6},{3,7},{4,0},{5,1},{6,2},{7,3},{8,12},{9,13},{10,... | collective-permute-start | bytes 589832 | tf_op jit(solution)/shard_map/ppermute | solution.py:484
  40.4 6.5 %collective-permute-start.8 = (bf16[256,384]{1,0:T(8,128)(2,1)S(1)}, bf16[256,384]{1,0:T(8,128)(2,1)S(1)}, u32[]{:S(2)}, u32[]{:S(2)}) collective-permute-start(bf16[256,384]{1,0:T(8,128)(2,1)S(1)} %get-tuple-element.74), channel_id=1, source_target_pairs={{0,1},{1,0},{2,3},{3,2},{4,8},{5,9},{6,10},{7,11},{8,4},{9,5},{10,... | collective-permute-start | bytes 589832 | tf_op jit(solution)/shard_map/ppermute | solution.py:484
  41.8 13.8 %collective-permute-start.14 = (bf16[2,256,384]{2,1,0:T(8,128)(2,1)S(1)}, bf16[2,256,384]{2,1,0:T(8,128)(2,1)S(1)}, u32[]{:S(2)}, u32[]{:S(2)}) collective-permute-start(bf16[2,256,384]{2,1,0:T(8,128)(2,1)S(1)} %get-tuple-element.84), channel_id=1, source_target_pairs={{0,2},{1,3},{2,0},{3,1},{4,6},{5,7},{6,4},{7,5},{8,10},{9,11},{10,... | collective-permute-start | bytes 1179656 | tf_op jit(solution)/shard_map/ppermute | solution.py:478
  46.0 6.3 %collective-permute-start.10 = (bf16[256,384]{1,0:T(8,128)(2,1)S(1)}, bf16[256,384]{1,0:T(8,128)(2,1)S(1)}, u32[]{:S(2)}, u32[]{:S(2)}) collective-permute-start(bf16[256,384]{1,0:T(8,128)(2,1)S(1)} %get-tuple-element.78), channel_id=1, source_target_pairs={{0,4},{1,5},{2,6},{3,7},{4,0},{5,1},{6,2},{7,3},{8,12},{9,13},{10,... | collective-permute-start | bytes 589832 | tf_op jit(solution)/shard_map/ppermute | solution.py:484
  48.9 12.5 %collective-permute-start.17 = (bf16[2,256,384]{2,1,0:T(8,128)(2,1)S(1)}, bf16[2,256,384]{2,1,0:T(8,128)(2,1)S(1)}, u32[]{:S(2)}, u32[]{:S(2)}) collective-permute-start(bf16[2,256,384]{2,1,0:T(8,128)(2,1)S(1)} %get-tuple-element.87), channel_id=1, source_target_pairs={{0,2},{1,3},{2,0},{3,1},{4,6},{5,7},{6,4},{7,5},{8,10},{9,11},{10,... | collective-permute-start | bytes 1179656 | tf_op jit(solution)/shard_map/ppermute | solution.py:478
  50.2 3.1 %collective-permute-start.11 = (bf16[256,384]{1,0:T(8,128)(2,1)S(1)}, bf16[256,384]{1,0:T(8,128)(2,1)S(1)}, u32[]{:S(2)}, u32[]{:S(2)}) collective-permute-start(bf16[256,384]{1,0:T(8,128)(2,1)S(1)} %get-tuple-element.79), channel_id=1, source_target_pairs={{0,1},{1,0},{2,3},{3,2},{4,8},{5,9},{6,10},{7,11},{8,4},{9,5},{10,... | collective-permute-start | bytes 589832 | tf_op jit(solution)/shard_map/ppermute | solution.py:484
  51.9 6.5 %collective-permute-start.12 = (bf16[256,384]{1,0:T(8,128)(2,1)S(1)}, bf16[256,384]{1,0:T(8,128)(2,1)S(1)}, u32[]{:S(2)}, u32[]{:S(2)}) collective-permute-start(bf16[256,384]{1,0:T(8,128)(2,1)S(1)} %get-tuple-element.82), channel_id=1, source_target_pairs={{0,4},{1,5},{2,6},{3,7},{4,0},{5,1},{6,2},{7,3},{8,12},{9,13},{10,... | collective-permute-start | bytes 589832 | tf_op jit(solution)/shard_map/ppermute | solution.py:484
  52.3 6.2 %collective-permute-start.13 = (bf16[256,384]{1,0:T(8,128)(2,1)S(1)}, bf16[256,384]{1,0:T(8,128)(2,1)S(1)}, u32[]{:S(2)}, u32[]{:S(2)}) collective-permute-start(bf16[256,384]{1,0:T(8,128)(2,1)S(1)} %get-tuple-element.83), channel_id=1, source_target_pairs={{0,1},{1,0},{2,3},{3,2},{4,8},{5,9},{6,10},{7,11},{8,4},{9,5},{10,... | collective-permute-start | bytes 589832 | tf_op jit(solution)/shard_map/ppermute | solution.py:484
  61.5 3.6 %copy-start.3 = (bf16[1024,768]{1,0:T(8,128)(2,1)S(1)}, bf16[1024,768]{1,0:T(8,128)(2,1)}, u32[]{:S(2)}) copy-start(bf16[1024,768]{1,0:T(8,128)(2,1)} %param.3) | copy-start | bytes 4718596
  61.6 3.5 %collective-permute-start.18 = (bf16[6,256,384]{2,1,0:T(8,128)(2,1)S(1)}, bf16[6,256,384]{2,1,0:T(8,128)(2,1)S(1)}, u32[]{:S(2)}, u32[]{:S(2)}) collective-permute-start(bf16[6,256,384]{2,1,0:T(8,128)(2,1)S(1)} %shard_map.49), channel_id=1, source_target_pairs={{0,1},{1,0},{2,3},{3,2},{4,5},{5,4},{6,7},{7,6},{8,9},{9,8},{10,11... | collective-permute-start | bytes 3538952 | tf_op jit(solution)/shard_map/ppermute | solution.py:478
  62.3 2.8 %collective-permute-start.19 = (bf16[256,384]{1,0:T(8,128)(2,1)S(1)}, bf16[256,384]{1,0:T(8,128)(2,1)S(1)}, u32[]{:S(2)}, u32[]{:S(2)}) collective-permute-start(bf16[256,384]{1,0:T(8,128)(2,1)S(1)} %get-tuple-element.92), channel_id=1, source_target_pairs={{0,1},{1,0},{2,3},{3,2},{4,5},{5,4},{6,7},{7,6},{8,9},{9,8},{10,11... | collective-permute-start | bytes 589832 | tf_op jit(solution)/shard_map/ppermute | solution.py:478
  62.4 7.4 %collective-permute-start.15 = (bf16[256,384]{1,0:T(8,128)(2,1)S(1)}, bf16[256,384]{1,0:T(8,128)(2,1)S(1)}, u32[]{:S(2)}, u32[]{:S(2)}) collective-permute-start(bf16[256,384]{1,0:T(8,128)(2,1)S(1)} %get-tuple-element.85), channel_id=1, source_target_pairs={{0,2},{1,3},{2,0},{3,1},{4,6},{5,7},{6,4},{7,5},{8,10},{9,11},{10,... | collective-permute-start | bytes 589832 | tf_op jit(solution)/shard_map/ppermute | solution.py:478
  63.7 9.6 %collective-permute-start.16 = (bf16[256,384]{1,0:T(8,128)(2,1)S(1)}, bf16[256,384]{1,0:T(8,128)(2,1)S(1)}, u32[]{:S(2)}, u32[]{:S(2)}) collective-permute-start(bf16[256,384]{1,0:T(8,128)(2,1)S(1)} %get-tuple-element.86), channel_id=1, source_target_pairs={{0,3},{1,2},{2,1},{3,0},{4,7},{5,6},{6,5},{7,4},{8,11},{9,10},{10,... | collective-permute-start | bytes 589832 | tf_op jit(solution)/shard_map/ppermute | solution.py:478

commit v4 on v3

--- a/solution.py
+++ b/solution.py
@@ -69,21 +69,43 @@
     return jax.ShapeDtypeStruct(shape, dtype)
 
 
-def split_kernel(s_ref, x, g0, g1, g2, g3, sems):
+def split_kernel(s_ref, x, own, beside, over, rest, sems):
     q = s_ref[0]
+    places = x.shape[0]
+    is_top = q == GROUP - 1
+    edge = pl.ds(jnp.where(is_top, places - 1, 0), 1)
+    others = pl.ds(jnp.where(is_top, 0, 1), places - 1)
     copies = [
-        pltpu.make_async_copy(x.at[:, q ^ k], piece, sems.at[k])
-        for k, piece in enumerate((g0, g1, g2, g3))
+        pltpu.make_async_copy(source, target, sems.at[i])
+        for i, (source, target) in enumerate(
+            (
+                (x.at[:, q ^ 2], over.at[pl.ds(0, places)]),
+                (x.at[edge, q ^ 3], over.at[pl.ds(places, 1)]),
+                (x.at[others, q ^ 3], rest),
+                (x.at[:, q ^ 1], beside),
+                (x.at[:, q], own),
+            )
+        )
     ]
     wait_all(start_all(copies))
 
 
 def split(scalars, x):
     places, group, r, c = x.shape
-    pieces = (array(places, r, c),) * group
-    sems = [pltpu.SemaphoreType.DMA((group,))]
-    pieces = call(split_kernel, pieces, (scalars, x), [SMEM, HBM], (VMEM,) * group, sems, 0, 4 * x.size)
-    return [piece.reshape(places * r, c) for piece in pieces]
+    x = pltpu.with_memory_space_constraint(x, pltpu.HBM)
+    outs = [array(n, r, c) for n in (places, places, places + 1, places - 1)]
+    sems = [pltpu.SemaphoreType.DMA((5,))]
+    pieces = call(split_kernel, outs, (scalars, x), [SMEM, HBM], (VMEM,) * 4, sems, 0, 4 * x.size)
+    return [piece.reshape(piece.shape[0] * r, c) for piece in pieces]
+
+
+def edge_part_kernel(over, out):
+    out[...] = over[pl.ds(over.shape[0] - out.shape[0], out.shape[0])]
+
+
+def edge_part(over, r, after):
+    out = array(r, over.shape[1])
+    return call(edge_part_kernel, out, (over,), [VMEM], VMEM, [], 0, 2 * out.size, after=after)
 
 
 def side_by_side_kernel(taps, w, sems):
@@ -104,6 +126,7 @@
 def side_by_side(taps):
     blocks, count, c, h = taps.shape
     sems = [pltpu.SemaphoreType.DMA((blocks, count))]
+    taps = pltpu.with_memory_space_constraint(taps, pltpu.HBM)
     return call(side_by_side_kernel, array(blocks, c, count * h), (taps,), [HBM], VMEM, sems, 0, 4 * taps.size)
 
 
@@ -121,29 +144,29 @@
     return below, above
 
 
-def open_kernel(r, s_ref, own, r1, r2, r3, w, even_ref, odd_ref, ends):
+def open_kernel(r, s_ref, own, beside, over, edge, w, even_ref, odd_ref, ends):
     q, parity = s_ref[0], s_ref[1]
-    rows = own.shape[0]
     h = even_ref.shape[1]
+    last = own.shape[0] - r
 
     def fetch(piece, at, to):
         ends[pl.ds(to, r)] = piece[pl.ds(at, r)]
 
-    for k, piece in enumerate((own, r1, r2, r3)):
-        pl.when(q ^ k == GROUP - 1)(functools.partial(fetch, piece, rows - r, 0))
+    for k, (piece, top) in enumerate(((own, last), (beside, last), (over, last), (edge, 0))):
+        pl.when(q ^ k == GROUP - 1)(functools.partial(fetch, piece, top, 0))
         pl.when(q ^ k == 0)(functools.partial(fetch, piece, 0, r))
     up = dot(ends[pl.ds(0, r)], w[0, :, :h])
     down = dot(ends[pl.ds(r, r)], w[0, :, 2 * h :])
     place_terms(parity, up, down, even_ref, odd_ref, 0, r)
 
 
-def open_terms(scalars, pieces, w, r, after):
+def open_terms(scalars, pieces, w, r):
     c, h = w.shape[1], w.shape[2] // 3
     terms = array(r, h)
     return call(
         functools.partial(open_kernel, r), (terms, terms), (scalars, *pieces, w),
         [SMEM] + [VMEM] * (GROUP + 1), (VMEM, VMEM), [pltpu.VMEM((2 * r, c), BF16)],
-        4 * r * c * h, 2**20, after=after,
+        4 * r * c * h, 2**20,
     )
 
 
@@ -154,12 +177,16 @@
     high[at] = terms[:, 2 * h :].astype(BF16)
 
 
-def piece_taps(q, first, pieces, w, x, low, mid, high):
-    for i, piece in enumerate(pieces):
-        rows = piece.shape[0]
-        at = pl.ds(pl.multiple_of((q ^ (first + i)) * rows, rows), rows)
-        x[at] = piece[...]
-        keep_terms(at, dot(piece[...], w[0]), low, mid, high)
+def piece_taps(at, piece, w, x, low, mid, high):
+    x[at] = piece
+    keep_terms(at, dot(piece, w[0]), low, mid, high)
+
+
+def part_rows(j, rows, r, first):
+    is_top = j == GROUP - 1
+    if first:
+        return pl.ds(pl.multiple_of(j * rows + jnp.where(is_top, rows - r, 0), r), r)
+    return pl.ds(pl.multiple_of(j * rows + jnp.where(is_top, 0, r), r), rows - r)
 
 
 def block_body(reach, x, point, x_ref, h_ref, part_ref, low, mid, high):
@@ -181,37 +208,92 @@
         h_ref[pl.ds(at, reach)] = jnp.zeros((reach, h_ref.shape[1]), BF16)
 
 
-def early_taps_kernel(s_ref, own, r1, w, x, low, mid, high):
-    piece_taps(s_ref[0], 0, (own, r1), w, x, low, mid, high)
-
-
-def early_taps(scalars, pieces, w):
+def early_taps_kernel(s_ref, own, beside, w, x, low, mid, high):
+    rows = own.shape[0]
+    for k, piece in enumerate((own, beside)):
+        at = pl.ds(pl.multiple_of((s_ref[0] ^ k) * rows, rows), rows)
+        piece_taps(at, piece[...], w, x, low, mid, high)
+
+
+def early_taps(scalars, own, beside, w):
     c, h = w.shape[1], w.shape[2] // 3
-    rows = pieces[0].shape[0]
+    rows = own.shape[0]
     length = GROUP * rows
     outs = (array(length, c), array(length, h), array(length, h, dtype=F32), array(length, h))
     return call(
-        early_taps_kernel, outs, (scalars, *pieces, w), [SMEM] + [VMEM] * 3, (VMEM,) * 4, [],
+        early_taps_kernel, outs, (scalars, own, beside, w), [SMEM] + [VMEM] * 3, (VMEM,) * 4, [],
         12 * rows * c * h, 2**20,
     )
 
 
-def first_kernel(reach, s_ref, r2, r3, x, low, mid, high, w, point, *refs):
-    piece_taps(s_ref[0], 2, (r2, r3), w, x, low, mid, high)
-    block_body(reach, x, point[0], *refs[:3], low, mid, high)
-
-
-def first_block(scalars, early, pieces, w, point, reach):
+def more_taps_kernel(s_ref, over, edge, w, *refs):
+    x, low, mid, high = refs[4:]
+    q = s_ref[0]
+    rows, r = x.shape[0] // GROUP, edge.shape[0]
+    at = pl.ds(pl.multiple_of((q ^ 2) * rows, rows), rows)
+    piece_taps(at, over[pl.ds(0, rows)], w, x, low, mid, high)
+    piece_taps(part_rows(q ^ 3, rows, r, True), edge[...], w, x, low, mid, high)
+
+
+def more_taps(scalars, over, edge, w, early):
+    c, h = w.shape[1], w.shape[2] // 3
+    return call(
+        more_taps_kernel, tuple(array(*e.shape, dtype=e.dtype) for e in early),
+        (scalars, over, edge, w, *early), [SMEM] + [VMEM] * 7, (VMEM,) * 4, [],
+        6 * over.shape[0] * c * h, 2**20, {4: 0, 5: 1, 6: 2, 7: 3},
+    )
+
+
+def first_kernel(
+    r, s_ref, rest, x, low, mid, high, from_even, from_odd, w, point,
+    x_ref, even_ref, odd_ref, far_ref, core_ref, *refs
+):
+    hidden = refs[-1]
+    q, parity = s_ref[0], s_ref[1]
+    length = x.shape[0]
+    rows = length // GROUP
+    h = mid.shape[1]
+    piece_taps(part_rows(q ^ 3, rows, r, False), rest[...], w, x, low, mid, high)
+    below, above = arrived(s_ref, from_even, from_odd, 0, r)
+
+    def finish(start, size, v):
+        at = pl.ds(start, size)
+        hidden[at] = gelu(v).astype(BF16)
+        x_ref[at] = (x[at].astype(F32) + dot(hidden[at], point[0])).astype(BF16)
+
+    def body(start, size):
+        v = mid[pl.ds(start, size)]
+        if start == 0:
+            low_terms = jnp.concatenate([below, low[pl.ds(0, size - r)].astype(F32)])
+        else:
+            low_terms = low[pl.ds(start - r, size)].astype(F32)
+        if start + size == length:
+            high_terms = jnp.concatenate([high[pl.ds(start + r, size - r)].astype(F32), above])
+        else:
+            high_terms = high[pl.ds(start + r, size)].astype(F32)
+        finish(start, size, v + low_terms + high_terms)
+
+    over_rows(length, body)
+    ahead = even_ref.shape[0]
+    up = dot(x_ref[pl.ds(length - ahead, ahead)], w[1, :, :h])
+    down = dot(x_ref[pl.ds(0, ahead)], w[1, :, 2 * h :])
+    place_terms(parity, up, down, even_ref, odd_ref, 0, ahead)
+    for k, ref in ((1, core_ref), (2, far_ref.at[0]), (3, far_ref.at[1])):
+        ref[...] = hidden[pl.ds(pl.multiple_of((q ^ k) * rows, rows), rows)]
+
+
+def first_block(scalars, rest, early, terms, w, point, r):
     c, h = w.shape[1], w.shape[2] // 3
     length = early[0].shape[0]
-    outs = (array(length, c), array(length, h), array(2 * reach, h, dtype=F32))
+    rows = length // GROUP
+    outs = (array(length, c), array(2 * r, h), array(2 * r, h), array(2, rows, h), array(rows, h))
     outs += tuple(array(*e.shape, dtype=e.dtype) for e in early)
     results = call(
-        functools.partial(first_kernel, reach), outs, (scalars, *pieces, *early, w, point),
-        [SMEM] + [VMEM] * 8, (VMEM,) * 7, [], 8 * length * c * h, 4 * 2**20,
-        {3: 3, 4: 4, 5: 5, 6: 6},
-    )
-    return results[:3]
+        functools.partial(first_kernel, r), outs, (scalars, rest, *early, *terms, w, point),
+        [SMEM] + [VMEM] * 9, (VMEM,) * 9, [pltpu.VMEM((length, h), BF16)],
+        8 * length * c * h, 4 * 2**20, {2: 5, 3: 6, 4: 7, 5: 8},
+    )
+    return results[:5]
 
 
 def middle_kernel(block, reach, parity_ref, x, w, point, x_ref, h_ref, part_ref, *refs):
@@ -231,7 +313,7 @@
         place_terms(parity_ref[1], up, down, *sent, 0, reach)
 
 
-def middle_block(block, scalars, x, w, point, reach):
+def middle_block(block, scalars, x, w, point, reach, after=()):
     c, h = w.shape[1], w.shape[2] // 3
     length = x.shape[0]
     outs = (array(length, c), array(length, h), array(2 * reach, h, dtype=F32))
@@ -244,7 +326,7 @@
     ]
     return call(
         functools.partial(middle_kernel, block, reach), outs, (scalars, x, w, point),
-        [SMEM] + [VMEM] * 3, (VMEM,) * len(outs), scratch, 8 * length * c * h, 4 * 2**20,
+        [SMEM] + [VMEM] * 3, (VMEM,) * len(outs), scratch, 8 * length * c * h, 4 * 2**20, after=after,
     )
 
 
@@ -483,29 +565,31 @@
     def across(even, odd):
         return lax.ppermute(even, "seq", even_pairs), lax.ppermute(odd, "seq", odd_pairs)
 
-    pieces = back(split(scalars, x))
+    mine, beside, over, rest = split(scalars, x)
+    over, rest, beside = swap(over, 2), swap(rest, 3), swap(beside, 1)
     w = side_by_side(taps)
-    early = early_taps(scalars, pieces[:2], w)
-    terms = across(*open_terms(scalars, pieces, w, r, early[:1]))
-    own, core, far = [], [], []
-    for block in range(2):
-        reach = r * 2**block
-        if block == 0:
-            current, hidden, part = first_block(scalars, early, pieces[2:], w, point, reach)
-        else:
-            current, hidden, part = middle_block(block, scalars, current, w, point, reach)
-        current, even, odd, over, beside = finish_edges(
-            block, scalars, current, hidden, part, terms, w, point, reach, 2 * reach
-        )
-        terms = across(even, odd)
-        own.append(current)
-        core.append(beside)
-        far.append(swap(over, 2))
+    early = early_taps(scalars, mine, beside, w)
+    edge = swap(edge_part(over, r, early[:1]), 1)
+    pieces = (mine, beside, over, edge)
+    terms = across(*open_terms(scalars, pieces, w, r))
+    early = more_taps(scalars, over, edge, w, early)
+    current, even, odd, over, beside = first_block(scalars, rest, early, terms, w, point, r)
+    terms = across(even, odd)
+    own, core, far = [current], [beside], [swap(over, 2)]
+    reach = 2 * r
+    current, hidden, part = middle_block(1, scalars, current, w, point, reach)
+    current, even, odd, over, beside = finish_edges(
+        1, scalars, current, hidden, part, terms, w, point, reach, 2 * reach
+    )
+    terms = across(even, odd)
+    own.append(current)
+    core.append(beside)
+    far.append(swap(over, 2))
     reach = 4 * r
-    current, hidden, part, *inner = middle_block(2, scalars, current, w, point, reach)
+    current, hidden, part, *inner = middle_block(2, scalars, current, w, point, reach, far[:1])
     inner = across(*inner)
     current, even, odd, over, ends = finish_edges(
-        2, scalars, current, hidden, part, terms, w, point, reach, reach, far[:1]
+        2, scalars, current, hidden, part, terms, w, point, reach, reach
     )
     terms = across(even, odd)
     own.append(current)

time: 75.5 us -> 71.9 us (0.952)
  waiting for transfers between devices: 21.2 us -> 14.2 us
  starting transfers between devices: 19.4 us -> 23.7 us
  local copies, waits for them, and re-layouts: 4.42 us -> 0.14 us
  Pallas kernels: 29.8 us -> 33.3 us
    ppermute x10 -> x11, waiting for transfers between devices: 18.1 us -> 11.1 us  [swap(): return lax.ppermute(value, 'seq', [(i, i ^ k) for i in range(size)])]
    unnamed x8 -> x4, local copies, waits for them, and re-layouts: 4.42 us -> 0.14 us
    pallas_call x15 -> x16, Pallas kernels: 29.8 us -> 33.3 us  [call(): pl.pallas_call(kernel, out_shape=outs, in_specs=specs, out_specs=out_spec...]
    ppermute x10 -> x11, starting transfers between devices: 8.53 us -> 11.4 us  [swap(): return lax.ppermute(value, 'seq', [(i, i ^ k) for i in range(size)])]
    ppermute x5, starting transfers between devices: 3.62 us -> 5.17 us  [across(): lax.ppermute(even, 'seq', even_pairs)]
  transfers between devices with their start and end apart: 20 -> 21, of which waited for: 7 -> 7; matrix products, arithmetic and copies ran while one was open for 0% -> 0% of each run, Pallas kernels for 33% -> 37%
where the time goes in v4:
time: 71.9 us; the launch traced here: 71.8 us
  Pallas kernels  33.3 us (46%)
  starting transfers between devices  23.7 us (33%)
  waiting for transfers between devices  14.2 us (20%)
    pallas_call x16, Pallas kernels, call(): pl.pallas_call(kernel, out_shape=outs, in_specs=specs, out_specs=out_spec...  33.3 us
    ppermute x11, starting transfers between devices, swap(): return lax.ppermute(value, 'seq', [(i, i ^ k) for i in range(size)])  11.4 us
    ppermute x11, waiting for transfers between devices, swap(): return lax.ppermute(value, 'seq', [(i, i ^ k) for i in range(size)])  11.1 us
    ppermute x5, starting transfers between devices, across(): lax.ppermute(odd, 'seq', odd_pairs)  7.12 us
    ppermute x5, starting transfers between devices, across(): lax.ppermute(even, 'seq', even_pairs)  5.17 us
    ppermute x5, waiting for transfers between devices, across(): lax.ppermute(even, 'seq', even_pairs)  3.08 us
  transfers between devices with their start and end apart: 21, of which 7 were waited for; matrix products, arithmetic and copies ran while one was open for 0% of the time, Pallas kernels for 37%

profile of v4, /device:TPU:1, one launch (start us, length us, event | category | flops | bytes accessed | tf_op | source)
XLA Modules:
  0.0 71.8 jit_solution(12223269449095494854)
XLA Ops:
  0.1 2.0 %shard_map.37 = (bf16[4,64,768]{2,1,0:T(8,128)(2,1)S(1)}, bf16[4,64,768]{2,1,0:T(8,128)(2,1)S(1)}, bf16[5,64,768]{2,1,0:T(8,128)(2,1)S(1)}, bf16[3,64,768]{2,1,0:T(8,128)(2,1)S(1)}) custom-call(s32[4]{0:T(128)S(1)} %pad_add_fusion.s_ref.parity_ref.refs_0_, bf16[4,4,64,768]{3,2,1,0:T(8,128)(2,1)} %bitcast.15), custom_call_target="tpu_custom_call" | custom-call | bytes 3145728 | tf_op jit(solution)/shard_map/pallas_call | solution.py:54
  2.0 2.1 %collective-permute-start.1 = (bf16[320,768]{1,0:T(8,128)(2,1)S(1)}, bf16[320,768]{1,0:T(8,128)(2,1)S(1)}, u32[]{:S(2)}, u32[]{:S(2)}) collective-permute-start(bf16[320,768]{1,0:T(8,128)(2,1)S(1)} %bitcast.20), channel_id=1, source_target_pairs={{0,2},{1,3},{2,0},{3,1},{4,6},{5,7},{6,4},{7,5},{8,10},{9,11},{10,... | collective-permute-start | bytes 1474568 | tf_op jit(solution)/shard_map/ppermute | solution.py:560
  4.2 1.0 %collective-permute-start.2 = (bf16[256,768]{1,0:T(8,128)(2,1)S(1)}, bf16[256,768]{1,0:T(8,128)(2,1)S(1)}, u32[]{:S(2)}, u32[]{:S(2)}) collective-permute-start(bf16[256,768]{1,0:T(8,128)(2,1)S(1)} %bitcast.21), channel_id=1, source_target_pairs={{0,1},{1,0},{2,3},{3,2},{4,5},{5,4},{6,7},{7,6},{8,9},{9,8},{10,11... | collective-permute-start | bytes 1179656 | tf_op jit(solution)/shard_map/ppermute | solution.py:560
  5.1 3.1 %shard_map.38.w.refs_2_ = bf16[4,768,1152]{2,1,0:T(8,128)(2,1)S(1)} custom-call(bf16[4,3,768,384]{3,2,1,0:T(8,128)(2,1)} %taps.1), custom_call_target="tpu_custom_call" | custom-call | bytes 14155776 | tf_op jit(solution)/shard_map/pallas_call | solution.py:54
  8.3 1.7 %shard_map.39 = (bf16[1024,768]{1,0:T(8,128)(2,1)S(1)}, bf16[1024,384]{1,0:T(8,128)(2,1)S(1)}, f32[1024,384]{1,0:T(8,128)S(1)}, bf16[1024,384]{1,0:T(8,128)(2,1)S(1)}) custom-call(s32[4]{0:T(128)S(1)} %pad_add_fusion.s_ref.parity_ref.refs_0_, bf16[256,768]{1,0:T(8,128)(2,1)S(1)} %bitcast.18, bf16[256,768]{1,0:T(8,128)(2,1)S(1)} %collective-permute-done.2.beside, ...), custom_call_target="tpu_custom_call" | custom-call | flops 905969664 | bytes 1048576 | tf_op jit(solution)/shard_map/pallas_call | solution.py:54
  10.0 5.1 %collective-permute-done.1.refs_0_.over = bf16[320,768]{1,0:T(8,128)(2,1)S(1)} collective-permute-done((bf16[320,768]{1,0:T(8,128)(2,1)S(1)}, bf16[320,768]{1,0:T(8,128)(2,1)S(1)}, u32[]{:S(2)}, u32[]{:S(2)}) %collective-permute-start.1) | collective-permute-done | bytes 491552 | tf_op jit(solution)/shard_map/ppermute | solution.py:560
  15.1 2.1 %collective-permute-start.3 = (bf16[64,768]{1,0:T(8,128)(2,1)S(1)}, bf16[64,768]{1,0:T(8,128)(2,1)S(1)}, u32[]{:S(2)}, u32[]{:S(2)}) collective-permute-start(bf16[64,768]{1,0:T(8,128)(2,1)S(1)} %shard_map.40), channel_id=1, source_target_pairs={{0,1},{1,0},{2,3},{3,2},{4,5},{5,4},{6,7},{7,6},{8,9},{9,8},{10,11... | collective-permute-start | bytes 294920 | tf_op jit(solution)/shard_map/ppermute | solution.py:560
  17.3 0.9 %collective-permute-done.3.edge = bf16[64,768]{1,0:T(8,128)(2,1)S(1)} collective-permute-done((bf16[64,768]{1,0:T(8,128)(2,1)S(1)}, bf16[64,768]{1,0:T(8,128)(2,1)S(1)}, u32[]{:S(2)}, u32[]{:S(2)}) %collective-permute-start.3) | collective-permute-done | bytes 98336 | tf_op jit(solution)/shard_map/ppermute | solution.py:560
  19.1 1.9 %collective-permute-start.4 = (bf16[64,384]{1,0:T(8,128)(2,1)S(1)}, bf16[64,384]{1,0:T(8,128)(2,1)S(1)}, u32[]{:S(2)}, u32[]{:S(2)}) collective-permute-start(bf16[64,384]{1,0:T(8,128)(2,1)S(1)} %get-tuple-element.63), channel_id=1, source_target_pairs={{0,4},{1,5},{2,6},{3,7},{4,0},{5,1},{6,2},{7,3},{8,12},{9,13},{10,... | collective-permute-start | bytes 147464 | tf_op jit(solution)/shard_map/ppermute | solution.py:566
  21.6 1.5 %shard_map.41 = (bf16[1024,768]{1,0:T(8,128)(2,1)S(1)}, bf16[1024,384]{1,0:T(8,128)(2,1)S(1)}, f32[1024,384]{1,0:T(8,128)S(1)}, bf16[1024,384]{1,0:T(8,128)(2,1)S(1)}) custom-call(s32[4]{0:T(128)S(1)} %pad_add_fusion.s_ref.parity_ref.refs_0_, ...), custom_call_target="tpu_custom_call", output_to_operand_aliasing={{0}: (4, {}), {1}: (5, {}), {2}: (6, {}), {3}: (7, {})} | custom-call | flops 566231040 | bytes 1048576 | tf_op jit(solution)/shard_map/pallas_call | solution.py:54
  23.3 2.9 %shard_map.43 = (bf16[1024,768]{1,0:T(8,128)(2,1)S(1)}, bf16[128,384]{1,0:T(8,128)(2,1)S(1)}, bf16[128,384]{1,0:T(8,128)(2,1)S(1)}, bf16[2,256,384]{2,1,0:T(8,12...) custom-call(s32[4]{0:T(128)S(1)} %pad_add_fusion.s_ref.parity_ref.re, ...), custom_call_target="tpu_custom_call", output_to_operand_aliasing={{5}: (2, {}), {6}: (3, {}), {7}: (4, {}), {8}: (5, {})} | custom-call | flops 2415919104 | bytes 4194304 | tf_op jit(solution)/shard_map/pallas_call | solution.py:54
  26.2 1.3 %collective-permute-start.8 = (bf16[2,256,384]{2,1,0:T(8,128)(2,1)S(1)}, bf16[2,256,384]{2,1,0:T(8,128)(2,1)S(1)}, u32[]{:S(2)}, u32[]{:S(2)}) collective-permute-start(bf16[2,256,384]{2,1,0:T(8,128)(2,1)S(1)} %get-tuple-element.72), channel_id=1, source_target_pairs={{0,2},{1,3},{2,0},{3,1},{4,6},{5,7},{6,4},{7,5},{8,10},{9,11},{10,... | collective-permute-start | bytes 1179656 | tf_op jit(solution)/shard_map/ppermute | solution.py:560
  27.5 2.0 %collective-permute-start.6 = (bf16[128,384]{1,0:T(8,128)(2,1)S(1)}, bf16[128,384]{1,0:T(8,128)(2,1)S(1)}, u32[]{:S(2)}, u32[]{:S(2)}) collective-permute-start(bf16[128,384]{1,0:T(8,128)(2,1)S(1)} %get-tuple-element.69), channel_id=1, source_target_pairs={{0,4},{1,5},{2,6},{3,7},{4,0},{5,1},{6,2},{7,3},{8,12},{9,13},{10,... | collective-permute-start | bytes 294920 | tf_op jit(solution)/shard_map/ppermute | solution.py:566
  29.4 1.9 %collective-permute-start.7 = (bf16[128,384]{1,0:T(8,128)(2,1)S(1)}, bf16[128,384]{1,0:T(8,128)(2,1)S(1)}, u32[]{:S(2)}, u32[]{:S(2)}) collective-permute-start(bf16[128,384]{1,0:T(8,128)(2,1)S(1)} %get-tuple-element.70), channel_id=1, source_target_pairs={{0,1},{1,0},{2,3},{3,2},{4,8},{5,9},{6,10},{7,11},{8,4},{9,5},{10,... | collective-permute-start | bytes 294920 | tf_op jit(solution)/shard_map/ppermute | solution.py:566
  31.3 3.6 %shard_map.44 = (bf16[1024,768]{1,0:T(8,128)(2,1)S(1)}, bf16[1024,384]{1,0:T(8,128)(2,1)S(1)}, f32[256,384]{1,0:T(8,128)S(1)}) custom-call(s32[4]{0:T(128)S(1)} %pad_add_fusion.s_ref.parity_ref.refs_0_, bf16[1024,768]{1,0:T(8,128)(2,1)S(1)} %get-tuple-element.65.x, bf16[4,768,1152]{2,1,0:T(8,128)(2,1)S(1)} %shard_map.38.w.refs_2_, ...), custom_call_target="tpu_custom_call" | custom-call | flops 2415919104 | bytes 4194304 | tf_op jit(solution)/shard_map/pallas_call | solution.py:54
  34.9 1.7 %shard_map.45 = (bf16[1024,768]{1,0:T(8,128)(2,1)S(1)}, bf16[256,384]{1,0:T(8,128)(2,1)S(1)}, bf16[256,384]{1,0:T(8,128)(2,1)S(1)}, bf16[2,256,384]{2,1,0:T(8,128)(2,1)S(1)}, bf16[256,384]{1,0:T(8,128)(2,1)S(1)}) custom-call(s32[4]{0:T(128)S(1)} %pad_add_fusion.s_ref.parity_ref.refs_0_, ...), custom_call_target="tpu_custom_call", output_to_operand_aliasing={{0}: (1, {})} | custom-call | flops 452984832 | bytes 4194304 | tf_op jit(solution)/shard_map/pallas_call | solution.py:54
  36.7 2.0 %collective-permute-start.10 = (bf16[256,384]{1,0:T(8,128)(2,1)S(1)}, bf16[256,384]{1,0:T(8,128)(2,1)S(1)}, u32[]{:S(2)}, u32[]{:S(2)}) collective-permute-start(bf16[256,384]{1,0:T(8,128)(2,1)S(1)} %get-tuple-element.77), channel_id=1, source_target_pairs={{0,1},{1,0},{2,3},{3,2},{4,8},{5,9},{6,10},{7,11},{8,4},{9,5},{10,... | collective-permute-start | bytes 589832 | tf_op jit(solution)/shard_map/ppermute | solution.py:566
  38.9 3.9 %shard_map.46 = (bf16[1024,768]{1,0:T(8,128)(2,1)S(1)}, bf16[1024,384]{1,0:T(8,128)(2,1)S(1)}, f32[512,384]{1,0:T(8,128)S(1)}, bf16[256,384]{1,0:T(8,128)(2,1)S(1)}, bf16[256,384]{1,0:T(8,128)(2,1)S(1)}) custom-call(s32[4]{0:T(128)S(1)} %pad_add_fusion.s_ref.parity_ref.refs_0_, bf16[1024,768]{1,0:T(8,128)(2,1)S(1)} %get-tuple-element.71.refs_1_, ...), custom_call_target="tpu_custom_call" | custom-call | flops 2415919104 | bytes 4194304 | tf_op jit(solution)/shard_map/pallas_call | solution.py:54
  42.8 1.2 %collective-permute-start.11 = (bf16[256,384]{1,0:T(8,128)(2,1)S(1)}, bf16[256,384]{1,0:T(8,128)(2,1)S(1)}, u32[]{:S(2)}, u32[]{:S(2)}) collective-permute-start(bf16[256,384]{1,0:T(8,128)(2,1)S(1)} %get-tuple-element.80), channel_id=1, source_target_pairs={{0,4},{1,5},{2,6},{3,7},{4,0},{5,1},{6,2},{7,3},{8,12},{9,13},{10,... | collective-permute-start | bytes 589832 | tf_op jit(solution)/shard_map/ppermute | solution.py:566
  44.1 2.0 %shard_map.47 = (bf16[1024,768]{1,0:T(8,128)(2,1)S(1)}, bf16[256,384]{1,0:T(8,128)(2,1)S(1)}, bf16[256,384]{1,0:T(8,128)(2,1)S(1)}, bf16[2,256,384]{2,1,0:T(8,128)(2,1)S(1)}, bf16[2,256,384]{2,1,0:T(8,128)(2,1)S(1)}) custom-call(s32[4]{0:T(128)S(1)} %pad_add_fusion.s_ref.parity_ref.refs_0_, ...), custom_call_target="tpu_custom_call", output_to_operand_aliasing={{0}: (1, {})} | custom-call | flops 603979776 | bytes 4194304 | tf_op jit(solution)/shard_map/pallas_call | solution.py:54
  46.1 1.3 %collective-permute-start.18 = (bf16[2,256,384]{2,1,0:T(8,128)(2,1)S(1)}, bf16[2,256,384]{2,1,0:T(8,128)(2,1)S(1)}, u32[]{:S(2)}, u32[]{:S(2)}) collective-permute-start(bf16[2,256,384]{2,1,0:T(8,128)(2,1)S(1)} %get-tuple-element.89), channel_id=1, source_target_pairs={{0,2},{1,3},{2,0},{3,1},{4,6},{5,7},{6,4},{7,5},{8,10},{9,11},{10,... | collective-permute-start | bytes 1179656 | tf_op jit(solution)/shard_map/ppermute | solution.py:560
  47.4 1.4 %collective-permute-start.12 = (bf16[256,384]{1,0:T(8,128)(2,1)S(1)}, bf16[256,384]{1,0:T(8,128)(2,1)S(1)}, u32[]{:S(2)}, u32[]{:S(2)}) collective-permute-start(bf16[256,384]{1,0:T(8,128)(2,1)S(1)} %get-tuple-element.81), channel_id=1, source_target_pairs={{0,1},{1,0},{2,3},{3,2},{4,8},{5,9},{6,10},{7,11},{8,4},{9,5},{10,... | collective-permute-start | bytes 589832 | tf_op jit(solution)/shard_map/ppermute | solution.py:566
  49.1 1.2 %collective-permute-start.14 = (bf16[256,384]{1,0:T(8,128)(2,1)S(1)}, bf16[256,384]{1,0:T(8,128)(2,1)S(1)}, u32[]{:S(2)}, u32[]{:S(2)}) collective-permute-start(bf16[256,384]{1,0:T(8,128)(2,1)S(1)} %get-tuple-element.85), channel_id=1, source_target_pairs={{0,1},{1,0},{2,3},{3,2},{4,8},{5,9},{6,10},{7,11},{8,4},{9,5},{10,... | collective-permute-start | bytes 589832 | tf_op jit(solution)/shard_map/ppermute | solution.py:566
  50.3 2.2 %shard_map.48 = (bf16[2,256,384]{2,1,0:T(8,128)(2,1)S(1)}, f32[512,384]{1,0:T(8,128)S(1)}, bf16[256,384]{1,0:T(8,128)(2,1)S(1)}) custom-call(s32[4]{0:T(128)S(1)} %pad_add_fusion.s_ref.parity_ref.refs_0_, bf16[1024,768]{1,0:T(8,128)(2,1)S(1)} %get-tuple-element.78.x, bf16[1024,384]{1,0:T(8,128)(2,1)S(1)} %get-tuple-element.74.hidden, ...), custom_call_target="tpu_custom_call" | custom-call | flops 1207959552 | bytes 4194304 | tf_op jit(solution)/shard_map/pallas_call | solution.py:54
  52.6 2.8 %collective-permute-done.13.refs_3_ = bf16[256,384]{1,0:T(8,128)(2,1)S(1)} collective-permute-done((bf16[256,384]{1,0:T(8,128)(2,1)S(1)}, bf16[256,384]{1,0:T(8,128)(2,1)S(1)}, u32[]{:S(2)}, u32[]{:S(2)}) %collective-permute-start.13) | collective-permute-done | bytes 196640 | tf_op jit(solution)/shard_map/ppermute | solution.py:566
  55.4 1.2 %shard_map.49 = (bf16[256,384]{1,0:T(8,128)(2,1)S(1)}, bf16[256,384]{1,0:T(8,128)(2,1)S(1)}, bf16[256,384]{1,0:T(8,128)(2,1)S(1)}, bf16[256,384]{1,0:T(8,128)(2,1)S(1)}) custom-call(s32[4]{0:T(128)S(1)} %pad_add_fusion.s_ref.parity_ref.refs_0_, bf16[2,256,384]{2,1,0:T(8,128)(2,1)S(1)} %get-tuple-element.82.refs_1_, ...), custom_call_target="tpu_custom_call" | custom-call | flops 3932160 | bytes 2097152 | tf_op jit(solution)/shard_map/pallas_call | solution.py:54
  56.5 1.0 %collective-permute-done.18.refs_5_ = bf16[2,256,384]{2,1,0:T(8,128)(2,1)S(1)} collective-permute-done((bf16[2,256,384]{2,1,0:T(8,128)(2,1)S(1)}, bf16[2,256,384]{2,1,0:T(8,128)(2,1)S(1)}, u32[]{:S(2)}, u32[]{:S(2)}) %collective-permute-start.18) | collective-permute-done | bytes 393248 | tf_op jit(solution)/shard_map/ppermute | solution.py:560
  57.7 1.2 %collective-permute-start.19 = (bf16[6,256,384]{2,1,0:T(8,128)(2,1)S(1)}, bf16[6,256,384]{2,1,0:T(8,128)(2,1)S(1)}, u32[]{:S(2)}, u32[]{:S(2)}) collective-permute-start(bf16[6,256,384]{2,1,0:T(8,128)(2,1)S(1)} %shard_map.50), channel_id=1, source_target_pairs={{0,1},{1,0},{2,3},{3,2},{4,5},{5,4},{6,7},{7,6},{8,9},{9,8},{10,11... | collective-permute-start | bytes 3538952 | tf_op jit(solution)/shard_map/ppermute | solution.py:560
  59.2 1.8 %collective-permute-start.17 = (bf16[256,384]{1,0:T(8,128)(2,1)S(1)}, bf16[256,384]{1,0:T(8,128)(2,1)S(1)}, u32[]{:S(2)}, u32[]{:S(2)}) collective-permute-start(bf16[256,384]{1,0:T(8,128)(2,1)S(1)} %get-tuple-element.88), channel_id=1, source_target_pairs={{0,3},{1,2},{2,1},{3,0},{4,7},{5,6},{6,5},{7,4},{8,11},{9,10},{10,... | collective-permute-start | bytes 589832 | tf_op jit(solution)/shard_map/ppermute | solution.py:560
  61.6 4.7 %shard_map.51 = (bf16[4,4,4,64,768]{4,3,2,1,0:T(8,128)(2,1)}, bf16[4,4,64,768]{3,2,1,0:T(8,128)(2,1)S(1)}) custom-call(s32[4]{0:T(128)S(1)} %pad_add_fusion.s_ref.parity_ref.refs_0_, bf16[4,4,64,768]{3,2,1,0:T(8,128)(2,1)S(1)} %bitcast.16, bf16[16,64,768]{2,1,0:T(8,128)(2,1)S(1)} %bitcast.17, bf16[16,64,768]{2,1,0:T(8,128)(2,1)S(1)} %bitcast.14, ...), custom_call_target="tpu_custom_call" | custom-call | flops 2415919104 | bytes 8388608 | tf_op jit(solution)/shard_map/pallas_call | solution.py:54
  66.4 3.4 %collective-permute-done.17.a3 = bf16[256,384]{1,0:T(8,128)(2,1)S(1)} collective-permute-done((bf16[256,384]{1,0:T(8,128)(2,1)S(1)}, bf16[256,384]{1,0:T(8,128)(2,1)S(1)}, u32[]{:S(2)}, u32[]{:S(2)}) %collective-permute-start.17) | collective-permute-done | bytes 196640 | tf_op jit(solution)/shard_map/ppermute | solution.py:560
  69.7 1.9 %shard_map.52 = bf16[4,4,4,64,768]{4,3,2,1,0:T(8,128)(2,1)} custom-call(s32[4]{0:T(128)S(1)} %pad_add_fusion.s_ref.parity_ref.refs_0_, bf16[256,384]{1,0:T(8,128)(2,1)S(1)} %collective-permute-done.16.a2, bf16[256,384]{1,0:T(8,128)(2,1)S(1)} %collective-permute-done.17.a3, ...), custom_call_target="tpu_custom_call", output_to_operand_aliasing={{}: (5, {})} | custom-call | flops 301989888 | bytes 2097152 | tf_op jit(solution)/shard_map/pallas_call | solution.py:54
  (31 shorter events, 3.5 us)
Async XLA Ops:
  2.0 13.1 %collective-permute-start.1 = (bf16[320,768]{1,0:T(8,128)(2,1)S(1)}, bf16[320,768]{1,0:T(8,128)(2,1)S(1)}, u32[]{:S(2)}, u32[]{:S(2)}) collective-permute-start(bf16[320,768]{1,0:T(8,128)(2,1)S(1)} %bitcast.20), channel_id=1, source_target_pairs={{0,2},{1,3},{2,0},{3,1},{4,6},{5,7},{6,4},{7,5},{8,10},{9,11},{10,... | collective-permute-start | bytes 1474568 | tf_op jit(solution)/shard_map/ppermute | solution.py:560
  4.2 4.1 %collective-permute-start.2 = (bf16[256,768]{1,0:T(8,128)(2,1)S(1)}, bf16[256,768]{1,0:T(8,128)(2,1)S(1)}, u32[]{:S(2)}, u32[]{:S(2)}) collective-permute-start(bf16[256,768]{1,0:T(8,128)(2,1)S(1)} %bitcast.21), channel_id=1, source_target_pairs={{0,1},{1,0},{2,3},{3,2},{4,5},{5,4},{6,7},{7,6},{8,9},{9,8},{10,11... | collective-permute-start | bytes 1179656 | tf_op jit(solution)/shard_map/ppermute | solution.py:560
  5.1 18.0 %collective-permute-start = (bf16[192,768]{1,0:T(8,128)(2,1)S(1)}, bf16[192,768]{1,0:T(8,128)(2,1)S(1)}, u32[]{:S(2)}, u32[]{:S(2)}) collective-permute-start(bf16[192,768]{1,0:T(8,128)(2,1)S(1)} %bitcast.22), channel_id=1, source_target_pairs={{0,3},{1,2},{2,1},{3,0},{4,7},{5,6},{6,5},{7,4},{8,11},{9,10},{10,... | collective-permute-start | bytes 884744 | tf_op jit(solution)/shard_map/ppermute | solution.py:560
  15.1 3.1 %collective-permute-start.3 = (bf16[64,768]{1,0:T(8,128)(2,1)S(1)}, bf16[64,768]{1,0:T(8,128)(2,1)S(1)}, u32[]{:S(2)}, u32[]{:S(2)}) collective-permute-start(bf16[64,768]{1,0:T(8,128)(2,1)S(1)} %shard_map.40), channel_id=1, source_target_pairs={{0,1},{1,0},{2,3},{3,2},{4,5},{5,4},{6,7},{7,6},{8,9},{9,8},{10,11... | collective-permute-start | bytes 294920 | tf_op jit(solution)/shard_map/ppermute | solution.py:560
  19.1 4.0 %collective-permute-start.4 = (bf16[64,384]{1,0:T(8,128)(2,1)S(1)}, bf16[64,384]{1,0:T(8,128)(2,1)S(1)}, u32[]{:S(2)}, u32[]{:S(2)}) collective-permute-start(bf16[64,384]{1,0:T(8,128)(2,1)S(1)} %get-tuple-element.63), channel_id=1, source_target_pairs={{0,4},{1,5},{2,6},{3,7},{4,0},{5,1},{6,2},{7,3},{8,12},{9,13},{10,... | collective-permute-start | bytes 147464 | tf_op jit(solution)/shard_map/ppermute | solution.py:566
  21.0 2.2 %collective-permute-start.5 = (bf16[64,384]{1,0:T(8,128)(2,1)S(1)}, bf16[64,384]{1,0:T(8,128)(2,1)S(1)}, u32[]{:S(2)}, u32[]{:S(2)}) collective-permute-start(bf16[64,384]{1,0:T(8,128)(2,1)S(1)} %get-tuple-element.64), channel_id=1, source_target_pairs={{0,1},{1,0},{2,3},{3,2},{4,8},{5,9},{6,10},{7,11},{8,4},{9,5},{10,... | collective-permute-start | bytes 147464 | tf_op jit(solution)/shard_map/ppermute | solution.py:566
  21.6 1.7 %copy-start = (bf16[4,384,768]{2,1,0:T(8,128)(2,1)S(1)}, bf16[4,384,768]{2,1,0:T(8,128)(2,1)}, u32[]{:S(2)}) copy-start(bf16[4,384,768]{2,1,0:T(8,128)(2,1)} %point.9) | copy-start | bytes 7077892
  26.2 12.8 %collective-permute-start.8 = (bf16[2,256,384]{2,1,0:T(8,128)(2,1)S(1)}, bf16[2,256,384]{2,1,0:T(8,128)(2,1)S(1)}, u32[]{:S(2)}, u32[]{:S(2)}) collective-permute-start(bf16[2,256,384]{2,1,0:T(8,128)(2,1)S(1)} %get-tuple-element.72), channel_id=1, source_target_pairs={{0,2},{1,3},{2,0},{3,1},{4,6},{5,7},{6,4},{7,5},{8,10},{9,11},{10,... | collective-permute-start | bytes 1179656 | tf_op jit(solution)/shard_map/ppermute | solution.py:560
  27.5 7.4 %collective-permute-start.6 = (bf16[128,384]{1,0:T(8,128)(2,1)S(1)}, bf16[128,384]{1,0:T(8,128)(2,1)S(1)}, u32[]{:S(2)}, u32[]{:S(2)}) collective-permute-start(bf16[128,384]{1,0:T(8,128)(2,1)S(1)} %get-tuple-element.69), channel_id=1, source_target_pairs={{0,4},{1,5},{2,6},{3,7},{4,0},{5,1},{6,2},{7,3},{8,12},{9,13},{10,... | collective-permute-start | bytes 294920 | tf_op jit(solution)/shard_map/ppermute | solution.py:566
  29.4 5.5 %collective-permute-start.7 = (bf16[128,384]{1,0:T(8,128)(2,1)S(1)}, bf16[128,384]{1,0:T(8,128)(2,1)S(1)}, u32[]{:S(2)}, u32[]{:S(2)}) collective-permute-start(bf16[128,384]{1,0:T(8,128)(2,1)S(1)} %get-tuple-element.70), channel_id=1, source_target_pairs={{0,1},{1,0},{2,3},{3,2},{4,8},{5,9},{6,10},{7,11},{8,4},{9,5},{10,... | collective-permute-start | bytes 294920 | tf_op jit(solution)/shard_map/ppermute | solution.py:566
  36.6 7.5 %collective-permute-start.9 = (bf16[256,384]{1,0:T(8,128)(2,1)S(1)}, bf16[256,384]{1,0:T(8,128)(2,1)S(1)}, u32[]{:S(2)}, u32[]{:S(2)}) collective-permute-start(bf16[256,384]{1,0:T(8,128)(2,1)S(1)} %get-tuple-element.76), channel_id=1, source_target_pairs={{0,4},{1,5},{2,6},{3,7},{4,0},{5,1},{6,2},{7,3},{8,12},{9,13},{10,... | collective-permute-start | bytes 589832 | tf_op jit(solution)/shard_map/ppermute | solution.py:566
  36.7 7.4 %collective-permute-start.10 = (bf16[256,384]{1,0:T(8,128)(2,1)S(1)}, bf16[256,384]{1,0:T(8,128)(2,1)S(1)}, u32[]{:S(2)}, u32[]{:S(2)}) collective-permute-start(bf16[256,384]{1,0:T(8,128)(2,1)S(1)} %get-tuple-element.77), channel_id=1, source_target_pairs={{0,1},{1,0},{2,3},{3,2},{4,8},{5,9},{6,10},{7,11},{8,4},{9,5},{10,... | collective-permute-start | bytes 589832 | tf_op jit(solution)/shard_map/ppermute | solution.py:566
  38.7 13.9 %collective-permute-start.15 = (bf16[2,256,384]{2,1,0:T(8,128)(2,1)S(1)}, bf16[2,256,384]{2,1,0:T(8,128)(2,1)S(1)}, u32[]{:S(2)}, u32[]{:S(2)}) collective-permute-start(bf16[2,256,384]{2,1,0:T(8,128)(2,1)S(1)} %get-tuple-element.86), channel_id=1, source_target_pairs={{0,2},{1,3},{2,0},{3,1},{4,6},{5,7},{6,4},{7,5},{8,10},{9,11},{10,... | collective-permute-start | bytes 1179656 | tf_op jit(solution)/shard_map/ppermute | solution.py:560
  42.8 6.3 %collective-permute-start.11 = (bf16[256,384]{1,0:T(8,128)(2,1)S(1)}, bf16[256,384]{1,0:T(8,128)(2,1)S(1)}, u32[]{:S(2)}, u32[]{:S(2)}) collective-permute-start(bf16[256,384]{1,0:T(8,128)(2,1)S(1)} %get-tuple-element.80), channel_id=1, source_target_pairs={{0,4},{1,5},{2,6},{3,7},{4,0},{5,1},{6,2},{7,3},{8,12},{9,13},{10,... | collective-permute-start | bytes 589832 | tf_op jit(solution)/shard_map/ppermute | solution.py:566
  46.1 11.5 %collective-permute-start.18 = (bf16[2,256,384]{2,1,0:T(8,128)(2,1)S(1)}, bf16[2,256,384]{2,1,0:T(8,128)(2,1)S(1)}, u32[]{:S(2)}, u32[]{:S(2)}) collective-permute-start(bf16[2,256,384]{2,1,0:T(8,128)(2,1)S(1)} %get-tuple-element.89), channel_id=1, source_target_pairs={{0,2},{1,3},{2,0},{3,1},{4,6},{5,7},{6,4},{7,5},{8,10},{9,11},{10,... | collective-permute-start | bytes 1179656 | tf_op jit(solution)/shard_map/ppermute | solution.py:560
  47.4 2.9 %collective-permute-start.12 = (bf16[256,384]{1,0:T(8,128)(2,1)S(1)}, bf16[256,384]{1,0:T(8,128)(2,1)S(1)}, u32[]{:S(2)}, u32[]{:S(2)}) collective-permute-start(bf16[256,384]{1,0:T(8,128)(2,1)S(1)} %get-tuple-element.81), channel_id=1, source_target_pairs={{0,1},{1,0},{2,3},{3,2},{4,8},{5,9},{6,10},{7,11},{8,4},{9,5},{10,... | collective-permute-start | bytes 589832 | tf_op jit(solution)/shard_map/ppermute | solution.py:566
  48.8 6.5 %collective-permute-start.13 = (bf16[256,384]{1,0:T(8,128)(2,1)S(1)}, bf16[256,384]{1,0:T(8,128)(2,1)S(1)}, u32[]{:S(2)}, u32[]{:S(2)}) collective-permute-start(bf16[256,384]{1,0:T(8,128)(2,1)S(1)} %get-tuple-element.84), channel_id=1, source_target_pairs={{0,4},{1,5},{2,6},{3,7},{4,0},{5,1},{6,2},{7,3},{8,12},{9,13},{10,... | collective-permute-start | bytes 589832 | tf_op jit(solution)/shard_map/ppermute | solution.py:566
  49.1 6.2 %collective-permute-start.14 = (bf16[256,384]{1,0:T(8,128)(2,1)S(1)}, bf16[256,384]{1,0:T(8,128)(2,1)S(1)}, u32[]{:S(2)}, u32[]{:S(2)}) collective-permute-start(bf16[256,384]{1,0:T(8,128)(2,1)S(1)} %get-tuple-element.85), channel_id=1, source_target_pairs={{0,1},{1,0},{2,3},{3,2},{4,8},{5,9},{6,10},{7,11},{8,4},{9,5},{10,... | collective-permute-start | bytes 589832 | tf_op jit(solution)/shard_map/ppermute | solution.py:566
  57.6 4.0 %copy-start.1 = (bf16[1024,768]{1,0:T(8,128)(2,1)S(1)}, bf16[1024,768]{1,0:T(8,128)(2,1)}, u32[]{:S(2)}) copy-start(bf16[1024,768]{1,0:T(8,128)(2,1)} %param.3) | copy-start | bytes 4718596
  57.7 3.9 %collective-permute-start.19 = (bf16[6,256,384]{2,1,0:T(8,128)(2,1)S(1)}, bf16[6,256,384]{2,1,0:T(8,128)(2,1)S(1)}, u32[]{:S(2)}, u32[]{:S(2)}) collective-permute-start(bf16[6,256,384]{2,1,0:T(8,128)(2,1)S(1)} %shard_map.50), channel_id=1, source_target_pairs={{0,1},{1,0},{2,3},{3,2},{4,5},{5,4},{6,7},{7,6},{8,9},{9,8},{10,11... | collective-permute-start | bytes 3538952 | tf_op jit(solution)/shard_map/ppermute | solution.py:560
  58.8 2.8 %collective-permute-start.20 = (bf16[256,384]{1,0:T(8,128)(2,1)S(1)}, bf16[256,384]{1,0:T(8,128)(2,1)S(1)}, u32[]{:S(2)}, u32[]{:S(2)}) collective-permute-start(bf16[256,384]{1,0:T(8,128)(2,1)S(1)} %get-tuple-element.94), channel_id=1, source_target_pairs={{0,1},{1,0},{2,3},{3,2},{4,5},{5,4},{6,7},{7,6},{8,9},{9,8},{10,11... | collective-permute-start | bytes 589832 | tf_op jit(solution)/shard_map/ppermute | solution.py:560
  58.9 7.4 %collective-permute-start.16 = (bf16[256,384]{1,0:T(8,128)(2,1)S(1)}, bf16[256,384]{1,0:T(8,128)(2,1)S(1)}, u32[]{:S(2)}, u32[]{:S(2)}) collective-permute-start(bf16[256,384]{1,0:T(8,128)(2,1)S(1)} %get-tuple-element.87), channel_id=1, source_target_pairs={{0,2},{1,3},{2,0},{3,1},{4,6},{5,7},{6,4},{7,5},{8,10},{9,11},{10,... | collective-permute-start | bytes 589832 | tf_op jit(solution)/shard_map/ppermute | solution.py:560
  59.2 10.5 %collective-permute-start.17 = (bf16[256,384]{1,0:T(8,128)(2,1)S(1)}, bf16[256,384]{1,0:T(8,128)(2,1)S(1)}, u32[]{:S(2)}, u32[]{:S(2)}) collective-permute-start(bf16[256,384]{1,0:T(8,128)(2,1)S(1)} %get-tuple-element.88), channel_id=1, source_target_pairs={{0,3},{1,2},{2,1},{3,0},{4,7},{5,6},{6,5},{7,4},{8,11},{9,10},{10,... | collective-permute-start | bytes 589832 | tf_op jit(solution)/shard_map/ppermute | solution.py:560

commit v5 on v4

--- a/solution.py
+++ b/solution.py
@@ -69,19 +69,22 @@
     return jax.ShapeDtypeStruct(shape, dtype)
 
 
-def split_kernel(s_ref, x, own, beside, over, rest, sems):
+def split_kernel(s_ref, x, own, beside, over, last, rest, sems):
     q = s_ref[0]
-    places = x.shape[0]
+    count = x.shape[0] - 1
     is_top = q == GROUP - 1
-    edge = pl.ds(jnp.where(is_top, places - 1, 0), 1)
-    others = pl.ds(jnp.where(is_top, 0, 1), places - 1)
+
+    def some(bottom, top, size):
+        return pl.ds(jnp.where(is_top, top, bottom), size)
+
     copies = [
         pltpu.make_async_copy(source, target, sems.at[i])
         for i, (source, target) in enumerate(
             (
-                (x.at[:, q ^ 2], over.at[pl.ds(0, places)]),
-                (x.at[edge, q ^ 3], over.at[pl.ds(places, 1)]),
-                (x.at[others, q ^ 3], rest),
+                (x.at[some(0, 1, count), q ^ 2], over.at[pl.ds(0, count)]),
+                (x.at[some(0, count, 1), q ^ 3], over.at[pl.ds(count, 1)]),
+                (x.at[some(1, 0, count), q ^ 3], rest),
+                (x.at[some(count, 0, 1), q ^ 2], last),
                 (x.at[:, q ^ 1], beside),
                 (x.at[:, q], own),
             )
@@ -93,9 +96,9 @@
 def split(scalars, x):
     places, group, r, c = x.shape
     x = pltpu.with_memory_space_constraint(x, pltpu.HBM)
-    outs = [array(n, r, c) for n in (places, places, places + 1, places - 1)]
-    sems = [pltpu.SemaphoreType.DMA((5,))]
-    pieces = call(split_kernel, outs, (scalars, x), [SMEM, HBM], (VMEM,) * 4, sems, 0, 4 * x.size)
+    outs = [array(n, r, c) for n in (places, places, places, 1, places - 1)]
+    sems = [pltpu.SemaphoreType.DMA((6,))]
+    pieces = call(split_kernel, outs, (scalars, x), [SMEM, HBM], (VMEM,) * 5, sems, 0, 4 * x.size)
     return [piece.reshape(piece.shape[0] * r, c) for piece in pieces]
 
 
@@ -152,7 +155,7 @@
     def fetch(piece, at, to):
         ends[pl.ds(to, r)] = piece[pl.ds(at, r)]
 
-    for k, (piece, top) in enumerate(((own, last), (beside, last), (over, last), (edge, 0))):
+    for k, (piece, top) in enumerate(((own, last), (beside, last), (over, last - r), (edge, 0))):
         pl.when(q ^ k == GROUP - 1)(functools.partial(fetch, piece, top, 0))
         pl.when(q ^ k == 0)(functools.partial(fetch, piece, 0, r))
     up = dot(ends[pl.ds(0, r)], w[0, :, :h])
@@ -182,11 +185,8 @@
     keep_terms(at, dot(piece, w[0]), low, mid, high)
 
 
-def part_rows(j, rows, r, first):
-    is_top = j == GROUP - 1
-    if first:
-        return pl.ds(pl.multiple_of(j * rows + jnp.where(is_top, rows - r, 0), r), r)
-    return pl.ds(pl.multiple_of(j * rows + jnp.where(is_top, 0, r), r), rows - r)
+def part_rows(j, rows, size, bottom, top):
+    return pl.ds(pl.multiple_of(j * rows + jnp.where(j == GROUP - 1, top, bottom), rows // GROUP), size)
 
 
 def block_body(reach, x, point, x_ref, h_ref, part_ref, low, mid, high):
@@ -230,9 +230,9 @@
     x, low, mid, high = refs[4:]
     q = s_ref[0]
     rows, r = x.shape[0] // GROUP, edge.shape[0]
-    at = pl.ds(pl.multiple_of((q ^ 2) * rows, rows), rows)
-    piece_taps(at, over[pl.ds(0, rows)], w, x, low, mid, high)
-    piece_taps(part_rows(q ^ 3, rows, r, True), edge[...], w, x, low, mid, high)
+    size = rows - r
+    piece_taps(part_rows(q ^ 2, rows, size, 0, r), over[pl.ds(0, size)], w, x, low, mid, high)
+    piece_taps(part_rows(q ^ 3, rows, r, 0, size), edge[...], w, x, low, mid, high)
 
 
 def more_taps(scalars, over, edge, w, early):
@@ -245,7 +245,7 @@
 
 
 def first_kernel(
-    r, s_ref, rest, x, low, mid, high, from_even, from_odd, w, point,
+    r, s_ref, rest, last, x, low, mid, high, from_even, from_odd, w, point,
     x_ref, even_ref, odd_ref, far_ref, core_ref, *refs
 ):
     hidden = refs[-1]
@@ -253,7 +253,9 @@
     length = x.shape[0]
     rows = length // GROUP
     h = mid.shape[1]
-    piece_taps(part_rows(q ^ 3, rows, r, False), rest[...], w, x, low, mid, high)
+    size = rows - r
+    piece_taps(part_rows(q ^ 3, rows, size, r, 0), rest[...], w, x, low, mid, high)
+    piece_taps(part_rows(q ^ 2, rows, r, size, 0), last[...], w, x, low, mid, high)
     below, above = arrived(s_ref, from_even, from_odd, 0, r)
 
     def finish(start, size, v):
@@ -282,16 +284,16 @@
         ref[...] = hidden[pl.ds(pl.multiple_of((q ^ k) * rows, rows), rows)]
 
 
-def first_block(scalars, rest, early, terms, w, point, r):
+def first_block(scalars, rests, early, terms, w, point, r):
     c, h = w.shape[1], w.shape[2] // 3
     length = early[0].shape[0]
     rows = length // GROUP
     outs = (array(length, c), array(2 * r, h), array(2 * r, h), array(2, rows, h), array(rows, h))
     outs += tuple(array(*e.shape, dtype=e.dtype) for e in early)
     results = call(
-        functools.partial(first_kernel, r), outs, (scalars, rest, *early, *terms, w, point),
-        [SMEM] + [VMEM] * 9, (VMEM,) * 9, [pltpu.VMEM((length, h), BF16)],
-        8 * length * c * h, 4 * 2**20, {2: 5, 3: 6, 4: 7, 5: 8},
+        functools.partial(first_kernel, r), outs, (scalars, *rests, *early, *terms, w, point),
+        [SMEM] + [VMEM] * 10, (VMEM,) * 9, [pltpu.VMEM((length, h), BF16)],
+        8 * length * c * h, 4 * 2**20, {3: 5, 4: 6, 5: 7, 6: 8},
     )
     return results[:5]
 
@@ -300,11 +302,20 @@
     sent, (low, mid, high) = refs[:-3], refs[-3:]
     h = mid.shape[1]
 
+    length = x.shape[0]
+    bottom, top = pl.ds(0, reach), pl.ds(length - reach, reach)
+    terms = dot(x[bottom], w[block, :, : 2 * h])
+    low[bottom] = terms[:, :h].astype(BF16)
+    mid[bottom] = terms[:, h:]
+
     def body(start, size):
-        at = pl.ds(start, size)
+        at = pl.ds(reach + start, size)
         keep_terms(at, dot(x[at], w[block]), low, mid, high)
 
-    over_rows(x.shape[0], body)
+    over_rows(length - 2 * reach, body)
+    terms = dot(x[top], w[block, :, h:])
+    mid[top] = terms[:, :h]
+    high[top] = terms[:, h:].astype(BF16)
     block_body(reach, x, point[block], x_ref, h_ref, part_ref, low, mid, high)
     if sent:
         middle = x.shape[0] // 2
@@ -414,21 +425,23 @@
     outs = (array(2, reach, h), array(half, h, dtype=F32), array(rows, h))
     return call(
         functools.partial(near_kernel, reach), outs, (scalars, x, hidden, ends, *terms, w),
-        [SMEM] + [VMEM] * 6, (VMEM,) * 3, scratch, 4 * x.shape[0] * c * h, 4 * 2**20,
-    )
-
-
-def forward_kernel(*refs):
+        [SMEM] + [VMEM] * 6, (VMEM,) * 3, scratch, 2.4e9, 4 * 2**20,
+    )
+
+
+def forward_kernel(count, *refs):
     out = refs[-1]
-    for i in range((len(refs) - 1) // 2):
-        out[2 * i] = refs[2 * i][...]
-        out[2 * i + 1] = refs[2 * i + 1][1]
-
-
-def forward(own, passing, after):
-    operands = [v for pair in zip(own, passing) for v in pair]
-    out = array(len(operands), *own[0].shape)
-    return call(forward_kernel, out, operands, [VMEM] * len(operands), VMEM, [], 0, 4 * out.size, after=after)
+    for i, ref in enumerate(refs[:-1]):
+        out[i] = ref[...] if i < count else ref[1]
+
+
+def forward(own, passing):
+    out = array(len(own) + len(passing), *own[0].shape)
+    operands = (*own, *passing)
+    return call(
+        functools.partial(forward_kernel, len(own)), out, operands, [VMEM] * len(operands), VMEM, [],
+        0, 4 * out.size,
+    )
 
 
 def last_kernel(s_ref, outer, near, from_even, from_odd, g0, g1, g2, g3, hidden):
@@ -452,71 +465,109 @@
     )
 
 
-def early_out_kernel(count, s_ref, x, *refs):
-    own, far = refs[:count], refs[count : 2 * count]
-    core, lasts, point = refs[2 * count], refs[2 * count + 1 : 2 * count + 3], refs[2 * count + 3]
-    out, last, xs, ys, sems, osems = refs[-6:]
+def add_blocks(x, hiddens, point, keep):
+    for b, hidden in enumerate(hiddens):
+        x = (x.astype(F32) + dot(hidden, point[b])).astype(BF16)
+        keep(b, x)
+    return x
+
+
+def chip_out_kernel(count, s_ref, x, *refs):
+    own, far, refs = refs[:count], refs[count : 2 * count], refs[2 * count :]
+    mine, point, out, kept, xs, ys, sem, osems = refs
+    q = s_ref[0]
+    places, r, c = xs.shape
+    rows = places * r
+    here = pl.ds(pl.multiple_of(q * places, places), places)
+    read = pltpu.make_async_copy(x.at[:, q ^ 2], xs, sem)
+    read.start()
+    writes = start_all(
+        [
+            pltpu.make_async_copy(own[b].at[here], out.at[b, :, q], osems.at[0, b])
+            for b in range(count)
+        ]
+    )
+
+    def write(k, b, value):
+        ys[b] = value.reshape(places, r, c)
+        writes.append(pltpu.make_async_copy(ys.at[b], out.at[b, :, q ^ k], osems.at[k // 2, b]))
+        writes[-1].start()
+
+    now = own[count - 1][here].reshape(rows, c).astype(F32) + dot(mine[...], point[count])
+    write(0, count, now.astype(BF16))
+    read.wait()
+    hiddens = [far[b][0] for b in range(count)]
+    now = add_blocks(xs[...].reshape(rows, c), hiddens, point, functools.partial(write, 2))
+    kept[...] = now
+    wait_all(writes)
+
+
+def chip_outputs(scalars, x, own, far, mine, point, flops):
+    places, group, r, c = x.shape
+    blocks = point.shape[0]
+    own = [v.reshape(group * places, r, c) for v in own]
+    operands = (scalars, x, *own, *far, mine, point)
+    scratch = [
+        pltpu.VMEM((places, r, c), BF16),
+        pltpu.VMEM((blocks, places, r, c), BF16),
+        pltpu.SemaphoreType.DMA,
+        pltpu.SemaphoreType.DMA((2, blocks)),
+    ]
+    return call(
+        functools.partial(chip_out_kernel, blocks - 1),
+        (array(blocks, places, group, r, c), array(places * r, c)),
+        operands, [SMEM, HBM] + [VMEM] * (len(operands) - 2), (HBM, VMEM), scratch, flops, 8 * 2**20,
+    )
+
+
+def core_out_kernel(count, s_ref, x, core, point, _, out, kept, xs, ys, sems, osems):
     q = s_ref[0]
     places, r, c = xs.shape[1:]
     rows = places * r
-    here = pl.ds(pl.multiple_of(q * places, places), places)
+    reads = start_all(
+        [pltpu.make_async_copy(x.at[:, q ^ k], xs.at[i], sems.at[i]) for i, k in enumerate((1, 3))]
+    )
     writes = []
-    for b in range(count):
-        writes.append(pltpu.make_async_copy(own[b].at[here], out.at[b, :, q], osems.at[b, 0]))
-    start_all(writes)
-    reads = start_all(
-        [pltpu.make_async_copy(x.at[:, q ^ k], xs.at[k], sems.at[k]) for k in range(1, GROUP)]
-    )
-
-    def write(b, k, now):
-        target = last if b + 1 == count else ys.at[min(b, count - 1)]
-        target[k] = now.reshape(places, r, c)
-        writes.append(pltpu.make_async_copy(target.at[k], out.at[b, :, q ^ k], osems.at[b, k]))
+
+    def write(i, k, b, value):
+        ys[i, b] = value.reshape(places, r, c)
+        writes.append(pltpu.make_async_copy(ys.at[i, b], out.at[b, :, q ^ k], osems.at[i, b]))
         writes[-1].start()
 
-    for k in range(GROUP):
-        if k == 0:
-            now = own[count - 1][here].reshape(rows, c)
-        else:
-            reads[k - 1].wait()
-            now = xs[k].reshape(rows, c)
-            for b in range(count):
-                hidden = (core[2 * b], far[b][0], core[2 * b + 1])[k - 1]
-                now = (now.astype(F32) + dot(hidden, point[b])).astype(BF16)
-                write(b, k, now)
-        if k < 2:
-            write(count, k, (now.astype(F32) + dot(lasts[k][...], point[count])).astype(BF16))
+    for i, k in enumerate((1, 3)):
+        reads[i].wait()
+        hiddens = [core[(count + 1) * i + b] for b in range(count + 1 - i)]
+        now = add_blocks(xs[i].reshape(rows, c), hiddens, point, functools.partial(write, i, k))
+    kept[...] = now
     wait_all(writes)
 
 
-def early_outputs(scalars, x, own, far, core, lasts, point):
+def core_outputs(scalars, x, core, point, before):
+    places, group, r, c = x.shape
     blocks, h = point.shape[:2]
-    places, group, r, c = x.shape
-    count = blocks - 1
-    own = [v.reshape(group * places, r, c) for v in own]
-    operands = [scalars, x, *own, *far, core, *lasts, point]
+    operands = (scalars, x, core, point, before)
     scratch = [
-        pltpu.VMEM((group, places, r, c), BF16),
-        pltpu.VMEM((count, group, places, r, c), BF16),
-        pltpu.SemaphoreType.DMA((group,)),
-        pltpu.SemaphoreType.DMA((blocks, group)),
+        pltpu.VMEM((2, places, r, c), BF16),
+        pltpu.VMEM((2, blocks, places, r, c), BF16),
+        pltpu.SemaphoreType.DMA((2,)),
+        pltpu.SemaphoreType.DMA((2, blocks)),
     ]
     return call(
-        functools.partial(early_out_kernel, count),
-        (array(blocks, places, group, r, c), array(group, places, r, c)),
-        operands, [SMEM, HBM] + [VMEM] * (len(operands) - 2), (HBM, VMEM), scratch,
-        2 * blocks * x.size * h, 8 * 2**20,
-    )
-
-
-def late_out_kernel(s_ref, a2, a3, xs, point, _, out, ys, osems):
+        functools.partial(core_out_kernel, blocks - 1),
+        (array(*before.shape), array(places * r, c)),
+        operands, [SMEM, HBM, VMEM, VMEM, HBM], (HBM, VMEM), scratch,
+        blocks * x.size * h, 4 * 2**20, {4: 0},
+    )
+
+
+def late_out_kernel(s_ref, a2, a3, x2, x3, point, _, out, ys, osems):
     q = s_ref[0]
-    places, r, c = xs.shape[1:]
+    places, r, c = ys.shape[1:]
     last = out.shape[0] - 1
     writes = []
-    for i, hidden in enumerate((a2, a3)):
-        x = xs[2 + i].reshape(places * r, c).astype(F32) + dot(hidden[...], point[last])
-        ys[i] = x.astype(BF16).reshape(places, r, c)
+    for i, (hidden, x) in enumerate(((a2, x2), (a3, x3))):
+        value = x[...].astype(F32) + dot(hidden[...], point[last])
+        ys[i] = value.astype(BF16).reshape(places, r, c)
         writes.append(pltpu.make_async_copy(ys.at[i], out.at[last, :, q ^ (2 + i)], osems.at[i]))
         writes[-1].start()
     wait_all(writes)
@@ -524,11 +575,11 @@
 
 def late_outputs(scalars, hiddens, xs, point, before):
     blocks, places, group, r, c = before.shape
-    operands = (scalars, *hiddens, xs, point, before)
+    operands = (scalars, *hiddens, *xs, point, before)
     scratch = [pltpu.VMEM((2, places, r, c), BF16), pltpu.SemaphoreType.DMA((2,))]
     return call(
         late_out_kernel, array(*before.shape), operands,
-        [SMEM] + [VMEM] * 4 + [HBM], HBM, scratch,
+        [SMEM] + [VMEM] * 5 + [HBM], HBM, scratch,
         4 * places * r * c * point.shape[1], 2 * 2**20, {len(operands) - 1: 0},
     )
 
@@ -559,21 +610,18 @@
     def swap(value, k):
         return lax.ppermute(value, "seq", [(i, i ^ k) for i in range(size)])
 
-    def back(pieces):
-        return [pieces[0]] + [swap(pieces[k], k) for k in range(1, GROUP)]
-
     def across(even, odd):
         return lax.ppermute(even, "seq", even_pairs), lax.ppermute(odd, "seq", odd_pairs)
 
-    mine, beside, over, rest = split(scalars, x)
-    over, rest, beside = swap(over, 2), swap(rest, 3), swap(beside, 1)
+    mine, beside, over, last, rest = split(scalars, x)
+    over, rest, last, beside = swap(over, 2), swap(rest, 3), swap(last, 2), swap(beside, 1)
     w = side_by_side(taps)
     early = early_taps(scalars, mine, beside, w)
     edge = swap(edge_part(over, r, early[:1]), 1)
     pieces = (mine, beside, over, edge)
     terms = across(*open_terms(scalars, pieces, w, r))
     early = more_taps(scalars, over, edge, w, early)
-    current, even, odd, over, beside = first_block(scalars, rest, early, terms, w, point, r)
+    current, even, odd, over, beside = first_block(scalars, (rest, last), early, terms, w, point, r)
     terms = across(even, odd)
     own, core, far = [current], [beside], [swap(over, 2)]
     reach = 2 * r
@@ -597,11 +645,11 @@
     outer, near, beside = near_terms(scalars, current, hidden, ends, inner, w, reach)
     core.append(beside)
     hidden = last_hidden(scalars, outer, near, terms, far[1:2])
-    after = (hidden[0],)
-    lasts = back(hidden)
-    beside = swap(forward(core, far, after), 1)
-    out, xs = early_outputs(scalars, x, own, far, beside, lasts[:2], point)
-    out = late_outputs(scalars, lasts[2:], xs, point, out)
+    lasts = [swap(hidden[k], k) for k in (2, 3)]
+    beside = swap(forward([*core, hidden[1]], far), 1)
+    out, x2 = chip_outputs(scalars, x, own, far, hidden[0], point, 5e10)
+    out, x3 = core_outputs(scalars, x, beside, point, out)
+    out = late_outputs(scalars, lasts, (x2, x3), point, out)
     return out.reshape(point.shape[0], length, c)
 
 

time: 71.9 us -> 68.3 us (0.950)
  waiting for transfers between devices: 14.2 us -> 8.97 us
  Pallas kernels: 33.3 us -> 34.3 us
    ppermute x11, waiting for transfers between devices: 11.1 us -> 7.14 us  [swap(): return lax.ppermute(value, 'seq', [(i, i ^ k) for i in range(size)])]
    ppermute x5, waiting for transfers between devices: 3.08 us -> 1.82 us  [across(): lax.ppermute(even, 'seq', even_pairs)]
    ppermute x11, starting transfers between devices: 11.4 us -> 12.6 us  [swap(): return lax.ppermute(value, 'seq', [(i, i ^ k) for i in range(size)])]
    pallas_call x16 -> x17, Pallas kernels: 33.3 us -> 34.3 us  [call(): pl.pallas_call(kernel, out_shape=outs, in_specs=specs, out_specs=out_spec...]
  transfers between devices with their start and end apart: 21 -> 21, of which waited for: 7 -> 6; matrix products, arithmetic and copies ran while one was open for 0% -> 0% of each run, Pallas kernels for 37% -> 40%
where the time goes in v5:
time: 68.3 us; the launch traced here: 67.9 us
  Pallas kernels  34.3 us (50%)
  starting transfers between devices  24.1 us (35%)
  waiting for transfers between devices  8.97 us (13%)
    pallas_call x17, Pallas kernels, call(): pl.pallas_call(kernel, out_shape=outs, in_specs=specs, out_specs=out_spec...  34.3 us
    ppermute x11, starting transfers between devices, swap(): return lax.ppermute(value, 'seq', [(i, i ^ k) for i in range(size)])  12.6 us
    ppermute x11, waiting for transfers between devices, swap(): return lax.ppermute(value, 'seq', [(i, i ^ k) for i in range(size)])  7.14 us
    ppermute x5, starting transfers between devices, across(): lax.ppermute(odd, 'seq', odd_pairs)  6.73 us
    ppermute x5, starting transfers between devices, across(): lax.ppermute(even, 'seq', even_pairs)  4.79 us
    ppermute x5, waiting for transfers between devices, across(): lax.ppermute(even, 'seq', even_pairs)  1.82 us
  transfers between devices with their start and end apart: 21, of which 6 were waited for; matrix products, arithmetic and copies ran while one was open for 0% of the time, Pallas kernels for 40%

profile of v5, /device:TPU:1, one launch (start us, length us, event | category | flops | bytes accessed | tf_op | source)
XLA Modules:
  0.0 67.9 jit_solution(4612185049646701289)
XLA Ops:
  0.1 2.0 %shard_map.37 = (bf16[4,64,768]{2,1,0:T(8,128)(2,1)S(1)}, bf16[4,64,768]{2,1,0:T(8,128)(2,1)S(1)}, bf16[4,64,768]{2,1,0:T(8,128)(2,1)S(1)}, bf16[1,64,768]{2,1,0:T(8,128)(2,1)S(1)}, bf16[3,64,768]{2,1,0:T(8,128)(2,1)S(1)}) custom-call(s32[4]{0:T(128)S(1)} %pad_add_fusion.s_ref.parity_ref.refs_0_, bf16[4,4,64,768]{3,2,1,0:T(8,128)(2,1)} %bitcast.16), custom_call_target="tpu_custom_call" | custom-call | bytes 3145728 | tf_op jit(solution)/shard_map/pallas_call | solution.py:54
  2.2 2.7 %collective-permute-start.2 = (bf16[256,768]{1,0:T(8,128)(2,1)S(1)}, bf16[256,768]{1,0:T(8,128)(2,1)S(1)}, u32[]{:S(2)}, u32[]{:S(2)}) collective-permute-start(bf16[256,768]{1,0:T(8,128)(2,1)S(1)} %bitcast.22), channel_id=1, source_target_pairs={{0,2},{1,3},{2,0},{3,1},{4,6},{5,7},{6,4},{7,5},{8,10},{9,11},{10,... | collective-permute-start | bytes 1179656 | tf_op jit(solution)/shard_map/ppermute | solution.py:611
  4.9 3.1 %shard_map.38.w.refs_2_ = bf16[4,768,1152]{2,1,0:T(8,128)(2,1)S(1)} custom-call(bf16[4,3,768,384]{3,2,1,0:T(8,128)(2,1)} %taps.1), custom_call_target="tpu_custom_call" | custom-call | bytes 14155776 | tf_op jit(solution)/shard_map/pallas_call | solution.py:54
  8.0 1.7 %shard_map.39 = (bf16[1024,768]{1,0:T(8,128)(2,1)S(1)}, bf16[1024,384]{1,0:T(8,128)(2,1)S(1)}, f32[1024,384]{1,0:T(8,128)S(1)}, bf16[1024,384]{1,0:T(8,128)(2,1)S(1)}) custom-call(s32[4]{0:T(128)S(1)} %pad_add_fusion.s_ref.parity_ref.refs_0_, bf16[256,768]{1,0:T(8,128)(2,1)S(1)} %bitcast.19, bf16[256,768]{1,0:T(8,128)(2,1)S(1)} %collective-permute-done.3.beside, ...), custom_call_target="tpu_custom_call" | custom-call | flops 905969664 | bytes 1048576 | tf_op jit(solution)/shard_map/pallas_call | solution.py:54
  9.8 4.5 %collective-permute-done.2.refs_0_.over = bf16[256,768]{1,0:T(8,128)(2,1)S(1)} collective-permute-done((bf16[256,768]{1,0:T(8,128)(2,1)S(1)}, bf16[256,768]{1,0:T(8,128)(2,1)S(1)}, u32[]{:S(2)}, u32[]{:S(2)}) %collective-permute-start.2) | collective-permute-done | bytes 393248 | tf_op jit(solution)/shard_map/ppermute | solution.py:611
  14.3 1.0 %collective-permute-start.4 = (bf16[64,768]{1,0:T(8,128)(2,1)S(1)}, bf16[64,768]{1,0:T(8,128)(2,1)S(1)}, u32[]{:S(2)}, u32[]{:S(2)}) collective-permute-start(bf16[64,768]{1,0:T(8,128)(2,1)S(1)} %shard_map.40), channel_id=1, source_target_pairs={{0,1},{1,0},{2,3},{3,2},{4,5},{5,4},{6,7},{7,6},{8,9},{9,8},{10,11... | collective-permute-start | bytes 294920 | tf_op jit(solution)/shard_map/ppermute | solution.py:611
  15.3 1.7 %collective-permute-start.1 = (bf16[64,768]{1,0:T(8,128)(2,1)S(1)}, bf16[64,768]{1,0:T(8,128)(2,1)S(1)}, u32[]{:S(2)}, u32[]{:S(2)}) collective-permute-start(bf16[64,768]{1,0:T(8,128)(2,1)S(1)} %bitcast.25), channel_id=1, source_target_pairs={{0,2},{1,3},{2,0},{3,1},{4,6},{5,7},{6,4},{7,5},{8,10},{9,11},{10,... | collective-permute-start | bytes 294920 | tf_op jit(solution)/shard_map/ppermute | solution.py:611
  17.8 1.4 %collective-permute-start.5 = (bf16[64,384]{1,0:T(8,128)(2,1)S(1)}, bf16[64,384]{1,0:T(8,128)(2,1)S(1)}, u32[]{:S(2)}, u32[]{:S(2)}) collective-permute-start(bf16[64,384]{1,0:T(8,128)(2,1)S(1)} %get-tuple-element.67), channel_id=1, source_target_pairs={{0,4},{1,5},{2,6},{3,7},{4,0},{5,1},{6,2},{7,3},{8,12},{9,13},{10,... | collective-permute-start | bytes 147464 | tf_op jit(solution)/shard_map/ppermute | solution.py:614
  19.8 1.3 %shard_map.41 = (bf16[1024,768]{1,0:T(8,128)(2,1)S(1)}, bf16[1024,384]{1,0:T(8,128)(2,1)S(1)}, f32[1024,384]{1,0:T(8,128)S(1)}, bf16[1024,384]{1,0:T(8,128)(2,1)S(1)}) custom-call(s32[4]{0:T(128)S(1)} %pad_add_fusion.s_ref.parity_ref.refs_0_, ...), custom_call_target="tpu_custom_call", output_to_operand_aliasing={{0}: (4, {}), {1}: (5, {}), {2}: (6, {}), {3}: (7, {})} | custom-call | flops 452984832 | bytes 1048576 | tf_op jit(solution)/shard_map/pallas_call | solution.py:54
  21.2 1.5 %collective-permute-done.1.last = bf16[64,768]{1,0:T(8,128)(2,1)S(1)} collective-permute-done((bf16[64,768]{1,0:T(8,128)(2,1)S(1)}, bf16[64,768]{1,0:T(8,128)(2,1)S(1)}, u32[]{:S(2)}, u32[]{:S(2)}) %collective-permute-start.1) | collective-permute-done | bytes 98336 | tf_op jit(solution)/shard_map/ppermute | solution.py:611
  22.7 3.1 %shard_map.43 = (bf16[1024,768]{1,0:T(8,128)(2,1)S(1)}, bf16[128,384]{1,0:T(8,128)(2,1)S(1)}, bf16[128,384]{1,0:T(8,128)(2,1)S(1)}, bf16[2,256,384]{2,1,0:T(8,12...) custom-call(s32[4]{0:T(128)S(1)} %pad_add_fusion.s_ref.parity_ref.re, ...), custom_call_target="tpu_custom_call", output_to_operand_aliasing={{5}: (3, {}), {6}: (4, {}), {7}: (5, {}), {8}: (6, {})} | custom-call | flops 2415919104 | bytes 4194304 | tf_op jit(solution)/shard_map/pallas_call | solution.py:54
  25.8 1.3 %collective-permute-start.9 = (bf16[2,256,384]{2,1,0:T(8,128)(2,1)S(1)}, bf16[2,256,384]{2,1,0:T(8,128)(2,1)S(1)}, u32[]{:S(2)}, u32[]{:S(2)}) collective-permute-start(bf16[2,256,384]{2,1,0:T(8,128)(2,1)S(1)} %get-tuple-element.76), channel_id=1, source_target_pairs={{0,2},{1,3},{2,0},{3,1},{4,6},{5,7},{6,4},{7,5},{8,10},{9,11},{10,... | collective-permute-start | bytes 1179656 | tf_op jit(solution)/shard_map/ppermute | solution.py:611
  27.1 1.3 %collective-permute-start.7 = (bf16[128,384]{1,0:T(8,128)(2,1)S(1)}, bf16[128,384]{1,0:T(8,128)(2,1)S(1)}, u32[]{:S(2)}, u32[]{:S(2)}) collective-permute-start(bf16[128,384]{1,0:T(8,128)(2,1)S(1)} %get-tuple-element.73), channel_id=1, source_target_pairs={{0,4},{1,5},{2,6},{3,7},{4,0},{5,1},{6,2},{7,3},{8,12},{9,13},{10,... | collective-permute-start | bytes 294920 | tf_op jit(solution)/shard_map/ppermute | solution.py:614
  28.4 1.4 %collective-permute-start.8 = (bf16[128,384]{1,0:T(8,128)(2,1)S(1)}, bf16[128,384]{1,0:T(8,128)(2,1)S(1)}, u32[]{:S(2)}, u32[]{:S(2)}) collective-permute-start(bf16[128,384]{1,0:T(8,128)(2,1)S(1)} %get-tuple-element.74), channel_id=1, source_target_pairs={{0,1},{1,0},{2,3},{3,2},{4,8},{5,9},{6,10},{7,11},{8,4},{9,5},{10,... | collective-permute-start | bytes 294920 | tf_op jit(solution)/shard_map/ppermute | solution.py:614
  29.8 3.3 %shard_map.44 = (bf16[1024,768]{1,0:T(8,128)(2,1)S(1)}, bf16[1024,384]{1,0:T(8,128)(2,1)S(1)}, f32[256,384]{1,0:T(8,128)S(1)}) custom-call(s32[4]{0:T(128)S(1)} %pad_add_fusion.s_ref.parity_ref.refs_0_, bf16[1024,768]{1,0:T(8,128)(2,1)S(1)} %get-tuple-element.69.x, bf16[4,768,1152]{2,1,0:T(8,128)(2,1)S(1)} %shard_map.38.w.refs_2_, ...), custom_call_target="tpu_custom_call" | custom-call | flops 2415919104 | bytes 4194304 | tf_op jit(solution)/shard_map/pallas_call | solution.py:54
  33.2 1.7 %shard_map.45 = (bf16[1024,768]{1,0:T(8,128)(2,1)S(1)}, bf16[256,384]{1,0:T(8,128)(2,1)S(1)}, bf16[256,384]{1,0:T(8,128)(2,1)S(1)}, bf16[2,256,384]{2,1,0:T(8,128)(2,1)S(1)}, bf16[256,384]{1,0:T(8,128)(2,1)S(1)}) custom-call(s32[4]{0:T(128)S(1)} %pad_add_fusion.s_ref.parity_ref.refs_0_, ...), custom_call_target="tpu_custom_call", output_to_operand_aliasing={{0}: (1, {})} | custom-call | flops 452984832 | bytes 4194304 | tf_op jit(solution)/shard_map/pallas_call | solution.py:54
  34.9 1.3 %collective-permute-start.10 = (bf16[256,384]{1,0:T(8,128)(2,1)S(1)}, bf16[256,384]{1,0:T(8,128)(2,1)S(1)}, u32[]{:S(2)}, u32[]{:S(2)}) collective-permute-start(bf16[256,384]{1,0:T(8,128)(2,1)S(1)} %get-tuple-element.80), channel_id=1, source_target_pairs={{0,4},{1,5},{2,6},{3,7},{4,0},{5,1},{6,2},{7,3},{8,12},{9,13},{10,... | collective-permute-start | bytes 589832 | tf_op jit(solution)/shard_map/ppermute | solution.py:614
  36.2 2.0 %collective-permute-start.11 = (bf16[256,384]{1,0:T(8,128)(2,1)S(1)}, bf16[256,384]{1,0:T(8,128)(2,1)S(1)}, u32[]{:S(2)}, u32[]{:S(2)}) collective-permute-start(bf16[256,384]{1,0:T(8,128)(2,1)S(1)} %get-tuple-element.81), channel_id=1, source_target_pairs={{0,1},{1,0},{2,3},{3,2},{4,8},{5,9},{6,10},{7,11},{8,4},{9,5},{10,... | collective-permute-start | bytes 589832 | tf_op jit(solution)/shard_map/ppermute | solution.py:614
  38.4 3.6 %shard_map.46 = (bf16[1024,768]{1,0:T(8,128)(2,1)S(1)}, bf16[1024,384]{1,0:T(8,128)(2,1)S(1)}, f32[512,384]{1,0:T(8,128)S(1)}, bf16[256,384]{1,0:T(8,128)(2,1)S(1)}, bf16[256,384]{1,0:T(8,128)(2,1)S(1)}) custom-call(s32[4]{0:T(128)S(1)} %pad_add_fusion.s_ref.parity_ref.refs_0_, bf16[1024,768]{1,0:T(8,128)(2,1)S(1)} %get-tuple-element.75.refs_1_, ...), custom_call_target="tpu_custom_call" | custom-call | flops 2415919104 | bytes 4194304 | tf_op jit(solution)/shard_map/pallas_call | solution.py:54
  42.0 1.6 %collective-permute-start.13 = (bf16[256,384]{1,0:T(8,128)(2,1)S(1)}, bf16[256,384]{1,0:T(8,128)(2,1)S(1)}, u32[]{:S(2)}, u32[]{:S(2)}) collective-permute-start(bf16[256,384]{1,0:T(8,128)(2,1)S(1)} %get-tuple-element.85), channel_id=1, source_target_pairs={{0,1},{1,0},{2,3},{3,2},{4,8},{5,9},{6,10},{7,11},{8,4},{9,5},{10,... | collective-permute-start | bytes 589832 | tf_op jit(solution)/shard_map/ppermute | solution.py:614
  43.6 2.0 %shard_map.47 = (bf16[1024,768]{1,0:T(8,128)(2,1)S(1)}, bf16[256,384]{1,0:T(8,128)(2,1)S(1)}, bf16[256,384]{1,0:T(8,128)(2,1)S(1)}, bf16[2,256,384]{2,1,0:T(8,128)(2,1)S(1)}, bf16[2,256,384]{2,1,0:T(8,128)(2,1)S(1)}) custom-call(s32[4]{0:T(128)S(1)} %pad_add_fusion.s_ref.parity_ref.refs_0_, ...), custom_call_target="tpu_custom_call", output_to_operand_aliasing={{0}: (1, {})} | custom-call | flops 603979776 | bytes 4194304 | tf_op jit(solution)/shard_map/pallas_call | solution.py:54
  45.6 1.3 %collective-permute-start.19 = (bf16[2,256,384]{2,1,0:T(8,128)(2,1)S(1)}, bf16[2,256,384]{2,1,0:T(8,128)(2,1)S(1)}, u32[]{:S(2)}, u32[]{:S(2)}) collective-permute-start(bf16[2,256,384]{2,1,0:T(8,128)(2,1)S(1)} %get-tuple-element.93), channel_id=1, source_target_pairs={{0,2},{1,3},{2,0},{3,1},{4,6},{5,7},{6,4},{7,5},{8,10},{9,11},{10,... | collective-permute-start | bytes 1179656 | tf_op jit(solution)/shard_map/ppermute | solution.py:611
  48.2 1.2 %collective-permute-start.15 = (bf16[256,384]{1,0:T(8,128)(2,1)S(1)}, bf16[256,384]{1,0:T(8,128)(2,1)S(1)}, u32[]{:S(2)}, u32[]{:S(2)}) collective-permute-start(bf16[256,384]{1,0:T(8,128)(2,1)S(1)} %get-tuple-element.89), channel_id=1, source_target_pairs={{0,1},{1,0},{2,3},{3,2},{4,8},{5,9},{6,10},{7,11},{8,4},{9,5},{10,... | collective-permute-start | bytes 589832 | tf_op jit(solution)/shard_map/ppermute | solution.py:614
  49.4 2.2 %shard_map.48 = (bf16[2,256,384]{2,1,0:T(8,128)(2,1)S(1)}, f32[512,384]{1,0:T(8,128)S(1)}, bf16[256,384]{1,0:T(8,128)(2,1)S(1)}) custom-call(s32[4]{0:T(128)S(1)} %pad_add_fusion.s_ref.parity_ref.refs_0_, bf16[1024,768]{1,0:T(8,128)(2,1)S(1)} %get-tuple-element.82.x, bf16[1024,384]{1,0:T(8,128)(2,1)S(1)} %get-tuple-element.78.hidden, ...), custom_call_target="tpu_custom_call" | custom-call | flops 2400000000 | bytes 4194304 | tf_op jit(solution)/shard_map/pallas_call | solution.py:54
  51.6 1.3 %collective-permute-done.14.refs_3_ = bf16[256,384]{1,0:T(8,128)(2,1)S(1)} collective-permute-done((bf16[256,384]{1,0:T(8,128)(2,1)S(1)}, bf16[256,384]{1,0:T(8,128)(2,1)S(1)}, u32[]{:S(2)}, u32[]{:S(2)}) %collective-permute-start.14) | collective-permute-done | bytes 196640 | tf_op jit(solution)/shard_map/ppermute | solution.py:614
  53.0 1.2 %shard_map.49 = (bf16[256,384]{1,0:T(8,128)(2,1)S(1)}, bf16[256,384]{1,0:T(8,128)(2,1)S(1)}, bf16[256,384]{1,0:T(8,128)(2,1)S(1)}, bf16[256,384]{1,0:T(8,128)(2,1)S(1)}) custom-call(s32[4]{0:T(128)S(1)} %pad_add_fusion.s_ref.parity_ref.refs_0_, bf16[2,256,384]{2,1,0:T(8,128)(2,1)S(1)} %get-tuple-element.86.refs_1_, ...), custom_call_target="tpu_custom_call" | custom-call | flops 3932160 | bytes 2097152 | tf_op jit(solution)/shard_map/pallas_call | solution.py:54
  55.0 2.1 %collective-permute-start.18 = (bf16[256,384]{1,0:T(8,128)(2,1)S(1)}, bf16[256,384]{1,0:T(8,128)(2,1)S(1)}, u32[]{:S(2)}, u32[]{:S(2)}) collective-permute-start(bf16[256,384]{1,0:T(8,128)(2,1)S(1)} %get-tuple-element.92), channel_id=1, source_target_pairs={{0,3},{1,2},{2,1},{3,0},{4,7},{5,6},{6,5},{7,4},{8,11},{9,10},{10,... | collective-permute-start | bytes 589832 | tf_op jit(solution)/shard_map/ppermute | solution.py:611
  57.4 1.2 %collective-permute-start.20 = (bf16[7,256,384]{2,1,0:T(8,128)(2,1)S(1)}, bf16[7,256,384]{2,1,0:T(8,128)(2,1)S(1)}, u32[]{:S(2)}, u32[]{:S(2)}) collective-permute-start(bf16[7,256,384]{2,1,0:T(8,128)(2,1)S(1)} %shard_map.51), channel_id=1, source_target_pairs={{0,1},{1,0},{2,3},{3,2},{4,5},{5,4},{6,7},{7,6},{8,9},{9,8},{10,11... | collective-permute-start | bytes 4128776 | tf_op jit(solution)/shard_map/ppermute | solution.py:611
  58.7 2.7 %shard_map.50 = (bf16[4,4,4,64,768]{4,3,2,1,0:T(8,128)(2,1)}, bf16[256,768]{1,0:T(8,128)(2,1)S(1)}) custom-call(s32[4]{0:T(128)S(1)} %pad_add_fusion.s_ref.parity_ref.refs_0_, bf16[4,4,64,768]{3,2,1,0:T(8,128)(2,1)S(1)} %bitcast.17, bf16[16,64,768]{2,1,0:T(8,128)(2,1)S(1)} %bitcast.21, bf16[16,64,768]{2,1,0:T(8,128)(2,1)S(1)} %bitcast.15, ...), custom_call_target="tpu_custom_call" | custom-call | flops 49999998976 | bytes 8388608 | tf_op jit(solution)/shard_map/pallas_call | solution.py:54
  61.5 3.4 %shard_map.52 = (bf16[4,4,4,64,768]{4,3,2,1,0:T(8,128)(2,1)}, bf16[256,768]{1,0:T(8,128)(2,1)S(1)}) custom-call(s32[4]{0:T(128)S(1)} %pad_add_fusion.s_ref.parity_ref.refs_0_, bf16[4,4,64,768]{3,2,1,0:T(8,128)(2,1)S(1)} %bitcast.18, bf16[7,256,384]{2,1,0:T(8,128)(2,1)S(1)} %collective-permute-done.20.core, ...), custom_call_target="tpu_custom_call", output_to_operand_aliasing={{0}: (4, {})} | custom-call | flops 1207959552 | bytes 4194304 | tf_op jit(solution)/shard_map/pallas_call | solution.py:54
  64.9 0.9 %collective-permute-done.18.a3 = bf16[256,384]{1,0:T(8,128)(2,1)S(1)} collective-permute-done((bf16[256,384]{1,0:T(8,128)(2,1)S(1)}, bf16[256,384]{1,0:T(8,128)(2,1)S(1)}, u32[]{:S(2)}, u32[]{:S(2)}) %collective-permute-start.18) | collective-permute-done | bytes 196640 | tf_op jit(solution)/shard_map/ppermute | solution.py:611
  65.8 1.9 %shard_map.53 = bf16[4,4,4,64,768]{4,3,2,1,0:T(8,128)(2,1)} custom-call(s32[4]{0:T(128)S(1)} %pad_add_fusion.s_ref.parity_ref.refs_0_, bf16[256,384]{1,0:T(8,128)(2,1)S(1)} %collective-permute-done.17.a2, bf16[256,384]{1,0:T(8,128)(2,1)S(1)} %collective-permute-done.18.a3, ...), custom_call_target="tpu_custom_call", output_to_operand_aliasing={{}: (6, {})} | custom-call | flops 301989888 | bytes 2097152 | tf_op jit(solution)/shard_map/pallas_call | solution.py:54
  (32 shorter events, 4.6 us)
Async XLA Ops:
  2.1 6.0 %collective-permute-start.3 = (bf16[256,768]{1,0:T(8,128)(2,1)S(1)}, bf16[256,768]{1,0:T(8,128)(2,1)S(1)}, u32[]{:S(2)}, u32[]{:S(2)}) collective-permute-start(bf16[256,768]{1,0:T(8,128)(2,1)S(1)} %bitcast.23), channel_id=1, source_target_pairs={{0,1},{1,0},{2,3},{3,2},{4,5},{5,4},{6,7},{7,6},{8,9},{9,8},{10,11... | collective-permute-start | bytes 1179656 | tf_op jit(solution)/shard_map/ppermute | solution.py:611
  2.2 12.1 %collective-permute-start.2 = (bf16[256,768]{1,0:T(8,128)(2,1)S(1)}, bf16[256,768]{1,0:T(8,128)(2,1)S(1)}, u32[]{:S(2)}, u32[]{:S(2)}) collective-permute-start(bf16[256,768]{1,0:T(8,128)(2,1)S(1)} %bitcast.22), channel_id=1, source_target_pairs={{0,2},{1,3},{2,0},{3,1},{4,6},{5,7},{6,4},{7,5},{8,10},{9,11},{10,... | collective-permute-start | bytes 1179656 | tf_op jit(solution)/shard_map/ppermute | solution.py:611
  4.9 17.8 %collective-permute-start = (bf16[192,768]{1,0:T(8,128)(2,1)S(1)}, bf16[192,768]{1,0:T(8,128)(2,1)S(1)}, u32[]{:S(2)}, u32[]{:S(2)}) collective-permute-start(bf16[192,768]{1,0:T(8,128)(2,1)S(1)} %bitcast.24), channel_id=1, source_target_pairs={{0,3},{1,2},{2,1},{3,0},{4,7},{5,6},{6,5},{7,4},{8,11},{9,10},{10,... | collective-permute-start | bytes 884744 | tf_op jit(solution)/shard_map/ppermute | solution.py:611
  14.3 2.7 %collective-permute-start.4 = (bf16[64,768]{1,0:T(8,128)(2,1)S(1)}, bf16[64,768]{1,0:T(8,128)(2,1)S(1)}, u32[]{:S(2)}, u32[]{:S(2)}) collective-permute-start(bf16[64,768]{1,0:T(8,128)(2,1)S(1)} %shard_map.40), channel_id=1, source_target_pairs={{0,1},{1,0},{2,3},{3,2},{4,5},{5,4},{6,7},{7,6},{8,9},{9,8},{10,11... | collective-permute-start | bytes 294920 | tf_op jit(solution)/shard_map/ppermute | solution.py:611
  15.3 7.4 %collective-permute-start.1 = (bf16[64,768]{1,0:T(8,128)(2,1)S(1)}, bf16[64,768]{1,0:T(8,128)(2,1)S(1)}, u32[]{:S(2)}, u32[]{:S(2)}) collective-permute-start(bf16[64,768]{1,0:T(8,128)(2,1)S(1)} %bitcast.25), channel_id=1, source_target_pairs={{0,2},{1,3},{2,0},{3,1},{4,6},{5,7},{6,4},{7,5},{8,10},{9,11},{10,... | collective-permute-start | bytes 294920 | tf_op jit(solution)/shard_map/ppermute | solution.py:611
  17.8 4.9 %collective-permute-start.5 = (bf16[64,384]{1,0:T(8,128)(2,1)S(1)}, bf16[64,384]{1,0:T(8,128)(2,1)S(1)}, u32[]{:S(2)}, u32[]{:S(2)}) collective-permute-start(bf16[64,384]{1,0:T(8,128)(2,1)S(1)} %get-tuple-element.67), channel_id=1, source_target_pairs={{0,4},{1,5},{2,6},{3,7},{4,0},{5,1},{6,2},{7,3},{8,12},{9,13},{10,... | collective-permute-start | bytes 147464 | tf_op jit(solution)/shard_map/ppermute | solution.py:614
  19.2 3.5 %collective-permute-start.6 = (bf16[64,384]{1,0:T(8,128)(2,1)S(1)}, bf16[64,384]{1,0:T(8,128)(2,1)S(1)}, u32[]{:S(2)}, u32[]{:S(2)}) collective-permute-start(bf16[64,384]{1,0:T(8,128)(2,1)S(1)} %get-tuple-element.68), channel_id=1, source_target_pairs={{0,1},{1,0},{2,3},{3,2},{4,8},{5,9},{6,10},{7,11},{8,4},{9,5},{10,... | collective-permute-start | bytes 147464 | tf_op jit(solution)/shard_map/ppermute | solution.py:614
  19.8 2.9 %copy-start = (bf16[4,384,768]{2,1,0:T(8,128)(2,1)S(1)}, bf16[4,384,768]{2,1,0:T(8,128)(2,1)}, u32[]{:S(2)}) copy-start(bf16[4,384,768]{2,1,0:T(8,128)(2,1)} %point.11) | copy-start | bytes 7077892
  25.8 12.6 %collective-permute-start.9 = (bf16[2,256,384]{2,1,0:T(8,128)(2,1)S(1)}, bf16[2,256,384]{2,1,0:T(8,128)(2,1)S(1)}, u32[]{:S(2)}, u32[]{:S(2)}) collective-permute-start(bf16[2,256,384]{2,1,0:T(8,128)(2,1)S(1)} %get-tuple-element.76), channel_id=1, source_target_pairs={{0,2},{1,3},{2,0},{3,1},{4,6},{5,7},{6,4},{7,5},{8,10},{9,11},{10,... | collective-permute-start | bytes 1179656 | tf_op jit(solution)/shard_map/ppermute | solution.py:611
  27.1 6.1 %collective-permute-start.7 = (bf16[128,384]{1,0:T(8,128)(2,1)S(1)}, bf16[128,384]{1,0:T(8,128)(2,1)S(1)}, u32[]{:S(2)}, u32[]{:S(2)}) collective-permute-start(bf16[128,384]{1,0:T(8,128)(2,1)S(1)} %get-tuple-element.73), channel_id=1, source_target_pairs={{0,4},{1,5},{2,6},{3,7},{4,0},{5,1},{6,2},{7,3},{8,12},{9,13},{10,... | collective-permute-start | bytes 294920 | tf_op jit(solution)/shard_map/ppermute | solution.py:614
  28.4 4.8 %collective-permute-start.8 = (bf16[128,384]{1,0:T(8,128)(2,1)S(1)}, bf16[128,384]{1,0:T(8,128)(2,1)S(1)}, u32[]{:S(2)}, u32[]{:S(2)}) collective-permute-start(bf16[128,384]{1,0:T(8,128)(2,1)S(1)} %get-tuple-element.74), channel_id=1, source_target_pairs={{0,1},{1,0},{2,3},{3,2},{4,8},{5,9},{6,10},{7,11},{8,4},{9,5},{10,... | collective-permute-start | bytes 294920 | tf_op jit(solution)/shard_map/ppermute | solution.py:614
  34.9 8.7 %collective-permute-start.10 = (bf16[256,384]{1,0:T(8,128)(2,1)S(1)}, bf16[256,384]{1,0:T(8,128)(2,1)S(1)}, u32[]{:S(2)}, u32[]{:S(2)}) collective-permute-start(bf16[256,384]{1,0:T(8,128)(2,1)S(1)} %get-tuple-element.80), channel_id=1, source_target_pairs={{0,4},{1,5},{2,6},{3,7},{4,0},{5,1},{6,2},{7,3},{8,12},{9,13},{10,... | collective-permute-start | bytes 589832 | tf_op jit(solution)/shard_map/ppermute | solution.py:614
  36.2 7.4 %collective-permute-start.11 = (bf16[256,384]{1,0:T(8,128)(2,1)S(1)}, bf16[256,384]{1,0:T(8,128)(2,1)S(1)}, u32[]{:S(2)}, u32[]{:S(2)}) collective-permute-start(bf16[256,384]{1,0:T(8,128)(2,1)S(1)} %get-tuple-element.81), channel_id=1, source_target_pairs={{0,1},{1,0},{2,3},{3,2},{4,8},{5,9},{6,10},{7,11},{8,4},{9,5},{10,... | collective-permute-start | bytes 589832 | tf_op jit(solution)/shard_map/ppermute | solution.py:614
  38.1 13.5 %collective-permute-start.16 = (bf16[2,256,384]{2,1,0:T(8,128)(2,1)S(1)}, bf16[2,256,384]{2,1,0:T(8,128)(2,1)S(1)}, u32[]{:S(2)}, u32[]{:S(2)}) collective-permute-start(bf16[2,256,384]{2,1,0:T(8,128)(2,1)S(1)} %get-tuple-element.90), channel_id=1, source_target_pairs={{0,2},{1,3},{2,0},{3,1},{4,6},{5,7},{6,4},{7,5},{8,10},{9,11},{10,... | collective-permute-start | bytes 1179656 | tf_op jit(solution)/shard_map/ppermute | solution.py:611
  41.9 6.3 %collective-permute-start.12 = (bf16[256,384]{1,0:T(8,128)(2,1)S(1)}, bf16[256,384]{1,0:T(8,128)(2,1)S(1)}, u32[]{:S(2)}, u32[]{:S(2)}) collective-permute-start(bf16[256,384]{1,0:T(8,128)(2,1)S(1)} %get-tuple-element.84), channel_id=1, source_target_pairs={{0,4},{1,5},{2,6},{3,7},{4,0},{5,1},{6,2},{7,3},{8,12},{9,13},{10,... | collective-permute-start | bytes 589832 | tf_op jit(solution)/shard_map/ppermute | solution.py:614
  42.0 7.4 %collective-permute-start.13 = (bf16[256,384]{1,0:T(8,128)(2,1)S(1)}, bf16[256,384]{1,0:T(8,128)(2,1)S(1)}, u32[]{:S(2)}, u32[]{:S(2)}) collective-permute-start(bf16[256,384]{1,0:T(8,128)(2,1)S(1)} %get-tuple-element.85), channel_id=1, source_target_pairs={{0,1},{1,0},{2,3},{3,2},{4,8},{5,9},{6,10},{7,11},{8,4},{9,5},{10,... | collective-permute-start | bytes 589832 | tf_op jit(solution)/shard_map/ppermute | solution.py:614
  45.6 11.7 %collective-permute-start.19 = (bf16[2,256,384]{2,1,0:T(8,128)(2,1)S(1)}, bf16[2,256,384]{2,1,0:T(8,128)(2,1)S(1)}, u32[]{:S(2)}, u32[]{:S(2)}) collective-permute-start(bf16[2,256,384]{2,1,0:T(8,128)(2,1)S(1)} %get-tuple-element.93), channel_id=1, source_target_pairs={{0,2},{1,3},{2,0},{3,1},{4,6},{5,7},{6,4},{7,5},{8,10},{9,11},{10,... | collective-permute-start | bytes 1179656 | tf_op jit(solution)/shard_map/ppermute | solution.py:611
  46.9 6.0 %collective-permute-start.14 = (bf16[256,384]{1,0:T(8,128)(2,1)S(1)}, bf16[256,384]{1,0:T(8,128)(2,1)S(1)}, u32[]{:S(2)}, u32[]{:S(2)}) collective-permute-start(bf16[256,384]{1,0:T(8,128)(2,1)S(1)} %get-tuple-element.88), channel_id=1, source_target_pairs={{0,4},{1,5},{2,6},{3,7},{4,0},{5,1},{6,2},{7,3},{8,12},{9,13},{10,... | collective-permute-start | bytes 589832 | tf_op jit(solution)/shard_map/ppermute | solution.py:614
  48.2 4.7 %collective-permute-start.15 = (bf16[256,384]{1,0:T(8,128)(2,1)S(1)}, bf16[256,384]{1,0:T(8,128)(2,1)S(1)}, u32[]{:S(2)}, u32[]{:S(2)}) collective-permute-start(bf16[256,384]{1,0:T(8,128)(2,1)S(1)} %get-tuple-element.89), channel_id=1, source_target_pairs={{0,1},{1,0},{2,3},{3,2},{4,8},{5,9},{6,10},{7,11},{8,4},{9,5},{10,... | collective-permute-start | bytes 589832 | tf_op jit(solution)/shard_map/ppermute | solution.py:614
  54.1 10.8 %collective-permute-start.17 = (bf16[256,384]{1,0:T(8,128)(2,1)S(1)}, bf16[256,384]{1,0:T(8,128)(2,1)S(1)}, u32[]{:S(2)}, u32[]{:S(2)}) collective-permute-start(bf16[256,384]{1,0:T(8,128)(2,1)S(1)} %get-tuple-element.91), channel_id=1, source_target_pairs={{0,2},{1,3},{2,0},{3,1},{4,6},{5,7},{6,4},{7,5},{8,10},{9,11},{10,... | collective-permute-start | bytes 589832 | tf_op jit(solution)/shard_map/ppermute | solution.py:611
  55.0 10.8 %collective-permute-start.18 = (bf16[256,384]{1,0:T(8,128)(2,1)S(1)}, bf16[256,384]{1,0:T(8,128)(2,1)S(1)}, u32[]{:S(2)}, u32[]{:S(2)}) collective-permute-start(bf16[256,384]{1,0:T(8,128)(2,1)S(1)} %get-tuple-element.92), channel_id=1, source_target_pairs={{0,3},{1,2},{2,1},{3,0},{4,7},{5,6},{6,5},{7,4},{8,11},{9,10},{10,... | collective-permute-start | bytes 589832 | tf_op jit(solution)/shard_map/ppermute | solution.py:611
  57.3 1.4 %copy-start.1 = (bf16[1024,768]{1,0:T(8,128)(2,1)S(1)}, bf16[1024,768]{1,0:T(8,128)(2,1)}, u32[]{:S(2)}) copy-start(bf16[1024,768]{1,0:T(8,128)(2,1)} %param.3) | copy-start | bytes 4718596
  57.4 4.0 %collective-permute-start.20 = (bf16[7,256,384]{2,1,0:T(8,128)(2,1)S(1)}, bf16[7,256,384]{2,1,0:T(8,128)(2,1)S(1)}, u32[]{:S(2)}, u32[]{:S(2)}) collective-permute-start(bf16[7,256,384]{2,1,0:T(8,128)(2,1)S(1)} %shard_map.51), channel_id=1, source_target_pairs={{0,1},{1,0},{2,3},{3,2},{4,5},{5,4},{6,7},{7,6},{8,9},{9,8},{10,11... | collective-permute-start | bytes 4128776 | tf_op jit(solution)/shard_map/ppermute | solution.py:611

commit v6 on v5

--- a/solution.py
+++ b/solution.py
@@ -11,6 +11,7 @@
 GROUP = 4
 ROWS = 512
 VMEM_LIMIT = 24 * 2**20
+NEAR_WORK, CHIP_WORK = 2.4e9, 5e10
 
 F32, BF16 = jnp.float32, jnp.bfloat16
 ANY = pl.BlockSpec(memory_space=pl.ANY)
@@ -173,20 +174,41 @@
     )
 
 
-def keep_terms(at, terms, low, mid, high):
+def keep_terms(at, terms, low, mid, high, low_at=None):
     h = mid.shape[1]
-    low[at] = terms[:, :h].astype(BF16)
+    low[at if low_at is None else low_at] = terms[:, :h].astype(BF16)
     mid[at] = terms[:, h : 2 * h]
     high[at] = terms[:, 2 * h :].astype(BF16)
 
 
-def piece_taps(at, piece, w, x, low, mid, high):
-    x[at] = piece
-    keep_terms(at, dot(piece, w[0]), low, mid, high)
-
-
-def part_rows(j, rows, size, bottom, top):
-    return pl.ds(pl.multiple_of(j * rows + jnp.where(j == GROUP - 1, top, bottom), rows // GROUP), size)
+def piece_taps(starts, r, pieces, w, x, low, mid, high):
+    terms = dot(jnp.concatenate(pieces), w[0])
+    done = 0
+    for start, piece in zip(starts, pieces):
+        size = piece.shape[0]
+        at, low_at = pl.ds(start, size), pl.ds(pl.multiple_of(start + r, r), size)
+        x[at] = piece
+        keep_terms(at, terms[done : done + size], low, mid, high, low_at)
+        done += size
+
+
+def first_finish(starts, sizes, r, point, x, low, mid, high, x_ref, hidden):
+    values = []
+    for start, size in zip(starts, sizes):
+        at, after = pl.ds(start, size), pl.ds(pl.multiple_of(start + r, r), size)
+        v = mid[at] + low[at].astype(F32) + high[after].astype(F32)
+        values.append(gelu(v).astype(BF16))
+        hidden[at] = values[-1]
+    more = dot(jnp.concatenate(values), point[0])
+    done = 0
+    for start, size in zip(starts, sizes):
+        at = pl.ds(start, size)
+        x_ref[at] = (x[at].astype(F32) + more[done : done + size]).astype(BF16)
+        done += size
+
+
+def part_start(j, rows, bottom, top, r):
+    return pl.multiple_of(j * rows + jnp.where(j == GROUP - 1, top, bottom), r)
 
 
 def block_body(reach, x, point, x_ref, h_ref, part_ref, low, mid, high):
@@ -208,20 +230,25 @@
         h_ref[pl.ds(at, reach)] = jnp.zeros((reach, h_ref.shape[1]), BF16)
 
 
-def early_taps_kernel(s_ref, own, beside, w, x, low, mid, high):
+def early_taps_kernel(r, s_ref, own, beside, w, point, x, low, mid, high, x_ref, hidden):
+    q = s_ref[0]
     rows = own.shape[0]
-    for k, piece in enumerate((own, beside)):
-        at = pl.ds(pl.multiple_of((s_ref[0] ^ k) * rows, rows), rows)
-        piece_taps(at, piece[...], w, x, low, mid, high)
-
-
-def early_taps(scalars, own, beside, w):
+    starts = [pl.multiple_of((q ^ k) * rows, rows) for k in range(2)]
+    piece_taps(starts, r, (own[...], beside[...]), w, x, low, mid, high)
+    half = jnp.where(q < GROUP // 2, 0, GROUP // 2) * rows
+    start = pl.multiple_of(half + r, r)
+    first_finish((start,), (2 * rows - 2 * r,), r, point, x, low, mid, high, x_ref, hidden)
+
+
+def early_taps(scalars, own, beside, w, point, r):
     c, h = w.shape[1], w.shape[2] // 3
     rows = own.shape[0]
     length = GROUP * rows
-    outs = (array(length, c), array(length, h), array(length, h, dtype=F32), array(length, h))
-    return call(
-        early_taps_kernel, outs, (scalars, own, beside, w), [SMEM] + [VMEM] * 3, (VMEM,) * 4, [],
+    outs = (array(length, c), array(length + r, h), array(length, h, dtype=F32))
+    outs += (array(length + r, h), array(length, c), array(length, h))
+    return call(
+        functools.partial(early_taps_kernel, r), outs, (scalars, own, beside, w, point),
+        [SMEM] + [VMEM] * 4, (VMEM,) * 6, [],
         12 * rows * c * h, 2**20,
     )
 
@@ -231,8 +258,8 @@
     q = s_ref[0]
     rows, r = x.shape[0] // GROUP, edge.shape[0]
     size = rows - r
-    piece_taps(part_rows(q ^ 2, rows, size, 0, r), over[pl.ds(0, size)], w, x, low, mid, high)
-    piece_taps(part_rows(q ^ 3, rows, r, 0, size), edge[...], w, x, low, mid, high)
+    starts = (part_start(q ^ 2, rows, 0, r, r), part_start(q ^ 3, rows, 0, size, r))
+    piece_taps(starts, r, (over[pl.ds(0, size)], edge[...]), w, x, low, mid, high)
 
 
 def more_taps(scalars, over, edge, w, early):
@@ -245,37 +272,24 @@
 
 
 def first_kernel(
-    r, s_ref, rest, last, x, low, mid, high, from_even, from_odd, w, point,
-    x_ref, even_ref, odd_ref, far_ref, core_ref, *refs
+    r, s_ref, rest, last, x, low, mid, high, x_in, hidden_in, from_even, from_odd, w, point,
+    even_ref, odd_ref, far_ref, core_ref, *refs
 ):
-    hidden = refs[-1]
+    x_ref, hidden = refs[-2:]
     q, parity = s_ref[0], s_ref[1]
     length = x.shape[0]
     rows = length // GROUP
     h = mid.shape[1]
     size = rows - r
-    piece_taps(part_rows(q ^ 3, rows, size, r, 0), rest[...], w, x, low, mid, high)
-    piece_taps(part_rows(q ^ 2, rows, r, size, 0), last[...], w, x, low, mid, high)
+    starts = (part_start(q ^ 3, rows, r, 0, r), part_start(q ^ 2, rows, size, 0, r))
+    piece_taps(starts, r, (rest[...], last[...]), w, x, low, mid, high)
     below, above = arrived(s_ref, from_even, from_odd, 0, r)
-
-    def finish(start, size, v):
-        at = pl.ds(start, size)
-        hidden[at] = gelu(v).astype(BF16)
-        x_ref[at] = (x[at].astype(F32) + dot(hidden[at], point[0])).astype(BF16)
-
-    def body(start, size):
-        v = mid[pl.ds(start, size)]
-        if start == 0:
-            low_terms = jnp.concatenate([below, low[pl.ds(0, size - r)].astype(F32)])
-        else:
-            low_terms = low[pl.ds(start - r, size)].astype(F32)
-        if start + size == length:
-            high_terms = jnp.concatenate([high[pl.ds(start + r, size - r)].astype(F32), above])
-        else:
-            high_terms = high[pl.ds(start + r, size)].astype(F32)
-        finish(start, size, v + low_terms + high_terms)
-
-    over_rows(length, body)
+    low[pl.ds(0, r)] = below.astype(BF16)
+    high[pl.ds(length, r)] = above.astype(BF16)
+    is_low = q < GROUP // 2
+    alone = pl.multiple_of(jnp.where(is_low, 0, length - r), r)
+    others = pl.multiple_of(jnp.where(is_low, 2 * rows - r, 0), r)
+    first_finish((alone, others), (r, 2 * rows + r), r, point, x, low, mid, high, x_ref, hidden)
     ahead = even_ref.shape[0]
     up = dot(x_ref[pl.ds(length - ahead, ahead)], w[1, :, :h])
     down = dot(x_ref[pl.ds(0, ahead)], w[1, :, 2 * h :])
@@ -288,14 +302,14 @@
     c, h = w.shape[1], w.shape[2] // 3
     length = early[0].shape[0]
     rows = length // GROUP
-    outs = (array(length, c), array(2 * r, h), array(2 * r, h), array(2, rows, h), array(rows, h))
+    outs = (array(2 * r, h), array(2 * r, h), array(2, rows, h), array(rows, h))
     outs += tuple(array(*e.shape, dtype=e.dtype) for e in early)
     results = call(
         functools.partial(first_kernel, r), outs, (scalars, *rests, *early, *terms, w, point),
-        [SMEM] + [VMEM] * 10, (VMEM,) * 9, [pltpu.VMEM((length, h), BF16)],
-        8 * length * c * h, 4 * 2**20, {3: 5, 4: 6, 5: 7, 6: 8},
-    )
-    return results[:5]
+        [SMEM] + [VMEM] * 12, (VMEM,) * 10, [],
+        8 * length * c * h, 4 * 2**20, {3 + i: 4 + i for i in range(6)},
+    )
+    return results[8], *results[:4]
 
 
 def middle_kernel(block, reach, parity_ref, x, w, point, x_ref, h_ref, part_ref, *refs):
@@ -397,8 +411,16 @@
     )
 
 
-def near_kernel(reach, s_ref, x, hidden, ends, from_even, from_odd, w, h_ref, near_ref, core_ref, other):
+def near_kernel(
+    reach, s_ref, x, hidden, ends, from_even, from_odd, w, signal, h_ref, near_ref, core_ref, xs_ref, other, sems
+):
     length = x.shape[0]
+    reads = start_all(
+        [
+            pltpu.make_async_copy(signal.at[:, s_ref[0] ^ k], xs_ref.at[k - 1], sems.at[k])
+            for k in range(1, GROUP)
+        ]
+    )
     half = length // 2
     h = near_ref.shape[1]
     block = w.shape[0] - 1
@@ -415,17 +437,21 @@
     near_ref[pl.ds(0, reach)] = lower[reach:]
     near_ref[pl.ds(reach, reach)] = upper[:reach]
     give_back(s_ref[0], hidden, reach, (ends[0], ends[1]), (core_ref,), 1)
-
-
-def near_terms(scalars, x, hidden, ends, terms, w, reach):
+    wait_all(reads)
+
+
+def near_terms(scalars, x, hidden, ends, terms, w, signal, reach):
     c, h = w.shape[1], w.shape[2] // 3
     rows = x.shape[0] // GROUP
     half = x.shape[0] // 2
-    scratch = [pltpu.VMEM((half, h), BF16)]
+    scratch = [pltpu.VMEM((half, h), BF16), pltpu.SemaphoreType.DMA((GROUP,))]
     outs = (array(2, reach, h), array(half, h, dtype=F32), array(rows, h))
-    return call(
-        functools.partial(near_kernel, reach), outs, (scalars, x, hidden, ends, *terms, w),
-        [SMEM] + [VMEM] * 6, (VMEM,) * 3, scratch, 2.4e9, 4 * 2**20,
+    places, _, r, _ = signal.shape
+    outs += (array(GROUP - 1, places, r, c),)
+    signal = pltpu.with_memory_space_constraint(signal, pltpu.HBM)
+    return call(
+        functools.partial(near_kernel, reach), outs, (scalars, x, hidden, ends, *terms, w, signal),
+        [SMEM] + [VMEM] * 6 + [HBM], (VMEM,) * 4, scratch, NEAR_WORK, 4 * 2**20,
     )
 
 
@@ -474,13 +500,11 @@
 
 def chip_out_kernel(count, s_ref, x, *refs):
     own, far, refs = refs[:count], refs[count : 2 * count], refs[2 * count :]
-    mine, point, out, kept, xs, ys, sem, osems = refs
+    mine, point, out, kept, ys, osems = refs
     q = s_ref[0]
-    places, r, c = xs.shape
+    places, r, c = x.shape[1:]
     rows = places * r
     here = pl.ds(pl.multiple_of(q * places, places), places)
-    read = pltpu.make_async_copy(x.at[:, q ^ 2], xs, sem)
-    read.start()
     writes = start_all(
         [
             pltpu.make_async_copy(own[b].at[here], out.at[b, :, q], osems.at[0, b])
@@ -495,38 +519,32 @@
 
     now = own[count - 1][here].reshape(rows, c).astype(F32) + dot(mine[...], point[count])
     write(0, count, now.astype(BF16))
-    read.wait()
     hiddens = [far[b][0] for b in range(count)]
-    now = add_blocks(xs[...].reshape(rows, c), hiddens, point, functools.partial(write, 2))
+    now = add_blocks(x[1].reshape(rows, c), hiddens, point, functools.partial(write, 2))
     kept[...] = now
     wait_all(writes)
 
 
-def chip_outputs(scalars, x, own, far, mine, point, flops):
-    places, group, r, c = x.shape
-    blocks = point.shape[0]
+def chip_outputs(scalars, x, own, far, mine, point):
+    places, r, c = x.shape[1:]
+    group, blocks = GROUP, point.shape[0]
     own = [v.reshape(group * places, r, c) for v in own]
     operands = (scalars, x, *own, *far, mine, point)
     scratch = [
-        pltpu.VMEM((places, r, c), BF16),
         pltpu.VMEM((blocks, places, r, c), BF16),
-        pltpu.SemaphoreType.DMA,
         pltpu.SemaphoreType.DMA((2, blocks)),
     ]
     return call(
         functools.partial(chip_out_kernel, blocks - 1),
         (array(blocks, places, group, r, c), array(places * r, c)),
-        operands, [SMEM, HBM] + [VMEM] * (len(operands) - 2), (HBM, VMEM), scratch, flops, 8 * 2**20,
-    )
-
-
-def core_out_kernel(count, s_ref, x, core, point, _, out, kept, xs, ys, sems, osems):
+        operands, [SMEM] + [VMEM] * (len(operands) - 1), (HBM, VMEM), scratch, CHIP_WORK, 8 * 2**20,
+    )
+
+
+def core_out_kernel(count, s_ref, x, core, point, _, out, kept, ys, osems):
     q = s_ref[0]
-    places, r, c = xs.shape[1:]
+    places, r, c = x.shape[1:]
     rows = places * r
-    reads = start_all(
-        [pltpu.make_async_copy(x.at[:, q ^ k], xs.at[i], sems.at[i]) for i, k in enumerate((1, 3))]
-    )
     writes = []
 
     def write(i, k, b, value):
@@ -535,52 +553,48 @@
         writes[-1].start()
 
     for i, k in enumerate((1, 3)):
-        reads[i].wait()
         hiddens = [core[(count + 1) * i + b] for b in range(count + 1 - i)]
-        now = add_blocks(xs[i].reshape(rows, c), hiddens, point, functools.partial(write, i, k))
+        now = add_blocks(x[2 * i].reshape(rows, c), hiddens, point, functools.partial(write, i, k))
     kept[...] = now
     wait_all(writes)
 
 
 def core_outputs(scalars, x, core, point, before):
-    places, group, r, c = x.shape
-    blocks, h = point.shape[:2]
+    blocks, places, group, r, c = before.shape
+    h = point.shape[1]
     operands = (scalars, x, core, point, before)
     scratch = [
-        pltpu.VMEM((2, places, r, c), BF16),
         pltpu.VMEM((2, blocks, places, r, c), BF16),
-        pltpu.SemaphoreType.DMA((2,)),
         pltpu.SemaphoreType.DMA((2, blocks)),
     ]
     return call(
         functools.partial(core_out_kernel, blocks - 1),
         (array(*before.shape), array(places * r, c)),
-        operands, [SMEM, HBM, VMEM, VMEM, HBM], (HBM, VMEM), scratch,
+        operands, [SMEM] + [VMEM] * 3 + [HBM], (HBM, VMEM), scratch,
         blocks * x.size * h, 4 * 2**20, {4: 0},
     )
 
 
-def late_out_kernel(s_ref, a2, a3, x2, x3, point, _, out, ys, osems):
-    q = s_ref[0]
+def late_out_kernel(s_ref, x2, x3, point, _, a2, a3, out, ys, sems):
     places, r, c = ys.shape[1:]
     last = out.shape[0] - 1
     writes = []
-    for i, (hidden, x) in enumerate(((a2, x2), (a3, x3))):
+    for i, (x, hidden) in enumerate(((x2, a2), (x3, a3))):
         value = x[...].astype(F32) + dot(hidden[...], point[last])
         ys[i] = value.astype(BF16).reshape(places, r, c)
-        writes.append(pltpu.make_async_copy(ys.at[i], out.at[last, :, q ^ (2 + i)], osems.at[i]))
+        writes.append(pltpu.make_async_copy(ys.at[i], out.at[last, :, s_ref[0] ^ (2 + i)], sems.at[i]))
         writes[-1].start()
     wait_all(writes)
 
 
 def late_outputs(scalars, hiddens, xs, point, before):
     blocks, places, group, r, c = before.shape
-    operands = (scalars, *hiddens, *xs, point, before)
+    operands = (scalars, *xs, point, before, *hiddens)
     scratch = [pltpu.VMEM((2, places, r, c), BF16), pltpu.SemaphoreType.DMA((2,))]
     return call(
         late_out_kernel, array(*before.shape), operands,
-        [SMEM] + [VMEM] * 5 + [HBM], HBM, scratch,
-        4 * places * r * c * point.shape[1], 2 * 2**20, {len(operands) - 1: 0},
+        [SMEM] + [VMEM] * 3 + [HBM] + [VMEM] * 2, HBM, scratch,
+        4 * places * r * c * point.shape[1], 2 * 2**20, {4: 0},
     )
 
 
@@ -616,12 +630,13 @@
     mine, beside, over, last, rest = split(scalars, x)
     over, rest, last, beside = swap(over, 2), swap(rest, 3), swap(last, 2), swap(beside, 1)
     w = side_by_side(taps)
-    early = early_taps(scalars, mine, beside, w)
+    early, ready = early_taps(scalars, mine, beside, w, point, r), ()
+    early, ready = early[:4], early[4:]
     edge = swap(edge_part(over, r, early[:1]), 1)
     pieces = (mine, beside, over, edge)
     terms = across(*open_terms(scalars, pieces, w, r))
     early = more_taps(scalars, over, edge, w, early)
-    current, even, odd, over, beside = first_block(scalars, (rest, last), early, terms, w, point, r)
+    current, even, odd, over, beside = first_block(scalars, (rest, last), (*early, *ready), terms, w, point, r)
     terms = across(even, odd)
     own, core, far = [current], [beside], [swap(over, 2)]
     reach = 2 * r
@@ -642,13 +657,13 @@
     terms = across(even, odd)
     own.append(current)
     far.append(swap(over, 2))
-    outer, near, beside = near_terms(scalars, current, hidden, ends, inner, w, reach)
+    outer, near, beside, xs = near_terms(scalars, current, hidden, ends, inner, w, x, reach)
     core.append(beside)
     hidden = last_hidden(scalars, outer, near, terms, far[1:2])
     lasts = [swap(hidden[k], k) for k in (2, 3)]
     beside = swap(forward([*core, hidden[1]], far), 1)
-    out, x2 = chip_outputs(scalars, x, own, far, hidden[0], point, 5e10)
-    out, x3 = core_outputs(scalars, x, beside, point, out)
+    out, x2 = chip_outputs(scalars, xs, own, far, hidden[0], point)
+    out, x3 = core_outputs(scalars, xs, beside, point, out)
     out = late_outputs(scalars, lasts, (x2, x3), point, out)
     return out.reshape(point.shape[0], length, c)
 

time: 68.3 us -> 67.8 us (level)
  waiting for transfers between devices: 8.97 us -> 7.64 us
  Pallas kernels: 34.3 us -> 35 us
    ppermute x5, waiting for transfers between devices: 1.82 us -> 0.88 us  [across(): lax.ppermute(even, 'seq', even_pairs)]
  transfers between devices with their start and end apart: 21 -> 21, of which waited for: 6 -> 7; matrix products, arithmetic and copies ran while one was open for 0% -> 0% of each run, Pallas kernels for 40% -> 42%
where the time goes in v6:
time: 67.8 us; the launch traced here: 67.7 us
  Pallas kernels  35 us (52%)
  starting transfers between devices  24.1 us (36%)
  waiting for transfers between devices  7.64 us (11%)
    pallas_call x17, Pallas kernels, call(): pl.pallas_call(kernel, out_shape=outs, in_specs=specs, out_specs=out_spec...  35 us
    ppermute x11, starting transfers between devices, swap(): return lax.ppermute(value, 'seq', [(i, i ^ k) for i in range(size)])  12.6 us
    ppermute x11, waiting for transfers between devices, swap(): return lax.ppermute(value, 'seq', [(i, i ^ k) for i in range(size)])  6.75 us
    ppermute x5, starting transfers between devices, across(): lax.ppermute(odd, 'seq', odd_pairs)  6.73 us
    ppermute x5, starting transfers between devices, across(): lax.ppermute(even, 'seq', even_pairs)  4.81 us
  transfers between devices with their start and end apart: 21, of which 7 were waited for; matrix products, arithmetic and copies ran while one was open for 0% of the time, Pallas kernels for 42%

profile of v6, /device:TPU:1, one launch (start us, length us, event | category | flops | bytes accessed | tf_op | source)
XLA Modules:
  0.0 67.7 jit_solution(7655720590037846544)
XLA Ops:
  0.1 2.0 %shard_map.37 = (bf16[4,64,768]{2,1,0:T(8,128)(2,1)S(1)}, bf16[4,64,768]{2,1,0:T(8,128)(2,1)S(1)}, bf16[4,64,768]{2,1,0:T(8,128)(2,1)S(1)}, bf16[1,64,768]{2,1,0:T(8,128)(2,1)S(1)}, bf16[3,64,768]{2,1,0:T(8,128)(2,1)S(1)}) custom-call(s32[4]{0:T(128)S(1)} %pad_add_fusion.s_ref.parity_ref.refs_0_, bf16[4,4,64,768]{3,2,1,0:T(8,128)(2,1)} %bitcast.23), custom_call_target="tpu_custom_call" | custom-call | bytes 3145728 | tf_op jit(solution)/shard_map/pallas_call | solution.py:55
  2.2 2.7 %collective-permute-start.2 = (bf16[256,768]{1,0:T(8,128)(2,1)S(1)}, bf16[256,768]{1,0:T(8,128)(2,1)S(1)}, u32[]{:S(2)}, u32[]{:S(2)}) collective-permute-start(bf16[256,768]{1,0:T(8,128)(2,1)S(1)} %bitcast.19), channel_id=1, source_target_pairs={{0,2},{1,3},{2,0},{3,1},{4,6},{5,7},{6,4},{7,5},{8,10},{9,11},{10,... | collective-permute-start | bytes 1179656 | tf_op jit(solution)/shard_map/ppermute | solution.py:625
  4.9 3.3 %shard_map.38.w.refs_2_ = bf16[4,768,1152]{2,1,0:T(8,128)(2,1)S(1)} custom-call(bf16[4,3,768,384]{3,2,1,0:T(8,128)(2,1)} %taps.1), custom_call_target="tpu_custom_call" | custom-call | bytes 14155776 | tf_op jit(solution)/shard_map/pallas_call | solution.py:55
  8.7 2.5 %shard_map.39 = (bf16[1024,768]{1,0:T(8,128)(2,1)S(1)}, bf16[1088,384]{1,0:T(8,128)(2,1)S(1)}, f32[1024,384]{1,0:T(8,128)S(1)}, bf16[1088,384]{1,0:T(8,128)(2,1)...) custom-call(s32[4]{0:T(128)S(1)} %pad_add_fusion.s_ref.parity_ref.refs_0_, ...), custom_call_target="tpu_custom_call" | custom-call | flops 905969664 | bytes 1048576 | tf_op jit(solution)/shard_map/pallas_call | solution.py:55
  11.2 3.1 %collective-permute-done.2.refs_0_.over = bf16[256,768]{1,0:T(8,128)(2,1)S(1)} collective-permute-done((bf16[256,768]{1,0:T(8,128)(2,1)S(1)}, bf16[256,768]{1,0:T(8,128)(2,1)S(1)}, u32[]{:S(2)}, u32[]{:S(2)}) %collective-permute-start.2) | collective-permute-done | bytes 393248 | tf_op jit(solution)/shard_map/ppermute | solution.py:625
  14.3 1.0 %collective-permute-start.4 = (bf16[64,768]{1,0:T(8,128)(2,1)S(1)}, bf16[64,768]{1,0:T(8,128)(2,1)S(1)}, u32[]{:S(2)}, u32[]{:S(2)}) collective-permute-start(bf16[64,768]{1,0:T(8,128)(2,1)S(1)} %shard_map.40), channel_id=1, source_target_pairs={{0,1},{1,0},{2,3},{3,2},{4,5},{5,4},{6,7},{7,6},{8,9},{9,8},{10,11... | collective-permute-start | bytes 294920 | tf_op jit(solution)/shard_map/ppermute | solution.py:625
  15.3 1.7 %collective-permute-start.1 = (bf16[64,768]{1,0:T(8,128)(2,1)S(1)}, bf16[64,768]{1,0:T(8,128)(2,1)S(1)}, u32[]{:S(2)}, u32[]{:S(2)}) collective-permute-start(bf16[64,768]{1,0:T(8,128)(2,1)S(1)} %bitcast.22), channel_id=1, source_target_pairs={{0,2},{1,3},{2,0},{3,1},{4,6},{5,7},{6,4},{7,5},{8,10},{9,11},{10,... | collective-permute-start | bytes 294920 | tf_op jit(solution)/shard_map/ppermute | solution.py:625
  17.8 1.4 %collective-permute-start.5 = (bf16[64,384]{1,0:T(8,128)(2,1)S(1)}, bf16[64,384]{1,0:T(8,128)(2,1)S(1)}, u32[]{:S(2)}, u32[]{:S(2)}) collective-permute-start(bf16[64,384]{1,0:T(8,128)(2,1)S(1)} %get-tuple-element.72), channel_id=1, source_target_pairs={{0,4},{1,5},{2,6},{3,7},{4,0},{5,1},{6,2},{7,3},{8,12},{9,13},{10,... | collective-permute-start | bytes 147464 | tf_op jit(solution)/shard_map/ppermute | solution.py:628
  19.8 1.2 %shard_map.41 = (bf16[1024,768]{1,0:T(8,128)(2,1)S(1)}, bf16[1088,384]{1,0:T(8,128)(2,1)S(1)}, f32[1024,384]{1,0:T(8,128)S(1)}, bf16[1088,384]{1,0:T(8,128)(2,1)S(1)}) custom-call(s32[4]{0:T(128)S(1)} %pad_add_fusion.s_ref.parity_ref.refs_0_, ...), custom_call_target="tpu_custom_call", output_to_operand_aliasing={{0}: (4, {}), {1}: (5, {}), {2}: (6, {}), {3}: (7, {})} | custom-call | flops 452984832 | bytes 1048576 | tf_op jit(solution)/shard_map/pallas_call | solution.py:55
  21.1 1.6 %collective-permute-done.1.last = bf16[64,768]{1,0:T(8,128)(2,1)S(1)} collective-permute-done((bf16[64,768]{1,0:T(8,128)(2,1)S(1)}, bf16[64,768]{1,0:T(8,128)(2,1)S(1)}, u32[]{:S(2)}, u32[]{:S(2)}) %collective-permute-start.1) | collective-permute-done | bytes 98336 | tf_op jit(solution)/shard_map/ppermute | solution.py:625
  22.7 2.9 %shard_map.43 = (bf16[128,384]{1,0:T(8,128)(2,1)S(1)}, bf16[128,384]{1,0:T(8,128)(2,1)S(1)}, bf16[2,256,384]{2,1,0:T(8,128)(2,1)S(1)}, bf16[256,384]{1,0:T(8,128...) custom-call(s32[4]{0:T(128)S(1)} %pad_add_fusion.s_ref.parity_ref.re, ...), custom_call_target="tpu_custom_call", output_to_operand_aliasing={{4}: (3, {}), {5}: (4, {}), {6}: (5, {}), {7}: (6, {}), {8}... | custom-call | flops 2415919104 | bytes 4194304 | tf_op jit(solution)/shard_map/pallas_call | solution.py:55
  25.6 1.3 %collective-permute-start.9 = (bf16[2,256,384]{2,1,0:T(8,128)(2,1)S(1)}, bf16[2,256,384]{2,1,0:T(8,128)(2,1)S(1)}, u32[]{:S(2)}, u32[]{:S(2)}) collective-permute-start(bf16[2,256,384]{2,1,0:T(8,128)(2,1)S(1)} %get-tuple-element.81), channel_id=1, source_target_pairs={{0,2},{1,3},{2,0},{3,1},{4,6},{5,7},{6,4},{7,5},{8,10},{9,11},{10,... | collective-permute-start | bytes 1179656 | tf_op jit(solution)/shard_map/ppermute | solution.py:625
  26.9 1.3 %collective-permute-start.7 = (bf16[128,384]{1,0:T(8,128)(2,1)S(1)}, bf16[128,384]{1,0:T(8,128)(2,1)S(1)}, u32[]{:S(2)}, u32[]{:S(2)}) collective-permute-start(bf16[128,384]{1,0:T(8,128)(2,1)S(1)} %get-tuple-element.78), channel_id=1, source_target_pairs={{0,4},{1,5},{2,6},{3,7},{4,0},{5,1},{6,2},{7,3},{8,12},{9,13},{10,... | collective-permute-start | bytes 294920 | tf_op jit(solution)/shard_map/ppermute | solution.py:628
  28.2 1.4 %collective-permute-start.8 = (bf16[128,384]{1,0:T(8,128)(2,1)S(1)}, bf16[128,384]{1,0:T(8,128)(2,1)S(1)}, u32[]{:S(2)}, u32[]{:S(2)}) collective-permute-start(bf16[128,384]{1,0:T(8,128)(2,1)S(1)} %get-tuple-element.79), channel_id=1, source_target_pairs={{0,1},{1,0},{2,3},{3,2},{4,8},{5,9},{6,10},{7,11},{8,4},{9,5},{10,... | collective-permute-start | bytes 294920 | tf_op jit(solution)/shard_map/ppermute | solution.py:628
  29.6 3.3 %shard_map.44 = (bf16[1024,768]{1,0:T(8,128)(2,1)S(1)}, bf16[1024,384]{1,0:T(8,128)(2,1)S(1)}, f32[256,384]{1,0:T(8,128)S(1)}) custom-call(s32[4]{0:T(128)S(1)} %pad_add_fusion.s_ref.parity_ref.refs_0_, bf16[1024,768]{1,0:T(8,128)(2,1)S(1)} %get-tuple-element.74.x, bf16[4,768,1152]{2,1,0:T(8,128)(2,1)S(1)} %shard_map.38.w.refs_2_, ...), custom_call_target="tpu_custom_call" | custom-call | flops 2415919104 | bytes 4194304 | tf_op jit(solution)/shard_map/pallas_call | solution.py:55
  33.0 1.7 %shard_map.45 = (bf16[1024,768]{1,0:T(8,128)(2,1)S(1)}, bf16[256,384]{1,0:T(8,128)(2,1)S(1)}, bf16[256,384]{1,0:T(8,128)(2,1)S(1)}, bf16[2,256,384]{2,1,0:T(8,128)(2,1)S(1)}, bf16[256,384]{1,0:T(8,128)(2,1)S(1)}) custom-call(s32[4]{0:T(128)S(1)} %pad_add_fusion.s_ref.parity_ref.refs_0_, ...), custom_call_target="tpu_custom_call", output_to_operand_aliasing={{0}: (1, {})} | custom-call | flops 452984832 | bytes 4194304 | tf_op jit(solution)/shard_map/pallas_call | solution.py:55
  34.7 1.3 %collective-permute-start.10 = (bf16[256,384]{1,0:T(8,128)(2,1)S(1)}, bf16[256,384]{1,0:T(8,128)(2,1)S(1)}, u32[]{:S(2)}, u32[]{:S(2)}) collective-permute-start(bf16[256,384]{1,0:T(8,128)(2,1)S(1)} %get-tuple-element.85), channel_id=1, source_target_pairs={{0,4},{1,5},{2,6},{3,7},{4,0},{5,1},{6,2},{7,3},{8,12},{9,13},{10,... | collective-permute-start | bytes 589832 | tf_op jit(solution)/shard_map/ppermute | solution.py:628
  36.0 2.0 %collective-permute-start.11 = (bf16[256,384]{1,0:T(8,128)(2,1)S(1)}, bf16[256,384]{1,0:T(8,128)(2,1)S(1)}, u32[]{:S(2)}, u32[]{:S(2)}) collective-permute-start(bf16[256,384]{1,0:T(8,128)(2,1)S(1)} %get-tuple-element.86), channel_id=1, source_target_pairs={{0,1},{1,0},{2,3},{3,2},{4,8},{5,9},{6,10},{7,11},{8,4},{9,5},{10,... | collective-permute-start | bytes 589832 | tf_op jit(solution)/shard_map/ppermute | solution.py:628
  38.2 3.6 %shard_map.46 = (bf16[1024,768]{1,0:T(8,128)(2,1)S(1)}, bf16[1024,384]{1,0:T(8,128)(2,1)S(1)}, f32[512,384]{1,0:T(8,128)S(1)}, bf16[256,384]{1,0:T(8,128)(2,1)S(1)}, bf16[256,384]{1,0:T(8,128)(2,1)S(1)}) custom-call(s32[4]{0:T(128)S(1)} %pad_add_fusion.s_ref.parity_ref.refs_0_, bf16[1024,768]{1,0:T(8,128)(2,1)S(1)} %get-tuple-element.80.refs_1_, ...), custom_call_target="tpu_custom_call" | custom-call | flops 2415919104 | bytes 4194304 | tf_op jit(solution)/shard_map/pallas_call | solution.py:55
  41.8 1.6 %collective-permute-start.13 = (bf16[256,384]{1,0:T(8,128)(2,1)S(1)}, bf16[256,384]{1,0:T(8,128)(2,1)S(1)}, u32[]{:S(2)}, u32[]{:S(2)}) collective-permute-start(bf16[256,384]{1,0:T(8,128)(2,1)S(1)} %get-tuple-element.90), channel_id=1, source_target_pairs={{0,1},{1,0},{2,3},{3,2},{4,8},{5,9},{6,10},{7,11},{8,4},{9,5},{10,... | collective-permute-start | bytes 589832 | tf_op jit(solution)/shard_map/ppermute | solution.py:628
  43.4 2.0 %shard_map.47 = (bf16[1024,768]{1,0:T(8,128)(2,1)S(1)}, bf16[256,384]{1,0:T(8,128)(2,1)S(1)}, bf16[256,384]{1,0:T(8,128)(2,1)S(1)}, bf16[2,256,384]{2,1,0:T(8,128)(2,1)S(1)}, bf16[2,256,384]{2,1,0:T(8,128)(2,1)S(1)}) custom-call(s32[4]{0:T(128)S(1)} %pad_add_fusion.s_ref.parity_ref.refs_0_, ...), custom_call_target="tpu_custom_call", output_to_operand_aliasing={{0}: (1, {})} | custom-call | flops 603979776 | bytes 4194304 | tf_op jit(solution)/shard_map/pallas_call | solution.py:55
  45.4 1.3 %collective-permute-start.15 = (bf16[2,256,384]{2,1,0:T(8,128)(2,1)S(1)}, bf16[2,256,384]{2,1,0:T(8,128)(2,1)S(1)}, u32[]{:S(2)}, u32[]{:S(2)}) collective-permute-start(bf16[2,256,384]{2,1,0:T(8,128)(2,1)S(1)} %get-tuple-element.93), channel_id=1, source_target_pairs={{0,2},{1,3},{2,0},{3,1},{4,6},{5,7},{6,4},{7,5},{8,10},{9,11},{10,... | collective-permute-start | bytes 1179656 | tf_op jit(solution)/shard_map/ppermute | solution.py:625
  48.0 1.2 %collective-permute-start.17 = (bf16[256,384]{1,0:T(8,128)(2,1)S(1)}, bf16[256,384]{1,0:T(8,128)(2,1)S(1)}, u32[]{:S(2)}, u32[]{:S(2)}) collective-permute-start(bf16[256,384]{1,0:T(8,128)(2,1)S(1)} %get-tuple-element.97), channel_id=1, source_target_pairs={{0,1},{1,0},{2,3},{3,2},{4,8},{5,9},{6,10},{7,11},{8,4},{9,5},{10,... | collective-permute-start | bytes 589832 | tf_op jit(solution)/shard_map/ppermute | solution.py:628
  49.2 3.2 %shard_map.48 = (bf16[2,256,384]{2,1,0:T(8,128)(2,1)S(1)}, f32[512,384]{1,0:T(8,128)S(1)}, bf16[256,384]{1,0:T(8,128)(2,1)S(1)}, bf16[3,4,64,768]{3,2,1,0:T(8,128)(2,1)S(1)}) custom-call(s32[4]{0:T(128)S(1)} %pad_add_fusion.s_ref.parity_ref.refs_0_, bf16[1024,768]{1,0:T(8,128)(2,1)S(1)} %get-tuple-element.87.x, ...), custom_call_target="tpu_custom_call" | custom-call | flops 2400000000 | bytes 4194304 | tf_op jit(solution)/shard_map/pallas_call | solution.py:55
  52.7 1.2 %shard_map.49 = (bf16[256,384]{1,0:T(8,128)(2,1)S(1)}, bf16[256,384]{1,0:T(8,128)(2,1)S(1)}, bf16[256,384]{1,0:T(8,128)(2,1)S(1)}, bf16[256,384]{1,0:T(8,128)(2,1)S(1)}) custom-call(s32[4]{0:T(128)S(1)} %pad_add_fusion.s_ref.parity_ref.refs_0_, bf16[2,256,384]{2,1,0:T(8,128)(2,1)S(1)} %get-tuple-element.94.refs_1_, ...), custom_call_target="tpu_custom_call" | custom-call | flops 3932160 | bytes 2097152 | tf_op jit(solution)/shard_map/pallas_call | solution.py:55
  53.9 1.1 %collective-permute-start.19 = (bf16[256,384]{1,0:T(8,128)(2,1)S(1)}, bf16[256,384]{1,0:T(8,128)(2,1)S(1)}, u32[]{:S(2)}, u32[]{:S(2)}) collective-permute-start(bf16[256,384]{1,0:T(8,128)(2,1)S(1)} %get-tuple-element.107), channel_id=1, source_target_pairs={{0,2},{1,3},{2,0},{3,1},{4,6},{5,7},{6,4},{7,5},{8,10},{9,11},{10,... | collective-permute-start | bytes 589832 | tf_op jit(solution)/shard_map/ppermute | solution.py:625
  55.0 1.9 %collective-permute-start.20 = (bf16[256,384]{1,0:T(8,128)(2,1)S(1)}, bf16[256,384]{1,0:T(8,128)(2,1)S(1)}, u32[]{:S(2)}, u32[]{:S(2)}) collective-permute-start(bf16[256,384]{1,0:T(8,128)(2,1)S(1)} %get-tuple-element.108), channel_id=1, source_target_pairs={{0,3},{1,2},{2,1},{3,0},{4,7},{5,6},{6,5},{7,4},{8,11},{9,10},{10,... | collective-permute-start | bytes 589832 | tf_op jit(solution)/shard_map/ppermute | solution.py:625
  57.2 1.2 %collective-permute-start.18 = (bf16[7,256,384]{2,1,0:T(8,128)(2,1)S(1)}, bf16[7,256,384]{2,1,0:T(8,128)(2,1)S(1)}, u32[]{:S(2)}, u32[]{:S(2)}) collective-permute-start(bf16[7,256,384]{2,1,0:T(8,128)(2,1)S(1)} %shard_map.51), channel_id=1, source_target_pairs={{0,1},{1,0},{2,3},{3,2},{4,5},{5,4},{6,7},{7,6},{8,9},{9,8},{10,11... | collective-permute-start | bytes 4128776 | tf_op jit(solution)/shard_map/ppermute | solution.py:625
  58.4 2.3 %shard_map.50 = (bf16[4,4,4,64,768]{4,3,2,1,0:T(8,128)(2,1)}, bf16[256,768]{1,0:T(8,128)(2,1)S(1)}) custom-call(s32[4]{0:T(128)S(1)} %pad_add_fusion.s_ref.parity_ref.refs_0_, bf16[3,4,64,768]{3,2,1,0:T(8,128)(2,1)S(1)} %get-tuple-element.91.x, bf16[16,64,768]{2,1,0:T(8,128)(2,1)S(1)} %bitcast.14, bf16[16,64,768]{2,1,0:T(8,128)(2,1)S(1)} %bitcast.16, ...), custom_call_target="tpu_custom_call" | custom-call | flops 49999998976 | bytes 8388608 | tf_op jit(solution)/shard_map/pallas_call | solution.py:55
  61.2 3.0 %shard_map.52 = (bf16[4,4,4,64,768]{4,3,2,1,0:T(8,128)(2,1)}, bf16[256,768]{1,0:T(8,128)(2,1)S(1)}) custom-call(s32[4]{0:T(128)S(1)} %pad_add_fusion.s_ref.parity_ref.refs_0_, bf16[3,4,64,768]{3,2,1,0:T(8,128)(2,1)S(1)} %get-tuple-element.91.x, bf16[7,256,384]{2,1,0:T(8,128)(2,1)S(1)} %collective-permute-done.18.core, ...), custom_call_target="tpu_custom_call", output_to_operand_aliasing={{0}: (4, {})} | custom-call | flops 905969664 | bytes 4194304 | tf_op jit(solution)/shard_map/pallas_call | solution.py:55
  64.2 1.4 %collective-permute-done.20.a3 = bf16[256,384]{1,0:T(8,128)(2,1)S(1)} collective-permute-done((bf16[256,384]{1,0:T(8,128)(2,1)S(1)}, bf16[256,384]{1,0:T(8,128)(2,1)S(1)}, u32[]{:S(2)}, u32[]{:S(2)}) %collective-permute-start.20) | collective-permute-done | bytes 196640 | tf_op jit(solution)/shard_map/ppermute | solution.py:625
  65.6 1.9 %shard_map.53 = bf16[4,4,4,64,768]{4,3,2,1,0:T(8,128)(2,1)} custom-call(s32[4]{0:T(128)S(1)} %pad_add_fusion.s_ref.parity_ref.refs_0_, bf16[256,768]{1,0:T(8,128)(2,1)S(1)} %get-tuple-element.99.x2, bf16[256,768]{1,0:T(8,128)(2,1)S(1)} %get-tuple-element.105.x3, bf16[4,384,768]{2,1,0:T(8,128)(2,1)S(1)} %copy-done, ...), custom_call_target="tpu_custom_call", output_to_operand_aliasing={{}: (4, {})} | custom-call | flops 301989888 | bytes 2097152 | tf_op jit(solution)/shard_map/pallas_call | solution.py:55
  (30 shorter events, 5.0 us)
Async XLA Ops:
  2.1 6.1 %collective-permute-start.3 = (bf16[256,768]{1,0:T(8,128)(2,1)S(1)}, bf16[256,768]{1,0:T(8,128)(2,1)S(1)}, u32[]{:S(2)}, u32[]{:S(2)}) collective-permute-start(bf16[256,768]{1,0:T(8,128)(2,1)S(1)} %bitcast.20), channel_id=1, source_target_pairs={{0,1},{1,0},{2,3},{3,2},{4,5},{5,4},{6,7},{7,6},{8,9},{9,8},{10,11... | collective-permute-start | bytes 1179656 | tf_op jit(solution)/shard_map/ppermute | solution.py:625
  2.2 12.1 %collective-permute-start.2 = (bf16[256,768]{1,0:T(8,128)(2,1)S(1)}, bf16[256,768]{1,0:T(8,128)(2,1)S(1)}, u32[]{:S(2)}, u32[]{:S(2)}) collective-permute-start(bf16[256,768]{1,0:T(8,128)(2,1)S(1)} %bitcast.19), channel_id=1, source_target_pairs={{0,2},{1,3},{2,0},{3,1},{4,6},{5,7},{6,4},{7,5},{8,10},{9,11},{10,... | collective-permute-start | bytes 1179656 | tf_op jit(solution)/shard_map/ppermute | solution.py:625
  4.9 17.8 %collective-permute-start = (bf16[192,768]{1,0:T(8,128)(2,1)S(1)}, bf16[192,768]{1,0:T(8,128)(2,1)S(1)}, u32[]{:S(2)}, u32[]{:S(2)}) collective-permute-start(bf16[192,768]{1,0:T(8,128)(2,1)S(1)} %bitcast.21), channel_id=1, source_target_pairs={{0,3},{1,2},{2,1},{3,0},{4,7},{5,6},{6,5},{7,4},{8,11},{9,10},{10,... | collective-permute-start | bytes 884744 | tf_op jit(solution)/shard_map/ppermute | solution.py:625
  4.9 3.8 %copy-start = (bf16[4,384,768]{2,1,0:T(8,128)(2,1)S(1)}, bf16[4,384,768]{2,1,0:T(8,128)(2,1)}, u32[]{:S(2)}) copy-start(bf16[4,384,768]{2,1,0:T(8,128)(2,1)} %point.13) | copy-start | bytes 7077892
  14.3 2.7 %collective-permute-start.4 = (bf16[64,768]{1,0:T(8,128)(2,1)S(1)}, bf16[64,768]{1,0:T(8,128)(2,1)S(1)}, u32[]{:S(2)}, u32[]{:S(2)}) collective-permute-start(bf16[64,768]{1,0:T(8,128)(2,1)S(1)} %shard_map.40), channel_id=1, source_target_pairs={{0,1},{1,0},{2,3},{3,2},{4,5},{5,4},{6,7},{7,6},{8,9},{9,8},{10,11... | collective-permute-start | bytes 294920 | tf_op jit(solution)/shard_map/ppermute | solution.py:625
  15.3 7.4 %collective-permute-start.1 = (bf16[64,768]{1,0:T(8,128)(2,1)S(1)}, bf16[64,768]{1,0:T(8,128)(2,1)S(1)}, u32[]{:S(2)}, u32[]{:S(2)}) collective-permute-start(bf16[64,768]{1,0:T(8,128)(2,1)S(1)} %bitcast.22), channel_id=1, source_target_pairs={{0,2},{1,3},{2,0},{3,1},{4,6},{5,7},{6,4},{7,5},{8,10},{9,11},{10,... | collective-permute-start | bytes 294920 | tf_op jit(solution)/shard_map/ppermute | solution.py:625
  17.8 4.9 %collective-permute-start.5 = (bf16[64,384]{1,0:T(8,128)(2,1)S(1)}, bf16[64,384]{1,0:T(8,128)(2,1)S(1)}, u32[]{:S(2)}, u32[]{:S(2)}) collective-permute-start(bf16[64,384]{1,0:T(8,128)(2,1)S(1)} %get-tuple-element.72), channel_id=1, source_target_pairs={{0,4},{1,5},{2,6},{3,7},{4,0},{5,1},{6,2},{7,3},{8,12},{9,13},{10,... | collective-permute-start | bytes 147464 | tf_op jit(solution)/shard_map/ppermute | solution.py:628
  19.2 3.5 %collective-permute-start.6 = (bf16[64,384]{1,0:T(8,128)(2,1)S(1)}, bf16[64,384]{1,0:T(8,128)(2,1)S(1)}, u32[]{:S(2)}, u32[]{:S(2)}) collective-permute-start(bf16[64,384]{1,0:T(8,128)(2,1)S(1)} %get-tuple-element.73), channel_id=1, source_target_pairs={{0,1},{1,0},{2,3},{3,2},{4,8},{5,9},{6,10},{7,11},{8,4},{9,5},{10,... | collective-permute-start | bytes 147464 | tf_op jit(solution)/shard_map/ppermute | solution.py:628
  25.6 12.6 %collective-permute-start.9 = (bf16[2,256,384]{2,1,0:T(8,128)(2,1)S(1)}, bf16[2,256,384]{2,1,0:T(8,128)(2,1)S(1)}, u32[]{:S(2)}, u32[]{:S(2)}) collective-permute-start(bf16[2,256,384]{2,1,0:T(8,128)(2,1)S(1)} %get-tuple-element.81), channel_id=1, source_target_pairs={{0,2},{1,3},{2,0},{3,1},{4,6},{5,7},{6,4},{7,5},{8,10},{9,11},{10,... | collective-permute-start | bytes 1179656 | tf_op jit(solution)/shard_map/ppermute | solution.py:625
  26.9 6.1 %collective-permute-start.7 = (bf16[128,384]{1,0:T(8,128)(2,1)S(1)}, bf16[128,384]{1,0:T(8,128)(2,1)S(1)}, u32[]{:S(2)}, u32[]{:S(2)}) collective-permute-start(bf16[128,384]{1,0:T(8,128)(2,1)S(1)} %get-tuple-element.78), channel_id=1, source_target_pairs={{0,4},{1,5},{2,6},{3,7},{4,0},{5,1},{6,2},{7,3},{8,12},{9,13},{10,... | collective-permute-start | bytes 294920 | tf_op jit(solution)/shard_map/ppermute | solution.py:628
  28.2 4.8 %collective-permute-start.8 = (bf16[128,384]{1,0:T(8,128)(2,1)S(1)}, bf16[128,384]{1,0:T(8,128)(2,1)S(1)}, u32[]{:S(2)}, u32[]{:S(2)}) collective-permute-start(bf16[128,384]{1,0:T(8,128)(2,1)S(1)} %get-tuple-element.79), channel_id=1, source_target_pairs={{0,1},{1,0},{2,3},{3,2},{4,8},{5,9},{6,10},{7,11},{8,4},{9,5},{10,... | collective-permute-start | bytes 294920 | tf_op jit(solution)/shard_map/ppermute | solution.py:628
  34.7 8.7 %collective-permute-start.10 = (bf16[256,384]{1,0:T(8,128)(2,1)S(1)}, bf16[256,384]{1,0:T(8,128)(2,1)S(1)}, u32[]{:S(2)}, u32[]{:S(2)}) collective-permute-start(bf16[256,384]{1,0:T(8,128)(2,1)S(1)} %get-tuple-element.85), channel_id=1, source_target_pairs={{0,4},{1,5},{2,6},{3,7},{4,0},{5,1},{6,2},{7,3},{8,12},{9,13},{10,... | collective-permute-start | bytes 589832 | tf_op jit(solution)/shard_map/ppermute | solution.py:628
  36.0 7.4 %collective-permute-start.11 = (bf16[256,384]{1,0:T(8,128)(2,1)S(1)}, bf16[256,384]{1,0:T(8,128)(2,1)S(1)}, u32[]{:S(2)}, u32[]{:S(2)}) collective-permute-start(bf16[256,384]{1,0:T(8,128)(2,1)S(1)} %get-tuple-element.86), channel_id=1, source_target_pairs={{0,1},{1,0},{2,3},{3,2},{4,8},{5,9},{6,10},{7,11},{8,4},{9,5},{10,... | collective-permute-start | bytes 589832 | tf_op jit(solution)/shard_map/ppermute | solution.py:628
  37.9 14.4 %collective-permute-start.14 = (bf16[2,256,384]{2,1,0:T(8,128)(2,1)S(1)}, bf16[2,256,384]{2,1,0:T(8,128)(2,1)S(1)}, u32[]{:S(2)}, u32[]{:S(2)}) collective-permute-start(bf16[2,256,384]{2,1,0:T(8,128)(2,1)S(1)} %get-tuple-element.92), channel_id=1, source_target_pairs={{0,2},{1,3},{2,0},{3,1},{4,6},{5,7},{6,4},{7,5},{8,10},{9,11},{10,... | collective-permute-start | bytes 1179656 | tf_op jit(solution)/shard_map/ppermute | solution.py:625
  41.7 6.3 %collective-permute-start.12 = (bf16[256,384]{1,0:T(8,128)(2,1)S(1)}, bf16[256,384]{1,0:T(8,128)(2,1)S(1)}, u32[]{:S(2)}, u32[]{:S(2)}) collective-permute-start(bf16[256,384]{1,0:T(8,128)(2,1)S(1)} %get-tuple-element.89), channel_id=1, source_target_pairs={{0,4},{1,5},{2,6},{3,7},{4,0},{5,1},{6,2},{7,3},{8,12},{9,13},{10,... | collective-permute-start | bytes 589832 | tf_op jit(solution)/shard_map/ppermute | solution.py:628
  41.8 7.4 %collective-permute-start.13 = (bf16[256,384]{1,0:T(8,128)(2,1)S(1)}, bf16[256,384]{1,0:T(8,128)(2,1)S(1)}, u32[]{:S(2)}, u32[]{:S(2)}) collective-permute-start(bf16[256,384]{1,0:T(8,128)(2,1)S(1)} %get-tuple-element.90), channel_id=1, source_target_pairs={{0,1},{1,0},{2,3},{3,2},{4,8},{5,9},{6,10},{7,11},{8,4},{9,5},{10,... | collective-permute-start | bytes 589832 | tf_op jit(solution)/shard_map/ppermute | solution.py:628
  45.4 11.7 %collective-permute-start.15 = (bf16[2,256,384]{2,1,0:T(8,128)(2,1)S(1)}, bf16[2,256,384]{2,1,0:T(8,128)(2,1)S(1)}, u32[]{:S(2)}, u32[]{:S(2)}) collective-permute-start(bf16[2,256,384]{2,1,0:T(8,128)(2,1)S(1)} %get-tuple-element.93), channel_id=1, source_target_pairs={{0,2},{1,3},{2,0},{3,1},{4,6},{5,7},{6,4},{7,5},{8,10},{9,11},{10,... | collective-permute-start | bytes 1179656 | tf_op jit(solution)/shard_map/ppermute | solution.py:625
  46.7 6.0 %collective-permute-start.16 = (bf16[256,384]{1,0:T(8,128)(2,1)S(1)}, bf16[256,384]{1,0:T(8,128)(2,1)S(1)}, u32[]{:S(2)}, u32[]{:S(2)}) collective-permute-start(bf16[256,384]{1,0:T(8,128)(2,1)S(1)} %get-tuple-element.96), channel_id=1, source_target_pairs={{0,4},{1,5},{2,6},{3,7},{4,0},{5,1},{6,2},{7,3},{8,12},{9,13},{10,... | collective-permute-start | bytes 589832 | tf_op jit(solution)/shard_map/ppermute | solution.py:628
  48.0 4.7 %collective-permute-start.17 = (bf16[256,384]{1,0:T(8,128)(2,1)S(1)}, bf16[256,384]{1,0:T(8,128)(2,1)S(1)}, u32[]{:S(2)}, u32[]{:S(2)}) collective-permute-start(bf16[256,384]{1,0:T(8,128)(2,1)S(1)} %get-tuple-element.97), channel_id=1, source_target_pairs={{0,1},{1,0},{2,3},{3,2},{4,8},{5,9},{6,10},{7,11},{8,4},{9,5},{10,... | collective-permute-start | bytes 589832 | tf_op jit(solution)/shard_map/ppermute | solution.py:628
  53.9 10.3 %collective-permute-start.19 = (bf16[256,384]{1,0:T(8,128)(2,1)S(1)}, bf16[256,384]{1,0:T(8,128)(2,1)S(1)}, u32[]{:S(2)}, u32[]{:S(2)}) collective-permute-start(bf16[256,384]{1,0:T(8,128)(2,1)S(1)} %get-tuple-element.107), channel_id=1, source_target_pairs={{0,2},{1,3},{2,0},{3,1},{4,6},{5,7},{6,4},{7,5},{8,10},{9,11},{10,... | collective-permute-start | bytes 589832 | tf_op jit(solution)/shard_map/ppermute | solution.py:625
  55.0 10.6 %collective-permute-start.20 = (bf16[256,384]{1,0:T(8,128)(2,1)S(1)}, bf16[256,384]{1,0:T(8,128)(2,1)S(1)}, u32[]{:S(2)}, u32[]{:S(2)}) collective-permute-start(bf16[256,384]{1,0:T(8,128)(2,1)S(1)} %get-tuple-element.108), channel_id=1, source_target_pairs={{0,3},{1,2},{2,1},{3,0},{4,7},{5,6},{6,5},{7,4},{8,11},{9,10},{10,... | collective-permute-start | bytes 589832 | tf_op jit(solution)/shard_map/ppermute | solution.py:625
  57.2 4.0 %collective-permute-start.18 = (bf16[7,256,384]{2,1,0:T(8,128)(2,1)S(1)}, bf16[7,256,384]{2,1,0:T(8,128)(2,1)S(1)}, u32[]{:S(2)}, u32[]{:S(2)}) collective-permute-start(bf16[7,256,384]{2,1,0:T(8,128)(2,1)S(1)} %shard_map.51), channel_id=1, source_target_pairs={{0,1},{1,0},{2,3},{3,2},{4,5},{5,4},{6,7},{7,6},{8,9},{9,8},{10,11... | collective-permute-start | bytes 4128776 | tf_op jit(solution)/shard_map/ppermute | solution.py:625

commit v7 on v6

--- a/solution.py
+++ b/solution.py
@@ -230,25 +230,37 @@
         h_ref[pl.ds(at, reach)] = jnp.zeros((reach, h_ref.shape[1]), BF16)
 
 
-def early_taps_kernel(r, s_ref, own, beside, w, point, x, low, mid, high, x_ref, hidden):
+def early_taps_kernel(
+    r, s_ref, own, beside, w, point, signal, x, low, mid, high, x_ref, hidden, xs_ref, sems
+):
     q = s_ref[0]
+    reads = start_all(
+        [
+            pltpu.make_async_copy(signal.at[:, q ^ k], xs_ref.at[k - 1], sems.at[k])
+            for k in range(1, GROUP)
+        ]
+    )
     rows = own.shape[0]
     starts = [pl.multiple_of((q ^ k) * rows, rows) for k in range(2)]
     piece_taps(starts, r, (own[...], beside[...]), w, x, low, mid, high)
     half = jnp.where(q < GROUP // 2, 0, GROUP // 2) * rows
     start = pl.multiple_of(half + r, r)
     first_finish((start,), (2 * rows - 2 * r,), r, point, x, low, mid, high, x_ref, hidden)
-
-
-def early_taps(scalars, own, beside, w, point, r):
+    wait_all(reads)
+
+
+def early_taps(scalars, own, beside, w, point, signal):
     c, h = w.shape[1], w.shape[2] // 3
     rows = own.shape[0]
     length = GROUP * rows
+    places, _, r, _ = signal.shape
+    signal = pltpu.with_memory_space_constraint(signal, pltpu.HBM)
     outs = (array(length, c), array(length + r, h), array(length, h, dtype=F32))
     outs += (array(length + r, h), array(length, c), array(length, h))
-    return call(
-        functools.partial(early_taps_kernel, r), outs, (scalars, own, beside, w, point),
-        [SMEM] + [VMEM] * 4, (VMEM,) * 6, [],
+    outs += (array(GROUP - 1, places, r, c),)
+    return call(
+        functools.partial(early_taps_kernel, r), outs, (scalars, own, beside, w, point, signal),
+        [SMEM] + [VMEM] * 4 + [HBM], (VMEM,) * 7, [pltpu.SemaphoreType.DMA((GROUP,))],
         12 * rows * c * h, 2**20,
     )
 
@@ -411,16 +423,51 @@
     )
 
 
+def edge_hidden_kernel(reach, s_ref, hidden, part, from_even, from_odd, far_ref, ends_ref):
+    below, above = arrived(s_ref, from_even, from_odd, 0, reach)
+    edges = (
+        gelu(part[pl.ds(0, reach)] + below).astype(BF16),
+        gelu(part[pl.ds(reach, reach)] + above).astype(BF16),
+    )
+    ends_ref[0] = edges[0]
+    ends_ref[1] = edges[1]
+    give_back(s_ref[0], hidden, reach, edges, (far_ref.at[0], far_ref.at[1]), 2)
+
+
+def edge_hidden(scalars, hidden, part, terms, reach):
+    length, h = hidden.shape
+    outs = (array(2, length // GROUP, h), array(2, reach, h))
+    return call(
+        functools.partial(edge_hidden_kernel, reach), outs, (scalars, hidden, part, *terms),
+        [SMEM] + [VMEM] * 4, (VMEM,) * 2, [], 40 * reach * h, 2**20,
+    )
+
+
+def edge_terms_kernel(block, reach, s_ref, x, ends, w, point, x_ref, even_ref, odd_ref):
+    length = x.shape[0]
+    h = ends.shape[2]
+    more = dot(ends[...].reshape(2 * reach, h), point[block])
+    for i, at in enumerate((0, length - reach)):
+        new = x[pl.ds(at, reach)].astype(F32) + more[i * reach : (i + 1) * reach]
+        x_ref[pl.ds(at, reach)] = new.astype(BF16)
+    up = dot(x_ref[pl.ds(length - reach, reach)], w[block + 1, :, :h])
+    down = dot(x_ref[pl.ds(0, reach)], w[block + 1, :, 2 * h :])
+    place_terms(s_ref[1], up, down, even_ref, odd_ref, 0, reach)
+
+
+def edge_terms(block, scalars, x, ends, w, point, reach):
+    c, h = w.shape[1], w.shape[2] // 3
+    outs = (array(*x.shape), array(reach, h), array(reach, h))
+    return call(
+        functools.partial(edge_terms_kernel, block, reach), outs, (scalars, x, ends, w, point),
+        [SMEM] + [VMEM] * 4, (VMEM,) * 3, [], 8 * c * h * reach, 2 * 2**20, {1: 0},
+    )
+
+
 def near_kernel(
-    reach, s_ref, x, hidden, ends, from_even, from_odd, w, signal, h_ref, near_ref, core_ref, xs_ref, other, sems
+    reach, s_ref, x, hidden, ends, from_even, from_odd, w, h_ref, near_ref, core_ref, other
 ):
     length = x.shape[0]
-    reads = start_all(
-        [
-            pltpu.make_async_copy(signal.at[:, s_ref[0] ^ k], xs_ref.at[k - 1], sems.at[k])
-            for k in range(1, GROUP)
-        ]
-    )
     half = length // 2
     h = near_ref.shape[1]
     block = w.shape[0] - 1
@@ -437,21 +484,17 @@
     near_ref[pl.ds(0, reach)] = lower[reach:]
     near_ref[pl.ds(reach, reach)] = upper[:reach]
     give_back(s_ref[0], hidden, reach, (ends[0], ends[1]), (core_ref,), 1)
-    wait_all(reads)
-
-
-def near_terms(scalars, x, hidden, ends, terms, w, signal, reach):
+
+
+def near_terms(scalars, x, hidden, ends, terms, w, reach, after):
     c, h = w.shape[1], w.shape[2] // 3
     rows = x.shape[0] // GROUP
     half = x.shape[0] // 2
-    scratch = [pltpu.VMEM((half, h), BF16), pltpu.SemaphoreType.DMA((GROUP,))]
+    scratch = [pltpu.VMEM((half, h), BF16)]
     outs = (array(2, reach, h), array(half, h, dtype=F32), array(rows, h))
-    places, _, r, _ = signal.shape
-    outs += (array(GROUP - 1, places, r, c),)
-    signal = pltpu.with_memory_space_constraint(signal, pltpu.HBM)
-    return call(
-        functools.partial(near_kernel, reach), outs, (scalars, x, hidden, ends, *terms, w, signal),
-        [SMEM] + [VMEM] * 6 + [HBM], (VMEM,) * 4, scratch, NEAR_WORK, 4 * 2**20,
+    return call(
+        functools.partial(near_kernel, reach), outs, (scalars, x, hidden, ends, *terms, w),
+        [SMEM] + [VMEM] * 6, (VMEM,) * 3, scratch, NEAR_WORK, 4 * 2**20, after=after,
     )
 
 
@@ -630,7 +673,7 @@
     mine, beside, over, last, rest = split(scalars, x)
     over, rest, last, beside = swap(over, 2), swap(rest, 3), swap(last, 2), swap(beside, 1)
     w = side_by_side(taps)
-    early, ready = early_taps(scalars, mine, beside, w, point, r), ()
+    *early, xs = early_taps(scalars, mine, beside, w, point, x)
     early, ready = early[:4], early[4:]
     edge = swap(edge_part(over, r, early[:1]), 1)
     pieces = (mine, beside, over, edge)
@@ -651,15 +694,16 @@
     reach = 4 * r
     current, hidden, part, *inner = middle_block(2, scalars, current, w, point, reach, far[:1])
     inner = across(*inner)
-    current, even, odd, over, ends = finish_edges(
-        2, scalars, current, hidden, part, terms, w, point, reach, reach
-    )
+    over, ends = edge_hidden(scalars, hidden, part, terms, reach)
+    current, even, odd = edge_terms(2, scalars, current, ends, w, point, reach)
     terms = across(even, odd)
     own.append(current)
     far.append(swap(over, 2))
-    outer, near, beside, xs = near_terms(scalars, current, hidden, ends, inner, w, x, reach)
+    outer, near, beside = near_terms(
+        scalars, current, hidden, ends, inner, w, reach, far[1:2]
+    )
     core.append(beside)
-    hidden = last_hidden(scalars, outer, near, terms, far[1:2])
+    hidden = last_hidden(scalars, outer, near, terms, ())
     lasts = [swap(hidden[k], k) for k in (2, 3)]
     beside = swap(forward([*core, hidden[1]], far), 1)
     out, x2 = chip_outputs(scalars, xs, own, far, hidden[0], point)

time: 67.8 us -> 67.6 us (level)
  Pallas kernels: 35 us -> 35.7 us
    ppermute x11, starting transfers between devices: 12.6 us -> 11.7 us  [swap(): return lax.ppermute(value, 'seq', [(i, i ^ k) for i in range(size)])]
    pallas_call x17 -> x18, Pallas kernels: 35 us -> 35.7 us  [call(): pl.pallas_call(kernel, out_shape=outs, in_specs=specs, out_specs=out_spec...]
  transfers between devices with their start and end apart: 21 -> 21, of which waited for: 7 -> 6; matrix products, arithmetic and copies ran while one was open for 0% -> 0% of each run, Pallas kernels for 42% -> 43%
where the time goes in v7:
time: 67.6 us; the launch traced here: 67.5 us
  Pallas kernels  35.7 us (53%)
  starting transfers between devices  23.8 us (35%)
  waiting for transfers between devices  7.09 us (10%)
    pallas_call x18, Pallas kernels, call(): pl.pallas_call(kernel, out_shape=outs, in_specs=specs, out_specs=out_spec...  35.7 us
    ppermute x11, starting transfers between devices, swap(): return lax.ppermute(value, 'seq', [(i, i ^ k) for i in range(size)])  11.7 us
    ppermute x5, starting transfers between devices, across(): lax.ppermute(odd, 'seq', odd_pairs)  7.2 us
    ppermute x11, waiting for transfers between devices, swap(): return lax.ppermute(value, 'seq', [(i, i ^ k) for i in range(size)])  6.13 us
    ppermute x5, starting transfers between devices, across(): lax.ppermute(even, 'seq', even_pairs)  4.89 us
  transfers between devices with their start and end apart: 21, of which 6 were waited for; matrix products, arithmetic and copies ran while one was open for 0% of the time, Pallas kernels for 43%

profile of v7, /device:TPU:1, one launch (start us, length us, event | category | flops | bytes accessed | tf_op | source)
XLA Modules:
  0.0 67.5 jit_solution(16649910597152197383)
XLA Ops:
  0.1 2.0 %shard_map.37 = (bf16[4,64,768]{2,1,0:T(8,128)(2,1)S(1)}, bf16[4,64,768]{2,1,0:T(8,128)(2,1)S(1)}, bf16[4,64,768]{2,1,0:T(8,128)(2,1)S(1)}, bf16[1,64,768]{2,1,0:T(8,128)(2,1)S(1)}, bf16[3,64,768]{2,1,0:T(8,128)(2,1)S(1)}) custom-call(s32[4]{0:T(128)S(1)} %pad_add_fusion.s_ref.parity_ref.refs_0_, bf16[4,4,64,768]{3,2,1,0:T(8,128)(2,1)} %bitcast.23), custom_call_target="tpu_custom_call" | custom-call | bytes 3145728 | tf_op jit(solution)/shard_map/pallas_call | solution.py:55
  2.2 2.7 %collective-permute-start.3 = (bf16[256,768]{1,0:T(8,128)(2,1)S(1)}, bf16[256,768]{1,0:T(8,128)(2,1)S(1)}, u32[]{:S(2)}, u32[]{:S(2)}) collective-permute-start(bf16[256,768]{1,0:T(8,128)(2,1)S(1)} %bitcast.19), channel_id=1, source_target_pairs={{0,2},{1,3},{2,0},{3,1},{4,6},{5,7},{6,4},{7,5},{8,10},{9,11},{10,... | collective-permute-start | bytes 1179656 | tf_op jit(solution)/shard_map/ppermute | solution.py:668
  4.9 3.3 %shard_map.38.w.refs_2_.refs_6_ = bf16[4,768,1152]{2,1,0:T(8,128)(2,1)S(1)} custom-call(bf16[4,3,768,384]{3,2,1,0:T(8,128)(2,1)} %taps.1), custom_call_target="tpu_custom_call" | custom-call | bytes 14155776 | tf_op jit(solution)/shard_map/pallas_call | solution.py:55
  8.7 3.5 %shard_map.39 = (bf16[1024,768]{1,0:T(8,128)(2,1)S(1)}, bf16[1088,384]{1,0:T(8,128)(2,1)S(1)}, f32[1024,384]{1,0:T(8,128)S(1)}, bf16[1088,384]{1,0:T(8,128)(2,1)...) custom-call(s32[4]{0:T(128)S(1)} %pad_add_fusion.s_ref.parity_ref.refs_0_, ...), custom_call_target="tpu_custom_call" | custom-call | flops 905969664 | bytes 1048576 | tf_op jit(solution)/shard_map/pallas_call | solution.py:55
  12.2 2.1 %collective-permute-done.3.refs_0_.over = bf16[256,768]{1,0:T(8,128)(2,1)S(1)} collective-permute-done((bf16[256,768]{1,0:T(8,128)(2,1)S(1)}, bf16[256,768]{1,0:T(8,128)(2,1)S(1)}, u32[]{:S(2)}, u32[]{:S(2)}) %collective-permute-start.3) | collective-permute-done | bytes 393248 | tf_op jit(solution)/shard_map/ppermute | solution.py:668
  14.3 1.0 %collective-permute-start.4 = (bf16[64,768]{1,0:T(8,128)(2,1)S(1)}, bf16[64,768]{1,0:T(8,128)(2,1)S(1)}, u32[]{:S(2)}, u32[]{:S(2)}) collective-permute-start(bf16[64,768]{1,0:T(8,128)(2,1)S(1)} %shard_map.40), channel_id=1, source_target_pairs={{0,1},{1,0},{2,3},{3,2},{4,5},{5,4},{6,7},{7,6},{8,9},{9,8},{10,11... | collective-permute-start | bytes 294920 | tf_op jit(solution)/shard_map/ppermute | solution.py:668
  15.3 1.7 %collective-permute-start.2 = (bf16[64,768]{1,0:T(8,128)(2,1)S(1)}, bf16[64,768]{1,0:T(8,128)(2,1)S(1)}, u32[]{:S(2)}, u32[]{:S(2)}) collective-permute-start(bf16[64,768]{1,0:T(8,128)(2,1)S(1)} %bitcast.22), channel_id=1, source_target_pairs={{0,2},{1,3},{2,0},{3,1},{4,6},{5,7},{6,4},{7,5},{8,10},{9,11},{10,... | collective-permute-start | bytes 294920 | tf_op jit(solution)/shard_map/ppermute | solution.py:668
  17.8 1.4 %collective-permute-start.5 = (bf16[64,384]{1,0:T(8,128)(2,1)S(1)}, bf16[64,384]{1,0:T(8,128)(2,1)S(1)}, u32[]{:S(2)}, u32[]{:S(2)}) collective-permute-start(bf16[64,384]{1,0:T(8,128)(2,1)S(1)} %get-tuple-element.73), channel_id=1, source_target_pairs={{0,4},{1,5},{2,6},{3,7},{4,0},{5,1},{6,2},{7,3},{8,12},{9,13},{10,... | collective-permute-start | bytes 147464 | tf_op jit(solution)/shard_map/ppermute | solution.py:671
  19.8 1.2 %shard_map.41 = (bf16[1024,768]{1,0:T(8,128)(2,1)S(1)}, bf16[1088,384]{1,0:T(8,128)(2,1)S(1)}, f32[1024,384]{1,0:T(8,128)S(1)}, bf16[1088,384]{1,0:T(8,128)(2,1)S(1)}) custom-call(s32[4]{0:T(128)S(1)} %pad_add_fusion.s_ref.parity_ref.refs_0_, ...), custom_call_target="tpu_custom_call", output_to_operand_aliasing={{0}: (4, {}), {1}: (5, {}), {2}: (6, {}), {3}: (7, {})} | custom-call | flops 452984832 | bytes 1048576 | tf_op jit(solution)/shard_map/pallas_call | solution.py:55
  21.1 1.6 %collective-permute-done.2.last = bf16[64,768]{1,0:T(8,128)(2,1)S(1)} collective-permute-done((bf16[64,768]{1,0:T(8,128)(2,1)S(1)}, bf16[64,768]{1,0:T(8,128)(2,1)S(1)}, u32[]{:S(2)}, u32[]{:S(2)}) %collective-permute-start.2) | collective-permute-done | bytes 98336 | tf_op jit(solution)/shard_map/ppermute | solution.py:668
  22.7 2.9 %shard_map.43 = (bf16[128,384]{1,0:T(8,128)(2,1)S(1)}, bf16[128,384]{1,0:T(8,128)(2,1)S(1)}, bf16[2,256,384]{2,1,0:T(8,128)(2,1)S(1)}, bf16[256,384]{1,0:T(8,128...) custom-call(s32[4]{0:T(128)S(1)} %pad_add_fusion.s_ref.parity_ref.re, ...), custom_call_target="tpu_custom_call", output_to_operand_aliasing={{4}: (3, {}), {5}: (4, {}), {6}: (5, {}), {7}: (6, {}), {8}... | custom-call | flops 2415919104 | bytes 4194304 | tf_op jit(solution)/shard_map/pallas_call | solution.py:55
  25.6 1.3 %collective-permute-start.9 = (bf16[2,256,384]{2,1,0:T(8,128)(2,1)S(1)}, bf16[2,256,384]{2,1,0:T(8,128)(2,1)S(1)}, u32[]{:S(2)}, u32[]{:S(2)}) collective-permute-start(bf16[2,256,384]{2,1,0:T(8,128)(2,1)S(1)} %get-tuple-element.82), channel_id=1, source_target_pairs={{0,2},{1,3},{2,0},{3,1},{4,6},{5,7},{6,4},{7,5},{8,10},{9,11},{10,... | collective-permute-start | bytes 1179656 | tf_op jit(solution)/shard_map/ppermute | solution.py:668
  26.9 1.3 %collective-permute-start.7 = (bf16[128,384]{1,0:T(8,128)(2,1)S(1)}, bf16[128,384]{1,0:T(8,128)(2,1)S(1)}, u32[]{:S(2)}, u32[]{:S(2)}) collective-permute-start(bf16[128,384]{1,0:T(8,128)(2,1)S(1)} %get-tuple-element.79), channel_id=1, source_target_pairs={{0,4},{1,5},{2,6},{3,7},{4,0},{5,1},{6,2},{7,3},{8,12},{9,13},{10,... | collective-permute-start | bytes 294920 | tf_op jit(solution)/shard_map/ppermute | solution.py:671
  28.2 1.4 %collective-permute-start.8 = (bf16[128,384]{1,0:T(8,128)(2,1)S(1)}, bf16[128,384]{1,0:T(8,128)(2,1)S(1)}, u32[]{:S(2)}, u32[]{:S(2)}) collective-permute-start(bf16[128,384]{1,0:T(8,128)(2,1)S(1)} %get-tuple-element.80), channel_id=1, source_target_pairs={{0,1},{1,0},{2,3},{3,2},{4,8},{5,9},{6,10},{7,11},{8,4},{9,5},{10,... | collective-permute-start | bytes 294920 | tf_op jit(solution)/shard_map/ppermute | solution.py:671
  29.6 3.3 %shard_map.44 = (bf16[1024,768]{1,0:T(8,128)(2,1)S(1)}, bf16[1024,384]{1,0:T(8,128)(2,1)S(1)}, f32[256,384]{1,0:T(8,128)S(1)}) custom-call(s32[4]{0:T(128)S(1)} %pad_add_fusion.s_ref.parity_ref.refs_0_, bf16[1024,768]{1,0:T(8,128)(2,1)S(1)} %get-tuple-element.75.x, bf16[4,768,1152]{2,1,0:T(8,128)(2,1)S(1)} %shard_map.38.w.refs_2_.refs_6_, ...), custom_call_target="tpu_custom_call" | custom-call | flops 2415919104 | bytes 4194304 | tf_op jit(solution)/shard_map/pallas_call | solution.py:55
  33.0 1.5 %shard_map.45 = (bf16[1024,768]{1,0:T(8,128)(2,1)S(1)}, bf16[256,384]{1,0:T(8,128)(2,1)S(1)}, bf16[256,384]{1,0:T(8,128)(2,1)S(1)}, bf16[2,256,384]{2,1,0:T(8,128)(2,1)S(1)}, bf16[256,384]{1,0:T(8,128)(2,1)S(1)}) custom-call(s32[4]{0:T(128)S(1)} %pad_add_fusion.s_ref.parity_ref.refs_0_, ...), custom_call_target="tpu_custom_call", output_to_operand_aliasing={{0}: (1, {})} | custom-call | flops 452984832 | bytes 4194304 | tf_op jit(solution)/shard_map/pallas_call | solution.py:55
  34.5 1.3 %collective-permute-start.10 = (bf16[256,384]{1,0:T(8,128)(2,1)S(1)}, bf16[256,384]{1,0:T(8,128)(2,1)S(1)}, u32[]{:S(2)}, u32[]{:S(2)}) collective-permute-start(bf16[256,384]{1,0:T(8,128)(2,1)S(1)} %get-tuple-element.86), channel_id=1, source_target_pairs={{0,4},{1,5},{2,6},{3,7},{4,0},{5,1},{6,2},{7,3},{8,12},{9,13},{10,... | collective-permute-start | bytes 589832 | tf_op jit(solution)/shard_map/ppermute | solution.py:671
  35.8 2.0 %collective-permute-start.11 = (bf16[256,384]{1,0:T(8,128)(2,1)S(1)}, bf16[256,384]{1,0:T(8,128)(2,1)S(1)}, u32[]{:S(2)}, u32[]{:S(2)}) collective-permute-start(bf16[256,384]{1,0:T(8,128)(2,1)S(1)} %get-tuple-element.87), channel_id=1, source_target_pairs={{0,1},{1,0},{2,3},{3,2},{4,8},{5,9},{6,10},{7,11},{8,4},{9,5},{10,... | collective-permute-start | bytes 589832 | tf_op jit(solution)/shard_map/ppermute | solution.py:671
  38.0 3.6 %shard_map.46 = (bf16[1024,768]{1,0:T(8,128)(2,1)S(1)}, bf16[1024,384]{1,0:T(8,128)(2,1)S(1)}, f32[512,384]{1,0:T(8,128)S(1)}, bf16[256,384]{1,0:T(8,128)(2,1)S(1)}, bf16[256,384]{1,0:T(8,128)(2,1)S(1)}) custom-call(s32[4]{0:T(128)S(1)} %pad_add_fusion.s_ref.parity_ref.refs_0_, bf16[1024,768]{1,0:T(8,128)(2,1)S(1)} %get-tuple-element.81.refs_1_, ...), custom_call_target="tpu_custom_call" | custom-call | flops 2415919104 | bytes 4194304 | tf_op jit(solution)/shard_map/pallas_call | solution.py:55
  41.6 1.6 %collective-permute-start.15 = (bf16[256,384]{1,0:T(8,128)(2,1)S(1)}, bf16[256,384]{1,0:T(8,128)(2,1)S(1)}, u32[]{:S(2)}, u32[]{:S(2)}) collective-permute-start(bf16[256,384]{1,0:T(8,128)(2,1)S(1)} %get-tuple-element.93), channel_id=1, source_target_pairs={{0,1},{1,0},{2,3},{3,2},{4,8},{5,9},{6,10},{7,11},{8,4},{9,5},{10,... | collective-permute-start | bytes 589832 | tf_op jit(solution)/shard_map/ppermute | solution.py:671
  43.2 1.1 %shard_map.47 = (bf16[2,256,384]{2,1,0:T(8,128)(2,1)S(1)}, bf16[2,256,384]{2,1,0:T(8,128)(2,1)S(1)}) custom-call(s32[4]{0:T(128)S(1)} %pad_add_fusion.s_ref.parity_ref.refs_0_, bf16[1024,384]{1,0:T(8,128)(2,1)S(1)} %get-tuple-element.84.hidden.refs_2_, f32[512,384]{1,0:T(8,128)S(1)} %get-tuple-element.85.part, ...), custom_call_target="tpu_custom_call" | custom-call | flops 3932160 | bytes 1048576 | tf_op jit(solution)/shard_map/pallas_call | solution.py:55
  44.4 1.3 %collective-permute-start.13 = (bf16[2,256,384]{2,1,0:T(8,128)(2,1)S(1)}, bf16[2,256,384]{2,1,0:T(8,128)(2,1)S(1)}, u32[]{:S(2)}, u32[]{:S(2)}) collective-permute-start(bf16[2,256,384]{2,1,0:T(8,128)(2,1)S(1)} %get-tuple-element.91), channel_id=1, source_target_pairs={{0,2},{1,3},{2,0},{3,1},{4,6},{5,7},{6,4},{7,5},{8,10},{9,11},{10,... | collective-permute-start | bytes 1179656 | tf_op jit(solution)/shard_map/ppermute | solution.py:668
  45.7 1.7 %shard_map.48 = (bf16[1024,768]{1,0:T(8,128)(2,1)S(1)}, bf16[256,384]{1,0:T(8,128)(2,1)S(1)}, bf16[256,384]{1,0:T(8,128)(2,1)S(1)}) custom-call(s32[4]{0:T(128)S(1)} %pad_add_fusion.s_ref.parity_ref.refs_0_, bf16[1024,768]{1,0:T(8,128)(2,1)S(1)} %get-tuple-element.83.x, ...), custom_call_target="tpu_custom_call", output_to_operand_aliasing={{0}: (1, {})} | custom-call | flops 603979776 | bytes 2097152 | tf_op jit(solution)/shard_map/pallas_call | solution.py:55
  48.5 1.6 %collective-permute-start.17 = (bf16[256,384]{1,0:T(8,128)(2,1)S(1)}, bf16[256,384]{1,0:T(8,128)(2,1)S(1)}, u32[]{:S(2)}, u32[]{:S(2)}) collective-permute-start(bf16[256,384]{1,0:T(8,128)(2,1)S(1)} %get-tuple-element.97), channel_id=1, source_target_pairs={{0,1},{1,0},{2,3},{3,2},{4,8},{5,9},{6,10},{7,11},{8,4},{9,5},{10,... | collective-permute-start | bytes 589832 | tf_op jit(solution)/shard_map/ppermute | solution.py:671
  50.1 2.2 %shard_map.49 = (bf16[2,256,384]{2,1,0:T(8,128)(2,1)S(1)}, f32[512,384]{1,0:T(8,128)S(1)}, bf16[256,384]{1,0:T(8,128)(2,1)S(1)}) custom-call(s32[4]{0:T(128)S(1)} %pad_add_fusion.s_ref.parity_ref.refs_0_, bf16[1024,768]{1,0:T(8,128)(2,1)S(1)} %get-tuple-element.89.refs_1_, bf16[1024,384]{1,0:T(8,128)(2,1)S(1)} %get-tuple-element.84.hidden.refs_2_, ...), custom_call_target="tpu_custom_call" | custom-call | flops 2400000000 | bytes 4194304 | tf_op jit(solution)/shard_map/pallas_call | solution.py:55
  52.4 0.9 %collective-permute-done.16.from_even = bf16[256,384]{1,0:T(8,128)(2,1)S(1)} collective-permute-done((bf16[256,384]{1,0:T(8,128)(2,1)S(1)}, bf16[256,384]{1,0:T(8,128)(2,1)S(1)}, u32[]{:S(2)}, u32[]{:S(2)}) %collective-permute-start.16) | collective-permute-done | bytes 196640 | tf_op jit(solution)/shard_map/ppermute | solution.py:671
  53.3 1.2 %shard_map.50 = (bf16[256,384]{1,0:T(8,128)(2,1)S(1)}, bf16[256,384]{1,0:T(8,128)(2,1)S(1)}, bf16[256,384]{1,0:T(8,128)(2,1)S(1)}, bf16[256,384]{1,0:T(8,128)(2,1)S(1)}) custom-call(s32[4]{0:T(128)S(1)} %pad_add_fusion.s_ref.parity_ref.refs_0_, bf16[2,256,384]{2,1,0:T(8,128)(2,1)S(1)} %get-tuple-element.94.outer, f32[512,384]{1,0:T(8,128)S(1)} %get-tuple-element.95.near, ...), custom_call_target="tpu_custom_call" | custom-call | flops 3932160 | bytes 2097152 | tf_op jit(solution)/shard_map/pallas_call | solution.py:55
  54.8 2.9 %collective-permute-start.20 = (bf16[256,384]{1,0:T(8,128)(2,1)S(1)}, bf16[256,384]{1,0:T(8,128)(2,1)S(1)}, u32[]{:S(2)}, u32[]{:S(2)}) collective-permute-start(bf16[256,384]{1,0:T(8,128)(2,1)S(1)} %get-tuple-element.108), channel_id=1, source_target_pairs={{0,3},{1,2},{2,1},{3,0},{4,7},{5,6},{6,5},{7,4},{8,11},{9,10},{10,... | collective-permute-start | bytes 589832 | tf_op jit(solution)/shard_map/ppermute | solution.py:668
  57.9 2.4 %shard_map.51 = (bf16[4,4,4,64,768]{4,3,2,1,0:T(8,128)(2,1)}, bf16[256,768]{1,0:T(8,128)(2,1)S(1)}) custom-call(s32[4]{0:T(128)S(1)} %pad_add_fusion.s_ref.parity_ref.refs_0_, bf16[3,4,64,768]{3,2,1,0:T(8,128)(2,1)S(1)} %get-tuple-element.59.x, bf16[16,64,768]{2,1,0:T(8,128)(2,1)S(1)} %bitcast.14, bf16[16,64,768]{2,1,0:T(8,128)(2,1)S(1)} %bitcast.15, ...), custom_call_target="tpu_custom_call" | custom-call | flops 49999998976 | bytes 8388608 | tf_op jit(solution)/shard_map/pallas_call | solution.py:55
  61.0 3.0 %shard_map.53 = (bf16[4,4,4,64,768]{4,3,2,1,0:T(8,128)(2,1)}, bf16[256,768]{1,0:T(8,128)(2,1)S(1)}) custom-call(s32[4]{0:T(128)S(1)} %pad_add_fusion.s_ref.parity_ref.refs_0_, bf16[3,4,64,768]{3,2,1,0:T(8,128)(2,1)S(1)} %get-tuple-element.59.x, bf16[7,256,384]{2,1,0:T(8,128)(2,1)S(1)} %collective-permute-done.18.core, ...), custom_call_target="tpu_custom_call", output_to_operand_aliasing={{0}: (4, {})} | custom-call | flops 905969664 | bytes 4194304 | tf_op jit(solution)/shard_map/pallas_call | solution.py:55
  64.0 1.5 %collective-permute-done.20.a3 = bf16[256,384]{1,0:T(8,128)(2,1)S(1)} collective-permute-done((bf16[256,384]{1,0:T(8,128)(2,1)S(1)}, bf16[256,384]{1,0:T(8,128)(2,1)S(1)}, u32[]{:S(2)}, u32[]{:S(2)}) %collective-permute-start.20) | collective-permute-done | bytes 196640 | tf_op jit(solution)/shard_map/ppermute | solution.py:668
  65.4 1.9 %shard_map.54 = bf16[4,4,4,64,768]{4,3,2,1,0:T(8,128)(2,1)} custom-call(s32[4]{0:T(128)S(1)} %pad_add_fusion.s_ref.parity_ref.refs_0_, bf16[256,768]{1,0:T(8,128)(2,1)S(1)} %get-tuple-element.99.x2, bf16[256,768]{1,0:T(8,128)(2,1)S(1)} %get-tuple-element.105.x3, bf16[4,384,768]{2,1,0:T(8,128)(2,1)S(1)} %copy-done, ...), custom_call_target="tpu_custom_call", output_to_operand_aliasing={{}: (4, {})} | custom-call | flops 301989888 | bytes 2097152 | tf_op jit(solution)/shard_map/pallas_call | solution.py:55
  (31 shorter events, 5.0 us)
Async XLA Ops:
  2.1 6.1 %collective-permute-start = (bf16[256,768]{1,0:T(8,128)(2,1)S(1)}, bf16[256,768]{1,0:T(8,128)(2,1)S(1)}, u32[]{:S(2)}, u32[]{:S(2)}) collective-permute-start(bf16[256,768]{1,0:T(8,128)(2,1)S(1)} %bitcast.20), channel_id=1, source_target_pairs={{0,1},{1,0},{2,3},{3,2},{4,5},{5,4},{6,7},{7,6},{8,9},{9,8},{10,11... | collective-permute-start | bytes 1179656 | tf_op jit(solution)/shard_map/ppermute | solution.py:668
  2.2 12.1 %collective-permute-start.3 = (bf16[256,768]{1,0:T(8,128)(2,1)S(1)}, bf16[256,768]{1,0:T(8,128)(2,1)S(1)}, u32[]{:S(2)}, u32[]{:S(2)}) collective-permute-start(bf16[256,768]{1,0:T(8,128)(2,1)S(1)} %bitcast.19), channel_id=1, source_target_pairs={{0,2},{1,3},{2,0},{3,1},{4,6},{5,7},{6,4},{7,5},{8,10},{9,11},{10,... | collective-permute-start | bytes 1179656 | tf_op jit(solution)/shard_map/ppermute | solution.py:668
  4.9 17.8 %collective-permute-start.1 = (bf16[192,768]{1,0:T(8,128)(2,1)S(1)}, bf16[192,768]{1,0:T(8,128)(2,1)S(1)}, u32[]{:S(2)}, u32[]{:S(2)}) collective-permute-start(bf16[192,768]{1,0:T(8,128)(2,1)S(1)} %bitcast.21), channel_id=1, source_target_pairs={{0,3},{1,2},{2,1},{3,0},{4,7},{5,6},{6,5},{7,4},{8,11},{9,10},{10,... | collective-permute-start | bytes 884744 | tf_op jit(solution)/shard_map/ppermute | solution.py:668
  4.9 3.8 %copy-start = (bf16[4,384,768]{2,1,0:T(8,128)(2,1)S(1)}, bf16[4,384,768]{2,1,0:T(8,128)(2,1)}, u32[]{:S(2)}) copy-start(bf16[4,384,768]{2,1,0:T(8,128)(2,1)} %point.13) | copy-start | bytes 7077892
  14.3 2.7 %collective-permute-start.4 = (bf16[64,768]{1,0:T(8,128)(2,1)S(1)}, bf16[64,768]{1,0:T(8,128)(2,1)S(1)}, u32[]{:S(2)}, u32[]{:S(2)}) collective-permute-start(bf16[64,768]{1,0:T(8,128)(2,1)S(1)} %shard_map.40), channel_id=1, source_target_pairs={{0,1},{1,0},{2,3},{3,2},{4,5},{5,4},{6,7},{7,6},{8,9},{9,8},{10,11... | collective-permute-start | bytes 294920 | tf_op jit(solution)/shard_map/ppermute | solution.py:668
  15.3 7.4 %collective-permute-start.2 = (bf16[64,768]{1,0:T(8,128)(2,1)S(1)}, bf16[64,768]{1,0:T(8,128)(2,1)S(1)}, u32[]{:S(2)}, u32[]{:S(2)}) collective-permute-start(bf16[64,768]{1,0:T(8,128)(2,1)S(1)} %bitcast.22), channel_id=1, source_target_pairs={{0,2},{1,3},{2,0},{3,1},{4,6},{5,7},{6,4},{7,5},{8,10},{9,11},{10,... | collective-permute-start | bytes 294920 | tf_op jit(solution)/shard_map/ppermute | solution.py:668
  17.8 4.9 %collective-permute-start.5 = (bf16[64,384]{1,0:T(8,128)(2,1)S(1)}, bf16[64,384]{1,0:T(8,128)(2,1)S(1)}, u32[]{:S(2)}, u32[]{:S(2)}) collective-permute-start(bf16[64,384]{1,0:T(8,128)(2,1)S(1)} %get-tuple-element.73), channel_id=1, source_target_pairs={{0,4},{1,5},{2,6},{3,7},{4,0},{5,1},{6,2},{7,3},{8,12},{9,13},{10,... | collective-permute-start | bytes 147464 | tf_op jit(solution)/shard_map/ppermute | solution.py:671
  19.2 3.5 %collective-permute-start.6 = (bf16[64,384]{1,0:T(8,128)(2,1)S(1)}, bf16[64,384]{1,0:T(8,128)(2,1)S(1)}, u32[]{:S(2)}, u32[]{:S(2)}) collective-permute-start(bf16[64,384]{1,0:T(8,128)(2,1)S(1)} %get-tuple-element.74), channel_id=1, source_target_pairs={{0,1},{1,0},{2,3},{3,2},{4,8},{5,9},{6,10},{7,11},{8,4},{9,5},{10,... | collective-permute-start | bytes 147464 | tf_op jit(solution)/shard_map/ppermute | solution.py:671
  25.6 12.4 %collective-permute-start.9 = (bf16[2,256,384]{2,1,0:T(8,128)(2,1)S(1)}, bf16[2,256,384]{2,1,0:T(8,128)(2,1)S(1)}, u32[]{:S(2)}, u32[]{:S(2)}) collective-permute-start(bf16[2,256,384]{2,1,0:T(8,128)(2,1)S(1)} %get-tuple-element.82), channel_id=1, source_target_pairs={{0,2},{1,3},{2,0},{3,1},{4,6},{5,7},{6,4},{7,5},{8,10},{9,11},{10,... | collective-permute-start | bytes 1179656 | tf_op jit(solution)/shard_map/ppermute | solution.py:668
  26.9 6.1 %collective-permute-start.7 = (bf16[128,384]{1,0:T(8,128)(2,1)S(1)}, bf16[128,384]{1,0:T(8,128)(2,1)S(1)}, u32[]{:S(2)}, u32[]{:S(2)}) collective-permute-start(bf16[128,384]{1,0:T(8,128)(2,1)S(1)} %get-tuple-element.79), channel_id=1, source_target_pairs={{0,4},{1,5},{2,6},{3,7},{4,0},{5,1},{6,2},{7,3},{8,12},{9,13},{10,... | collective-permute-start | bytes 294920 | tf_op jit(solution)/shard_map/ppermute | solution.py:671
  28.2 4.8 %collective-permute-start.8 = (bf16[128,384]{1,0:T(8,128)(2,1)S(1)}, bf16[128,384]{1,0:T(8,128)(2,1)S(1)}, u32[]{:S(2)}, u32[]{:S(2)}) collective-permute-start(bf16[128,384]{1,0:T(8,128)(2,1)S(1)} %get-tuple-element.80), channel_id=1, source_target_pairs={{0,1},{1,0},{2,3},{3,2},{4,8},{5,9},{6,10},{7,11},{8,4},{9,5},{10,... | collective-permute-start | bytes 294920 | tf_op jit(solution)/shard_map/ppermute | solution.py:671
  34.5 8.7 %collective-permute-start.10 = (bf16[256,384]{1,0:T(8,128)(2,1)S(1)}, bf16[256,384]{1,0:T(8,128)(2,1)S(1)}, u32[]{:S(2)}, u32[]{:S(2)}) collective-permute-start(bf16[256,384]{1,0:T(8,128)(2,1)S(1)} %get-tuple-element.86), channel_id=1, source_target_pairs={{0,4},{1,5},{2,6},{3,7},{4,0},{5,1},{6,2},{7,3},{8,12},{9,13},{10,... | collective-permute-start | bytes 589832 | tf_op jit(solution)/shard_map/ppermute | solution.py:671
  35.8 7.4 %collective-permute-start.11 = (bf16[256,384]{1,0:T(8,128)(2,1)S(1)}, bf16[256,384]{1,0:T(8,128)(2,1)S(1)}, u32[]{:S(2)}, u32[]{:S(2)}) collective-permute-start(bf16[256,384]{1,0:T(8,128)(2,1)S(1)} %get-tuple-element.87), channel_id=1, source_target_pairs={{0,1},{1,0},{2,3},{3,2},{4,8},{5,9},{6,10},{7,11},{8,4},{9,5},{10,... | collective-permute-start | bytes 589832 | tf_op jit(solution)/shard_map/ppermute | solution.py:671
  37.7 10.7 %collective-permute-start.12 = (bf16[2,256,384]{2,1,0:T(8,128)(2,1)S(1)}, bf16[2,256,384]{2,1,0:T(8,128)(2,1)S(1)}, u32[]{:S(2)}, u32[]{:S(2)}) collective-permute-start(bf16[2,256,384]{2,1,0:T(8,128)(2,1)S(1)} %get-tuple-element.90), channel_id=1, source_target_pairs={{0,2},{1,3},{2,0},{3,1},{4,6},{5,7},{6,4},{7,5},{8,10},{9,11},{10,... | collective-permute-start | bytes 1179656 | tf_op jit(solution)/shard_map/ppermute | solution.py:668
  41.5 8.6 %collective-permute-start.14 = (bf16[256,384]{1,0:T(8,128)(2,1)S(1)}, bf16[256,384]{1,0:T(8,128)(2,1)S(1)}, u32[]{:S(2)}, u32[]{:S(2)}) collective-permute-start(bf16[256,384]{1,0:T(8,128)(2,1)S(1)} %get-tuple-element.92), channel_id=1, source_target_pairs={{0,4},{1,5},{2,6},{3,7},{4,0},{5,1},{6,2},{7,3},{8,12},{9,13},{10,... | collective-permute-start | bytes 589832 | tf_op jit(solution)/shard_map/ppermute | solution.py:671
  41.6 8.5 %collective-permute-start.15 = (bf16[256,384]{1,0:T(8,128)(2,1)S(1)}, bf16[256,384]{1,0:T(8,128)(2,1)S(1)}, u32[]{:S(2)}, u32[]{:S(2)}) collective-permute-start(bf16[256,384]{1,0:T(8,128)(2,1)S(1)} %get-tuple-element.93), channel_id=1, source_target_pairs={{0,1},{1,0},{2,3},{3,2},{4,8},{5,9},{6,10},{7,11},{8,4},{9,5},{10,... | collective-permute-start | bytes 589832 | tf_op jit(solution)/shard_map/ppermute | solution.py:671
  44.4 13.3 %collective-permute-start.13 = (bf16[2,256,384]{2,1,0:T(8,128)(2,1)S(1)}, bf16[2,256,384]{2,1,0:T(8,128)(2,1)S(1)}, u32[]{:S(2)}, u32[]{:S(2)}) collective-permute-start(bf16[2,256,384]{2,1,0:T(8,128)(2,1)S(1)} %get-tuple-element.91), channel_id=1, source_target_pairs={{0,2},{1,3},{2,0},{3,1},{4,6},{5,7},{6,4},{7,5},{8,10},{9,11},{10,... | collective-permute-start | bytes 1179656 | tf_op jit(solution)/shard_map/ppermute | solution.py:668
  47.4 5.9 %collective-permute-start.16 = (bf16[256,384]{1,0:T(8,128)(2,1)S(1)}, bf16[256,384]{1,0:T(8,128)(2,1)S(1)}, u32[]{:S(2)}, u32[]{:S(2)}) collective-permute-start(bf16[256,384]{1,0:T(8,128)(2,1)S(1)} %get-tuple-element.96), channel_id=1, source_target_pairs={{0,4},{1,5},{2,6},{3,7},{4,0},{5,1},{6,2},{7,3},{8,12},{9,13},{10,... | collective-permute-start | bytes 589832 | tf_op jit(solution)/shard_map/ppermute | solution.py:671
  48.5 4.8 %collective-permute-start.17 = (bf16[256,384]{1,0:T(8,128)(2,1)S(1)}, bf16[256,384]{1,0:T(8,128)(2,1)S(1)}, u32[]{:S(2)}, u32[]{:S(2)}) collective-permute-start(bf16[256,384]{1,0:T(8,128)(2,1)S(1)} %get-tuple-element.97), channel_id=1, source_target_pairs={{0,1},{1,0},{2,3},{3,2},{4,8},{5,9},{6,10},{7,11},{8,4},{9,5},{10,... | collective-permute-start | bytes 589832 | tf_op jit(solution)/shard_map/ppermute | solution.py:671
  54.5 9.5 %collective-permute-start.19 = (bf16[256,384]{1,0:T(8,128)(2,1)S(1)}, bf16[256,384]{1,0:T(8,128)(2,1)S(1)}, u32[]{:S(2)}, u32[]{:S(2)}) collective-permute-start(bf16[256,384]{1,0:T(8,128)(2,1)S(1)} %get-tuple-element.107), channel_id=1, source_target_pairs={{0,2},{1,3},{2,0},{3,1},{4,6},{5,7},{6,4},{7,5},{8,10},{9,11},{10,... | collective-permute-start | bytes 589832 | tf_op jit(solution)/shard_map/ppermute | solution.py:668
  54.8 10.7 %collective-permute-start.20 = (bf16[256,384]{1,0:T(8,128)(2,1)S(1)}, bf16[256,384]{1,0:T(8,128)(2,1)S(1)}, u32[]{:S(2)}, u32[]{:S(2)}) collective-permute-start(bf16[256,384]{1,0:T(8,128)(2,1)S(1)} %get-tuple-element.108), channel_id=1, source_target_pairs={{0,3},{1,2},{2,1},{3,0},{4,7},{5,6},{6,5},{7,4},{8,11},{9,10},{10,... | collective-permute-start | bytes 589832 | tf_op jit(solution)/shard_map/ppermute | solution.py:668
  57.8 3.2 %collective-permute-start.18 = (bf16[7,256,384]{2,1,0:T(8,128)(2,1)S(1)}, bf16[7,256,384]{2,1,0:T(8,128)(2,1)S(1)}, u32[]{:S(2)}, u32[]{:S(2)}) collective-permute-start(bf16[7,256,384]{2,1,0:T(8,128)(2,1)S(1)} %shard_map.52), channel_id=1, source_target_pairs={{0,1},{1,0},{2,3},{3,2},{4,5},{5,4},{6,7},{7,6},{8,9},{9,8},{10,11... | collective-permute-start | bytes 4128776 | tf_op jit(solution)/shard_map/ppermute | solution.py:668

commit v8 on v7

--- a/solution.py
+++ b/solution.py
@@ -622,18 +622,22 @@
     places, r, c = ys.shape[1:]
     last = out.shape[0] - 1
     writes = []
-    for i, (x, hidden) in enumerate(((x2, a2), (x3, a3))):
-        value = x[...].astype(F32) + dot(hidden[...], point[last])
-        ys[i] = value.astype(BF16).reshape(places, r, c)
-        writes.append(pltpu.make_async_copy(ys.at[i], out.at[last, :, s_ref[0] ^ (2 + i)], sems.at[i]))
-        writes[-1].start()
+    more = dot(jnp.concatenate([a2[...], a3[...]]), point[last])
+    for i, x in enumerate((x2, x3)):
+        for p in range(places):
+            rows = pl.ds(p * r, r)
+            at = (i * places + p) * r
+            ys[i, p] = (x[rows].astype(F32) + more[at : at + r]).astype(BF16)
+            to = out.at[last, p, s_ref[0] ^ (2 + i)]
+            writes.append(pltpu.make_async_copy(ys.at[i, p], to, sems.at[i, p]))
+            writes[-1].start()
     wait_all(writes)
 
 
 def late_outputs(scalars, hiddens, xs, point, before):
     blocks, places, group, r, c = before.shape
     operands = (scalars, *xs, point, before, *hiddens)
-    scratch = [pltpu.VMEM((2, places, r, c), BF16), pltpu.SemaphoreType.DMA((2,))]
+    scratch = [pltpu.VMEM((2, places, r, c), BF16), pltpu.SemaphoreType.DMA((2, places))]
     return call(
         late_out_kernel, array(*before.shape), operands,
         [SMEM] + [VMEM] * 3 + [HBM] + [VMEM] * 2, HBM, scratch,

time: 67.6 us -> 67.7 us (level)
  no operation moved by 1% of the time
where the time goes in v8:
time: 67.7 us; the launch traced here: 67.5 us
  Pallas kernels  35.7 us (53%)
  starting transfers between devices  23.8 us (35%)
  waiting for transfers between devices  7.09 us (10%)
    pallas_call x18, Pallas kernels, call(): pl.pallas_call(kernel, out_shape=outs, in_specs=specs, out_specs=out_spec...  35.7 us
    ppermute x11, starting transfers between devices, swap(): return lax.ppermute(value, 'seq', [(i, i ^ k) for i in range(size)])  11.7 us
    ppermute x5, starting transfers between devices, across(): lax.ppermute(odd, 'seq', odd_pairs)  7.2 us
    ppermute x11, waiting for transfers between devices, swap(): return lax.ppermute(value, 'seq', [(i, i ^ k) for i in range(size)])  6.13 us
    ppermute x5, starting transfers between devices, across(): lax.ppermute(even, 'seq', even_pairs)  4.89 us
  transfers between devices with their start and end apart: 21, of which 6 were waited for; matrix products, arithmetic and copies ran while one was open for 0% of the time, Pallas kernels for 43%

profile of v8, /device:TPU:1, one launch (start us, length us, event | category | flops | bytes accessed | tf_op | source)
XLA Modules:
  0.0 67.5 jit_solution(3271690885716571573)
XLA Ops:
  0.1 2.0 %shard_map.37 = (bf16[4,64,768]{2,1,0:T(8,128)(2,1)S(1)}, bf16[4,64,768]{2,1,0:T(8,128)(2,1)S(1)}, bf16[4,64,768]{2,1,0:T(8,128)(2,1)S(1)}, bf16[1,64,768]{2,1,0:T(8,128)(2,1)S(1)}, bf16[3,64,768]{2,1,0:T(8,128)(2,1)S(1)}) custom-call(s32[4]{0:T(128)S(1)} %pad_add_fusion.s_ref.parity_ref.refs_0_, bf16[4,4,64,768]{3,2,1,0:T(8,128)(2,1)} %bitcast.23), custom_call_target="tpu_custom_call" | custom-call | bytes 3145728 | tf_op jit(solution)/shard_map/pallas_call | solution.py:55
  2.2 2.7 %collective-permute-start.3 = (bf16[256,768]{1,0:T(8,128)(2,1)S(1)}, bf16[256,768]{1,0:T(8,128)(2,1)S(1)}, u32[]{:S(2)}, u32[]{:S(2)}) collective-permute-start(bf16[256,768]{1,0:T(8,128)(2,1)S(1)} %bitcast.19), channel_id=1, source_target_pairs={{0,2},{1,3},{2,0},{3,1},{4,6},{5,7},{6,4},{7,5},{8,10},{9,11},{10,... | collective-permute-start | bytes 1179656 | tf_op jit(solution)/shard_map/ppermute | solution.py:672
  4.9 3.3 %shard_map.38.w.refs_2_.refs_6_ = bf16[4,768,1152]{2,1,0:T(8,128)(2,1)S(1)} custom-call(bf16[4,3,768,384]{3,2,1,0:T(8,128)(2,1)} %taps.1), custom_call_target="tpu_custom_call" | custom-call | bytes 14155776 | tf_op jit(solution)/shard_map/pallas_call | solution.py:55
  8.7 3.5 %shard_map.39 = (bf16[1024,768]{1,0:T(8,128)(2,1)S(1)}, bf16[1088,384]{1,0:T(8,128)(2,1)S(1)}, f32[1024,384]{1,0:T(8,128)S(1)}, bf16[1088,384]{1,0:T(8,128)(2,1)...) custom-call(s32[4]{0:T(128)S(1)} %pad_add_fusion.s_ref.parity_ref.refs_0_, ...), custom_call_target="tpu_custom_call" | custom-call | flops 905969664 | bytes 1048576 | tf_op jit(solution)/shard_map/pallas_call | solution.py:55
  12.2 2.1 %collective-permute-done.3.refs_0_.over = bf16[256,768]{1,0:T(8,128)(2,1)S(1)} collective-permute-done((bf16[256,768]{1,0:T(8,128)(2,1)S(1)}, bf16[256,768]{1,0:T(8,128)(2,1)S(1)}, u32[]{:S(2)}, u32[]{:S(2)}) %collective-permute-start.3) | collective-permute-done | bytes 393248 | tf_op jit(solution)/shard_map/ppermute | solution.py:672
  14.3 1.0 %collective-permute-start.4 = (bf16[64,768]{1,0:T(8,128)(2,1)S(1)}, bf16[64,768]{1,0:T(8,128)(2,1)S(1)}, u32[]{:S(2)}, u32[]{:S(2)}) collective-permute-start(bf16[64,768]{1,0:T(8,128)(2,1)S(1)} %shard_map.40), channel_id=1, source_target_pairs={{0,1},{1,0},{2,3},{3,2},{4,5},{5,4},{6,7},{7,6},{8,9},{9,8},{10,11... | collective-permute-start | bytes 294920 | tf_op jit(solution)/shard_map/ppermute | solution.py:672
  15.3 1.7 %collective-permute-start.2 = (bf16[64,768]{1,0:T(8,128)(2,1)S(1)}, bf16[64,768]{1,0:T(8,128)(2,1)S(1)}, u32[]{:S(2)}, u32[]{:S(2)}) collective-permute-start(bf16[64,768]{1,0:T(8,128)(2,1)S(1)} %bitcast.22), channel_id=1, source_target_pairs={{0,2},{1,3},{2,0},{3,1},{4,6},{5,7},{6,4},{7,5},{8,10},{9,11},{10,... | collective-permute-start | bytes 294920 | tf_op jit(solution)/shard_map/ppermute | solution.py:672
  17.8 1.4 %collective-permute-start.5 = (bf16[64,384]{1,0:T(8,128)(2,1)S(1)}, bf16[64,384]{1,0:T(8,128)(2,1)S(1)}, u32[]{:S(2)}, u32[]{:S(2)}) collective-permute-start(bf16[64,384]{1,0:T(8,128)(2,1)S(1)} %get-tuple-element.73), channel_id=1, source_target_pairs={{0,4},{1,5},{2,6},{3,7},{4,0},{5,1},{6,2},{7,3},{8,12},{9,13},{10,... | collective-permute-start | bytes 147464 | tf_op jit(solution)/shard_map/ppermute | solution.py:675
  19.8 1.2 %shard_map.41 = (bf16[1024,768]{1,0:T(8,128)(2,1)S(1)}, bf16[1088,384]{1,0:T(8,128)(2,1)S(1)}, f32[1024,384]{1,0:T(8,128)S(1)}, bf16[1088,384]{1,0:T(8,128)(2,1)S(1)}) custom-call(s32[4]{0:T(128)S(1)} %pad_add_fusion.s_ref.parity_ref.refs_0_, ...), custom_call_target="tpu_custom_call", output_to_operand_aliasing={{0}: (4, {}), {1}: (5, {}), {2}: (6, {}), {3}: (7, {})} | custom-call | flops 452984832 | bytes 1048576 | tf_op jit(solution)/shard_map/pallas_call | solution.py:55
  21.1 1.6 %collective-permute-done.2.last = bf16[64,768]{1,0:T(8,128)(2,1)S(1)} collective-permute-done((bf16[64,768]{1,0:T(8,128)(2,1)S(1)}, bf16[64,768]{1,0:T(8,128)(2,1)S(1)}, u32[]{:S(2)}, u32[]{:S(2)}) %collective-permute-start.2) | collective-permute-done | bytes 98336 | tf_op jit(solution)/shard_map/ppermute | solution.py:672
  22.7 2.9 %shard_map.43 = (bf16[128,384]{1,0:T(8,128)(2,1)S(1)}, bf16[128,384]{1,0:T(8,128)(2,1)S(1)}, bf16[2,256,384]{2,1,0:T(8,128)(2,1)S(1)}, bf16[256,384]{1,0:T(8,128...) custom-call(s32[4]{0:T(128)S(1)} %pad_add_fusion.s_ref.parity_ref.re, ...), custom_call_target="tpu_custom_call", output_to_operand_aliasing={{4}: (3, {}), {5}: (4, {}), {6}: (5, {}), {7}: (6, {}), {8}... | custom-call | flops 2415919104 | bytes 4194304 | tf_op jit(solution)/shard_map/pallas_call | solution.py:55
  25.6 1.3 %collective-permute-start.9 = (bf16[2,256,384]{2,1,0:T(8,128)(2,1)S(1)}, bf16[2,256,384]{2,1,0:T(8,128)(2,1)S(1)}, u32[]{:S(2)}, u32[]{:S(2)}) collective-permute-start(bf16[2,256,384]{2,1,0:T(8,128)(2,1)S(1)} %get-tuple-element.82), channel_id=1, source_target_pairs={{0,2},{1,3},{2,0},{3,1},{4,6},{5,7},{6,4},{7,5},{8,10},{9,11},{10,... | collective-permute-start | bytes 1179656 | tf_op jit(solution)/shard_map/ppermute | solution.py:672
  26.9 1.3 %collective-permute-start.7 = (bf16[128,384]{1,0:T(8,128)(2,1)S(1)}, bf16[128,384]{1,0:T(8,128)(2,1)S(1)}, u32[]{:S(2)}, u32[]{:S(2)}) collective-permute-start(bf16[128,384]{1,0:T(8,128)(2,1)S(1)} %get-tuple-element.79), channel_id=1, source_target_pairs={{0,4},{1,5},{2,6},{3,7},{4,0},{5,1},{6,2},{7,3},{8,12},{9,13},{10,... | collective-permute-start | bytes 294920 | tf_op jit(solution)/shard_map/ppermute | solution.py:675
  28.2 1.4 %collective-permute-start.8 = (bf16[128,384]{1,0:T(8,128)(2,1)S(1)}, bf16[128,384]{1,0:T(8,128)(2,1)S(1)}, u32[]{:S(2)}, u32[]{:S(2)}) collective-permute-start(bf16[128,384]{1,0:T(8,128)(2,1)S(1)} %get-tuple-element.80), channel_id=1, source_target_pairs={{0,1},{1,0},{2,3},{3,2},{4,8},{5,9},{6,10},{7,11},{8,4},{9,5},{10,... | collective-permute-start | bytes 294920 | tf_op jit(solution)/shard_map/ppermute | solution.py:675
  29.6 3.3 %shard_map.44 = (bf16[1024,768]{1,0:T(8,128)(2,1)S(1)}, bf16[1024,384]{1,0:T(8,128)(2,1)S(1)}, f32[256,384]{1,0:T(8,128)S(1)}) custom-call(s32[4]{0:T(128)S(1)} %pad_add_fusion.s_ref.parity_ref.refs_0_, bf16[1024,768]{1,0:T(8,128)(2,1)S(1)} %get-tuple-element.75.x, bf16[4,768,1152]{2,1,0:T(8,128)(2,1)S(1)} %shard_map.38.w.refs_2_.refs_6_, ...), custom_call_target="tpu_custom_call" | custom-call | flops 2415919104 | bytes 4194304 | tf_op jit(solution)/shard_map/pallas_call | solution.py:55
  33.0 1.5 %shard_map.45 = (bf16[1024,768]{1,0:T(8,128)(2,1)S(1)}, bf16[256,384]{1,0:T(8,128)(2,1)S(1)}, bf16[256,384]{1,0:T(8,128)(2,1)S(1)}, bf16[2,256,384]{2,1,0:T(8,128)(2,1)S(1)}, bf16[256,384]{1,0:T(8,128)(2,1)S(1)}) custom-call(s32[4]{0:T(128)S(1)} %pad_add_fusion.s_ref.parity_ref.refs_0_, ...), custom_call_target="tpu_custom_call", output_to_operand_aliasing={{0}: (1, {})} | custom-call | flops 452984832 | bytes 4194304 | tf_op jit(solution)/shard_map/pallas_call | solution.py:55
  34.5 1.3 %collective-permute-start.10 = (bf16[256,384]{1,0:T(8,128)(2,1)S(1)}, bf16[256,384]{1,0:T(8,128)(2,1)S(1)}, u32[]{:S(2)}, u32[]{:S(2)}) collective-permute-start(bf16[256,384]{1,0:T(8,128)(2,1)S(1)} %get-tuple-element.86), channel_id=1, source_target_pairs={{0,4},{1,5},{2,6},{3,7},{4,0},{5,1},{6,2},{7,3},{8,12},{9,13},{10,... | collective-permute-start | bytes 589832 | tf_op jit(solution)/shard_map/ppermute | solution.py:675
  35.8 2.0 %collective-permute-start.11 = (bf16[256,384]{1,0:T(8,128)(2,1)S(1)}, bf16[256,384]{1,0:T(8,128)(2,1)S(1)}, u32[]{:S(2)}, u32[]{:S(2)}) collective-permute-start(bf16[256,384]{1,0:T(8,128)(2,1)S(1)} %get-tuple-element.87), channel_id=1, source_target_pairs={{0,1},{1,0},{2,3},{3,2},{4,8},{5,9},{6,10},{7,11},{8,4},{9,5},{10,... | collective-permute-start | bytes 589832 | tf_op jit(solution)/shard_map/ppermute | solution.py:675
  38.0 3.6 %shard_map.46 = (bf16[1024,768]{1,0:T(8,128)(2,1)S(1)}, bf16[1024,384]{1,0:T(8,128)(2,1)S(1)}, f32[512,384]{1,0:T(8,128)S(1)}, bf16[256,384]{1,0:T(8,128)(2,1)S(1)}, bf16[256,384]{1,0:T(8,128)(2,1)S(1)}) custom-call(s32[4]{0:T(128)S(1)} %pad_add_fusion.s_ref.parity_ref.refs_0_, bf16[1024,768]{1,0:T(8,128)(2,1)S(1)} %get-tuple-element.81.refs_1_, ...), custom_call_target="tpu_custom_call" | custom-call | flops 2415919104 | bytes 4194304 | tf_op jit(solution)/shard_map/pallas_call | solution.py:55
  41.6 1.6 %collective-permute-start.15 = (bf16[256,384]{1,0:T(8,128)(2,1)S(1)}, bf16[256,384]{1,0:T(8,128)(2,1)S(1)}, u32[]{:S(2)}, u32[]{:S(2)}) collective-permute-start(bf16[256,384]{1,0:T(8,128)(2,1)S(1)} %get-tuple-element.93), channel_id=1, source_target_pairs={{0,1},{1,0},{2,3},{3,2},{4,8},{5,9},{6,10},{7,11},{8,4},{9,5},{10,... | collective-permute-start | bytes 589832 | tf_op jit(solution)/shard_map/ppermute | solution.py:675
  43.2 1.1 %shard_map.47 = (bf16[2,256,384]{2,1,0:T(8,128)(2,1)S(1)}, bf16[2,256,384]{2,1,0:T(8,128)(2,1)S(1)}) custom-call(s32[4]{0:T(128)S(1)} %pad_add_fusion.s_ref.parity_ref.refs_0_, bf16[1024,384]{1,0:T(8,128)(2,1)S(1)} %get-tuple-element.84.hidden.refs_2_, f32[512,384]{1,0:T(8,128)S(1)} %get-tuple-element.85.part, ...), custom_call_target="tpu_custom_call" | custom-call | flops 3932160 | bytes 1048576 | tf_op jit(solution)/shard_map/pallas_call | solution.py:55
  44.4 1.3 %collective-permute-start.13 = (bf16[2,256,384]{2,1,0:T(8,128)(2,1)S(1)}, bf16[2,256,384]{2,1,0:T(8,128)(2,1)S(1)}, u32[]{:S(2)}, u32[]{:S(2)}) collective-permute-start(bf16[2,256,384]{2,1,0:T(8,128)(2,1)S(1)} %get-tuple-element.91), channel_id=1, source_target_pairs={{0,2},{1,3},{2,0},{3,1},{4,6},{5,7},{6,4},{7,5},{8,10},{9,11},{10,... | collective-permute-start | bytes 1179656 | tf_op jit(solution)/shard_map/ppermute | solution.py:672
  45.7 1.7 %shard_map.48 = (bf16[1024,768]{1,0:T(8,128)(2,1)S(1)}, bf16[256,384]{1,0:T(8,128)(2,1)S(1)}, bf16[256,384]{1,0:T(8,128)(2,1)S(1)}) custom-call(s32[4]{0:T(128)S(1)} %pad_add_fusion.s_ref.parity_ref.refs_0_, bf16[1024,768]{1,0:T(8,128)(2,1)S(1)} %get-tuple-element.83.x, ...), custom_call_target="tpu_custom_call", output_to_operand_aliasing={{0}: (1, {})} | custom-call | flops 603979776 | bytes 2097152 | tf_op jit(solution)/shard_map/pallas_call | solution.py:55
  48.5 1.6 %collective-permute-start.17 = (bf16[256,384]{1,0:T(8,128)(2,1)S(1)}, bf16[256,384]{1,0:T(8,128)(2,1)S(1)}, u32[]{:S(2)}, u32[]{:S(2)}) collective-permute-start(bf16[256,384]{1,0:T(8,128)(2,1)S(1)} %get-tuple-element.97), channel_id=1, source_target_pairs={{0,1},{1,0},{2,3},{3,2},{4,8},{5,9},{6,10},{7,11},{8,4},{9,5},{10,... | collective-permute-start | bytes 589832 | tf_op jit(solution)/shard_map/ppermute | solution.py:675
  50.1 2.2 %shard_map.49 = (bf16[2,256,384]{2,1,0:T(8,128)(2,1)S(1)}, f32[512,384]{1,0:T(8,128)S(1)}, bf16[256,384]{1,0:T(8,128)(2,1)S(1)}) custom-call(s32[4]{0:T(128)S(1)} %pad_add_fusion.s_ref.parity_ref.refs_0_, bf16[1024,768]{1,0:T(8,128)(2,1)S(1)} %get-tuple-element.89.refs_1_, bf16[1024,384]{1,0:T(8,128)(2,1)S(1)} %get-tuple-element.84.hidden.refs_2_, ...), custom_call_target="tpu_custom_call" | custom-call | flops 2400000000 | bytes 4194304 | tf_op jit(solution)/shard_map/pallas_call | solution.py:55
  52.4 0.9 %collective-permute-done.16.from_even = bf16[256,384]{1,0:T(8,128)(2,1)S(1)} collective-permute-done((bf16[256,384]{1,0:T(8,128)(2,1)S(1)}, bf16[256,384]{1,0:T(8,128)(2,1)S(1)}, u32[]{:S(2)}, u32[]{:S(2)}) %collective-permute-start.16) | collective-permute-done | bytes 196640 | tf_op jit(solution)/shard_map/ppermute | solution.py:675
  53.3 1.2 %shard_map.50 = (bf16[256,384]{1,0:T(8,128)(2,1)S(1)}, bf16[256,384]{1,0:T(8,128)(2,1)S(1)}, bf16[256,384]{1,0:T(8,128)(2,1)S(1)}, bf16[256,384]{1,0:T(8,128)(2,1)S(1)}) custom-call(s32[4]{0:T(128)S(1)} %pad_add_fusion.s_ref.parity_ref.refs_0_, bf16[2,256,384]{2,1,0:T(8,128)(2,1)S(1)} %get-tuple-element.94.outer, f32[512,384]{1,0:T(8,128)S(1)} %get-tuple-element.95.near, ...), custom_call_target="tpu_custom_call" | custom-call | flops 3932160 | bytes 2097152 | tf_op jit(solution)/shard_map/pallas_call | solution.py:55
  54.8 2.9 %collective-permute-start.20 = (bf16[256,384]{1,0:T(8,128)(2,1)S(1)}, bf16[256,384]{1,0:T(8,128)(2,1)S(1)}, u32[]{:S(2)}, u32[]{:S(2)}) collective-permute-start(bf16[256,384]{1,0:T(8,128)(2,1)S(1)} %get-tuple-element.108), channel_id=1, source_target_pairs={{0,3},{1,2},{2,1},{3,0},{4,7},{5,6},{6,5},{7,4},{8,11},{9,10},{10,... | collective-permute-start | bytes 589832 | tf_op jit(solution)/shard_map/ppermute | solution.py:672
  57.9 2.4 %shard_map.51 = (bf16[4,4,4,64,768]{4,3,2,1,0:T(8,128)(2,1)}, bf16[256,768]{1,0:T(8,128)(2,1)S(1)}) custom-call(s32[4]{0:T(128)S(1)} %pad_add_fusion.s_ref.parity_ref.refs_0_, bf16[3,4,64,768]{3,2,1,0:T(8,128)(2,1)S(1)} %get-tuple-element.59.x, bf16[16,64,768]{2,1,0:T(8,128)(2,1)S(1)} %bitcast.14, bf16[16,64,768]{2,1,0:T(8,128)(2,1)S(1)} %bitcast.15, ...), custom_call_target="tpu_custom_call" | custom-call | flops 49999998976 | bytes 8388608 | tf_op jit(solution)/shard_map/pallas_call | solution.py:55
  61.0 3.0 %shard_map.53 = (bf16[4,4,4,64,768]{4,3,2,1,0:T(8,128)(2,1)}, bf16[256,768]{1,0:T(8,128)(2,1)S(1)}) custom-call(s32[4]{0:T(128)S(1)} %pad_add_fusion.s_ref.parity_ref.refs_0_, bf16[3,4,64,768]{3,2,1,0:T(8,128)(2,1)S(1)} %get-tuple-element.59.x, bf16[7,256,384]{2,1,0:T(8,128)(2,1)S(1)} %collective-permute-done.18.core, ...), custom_call_target="tpu_custom_call", output_to_operand_aliasing={{0}: (4, {})} | custom-call | flops 905969664 | bytes 4194304 | tf_op jit(solution)/shard_map/pallas_call | solution.py:55
  64.0 1.5 %collective-permute-done.20.a3 = bf16[256,384]{1,0:T(8,128)(2,1)S(1)} collective-permute-done((bf16[256,384]{1,0:T(8,128)(2,1)S(1)}, bf16[256,384]{1,0:T(8,128)(2,1)S(1)}, u32[]{:S(2)}, u32[]{:S(2)}) %collective-permute-start.20) | collective-permute-done | bytes 196640 | tf_op jit(solution)/shard_map/ppermute | solution.py:672
  65.4 1.9 %shard_map.54 = bf16[4,4,4,64,768]{4,3,2,1,0:T(8,128)(2,1)} custom-call(s32[4]{0:T(128)S(1)} %pad_add_fusion.s_ref.parity_ref.refs_0_, bf16[256,768]{1,0:T(8,128)(2,1)S(1)} %get-tuple-element.99.x2, bf16[256,768]{1,0:T(8,128)(2,1)S(1)} %get-tuple-element.105.x3, bf16[4,384,768]{2,1,0:T(8,128)(2,1)S(1)} %copy-done, ...), custom_call_target="tpu_custom_call", output_to_operand_aliasing={{}: (4, {})} | custom-call | flops 301989888 | bytes 2097152 | tf_op jit(solution)/shard_map/pallas_call | solution.py:55
  (31 shorter events, 5.0 us)
Async XLA Ops:
  2.1 6.1 %collective-permute-start = (bf16[256,768]{1,0:T(8,128)(2,1)S(1)}, bf16[256,768]{1,0:T(8,128)(2,1)S(1)}, u32[]{:S(2)}, u32[]{:S(2)}) collective-permute-start(bf16[256,768]{1,0:T(8,128)(2,1)S(1)} %bitcast.20), channel_id=1, source_target_pairs={{0,1},{1,0},{2,3},{3,2},{4,5},{5,4},{6,7},{7,6},{8,9},{9,8},{10,11... | collective-permute-start | bytes 1179656 | tf_op jit(solution)/shard_map/ppermute | solution.py:672
  2.2 12.1 %collective-permute-start.3 = (bf16[256,768]{1,0:T(8,128)(2,1)S(1)}, bf16[256,768]{1,0:T(8,128)(2,1)S(1)}, u32[]{:S(2)}, u32[]{:S(2)}) collective-permute-start(bf16[256,768]{1,0:T(8,128)(2,1)S(1)} %bitcast.19), channel_id=1, source_target_pairs={{0,2},{1,3},{2,0},{3,1},{4,6},{5,7},{6,4},{7,5},{8,10},{9,11},{10,... | collective-permute-start | bytes 1179656 | tf_op jit(solution)/shard_map/ppermute | solution.py:672
  4.9 17.8 %collective-permute-start.1 = (bf16[192,768]{1,0:T(8,128)(2,1)S(1)}, bf16[192,768]{1,0:T(8,128)(2,1)S(1)}, u32[]{:S(2)}, u32[]{:S(2)}) collective-permute-start(bf16[192,768]{1,0:T(8,128)(2,1)S(1)} %bitcast.21), channel_id=1, source_target_pairs={{0,3},{1,2},{2,1},{3,0},{4,7},{5,6},{6,5},{7,4},{8,11},{9,10},{10,... | collective-permute-start | bytes 884744 | tf_op jit(solution)/shard_map/ppermute | solution.py:672
  4.9 3.8 %copy-start = (bf16[4,384,768]{2,1,0:T(8,128)(2,1)S(1)}, bf16[4,384,768]{2,1,0:T(8,128)(2,1)}, u32[]{:S(2)}) copy-start(bf16[4,384,768]{2,1,0:T(8,128)(2,1)} %point.13) | copy-start | bytes 7077892
  14.3 2.7 %collective-permute-start.4 = (bf16[64,768]{1,0:T(8,128)(2,1)S(1)}, bf16[64,768]{1,0:T(8,128)(2,1)S(1)}, u32[]{:S(2)}, u32[]{:S(2)}) collective-permute-start(bf16[64,768]{1,0:T(8,128)(2,1)S(1)} %shard_map.40), channel_id=1, source_target_pairs={{0,1},{1,0},{2,3},{3,2},{4,5},{5,4},{6,7},{7,6},{8,9},{9,8},{10,11... | collective-permute-start | bytes 294920 | tf_op jit(solution)/shard_map/ppermute | solution.py:672
  15.3 7.4 %collective-permute-start.2 = (bf16[64,768]{1,0:T(8,128)(2,1)S(1)}, bf16[64,768]{1,0:T(8,128)(2,1)S(1)}, u32[]{:S(2)}, u32[]{:S(2)}) collective-permute-start(bf16[64,768]{1,0:T(8,128)(2,1)S(1)} %bitcast.22), channel_id=1, source_target_pairs={{0,2},{1,3},{2,0},{3,1},{4,6},{5,7},{6,4},{7,5},{8,10},{9,11},{10,... | collective-permute-start | bytes 294920 | tf_op jit(solution)/shard_map/ppermute | solution.py:672
  17.8 4.9 %collective-permute-start.5 = (bf16[64,384]{1,0:T(8,128)(2,1)S(1)}, bf16[64,384]{1,0:T(8,128)(2,1)S(1)}, u32[]{:S(2)}, u32[]{:S(2)}) collective-permute-start(bf16[64,384]{1,0:T(8,128)(2,1)S(1)} %get-tuple-element.73), channel_id=1, source_target_pairs={{0,4},{1,5},{2,6},{3,7},{4,0},{5,1},{6,2},{7,3},{8,12},{9,13},{10,... | collective-permute-start | bytes 147464 | tf_op jit(solution)/shard_map/ppermute | solution.py:675
  19.2 3.5 %collective-permute-start.6 = (bf16[64,384]{1,0:T(8,128)(2,1)S(1)}, bf16[64,384]{1,0:T(8,128)(2,1)S(1)}, u32[]{:S(2)}, u32[]{:S(2)}) collective-permute-start(bf16[64,384]{1,0:T(8,128)(2,1)S(1)} %get-tuple-element.74), channel_id=1, source_target_pairs={{0,1},{1,0},{2,3},{3,2},{4,8},{5,9},{6,10},{7,11},{8,4},{9,5},{10,... | collective-permute-start | bytes 147464 | tf_op jit(solution)/shard_map/ppermute | solution.py:675
  25.6 12.4 %collective-permute-start.9 = (bf16[2,256,384]{2,1,0:T(8,128)(2,1)S(1)}, bf16[2,256,384]{2,1,0:T(8,128)(2,1)S(1)}, u32[]{:S(2)}, u32[]{:S(2)}) collective-permute-start(bf16[2,256,384]{2,1,0:T(8,128)(2,1)S(1)} %get-tuple-element.82), channel_id=1, source_target_pairs={{0,2},{1,3},{2,0},{3,1},{4,6},{5,7},{6,4},{7,5},{8,10},{9,11},{10,... | collective-permute-start | bytes 1179656 | tf_op jit(solution)/shard_map/ppermute | solution.py:672
  26.9 6.1 %collective-permute-start.7 = (bf16[128,384]{1,0:T(8,128)(2,1)S(1)}, bf16[128,384]{1,0:T(8,128)(2,1)S(1)}, u32[]{:S(2)}, u32[]{:S(2)}) collective-permute-start(bf16[128,384]{1,0:T(8,128)(2,1)S(1)} %get-tuple-element.79), channel_id=1, source_target_pairs={{0,4},{1,5},{2,6},{3,7},{4,0},{5,1},{6,2},{7,3},{8,12},{9,13},{10,... | collective-permute-start | bytes 294920 | tf_op jit(solution)/shard_map/ppermute | solution.py:675
  28.2 4.8 %collective-permute-start.8 = (bf16[128,384]{1,0:T(8,128)(2,1)S(1)}, bf16[128,384]{1,0:T(8,128)(2,1)S(1)}, u32[]{:S(2)}, u32[]{:S(2)}) collective-permute-start(bf16[128,384]{1,0:T(8,128)(2,1)S(1)} %get-tuple-element.80), channel_id=1, source_target_pairs={{0,1},{1,0},{2,3},{3,2},{4,8},{5,9},{6,10},{7,11},{8,4},{9,5},{10,... | collective-permute-start | bytes 294920 | tf_op jit(solution)/shard_map/ppermute | solution.py:675
  34.5 8.7 %collective-permute-start.10 = (bf16[256,384]{1,0:T(8,128)(2,1)S(1)}, bf16[256,384]{1,0:T(8,128)(2,1)S(1)}, u32[]{:S(2)}, u32[]{:S(2)}) collective-permute-start(bf16[256,384]{1,0:T(8,128)(2,1)S(1)} %get-tuple-element.86), channel_id=1, source_target_pairs={{0,4},{1,5},{2,6},{3,7},{4,0},{5,1},{6,2},{7,3},{8,12},{9,13},{10,... | collective-permute-start | bytes 589832 | tf_op jit(solution)/shard_map/ppermute | solution.py:675
  35.8 7.4 %collective-permute-start.11 = (bf16[256,384]{1,0:T(8,128)(2,1)S(1)}, bf16[256,384]{1,0:T(8,128)(2,1)S(1)}, u32[]{:S(2)}, u32[]{:S(2)}) collective-permute-start(bf16[256,384]{1,0:T(8,128)(2,1)S(1)} %get-tuple-element.87), channel_id=1, source_target_pairs={{0,1},{1,0},{2,3},{3,2},{4,8},{5,9},{6,10},{7,11},{8,4},{9,5},{10,... | collective-permute-start | bytes 589832 | tf_op jit(solution)/shard_map/ppermute | solution.py:675
  37.7 10.7 %collective-permute-start.12 = (bf16[2,256,384]{2,1,0:T(8,128)(2,1)S(1)}, bf16[2,256,384]{2,1,0:T(8,128)(2,1)S(1)}, u32[]{:S(2)}, u32[]{:S(2)}) collective-permute-start(bf16[2,256,384]{2,1,0:T(8,128)(2,1)S(1)} %get-tuple-element.90), channel_id=1, source_target_pairs={{0,2},{1,3},{2,0},{3,1},{4,6},{5,7},{6,4},{7,5},{8,10},{9,11},{10,... | collective-permute-start | bytes 1179656 | tf_op jit(solution)/shard_map/ppermute | solution.py:672
  41.5 8.6 %collective-permute-start.14 = (bf16[256,384]{1,0:T(8,128)(2,1)S(1)}, bf16[256,384]{1,0:T(8,128)(2,1)S(1)}, u32[]{:S(2)}, u32[]{:S(2)}) collective-permute-start(bf16[256,384]{1,0:T(8,128)(2,1)S(1)} %get-tuple-element.92), channel_id=1, source_target_pairs={{0,4},{1,5},{2,6},{3,7},{4,0},{5,1},{6,2},{7,3},{8,12},{9,13},{10,... | collective-permute-start | bytes 589832 | tf_op jit(solution)/shard_map/ppermute | solution.py:675
  41.6 8.5 %collective-permute-start.15 = (bf16[256,384]{1,0:T(8,128)(2,1)S(1)}, bf16[256,384]{1,0:T(8,128)(2,1)S(1)}, u32[]{:S(2)}, u32[]{:S(2)}) collective-permute-start(bf16[256,384]{1,0:T(8,128)(2,1)S(1)} %get-tuple-element.93), channel_id=1, source_target_pairs={{0,1},{1,0},{2,3},{3,2},{4,8},{5,9},{6,10},{7,11},{8,4},{9,5},{10,... | collective-permute-start | bytes 589832 | tf_op jit(solution)/shard_map/ppermute | solution.py:675
  44.4 13.3 %collective-permute-start.13 = (bf16[2,256,384]{2,1,0:T(8,128)(2,1)S(1)}, bf16[2,256,384]{2,1,0:T(8,128)(2,1)S(1)}, u32[]{:S(2)}, u32[]{:S(2)}) collective-permute-start(bf16[2,256,384]{2,1,0:T(8,128)(2,1)S(1)} %get-tuple-element.91), channel_id=1, source_target_pairs={{0,2},{1,3},{2,0},{3,1},{4,6},{5,7},{6,4},{7,5},{8,10},{9,11},{10,... | collective-permute-start | bytes 1179656 | tf_op jit(solution)/shard_map/ppermute | solution.py:672
  47.4 5.9 %collective-permute-start.16 = (bf16[256,384]{1,0:T(8,128)(2,1)S(1)}, bf16[256,384]{1,0:T(8,128)(2,1)S(1)}, u32[]{:S(2)}, u32[]{:S(2)}) collective-permute-start(bf16[256,384]{1,0:T(8,128)(2,1)S(1)} %get-tuple-element.96), channel_id=1, source_target_pairs={{0,4},{1,5},{2,6},{3,7},{4,0},{5,1},{6,2},{7,3},{8,12},{9,13},{10,... | collective-permute-start | bytes 589832 | tf_op jit(solution)/shard_map/ppermute | solution.py:675
  48.5 4.8 %collective-permute-start.17 = (bf16[256,384]{1,0:T(8,128)(2,1)S(1)}, bf16[256,384]{1,0:T(8,128)(2,1)S(1)}, u32[]{:S(2)}, u32[]{:S(2)}) collective-permute-start(bf16[256,384]{1,0:T(8,128)(2,1)S(1)} %get-tuple-element.97), channel_id=1, source_target_pairs={{0,1},{1,0},{2,3},{3,2},{4,8},{5,9},{6,10},{7,11},{8,4},{9,5},{10,... | collective-permute-start | bytes 589832 | tf_op jit(solution)/shard_map/ppermute | solution.py:675
  54.5 9.5 %collective-permute-start.19 = (bf16[256,384]{1,0:T(8,128)(2,1)S(1)}, bf16[256,384]{1,0:T(8,128)(2,1)S(1)}, u32[]{:S(2)}, u32[]{:S(2)}) collective-permute-start(bf16[256,384]{1,0:T(8,128)(2,1)S(1)} %get-tuple-element.107), channel_id=1, source_target_pairs={{0,2},{1,3},{2,0},{3,1},{4,6},{5,7},{6,4},{7,5},{8,10},{9,11},{10,... | collective-permute-start | bytes 589832 | tf_op jit(solution)/shard_map/ppermute | solution.py:672
  54.8 10.7 %collective-permute-start.20 = (bf16[256,384]{1,0:T(8,128)(2,1)S(1)}, bf16[256,384]{1,0:T(8,128)(2,1)S(1)}, u32[]{:S(2)}, u32[]{:S(2)}) collective-permute-start(bf16[256,384]{1,0:T(8,128)(2,1)S(1)} %get-tuple-element.108), channel_id=1, source_target_pairs={{0,3},{1,2},{2,1},{3,0},{4,7},{5,6},{6,5},{7,4},{8,11},{9,10},{10,... | collective-permute-start | bytes 589832 | tf_op jit(solution)/shard_map/ppermute | solution.py:672
  57.8 3.2 %collective-permute-start.18 = (bf16[7,256,384]{2,1,0:T(8,128)(2,1)S(1)}, bf16[7,256,384]{2,1,0:T(8,128)(2,1)S(1)}, u32[]{:S(2)}, u32[]{:S(2)}) collective-permute-start(bf16[7,256,384]{2,1,0:T(8,128)(2,1)S(1)} %shard_map.52), channel_id=1, source_target_pairs={{0,1},{1,0},{2,3},{3,2},{4,5},{5,4},{6,7},{7,6},{8,9},{9,8},{10,11... | collective-permute-start | bytes 4128776 | tf_op jit(solution)/shard_map/ppermute | solution.py:672
